TPU v7x, 32 devices: a whole 2x2x4 slice. The times are simulated.
32 devices in a mesh: space: 8 (over z, x), mode: 4 (over y, core).
Axes of the slice: x: 2, y: 2, z: 4, core: 2. Of those that a mesh axis runs over, the one named last changes fastest.
Arguments:
- chaos_field: float32 [84, 8, 128, 128], P('mode', 'space'), may hold values from -6 to 6
- mean_field: float32 [8, 128, 128], P('space'), may hold values from 0.5 to 2
- kl_fields: float32 [6, 8, 128, 128], P(None, 'space'), may hold values from -1.8 to 1.8
- pattern: int32 [7, 84, 84], replicated, may hold values from 0 to 1, as said below
- coupling: float32 [7, 84, 84], replicated, as said below
- slot_mode: int32 [84], replicated, may hold values from 0 to 83, each once
Outputs:
- product: float32 [84, 8, 128, 128], P('mode', 'space')
Inputs may be any that keep to these rules, and one draw needn't show every extreme that they name: Modes are the 84 multi-indices of total degree at most 3 in 6 variables; pattern[0] is the identity; each term k >= 1 belongs to one variable, each variable to one term, and pattern[k, a, b] is 1 exactly where the multi-indices of modes a and b differ by one in that variable and agree elsewhere. coupling[0] is the identity; for k >= 1, coupling[k, a, b] is the square root of the larger of the two degrees in the term's variable where pattern[k, a, b] is 1, and zero elsewhere; pattern and coupling name the same variable for each term. `slot_mode`: each slot holds a different chaos mode.
All inputs are finite; a program needn't handle non-finite values.
Results may differ from a plain program's by a relative error of at most 0.000082.
Values sent between devices are 32-bit elements; how exact they have to be, the bound alone decides.
No kernel may reach another device: no remote copies, remote signals or barrier semaphores. Data moves between devices by JAX's collectives and lax.ppermute only.
A program may use at most 320 MiB of HBM per device.

v0:
```python
import jax
import jax.numpy as jnp
from jax import lax
from jax.sharding import PartitionSpec as P


def with_halo(block, sides, width):
    for axis, dim in sides:
        count = lax.axis_size(axis)
        forward = [(i, i + 1) for i in range(count - 1)]
        backward = [(target, source) for source, target in forward]
        low = lax.ppermute(
            lax.slice_in_dim(block, block.shape[dim] - width, None, axis=dim), axis, forward
        )
        high = lax.ppermute(lax.slice_in_dim(block, 0, width, axis=dim), axis, backward)
        block = jnp.concatenate([low, block, high], axis=dim)
    return block


def face_weights(coef_ext):
    coef_here = coef_ext[:, 1:-1]
    height = coef_here.shape[2]
    breadth = coef_here.shape[3]
    coef_pad = jnp.pad(coef_here, ((0, 0), (0, 0), (1, 1), (1, 1)))
    weights = [0.5 * (coef_here + coef_ext[:, 2:]), 0.5 * (coef_here + coef_ext[:, :-2])]
    for shift_y, shift_x in ((2, 1), (0, 1), (1, 2), (1, 0)):
        weights.append(
            0.5
            * (coef_here + coef_pad[:, :, shift_y : shift_y + height, shift_x : shift_x + breadth])
        )
    diagonal = weights[0] + weights[1] + weights[2] + weights[3] + weights[4] + weights[5]
    return (diagonal, weights)


def apply_operator(coef_ext, field_ext):
    diagonal, weights = face_weights(coef_ext)
    field_here = field_ext[:, 1:-1]
    height = field_here.shape[2]
    breadth = field_here.shape[3]
    field_pad = jnp.pad(field_here, ((0, 0), (0, 0), (1, 1), (1, 1)))
    total = diagonal * field_here - weights[0] * field_ext[:, 2:] - weights[1] * field_ext[:, :-2]
    index = 2
    for shift_y, shift_x in ((2, 1), (0, 1), (1, 2), (1, 0)):
        total = (
            total
            - weights[index]
            * field_pad[:, :, shift_y : shift_y + height, shift_x : shift_x + breadth]
        )
        index = index + 1
    return total


def slot_coupling(pattern, coupling, slot_mode):
    masked = coupling * pattern.astype(jnp.float32)
    modes = coupling.shape[1]
    one_hot = (slot_mode[:, None] == jnp.arange(modes, dtype=jnp.int32)[None, :]).astype(
        jnp.float32
    )
    return jnp.einsum("sa,kab,tb->kst", one_hot, masked, one_hot, precision=lax.Precision.HIGHEST)


def on_device(chaos_field, mean_field, kl_fields, pattern, coupling, slot_mode):
    quota = chaos_field.shape[0]
    position = lax.axis_index("mode")
    coupled = slot_coupling(pattern, coupling, slot_mode)
    coefs = jnp.concatenate([mean_field[None], kl_fields], 0)
    terms = coefs.shape[0]
    own_rows = lax.dynamic_slice_in_dim(coupled, position * quota, quota, 1)
    gathered = lax.all_gather(chaos_field, "mode", axis=0, tiled=True)
    result = jnp.zeros(chaos_field.shape, jnp.float32)
    for kl_term in range(terms):
        mixed = jnp.einsum(
            "st,tzyx->szyx", own_rows[kl_term], gathered, precision=lax.Precision.HIGHEST
        )
        stacked = jnp.concatenate([coefs[kl_term : kl_term + 1], mixed], 0)
        extended = with_halo(stacked, (("space", 1),), 1)
        result = result + apply_operator(extended[:1], extended[1:])
    return result


def solution(mesh):
    in_specs = (
        P("mode", "space", None, None),
        P("space", None, None),
        P(None, "space", None, None),
        P(),
        P(),
        P(),
    )
    out_specs = P("mode", "space", None, None)
    return jax.shard_map(
        on_device, mesh=mesh, in_specs=in_specs, out_specs=out_specs, check_vma=False
    )
```

profile of v0, /device:TPU:0, one launch (start us, length us, event | category | flops | bytes accessed | tf_op | source)
XLA Modules:
  0.0 578.7 jit_solution(16833640298119314066)
XLA Ops:
  6.6 0.7 all-gather.2.cloned.1.call-update
  8.1 0.5 fusion.101
  8.6 45.0 %all-gather.2.cloned.1.call-done = f32[84,1,128,128]{3,2,1,0:T(8,128)} async-done(((f32[21,1,128,128]{3,2,1,0:T(8,128)}), f32[84,1,128,128]{3,2,1,0:T(8,128)}) %all-gather.2.cloned.1.call-update) | async-done | bytes 5505040 | tf_op jit(solution)/shard_map/all_gather | solution.py:69
  53.6 8.6 %fusion = f32[21,128,128]{2,0,1:T(8,128)S(1)} fusion(f32[84,1,128,128]{3,2,1,0:T(8,128)} %all-gather.2.cloned.1.call-done, f32[7,84,84]{2,1,0:T(8,128)S(1)} %fusion.101, s32[]{:T(128)S(6)} %add.369, s32[]{:T(128)S(6)} %select_n.3), kind=kOutput, calls=%fused_computation | convolution fusion | flops 346816512 | bytes 6893576 | tf_op jit(solution)/shard_map/st,tzyx->szyx/dot_general | solution.py:72
  62.4 1.5 copy.58
  63.9 4.6 collective-permute-start.13
  68.5 1.3 collective-permute-start.12
  69.8 5.9 %fusion.12 = f32[21,128,128]{2,0,1:T(8,128)S(1)} fusion(f32[84,1,128,128]{3,2,1,0:T(8,128)S(1)} %copy-done, f32[7,84,84]{2,1,0:T(8,128)S(1)} %fusion.101, s32[]{:T(128)S(6)} %select_n.3), kind=kOutput, calls=%fused_computation.12 | convolution fusion | flops 346816512 | bytes 6893572 | tf_op jit(solution)/shard_map/st,tzyx->szyx/dot_general | solution.py:72
  76.0 0.9 copy-done.1
  76.9 1.4 copy.16
  78.3 5.7 collective-permute-start.1
  84.0 1.7 collective-permute-start
  85.7 8.7 %fusion.10 = f32[21,128,128]{2,0,1:T(8,128)S(1)} fusion(f32[84,1,128,128]{3,2,1,0:T(8,128)} %all-gather.2.cloned.1.call-done, f32[7,84,84]{2,1,0:T(8,128)} %copy-done.12, s32[]{:T(128)S(6)} %add.364, s32[]{:T(128)S(6)} %select_n.3), kind=kOutput, calls=%fused_computation.10 | convolution fusion | flops 346816512 | bytes 6893576 | tf_op jit(solution)/shard_map/st,tzyx->szyx/dot_general | solution.py:72
  94.9 4.6 collective-permute-start.3
  99.6 6.6 %fusion.8 = f32[21,128,128]{2,0,1:T(8,128)S(1)} fusion(f32[84,1,128,128]{3,2,1,0:T(8,128)S(1)} %bitcast.140, f32[7,84,84]{2,1,0:T(8,128)} %copy-done.12, s32[]{:T(128)S(6)} %add.365, s32[]{:T(128)S(6)} %select_n.3), kind=kOutput, calls=%fused_computation.8 | convolution fusion | flops 346816512 | bytes 6893576 | tf_op jit(solution)/shard_map/st,tzyx->szyx/dot_general | solution.py:72
  106.5 0.9 copy-done.3
  107.7 53.7 %collective-permute-done.13 = f32[22,1,128,128]{3,2,1,0:T(8,128)} collective-permute-done((f32[22,1,128,128]{3,2,1,0:T(8,128)}, f32[22,1,128,128]{3,2,1,0:T(8,128)}, u32[]{:S(2)}, u32[]{:S(2)}) %collective-permute-start.13) | collective-permute-done | bytes 1441824 | tf_op jit(solution)/shard_map/ppermute | solution.py:12
  161.4 1.3 collective-permute-start.2
  162.7 5.1 collective-permute-start.5
  167.8 55.4 %collective-permute-done.1 = f32[22,1,128,128]{3,2,1,0:T(8,128)} collective-permute-done((f32[22,1,128,128]{3,2,1,0:T(8,128)}, f32[22,1,128,128]{3,2,1,0:T(8,128)}, u32[]{:S(2)}, u32[]{:S(2)}) %collective-permute-start.1) | collective-permute-done | bytes 1441824 | tf_op jit(solution)/shard_map/ppermute | solution.py:12
  223.2 1.5 collective-permute-start.4
  224.7 6.6 %fusion.6 = f32[21,128,128]{2,0,1:T(8,128)S(1)} fusion(f32[84,1,128,128]{3,2,1,0:T(8,128)S(1)} %bitcast.140, f32[7,84,84]{2,1,0:T(8,128)} %copy-done.12, s32[]{:T(128)S(6)} %add.366, s32[]{:T(128)S(6)} %select_n.3), kind=kOutput, calls=%fused_computation.6 | convolution fusion | flops 346816512 | bytes 6893576 | tf_op jit(solution)/shard_map/st,tzyx->szyx/dot_general | solution.py:72
  231.6 0.9 copy-done.5
  232.8 7.0 %fusion.4 = f32[21,128,128]{2,0,1:T(8,128)S(1)} fusion(f32[84,1,128,128]{3,2,1,0:T(8,128)S(1)} %bitcast.140, f32[7,84,84]{2,1,0:T(8,128)} %copy-done.12, s32[]{:T(128)S(6)} %add.367, s32[]{:T(128)S(6)} %select_n.3), kind=kOutput, calls=%fused_computation.4 | convolution fusion | flops 346816512 | bytes 6893576 | tf_op jit(solution)/shard_map/st,tzyx->szyx/dot_general | solution.py:72
  240.0 1.0 copy-done.7
  241.3 6.6 %fusion.2 = f32[21,128,128]{2,0,1:T(8,128)S(1)} fusion(f32[84,1,128,128]{3,2,1,0:T(8,128)S(1)} %bitcast.140, f32[7,84,84]{2,1,0:T(8,128)} %copy-done.12, s32[]{:T(128)S(6)} %add.368, s32[]{:T(128)S(6)} %select_n.3), kind=kOutput, calls=%fused_computation.2 | convolution fusion | flops 346816512 | bytes 6893576 | tf_op jit(solution)/shard_map/st,tzyx->szyx/dot_general | solution.py:72
  248.2 5.1 collective-permute-start.7
  253.6 31.3 %collective-permute-done.3 = f32[22,1,128,128]{3,2,1,0:T(8,128)S(1)} collective-permute-done((f32[22,1,128,128]{3,2,1,0:T(8,128)S(1)}, f32[22,1,128,128]{3,2,1,0:T(8,128)S(1)}, u32[]{:S(2)}, u32[]{:S(2)}) %collective-permute-start.3) | collective-permute-done | bytes 1441824 | tf_op jit(solution)/shard_map/ppermute | solution.py:12
  284.9 1.3 collective-permute-start.6
  286.2 5.1 collective-permute-start.9
  291.3 55.4 %collective-permute-done.5 = f32[22,1,128,128]{3,2,1,0:T(8,128)S(1)} collective-permute-done((f32[22,1,128,128]{3,2,1,0:T(8,128)S(1)}, f32[22,1,128,128]{3,2,1,0:T(8,128)S(1)}, u32[]{:S(2)}, u32[]{:S(2)}) %collective-permute-start.5) | collective-permute-done | bytes 1441824 | tf_op jit(solution)/shard_map/ppermute | solution.py:12
  346.7 1.3 collective-permute-start.8
  348.0 5.1 collective-permute-start.11
  353.1 0.8 slice.525
  354.0 0.8 slice.524
  354.8 0.8 slice.501
  355.7 52.8 %collective-permute-done.7 = f32[22,1,128,128]{3,2,1,0:T(8,128)S(1)} collective-permute-done((f32[22,1,128,128]{3,2,1,0:T(8,128)S(1)}, f32[22,1,128,128]{3,2,1,0:T(8,128)S(1)}, u32[]{:S(2)}, u32[]{:S(2)}) %collective-permute-start.7) | collective-permute-done | bytes 1441824 | tf_op jit(solution)/shard_map/ppermute | solution.py:12
  408.5 1.5 collective-permute-start.10
  410.0 60.3 %collective-permute-done.9 = f32[22,1,128,128]{3,2,1,0:T(8,128)S(1)} collective-permute-done((f32[22,1,128,128]{3,2,1,0:T(8,128)S(1)}, f32[22,1,128,128]{3,2,1,0:T(8,128)S(1)}, u32[]{:S(2)}, u32[]{:S(2)}) %collective-permute-start.9) | collective-permute-done | bytes 1441824 | tf_op jit(solution)/shard_map/ppermute | solution.py:12
  470.3 30.2 %collective-permute-done.11 = f32[22,1,128,128]{3,2,1,0:T(8,128)S(1)} collective-permute-done((f32[22,1,128,128]{3,2,1,0:T(8,128)S(1)}, f32[22,1,128,128]{3,2,1,0:T(8,128)S(1)}, u32[]{:S(2)}, u32[]{:S(2)}) %collective-permute-start.11) | collective-permute-done | bytes 1441824 | tf_op jit(solution)/shard_map/ppermute | solution.py:12
  500.5 1.1 add_add_fusion
  501.6 1.2 add_add_fusion.6
  502.8 1.2 add_add_fusion.5
  503.9 1.2 add_add_fusion.4
  505.1 1.2 add_add_fusion.3
  506.3 1.2 add_add_fusion.2
  507.4 1.2 add_add_fusion.1
  508.6 1.4 slice.527
  510.1 2.6 slice.526
  512.6 2.7 slice.503
  515.3 1.3 slice.502
  516.6 1.2 slice.507
  517.8 1.2 slice.506
  519.0 1.2 slice.511
  520.2 1.2 slice.510
  521.4 1.2 slice.515
  522.5 1.2 slice.514
  523.8 1.2 slice.519
  524.9 1.2 slice.518
  526.1 1.2 slice.523
  527.3 1.3 slice.522
  528.9 0.7 copy-done.2
  529.6 39.3 %fusion.31 = f32[21,1,128,128]{3,0,2,1:T(8,128)} fusion(f32[21,1,128,128]{3,0,2,1:T(8,128)S(1)} %bitcast.144, f32[21,1,128,128]{3,0,2,1:T(8,128)S(1)} %bitcast.146, f32[21,1,128,128]{3,0,2,1:T(8,128)S(1)} %bitcast.148, f32[21,1,128,128]{3,0,2,1:T(8,128)S(1)} %bitcast.150, f32[21,1,128,128]{3,0,2,1:T(8,128)S(1)} %bitcast.152, ...), kind=kLoop, calls=%fused_computation.59 | loop fusion | flops 33374208 | bytes 43122688 | tf_op jit(solution)/shard_map/add | solution.py:77
  568.9 2.8 copy.64
  (82 shorter events, 4.0 us)
Async XLA Ops:
  6.5 1.0 copy-start.13
  6.5 1.0 copy-start.23
  6.5 1.1 copy-start.14
  6.5 1.2 copy-start.15
  6.5 47.0 %all-gather.2.cloned.1.call-start = ((), (), s32[]{:S(2)}) async-start(), calls=%async_computation | async-start | bytes 6881280 | tf_op jit(solution)/shard_map/all_gather | solution.py:69
  8.6 61.2 %copy-start.12 = (f32[7,84,84]{2,1,0:T(8,128)}, f32[7,84,84]{2,1,0:T(8,128)S(1)}, u32[]{:S(2)}) copy-start(f32[7,84,84]{2,1,0:T(8,128)S(1)} %fusion.101) | copy-start | bytes 592708
  62.2 7.6 %copy-start = (f32[84,1,128,128]{3,2,1,0:T(8,128)S(1)}, f32[84,1,128,128]{3,2,1,0:T(8,128)}, u32[]{:S(2)}) copy-start(f32[84,1,128,128]{3,2,1,0:T(8,128)} %all-gather.2.cloned.1.call-done) | copy-start | bytes 16515076
  63.9 11.9 %copy-start.21 = (f32[1,128,128]{2,1,0:T(8,128)S(1)}, f32[1,128,128]{2,1,0:T(8,128)}, u32[]{:S(2)}) copy-start(f32[1,128,128]{2,1,0:T(8,128)} %param.7) | copy-start | bytes 196612
  63.9 97.5 %collective-permute-start.13 = (f32[22,1,128,128]{3,2,1,0:T(8,128)}, f32[22,1,128,128]{3,2,1,0:T(8,128)}, u32[]{:S(2)}, u32[]{:S(2)}) collective-permute-start(f32[22,1,128,128]{3,2,1,0:T(8,128)} %copy.58), channel_id=1, source_target_pairs={{0,4},{4,8},{8,12},{12,16},{16,20},{20,24},{24,28},{1,5},{5,9},{9,... | collective-permute-start | bytes 4325384 | tf_op jit(solution)/shard_map/ppermute | solution.py:12
  68.5 94.2 %collective-permute-start.12 = (f32[22,1,128,128]{3,2,1,0:T(8,128)}, f32[22,1,128,128]{3,2,1,0:T(8,128)}, u32[]{:S(2)}, u32[]{:S(2)}) collective-permute-start(f32[22,1,128,128]{3,2,1,0:T(8,128)} %copy.58), channel_id=1, source_target_pairs={{4,0},{8,4},{12,8},{16,12},{20,16},{24,20},{28,24},{5,1},{9,5},{13... | collective-permute-start | bytes 4325384 | tf_op jit(solution)/shard_map/ppermute | solution.py:15
  75.7 1.1 copy-start.1
  76.9 22.7 %slice-start = ((s8[5505024]{0:T(1024)(128)(4,1)}), s8[1310720]{0:T(1024)(128)(4,1)S(1)}, s32[]{:S(2)}) async-start(s8[5505024]{0:T(1024)(128)(4,1)} %bitcast.139), calls=%async_computation.1 | async-start | bytes 2621440
  78.3 144.9 %collective-permute-start.1 = (f32[22,1,128,128]{3,2,1,0:T(8,128)}, f32[22,1,128,128]{3,2,1,0:T(8,128)}, u32[]{:S(2)}, u32[]{:S(2)}) collective-permute-start(f32[22,1,128,128]{3,2,1,0:T(8,128)} %copy.16), channel_id=1, source_target_pairs={{0,4},{4,8},{8,12},{12,16},{16,20},{20,24},{24,28},{1,5},{5,9},{9,... | collective-permute-start | bytes 4325384 | tf_op jit(solution)/shard_map/ppermute | solution.py:12
  84.0 15.6 %slice-start.1 = ((s8[5505024]{0:T(1024)(128)(4,1)}), s8[4194304]{0:T(1024)(128)(4,1)S(1)}, s32[]{:S(2)}) async-start(s8[5505024]{0:T(1024)(128)(4,1)} %bitcast.139), calls=%async_computation.2 | async-start | bytes 8388608
  84.0 164.2 %collective-permute-start = (f32[22,1,128,128]{3,2,1,0:T(8,128)}, f32[22,1,128,128]{3,2,1,0:T(8,128)S(1)}, u32[]{:S(2)}, u32[]{:S(2)}) collective-permute-start(f32[22,1,128,128]{3,2,1,0:T(8,128)} %copy.16), channel_id=1, source_target_pairs={{4,0},{8,4},{12,8},{16,12},{20,16},{24,20},{28,24},{5,1},{9,5},{13... | collective-permute-start | bytes 4325384 | tf_op jit(solution)/shard_map/ppermute | solution.py:15
  94.9 190.0 %collective-permute-start.3 = (f32[22,1,128,128]{3,2,1,0:T(8,128)S(1)}, f32[22,1,128,128]{3,2,1,0:T(8,128)S(1)}, u32[]{:S(2)}, u32[]{:S(2)}) collective-permute-start(f32[22,1,128,128]{3,2,1,0:T(8,128)S(1)} %copy.23), channel_id=1, source_target_pairs={{0,4},{4,8},{8,12},{12,16},{16,20},{20,24},{24,28},{1,5},{5,9},{9,... | collective-permute-start | bytes 4325384 | tf_op jit(solution)/shard_map/ppermute | solution.py:12
  106.2 1.1 copy-start.3
  161.4 124.8 %collective-permute-start.2 = (f32[22,1,128,128]{3,2,1,0:T(8,128)S(1)}, f32[22,1,128,128]{3,2,1,0:T(8,128)S(1)}, u32[]{:S(2)}, u32[]{:S(2)}) collective-permute-start(f32[22,1,128,128]{3,2,1,0:T(8,128)S(1)} %copy.23), channel_id=1, source_target_pairs={{4,0},{8,4},{12,8},{16,12},{20,16},{24,20},{28,24},{5,1},{9,5},{13... | collective-permute-start | bytes 4325384 | tf_op jit(solution)/shard_map/ppermute | solution.py:15
  162.7 184.0 %collective-permute-start.5 = (f32[22,1,128,128]{3,2,1,0:T(8,128)S(1)}, f32[22,1,128,128]{3,2,1,0:T(8,128)S(1)}, u32[]{:S(2)}, u32[]{:S(2)}) collective-permute-start(f32[22,1,128,128]{3,2,1,0:T(8,128)S(1)} %copy.30), channel_id=1, source_target_pairs={{0,4},{4,8},{8,12},{12,16},{16,20},{20,24},{24,28},{1,5},{5,9},{9,... | collective-permute-start | bytes 4325384 | tf_op jit(solution)/shard_map/ppermute | solution.py:12
  223.2 124.8 %collective-permute-start.4 = (f32[22,1,128,128]{3,2,1,0:T(8,128)S(1)}, f32[22,1,128,128]{3,2,1,0:T(8,128)S(1)}, u32[]{:S(2)}, u32[]{:S(2)}) collective-permute-start(f32[22,1,128,128]{3,2,1,0:T(8,128)S(1)} %copy.30), channel_id=1, source_target_pairs={{4,0},{8,4},{12,8},{16,12},{20,16},{24,20},{28,24},{5,1},{9,5},{13... | collective-permute-start | bytes 4325384 | tf_op jit(solution)/shard_map/ppermute | solution.py:15
  231.4 1.2 copy-start.5
  239.8 1.2 copy-start.7
  248.0 256.0 %copy-start.9 = (f32[21,128,128]{2,0,1:T(8,128)}, f32[21,128,128]{2,0,1:T(8,128)S(1)}, u32[]{:S(2)}) copy-start(f32[21,128,128]{2,0,1:T(8,128)S(1)} %fusion.2) | copy-start | bytes 4128772
  248.2 107.4 %copy-start.10 = (f32[22,1,128,128]{3,2,1,0:T(8,128)}, f32[22,1,128,128]{3,2,1,0:T(8,128)S(1)}, u32[]{:S(2)}) copy-start(f32[22,1,128,128]{3,2,1,0:T(8,128)S(1)} %collective-permute-done) | copy-start | bytes 4325380
  248.2 160.3 %collective-permute-start.7 = (f32[22,1,128,128]{3,2,1,0:T(8,128)S(1)}, f32[22,1,128,128]{3,2,1,0:T(8,128)S(1)}, u32[]{:S(2)}, u32[]{:S(2)}) collective-permute-start(f32[22,1,128,128]{3,2,1,0:T(8,128)S(1)} %copy.37), channel_id=1, source_target_pairs={{0,4},{4,8},{8,12},{12,16},{16,20},{20,24},{24,28},{1,5},{5,9},{9,... | collective-permute-start | bytes 4325384 | tf_op jit(solution)/shard_map/ppermute | solution.py:12
  253.6 248.0 %copy-start.22 = (f32[1,128,128]{2,1,0:T(8,128)S(1)}, f32[1,128,128]{2,1,0:T(8,128)}, u32[]{:S(2)}) copy-start(f32[1,128,128]{2,1,0:T(8,128)} %param.7) | copy-start | bytes 196612
  284.9 125.1 %collective-permute-start.6 = (f32[22,1,128,128]{3,2,1,0:T(8,128)S(1)}, f32[22,1,128,128]{3,2,1,0:T(8,128)S(1)}, u32[]{:S(2)}, u32[]{:S(2)}) collective-permute-start(f32[22,1,128,128]{3,2,1,0:T(8,128)S(1)} %copy.37), channel_id=1, source_target_pairs={{4,0},{8,4},{12,8},{16,12},{20,16},{24,20},{28,24},{5,1},{9,5},{13... | collective-permute-start | bytes 4325384 | tf_op jit(solution)/shard_map/ppermute | solution.py:15
  286.2 184.1 %collective-permute-start.9 = (f32[22,1,128,128]{3,2,1,0:T(8,128)S(1)}, f32[22,1,128,128]{3,2,1,0:T(8,128)S(1)}, u32[]{:S(2)}, u32[]{:S(2)}) collective-permute-start(f32[22,1,128,128]{3,2,1,0:T(8,128)S(1)} %copy.44), channel_id=1, source_target_pairs={{0,4},{4,8},{8,12},{12,16},{16,20},{20,24},{24,28},{1,5},{5,9},{9,... | collective-permute-start | bytes 4325384 | tf_op jit(solution)/shard_map/ppermute | solution.py:12
  346.7 123.6 %collective-permute-start.8 = (f32[22,1,128,128]{3,2,1,0:T(8,128)S(1)}, f32[22,1,128,128]{3,2,1,0:T(8,128)S(1)}, u32[]{:S(2)}, u32[]{:S(2)}) collective-permute-start(f32[22,1,128,128]{3,2,1,0:T(8,128)S(1)} %copy.44), channel_id=1, source_target_pairs={{4,0},{8,4},{12,8},{16,12},{20,16},{24,20},{28,24},{5,1},{9,5},{13... | collective-permute-start | bytes 4325384 | tf_op jit(solution)/shard_map/ppermute | solution.py:15
  348.0 152.5 %collective-permute-start.11 = (f32[22,1,128,128]{3,2,1,0:T(8,128)S(1)}, f32[22,1,128,128]{3,2,1,0:T(8,128)S(1)}, u32[]{:S(2)}, u32[]{:S(2)}) collective-permute-start(f32[22,1,128,128]{3,2,1,0:T(8,128)S(1)} %copy.51), channel_id=1, source_target_pairs={{0,4},{4,8},{8,12},{12,16},{16,20},{20,24},{24,28},{1,5},{5,9},{9,... | collective-permute-start | bytes 4325384 | tf_op jit(solution)/shard_map/ppermute | solution.py:12
  355.6 146.0 %slice-start.2 = ((f32[22,1,128,128]{3,2,1,0:T(8,128)}), f32[1,1,128,128]{3,2,1,0:T(8,128)S(1)}, s32[]{:S(2)}) async-start(f32[22,1,128,128]{3,2,1,0:T(8,128)} %copy-done.10), calls=%async_computation.3 | async-start | bytes 131072 | tf_op jit(solution)/shard_map/slice | solution.py:25
  408.5 98.9 %collective-permute-start.10 = (f32[22,1,128,128]{3,2,1,0:T(8,128)S(1)}, f32[22,1,128,128]{3,2,1,0:T(8,128)S(1)}, u32[]{:S(2)}, u32[]{:S(2)}) collective-permute-start(f32[22,1,128,128]{3,2,1,0:T(8,128)S(1)} %copy.51), channel_id=1, source_target_pairs={{4,0},{8,4},{12,8},{16,12},{20,16},{24,20},{28,24},{5,1},{9,5},{13... | collective-permute-start | bytes 4325384 | tf_op jit(solution)/shard_map/ppermute | solution.py:15
  512.6 2.7 copy-start.11
  524.9 3.7 copy-start.8
  526.1 2.5 copy-start.4
  526.1 2.8 copy-start.6
  527.3 2.3 copy-start.2
  527.3 2.3 copy-start.16
  527.3 2.3 copy-start.17
  527.3 2.3 copy-start.18
  527.3 2.3 copy-start.19
  527.3 2.3 copy-start.20
Sparse Core Ops, SparseCore 0:
  8.9 44.6 all-gather.1
where the time goes:
time: 588 us; the launch traced here: 579 us
  waiting for transfers between devices  385 us (65%)
  matrix products  51 us (9%)
  other arithmetic  48.7 us (8%)
  starting transfers between devices  45.2 us (8%)
  local copies, waits for them, and re-layouts  34.9 us (6%)
  between operations  14.1 us (2%)
    ppermute x7, waiting for transfers between devices, with_halo(): lax.ppermute(lax.slice_in_dim(block, block.shape[dim] - width, None, axis...  339 us
    dot_general x7, matrix products, on_device(): jnp.einsum('st,tzyx->szyx', own_rows[kl_term], gathered, precision=lax.Pr...  50.2 us
    all_gather x1, waiting for transfers between devices, on_device(): gathered = lax.all_gather(chaos_field, 'mode', axis=0, tiled=True)  45 us
    add x1, other arithmetic, on_device(): result = result + apply_operator(extended[:1], extended[1:])  39.3 us
    ppermute x7, starting transfers between devices, with_halo(): lax.ppermute(lax.slice_in_dim(block, block.shape[dim] - width, None, axis...  35.4 us
  transfers between devices with their start and end apart: 15, of which 8 were waited for; matrix products, arithmetic and copies ran while one was open for 10% of the time, Pallas kernels for 0%

commit v1 on v0

v1 whole, which is shorter than its diff:
```python
import jax
import jax.numpy as jnp
from jax import lax
from jax.experimental import pallas as pl
from jax.experimental.pallas import tpu as pltpu
from jax.sharding import PartitionSpec as P

VMEM_LIMIT = 48 * 1024 * 1024
PLANES = 2


class Layout:
    def __init__(self, quota, terms, modes, height):
        self.modes = modes
        self.group = PLANES * modes
        self.rows = height // self.group
        self.quota = quota
        self.share = -(-terms // modes)
        self.fields = quota + self.share
        self.main = self.fields * self.rows
        self.block = -(-(self.main + 2 * self.fields) // 8) * 8

    def coef(self, term):
        return term // self.share, self.quota + term % self.share


def vmem(count):
    return [pl.BlockSpec(memory_space=pltpu.VMEM)] * count


def smem(count):
    return [pl.BlockSpec(memory_space=pltpu.SMEM)] * count


def pack(field, mean, kl, mode, lay):
    kl_terms = kl.shape[0]
    width = field.shape[2]
    zero_row = (1, width)

    def kernel(mode_ref, field_ref, mean_ref, kl_ref, out_ref):
        for i in range(lay.fields):
            if i < lay.quota:
                value = field_ref[i]
            else:
                term = mode_ref[0] * lay.share + (i - lay.quota)
                other = kl_ref[jnp.clip(term - 1, 0, kl_terms - 1)]
                value = jnp.where(term == 0, mean_ref[0], other)
            for j in range(lay.group):
                first = j * lay.rows
                last = first + lay.rows
                out_ref[j, i * lay.rows : (i + 1) * lay.rows, :] = value[first:last]
                low = value[first - 1 : first] if j > 0 else jnp.zeros(zero_row, jnp.float32)
                high = value[last : last + 1] if j < lay.group - 1 else jnp.zeros(zero_row, jnp.float32)
                at = lay.main + 2 * i
                out_ref[j, at : at + 1, :] = low
                out_ref[j, at + 1 : at + 2, :] = high
        spare = lay.block - lay.main - 2 * lay.fields
        if spare:
            for j in range(lay.group):
                out_ref[j, lay.block - spare :, :] = jnp.zeros((spare, width), jnp.float32)

    return pl.pallas_call(
        kernel,
        out_shape=jax.ShapeDtypeStruct((lay.group, lay.block, width), jnp.float32),
        in_specs=smem(1) + vmem(3),
        out_specs=vmem(1)[0],
        compiler_params=pltpu.CompilerParams(vmem_limit_bytes=VMEM_LIMIT),
        name="pack",
    )(mode, field, mean, kl)


def coupling_entries(pattern, coupling, slot_mode, lay):
    masked = (coupling * pattern.astype(jnp.float32))[1:]
    terms, modes = masked.shape[0], masked.shape[1]
    per_term = 56
    number = jnp.arange(modes, dtype=jnp.int32)
    slot_of = jnp.sum(jnp.where(slot_mode[:, None] == number[None, :], number[:, None], 0), 0)
    column = number[None, None, :]
    there = pattern[1:] != 0
    first = jnp.min(jnp.where(there, column, modes), 2)
    last = jnp.max(jnp.where(there, column, -1), 2)
    mode_t = jnp.concatenate([first, last], 1)
    valid = jnp.concatenate([first < modes, last > first], 1)
    value = jnp.concatenate(
        [
            jnp.sum(jnp.where(column == first[:, :, None], masked, 0.0), 2),
            jnp.sum(jnp.where(column == last[:, :, None], masked, 0.0), 2),
        ],
        1,
    )
    slot_s = jnp.concatenate([slot_of, slot_of])
    slot_t = jnp.sum(jnp.where(mode_t[:, :, None] == column, slot_of[None, None, :], 0), 2)
    candidates = 2 * modes
    index = jnp.arange(candidates, dtype=jnp.int32)
    before = index[None, None, :] < index[None, :, None]
    rank = jnp.sum(jnp.where(valid[:, None, :] & before, 1, 0), 2)
    place = jnp.arange(per_term, dtype=jnp.int32)
    chosen = (rank[:, None, :] == place[None, :, None]) & valid[:, None, :]
    entry_s = jnp.sum(jnp.where(chosen, slot_s[None, None, :], 0), 2)
    entry_t = jnp.sum(jnp.where(chosen, slot_t[:, None, :], 0), 2)
    entry_v = jnp.sum(jnp.where(chosen, value[:, None, :], 0.0), 2)
    return entry_s.reshape(-1), entry_t.reshape(-1), entry_v.reshape(-1), per_term


def inner(gathered, entries, terms, lay):
    entry_s, entry_t, entry_v, per_term = entries
    slots = lay.quota * lay.modes
    rows = lay.rows
    width = gathered.shape[2]
    full = (rows, width)

    def kernel(s_ref, t_ref, v_ref, g_ref, out_ref, near_ref):
        lane = lax.broadcasted_iota(jnp.int32, full, 1)
        line = lax.broadcasted_iota(jnp.int32, full, 0)

        def neighbours(p, block, i):
            at = block * lay.block
            here = g_ref[p, pl.ds(at + i * rows, rows), :]
            low = g_ref[p, pl.ds(at + lay.main + 2 * i, 1), :]
            high = g_ref[p, pl.ds(at + lay.main + 2 * i + 1, 1), :]
            right = pltpu.roll(here, width - 1, 1)
            left = pltpu.roll(here, 1, 1)
            above = jnp.where(line == rows - 1, high, pltpu.roll(here, rows - 1, 0))
            below = jnp.where(line == 0, low, pltpu.roll(here, 1, 0))
            return here, right, left, above, below

        for block in range(lay.modes):

            def spread(i, carry, block=block):
                for p in range(PLANES):
                    for n, value in enumerate(neighbours(p, block, i)):
                        near_ref[block * lay.quota + i, p, n] = value
                return carry

            lax.fori_loop(0, lay.quota, spread, 0)

        for term in range(terms):
            block, i = lay.coef(term)
            weights = []
            centres = []
            for p in range(PLANES):
                here, right, left, above, below = neighbours(p, block, i)
                right = jnp.where(lane == width - 1, 0.0, right)
                left = jnp.where(lane == 0, 0.0, left)
                faces = [0.5 * (here + n) for n in (right, left, above, below)]
                centres.append(here)
                diagonal = faces[0] + faces[1] + faces[2] + faces[3] + 0.5 * here
                faces[0] = jnp.where(lane == width - 1, 0.0, faces[0])
                faces[1] = jnp.where(lane == 0, 0.0, faces[1])
                weights.append([diagonal] + [-f for f in faces])
            between = 0.5 * (centres[0] + centres[1])
            for p in range(PLANES):
                weights[p][0] = weights[p][0] + between

            def operator(t, weights=weights, between=between):
                outs = []
                for p in range(PLANES):
                    total = weights[p][0] * near_ref[t, p, 0]
                    for n in range(1, 5):
                        total = total + weights[p][n] * near_ref[t, p, n]
                    outs.append(total - between * near_ref[t, 1 - p, 0])
                return outs

            if term == 0:

                def own(s, carry, operator=operator):
                    for p, total in enumerate(operator(s)):
                        out_ref[p, s] = total
                    return carry

                lax.fori_loop(0, slots, own, 0)
            else:

                def mix(e, carry, operator=operator):
                    s, t, v = s_ref[e], t_ref[e], v_ref[e]
                    for p, total in enumerate(operator(t)):
                        out_ref[p, s] += v * total
                    return carry

                lax.fori_loop((term - 1) * per_term, term * per_term, mix, 0)

    return pl.pallas_call(
        kernel,
        out_shape=jax.ShapeDtypeStruct((PLANES, slots, rows, width), jnp.float32),
        in_specs=smem(3) + vmem(1),
        out_specs=vmem(1)[0],
        scratch_shapes=[pltpu.VMEM((slots, PLANES, 5, rows, width), jnp.float32)],
        compiler_params=pltpu.CompilerParams(vmem_limit_bytes=VMEM_LIMIT),
        name="inner",
    )(entry_s, entry_t, entry_v, gathered)


def outer(gathered, below, above, partial, entries, terms, lay):
    entry_s, entry_t, entry_v, per_term = entries
    slots = lay.quota * lay.modes
    rows = lay.rows
    width = gathered.shape[2]
    quota = lay.quota

    def kernel(s_ref, t_ref, v_ref, g_ref, below_ref, above_ref, part_ref, out_ref):
        far_refs = (below_ref, above_ref)

        for term in range(terms):
            block, i = lay.coef(term)
            weights = []
            for p in range(PLANES):
                here = g_ref[p, pl.ds(block * lay.block + i * rows, rows), :]
                far = far_refs[p][pl.ds(block * lay.main + i * rows, rows), :]
                weights.append((0.5 * far, 0.5 * (here + far)))

            def operator(t, weights=weights):
                block = t // quota
                i = t - block * quota
                near_at = pl.multiple_of(block * lay.block + i * rows, 8)
                far_at = pl.multiple_of(block * lay.main + i * rows, 8)
                outs = []
                for p in range(PLANES):
                    here = g_ref[p, pl.ds(near_at, rows), :]
                    far = far_refs[p][pl.ds(far_at, rows), :]
                    outs.append(weights[p][0] * here - weights[p][1] * far)
                return outs

            if term == 0:

                def own(s, carry, operator=operator):
                    for p, total in enumerate(operator(s)):
                        out_ref[p, s] = part_ref[p, s] + total
                    return carry

                lax.fori_loop(0, slots, own, 0)
            else:

                def mix(e, carry, operator=operator):
                    s, t, v = s_ref[e], t_ref[e], v_ref[e]
                    for p, total in enumerate(operator(t)):
                        out_ref[p, s] += v * total
                    return carry

                lax.fori_loop((term - 1) * per_term, term * per_term, mix, 0)

    return pl.pallas_call(
        kernel,
        out_shape=jax.ShapeDtypeStruct((PLANES, slots, rows, width), jnp.float32),
        in_specs=smem(3) + vmem(4),
        out_specs=vmem(1)[0],
        compiler_params=pltpu.CompilerParams(vmem_limit_bytes=VMEM_LIMIT),
        name="outer",
    )(entry_s, entry_t, entry_v, gathered, below, above, partial)


def on_device(chaos_field, mean_field, kl_fields, pattern, coupling, slot_mode):
    spaces, modes = lax.axis_size("space"), lax.axis_size("mode")
    quota, _, height, width = chaos_field.shape
    terms = kl_fields.shape[0] + 1
    lay = Layout(quota, terms, modes, height)
    groups = [
        list(range(start, start + lay.group)) for start in range(0, spaces * modes, lay.group)
    ]

    def exchange(blocks):
        return lax.all_to_all(
            blocks, ("space", "mode"), 0, 0, axis_index_groups=groups, tiled=True
        )

    mode = lax.axis_index("mode").astype(jnp.int32).reshape(1)
    blocks = pack(chaos_field[:, 0], mean_field, kl_fields[:, 0], mode, lay)
    entries = coupling_entries(pattern, coupling, slot_mode, lay)
    gathered = exchange(blocks)

    main = gathered.reshape(PLANES, modes, lay.block, width)[:, :, : lay.main]
    main = main.reshape(PLANES, modes * lay.main, width)
    up = [(i, i + PLANES) for i in range(spaces - PLANES)]
    down = [(target, source) for source, target in up]
    below = lax.ppermute(main[PLANES - 1], "space", up)
    above = lax.ppermute(main[0], "space", down)

    planes = gathered.reshape(PLANES, modes * lay.block, width)
    partial = inner(planes, entries, terms, lay)
    total = outer(planes, below, above, partial, entries, terms, lay)

    back = exchange(total.reshape(lay.group, quota * lay.rows, width))
    back = back.reshape(lay.group, quota, lay.rows, width).transpose(1, 0, 2, 3)
    return back.reshape(chaos_field.shape)


def solution(mesh):
    in_specs = (
        P("mode", "space", None, None),
        P("space", None, None),
        P(None, "space", None, None),
        P(),
        P(),
        P(),
    )
    out_specs = P("mode", "space", None, None)
    return jax.shard_map(
        on_device, mesh=mesh, in_specs=in_specs, out_specs=out_specs, check_vma=False
    )
```

time: 588 us -> 89.6 us (0.15); the launches traced: 579 us -> 89.2 us
  waiting for transfers between devices: 385 us -> 23.8 us
  matrix products: 51 us -> 0 us
  other arithmetic: 48.7 us -> 2.39 us
  starting transfers between devices: 45.2 us -> 10.1 us
  local copies, waits for them, and re-layouts: 34.9 us -> 5.88 us
  Pallas kernels: 0 us -> 25.4 us
  blocking collectives: 0 us -> 21.5 us
  between operations: 14.1 us -> 0.11 us
    ppermute x14 -> x2, waiting for transfers between devices: 339 us -> 3.5 us  [the longest x1 3.49 us: on_device(): above = lax.ppermute(main[0], 'space', down)]
    dot_general x9 -> x0, matrix products: 51 us -> none  [the longest x7 50.2 us: on_device(): jnp.einsum('st,tzyx->szyx', own_rows[kl_term], gathered, precision=lax.Pr...]
    add x8 -> x0, other arithmetic: 47.4 us -> none  [the longest x1 39.3 us: on_device(): result = result + apply_operator(extended[:1], extended[1:])]
    all_gather x1 -> x0, waiting for transfers between devices: 45 us -> none  [on_device(): gathered = lax.all_gather(chaos_field, 'mode', axis=0, tiled=True)]
    ppermute x14 -> x2, starting transfers between devices: 45.2 us -> 4.81 us  [the longest x1 3.52 us: on_device(): below = lax.ppermute(main[PLANES - 1], 'space', up)]
    pallas_call x0 -> x3, Pallas kernels: none -> 25.4 us  [the longest x1 13.9 us: inner(): pl.pallas_call(kernel, out_shape=jax.ShapeDtypeStruct((PLANES, slots, row...]
    all_to_all x0 -> x1, blocking collectives: none -> 21.5 us  [exchange(): lax.all_to_all(blocks, ('space', 'mode'), 0, 0, axis_index_groups=groups,...]
    slice x30 -> x1, local copies, waits for them, and re-layouts: 22.5 us -> 1.22 us  [on_device(): above = lax.ppermute(main[0], 'space', down)]
  transfers between devices with their start and end apart: 15 -> 3, of which waited for: 8 -> 2; matrix products, arithmetic and copies ran while one was open for 10% -> 3% of each run, Pallas kernels for 0% -> 16%
where the time goes in v1:
time: 89.6 us; the launch traced here: 89.2 us
  Pallas kernels  25.4 us (28%)
  waiting for transfers between devices  23.8 us (27%)
  blocking collectives  21.5 us (24%)
  starting transfers between devices  10.1 us (11%)
  local copies, waits for them, and re-layouts  5.88 us (7%)
  other arithmetic  2.39 us (3%)
    all_to_all x1, blocking collectives, exchange(): lax.all_to_all(blocks, ('space', 'mode'), 0, 0, axis_index_groups=groups,...  21.5 us
    all_to_all x1, waiting for transfers between devices, exchange(): lax.all_to_all(blocks, ('space', 'mode'), 0, 0, axis_index_groups=groups,...  20.3 us
    pallas_call x1, Pallas kernels, inner(): pl.pallas_call(kernel, out_shape=jax.ShapeDtypeStruct((PLANES, slots, row...  13.9 us
    pallas_call x1, Pallas kernels, outer(): pl.pallas_call(kernel, out_shape=jax.ShapeDtypeStruct((PLANES, slots, row...  10.2 us
    all_to_all x1, starting transfers between devices, exchange(): lax.all_to_all(blocks, ('space', 'mode'), 0, 0, axis_index_groups=groups,...  5.3 us
    ppermute x1, starting transfers between devices, on_device(): below = lax.ppermute(main[PLANES - 1], 'space', up)  3.52 us
    ppermute x1, waiting for transfers between devices, on_device(): above = lax.ppermute(main[0], 'space', down)  3.49 us
    unnamed x12, local copies, waits for them, and re-layouts  3.18 us
  transfers between devices with their start and end apart: 3, of which 2 were waited for; matrix products, arithmetic and copies ran while one was open for 3% of the time, Pallas kernels for 16%

profile of v1, /device:TPU:0, one launch (start us, length us, event | category | flops | bytes accessed | tf_op | source)
XLA Modules:
  0.0 89.2 jit_solution(8843139554058319392)
XLA Ops:
  0.0 0.0 copy-start
  0.0 1.3 %copy-done = f32[21,1,128,128]{3,2,1,0:T(8,128)S(1)} copy-done((f32[21,1,128,128]{3,2,1,0:T(8,128)S(1)}, f32[21,1,128,128]{3,2,1,0:T(8,128)}, u32[]{:S(2)}) %copy-start) | copy-done | bytes 1376280
  1.3 0.0 copy-start.1
  1.3 1.0 %copy-done.1 = f32[6,1,128,128]{3,2,1,0:T(8,128)S(1)} copy-done((f32[6,1,128,128]{3,2,1,0:T(8,128)S(1)}, f32[6,1,128,128]{3,2,1,0:T(8,128)}, u32[]{:S(2)}) %copy-start.1) | copy-done | bytes 393240
  2.3 0.0 copy-start.2
  2.3 0.8 copy-done.2
  3.2 1.4 %pack.1 = f32[8,416,128]{2,1,0:T(8,128)} custom-call(s32[1]{0:T(128)} %bitcast.mode_ref, f32[21,128,128]{2,1,0:T(8,128)S(1)} %bitcast.16, f32[1,128,128]{2,1,0:T(8,128)S(1)} %copy-done.2, f32[6,128,128]{2,1,0:T(8,128)S(1)} %bitcast.17), custom_call_target="tpu_custom_call" | custom-call | tf_op jit(solution)/shard_map/pack/pallas_call | solution.py:62
  4.6 0.0 copy-start.3
  4.6 0.0 copy-start.4
  4.6 5.3 %all-to-all-start = ((f32[8,416,128]{2,1,0:T(8,128)}), f32[8,416,128]{2,1,0:T(8,128)S(1)}, u32[]{:S(2)}, u32[]{:S(2)}) async-start(f32[8,416,128]{2,1,0:T(8,128)} %pack.1), calls=%async_computation | async-start | bytes 3407872 | tf_op jit(solution)/shard_map/all_to_all | solution.py:261
  9.9 0.0 copy-done.3
  9.9 0.3 select_reduce_fusion.8
  10.2 0.1 pad_add_fusion.1
  10.3 0.3 select_reduce_fusion
  10.6 0.0 copy-done.4
  10.6 0.5 select_reduce_fusion.6
  11.0 20.3 %all-to-all-done = f32[8,416,128]{2,1,0:T(8,128)S(1)} async-done(((f32[8,416,128]{2,1,0:T(8,128)}), f32[8,416,128]{2,1,0:T(8,128)S(1)}, u32[]{:S(2)}, u32[]{:S(2)}) %all-to-all-start) | async-done | bytes 1703968 | tf_op jit(solution)/shard_map/all_to_all | solution.py:261
  31.4 0.0 copy-start.5
  31.4 1.2 %fusion.1 = (f32[1,4,368,128]{3,2,1,0:T(8,128)}, f32[1,4,368,128]{3,2,1,0:T(8,128)}) fusion(f32[2,4,416,128]{3,2,1,0:T(8,128)S(1)} %bitcast.12), kind=kLoop, calls=%fused_computation.24 | loop fusion | bytes 3014656 | tf_op jit(solution)/shard_map/slice | solution.py:275
  32.6 3.5 %collective-permute-start = (f32[1472,128]{1,0:T(8,128)}, f32[1472,128]{1,0:T(8,128)S(1)}, u32[]{:S(2)}, u32[]{:S(2)}) collective-permute-start(f32[1472,128]{1,0:T(8,128)} %bitcast.5), channel_id=1, source_target_pairs={{0,8},{4,12},{8,16},{12,20},{16,24},{20,28},{1,9},{5,13},{9,17},{1... | collective-permute-start | bytes 2261000 | tf_op jit(solution)/shard_map/ppermute | solution.py:274
  36.1 1.3 %collective-permute-start.1 = (f32[1472,128]{1,0:T(8,128)}, f32[1472,128]{1,0:T(8,128)S(1)}, u32[]{:S(2)}, u32[]{:S(2)}) collective-permute-start(f32[1472,128]{1,0:T(8,128)} %bitcast.6), channel_id=1, source_target_pairs={{8,0},{12,4},{16,8},{20,12},{24,16},{28,20},{9,1},{13,5},{17,9},{2... | collective-permute-start | bytes 2261000 | tf_op jit(solution)/shard_map/ppermute | solution.py:275
  37.4 0.1 pad_maximum_fusion
  37.5 0.1 select_reduce_fusion.2
  37.6 0.1 reshape.59.v_ref
  37.7 0.0 copy-done.5
  37.7 0.1 select_reduce_fusion.9
  37.8 0.1 pad_add_fusion.2
  37.9 0.1 pad_add_fusion
  38.0 0.5 select_reduce_fusion.1
  38.4 0.3 select_reduce_fusion.3
  38.7 0.1 reshape.58.t_ref
  38.8 0.1 reshape.57.s_ref
  38.9 13.9 %inner.1.part_ref = f32[2,84,16,128]{3,2,1,0:T(8,128)S(1)} custom-call(s32[336]{0:T(512)S(1)} %reshape.57.s_ref, s32[336]{0:T(512)S(1)} %reshape.58.t_ref, f32[336]{0:T(512)S(1)} %reshape.59.v_ref, f32[2,1664,128]{2,1,0:T(8,128)S(1)} %bitcast.13), custom_call_target="tpu_custom_call" | custom-call | tf_op jit(solution)/shard_map/inner/pallas_call | solution.py:182
  52.8 0.0 collective-permute-done.below_ref
  52.8 3.5 %collective-permute-done.1.above_ref = f32[1472,128]{1,0:T(8,128)S(1)} collective-permute-done((f32[1472,128]{1,0:T(8,128)}, f32[1472,128]{1,0:T(8,128)S(1)}, u32[]{:S(2)}, u32[]{:S(2)}) %collective-permute-start.1) | collective-permute-done | bytes 753696 | tf_op jit(solution)/shard_map/ppermute | solution.py:275
  56.3 10.2 %outer.1 = f32[2,84,16,128]{3,2,1,0:T(8,128)S(1)} custom-call(s32[336]{0:T(512)S(1)} %reshape.57.s_ref, s32[336]{0:T(512)S(1)} %reshape.58.t_ref, f32[336]{0:T(512)S(1)} %reshape.59.v_ref, f32[2,1664,128]{2,1,0:T(8,128)S(1)} %bitcast.14, f32[1472,128]{1,0:T(8,128)S(1)} %collective-permute-done.below_ref, f32[1472,128]{1,0:T(8,128)S(1)} %collective-permute-done.1.above_ref, ...), custom_call_target="tpu_custom_call" | custom-call | tf_op jit(solution)/shard_map/outer/pallas_call | solution.py:241
  66.5 21.5 %all_to_all.10 = f32[8,336,128]{2,1,0:T(8,128)S(1)} all-to-all(f32[8,336,128]{2,1,0:T(8,128)S(1)} %bitcast.15), channel_id=1, replica_groups={{0,1,2,3,4,5,6,7},{8,9,10,11,12,13,14,15},{16,17,18,19,20,21,22,23},{24..., dimensions={0} | all-to-all | bytes 2752512 | tf_op jit(solution)/shard_map/all_to_all | solution.py:261
  87.9 1.2 %copy.8 = f32[8,21,16,128]{3,2,0,1:T(8,128)} copy(f32[8,21,16,128]{3,2,1,0:T(8,128)S(1)} %bitcast.18) | data formatting | bytes 2752512 | tf_op jit(solution)/shard_map/reshape | solution.py:282
  (2 shorter events, 0.0 us)
Async XLA Ops:
  0.0 1.3 %copy-start = (f32[21,1,128,128]{3,2,1,0:T(8,128)S(1)}, f32[21,1,128,128]{3,2,1,0:T(8,128)}, u32[]{:S(2)}) copy-start(f32[21,1,128,128]{3,2,1,0:T(8,128)} %param.6) | copy-start | bytes 4128772
  1.3 1.0 %copy-start.1 = (f32[6,1,128,128]{3,2,1,0:T(8,128)S(1)}, f32[6,1,128,128]{3,2,1,0:T(8,128)}, u32[]{:S(2)}) copy-start(f32[6,1,128,128]{3,2,1,0:T(8,128)} %param.8) | copy-start | bytes 1179652
  2.3 0.8 copy-start.2
  4.6 5.3 %copy-start.3 = (s32[7,84,84]{2,1,0:T(8,128)S(1)}, s32[7,84,84]{2,1,0:T(8,128)}, u32[]{:S(2)}) copy-start(s32[7,84,84]{2,1,0:T(8,128)} %param.9) | copy-start | bytes 592708
  4.6 6.0 %copy-start.4 = (f32[7,84,84]{2,1,0:T(8,128)S(1)}, f32[7,84,84]{2,1,0:T(8,128)}, u32[]{:S(2)}) copy-start(f32[7,84,84]{2,1,0:T(8,128)} %param.10) | copy-start | bytes 592708
  4.6 26.8 %all-to-all-start = ((f32[8,416,128]{2,1,0:T(8,128)}), f32[8,416,128]{2,1,0:T(8,128)S(1)}, u32[]{:S(2)}, u32[]{:S(2)}) async-start(f32[8,416,128]{2,1,0:T(8,128)} %pack.1), calls=%async_computation | async-start | bytes 3407872 | tf_op jit(solution)/shard_map/all_to_all | solution.py:261
  31.4 6.4 %copy-start.5 = (s32[84]{0:T(128)S(1)}, s32[84]{0:T(128)}, u32[]{:S(2)}) copy-start(s32[84]{0:T(128)} %param.11) | copy-start | bytes 1012
  32.6 20.2 %collective-permute-start = (f32[1472,128]{1,0:T(8,128)}, f32[1472,128]{1,0:T(8,128)S(1)}, u32[]{:S(2)}, u32[]{:S(2)}) collective-permute-start(f32[1472,128]{1,0:T(8,128)} %bitcast.5), channel_id=1, source_target_pairs={{0,8},{4,12},{8,16},{12,20},{16,24},{20,28},{1,9},{5,13},{9,17},{1... | collective-permute-start | bytes 2261000 | tf_op jit(solution)/shard_map/ppermute | solution.py:274
  36.1 20.2 %collective-permute-start.1 = (f32[1472,128]{1,0:T(8,128)}, f32[1472,128]{1,0:T(8,128)S(1)}, u32[]{:S(2)}, u32[]{:S(2)}) collective-permute-start(f32[1472,128]{1,0:T(8,128)} %bitcast.6), channel_id=1, source_target_pairs={{8,0},{12,4},{16,8},{20,12},{24,16},{28,20},{9,1},{13,5},{17,9},{2... | collective-permute-start | bytes 2261000 | tf_op jit(solution)/shard_map/ppermute | solution.py:275

commit v2 on v1

v2 whole, which is shorter than its diff:
```python
import jax
import jax.numpy as jnp
from jax import lax
from jax.experimental import pallas as pl
from jax.experimental.pallas import tpu as pltpu
from jax.sharding import PartitionSpec as P

VMEM_LIMIT = 48 * 1024 * 1024
PLANES = 2
ACTIVE = 49
MOST = 8
UNROLL = 7


class Layout:
    def __init__(self, quota, terms, modes, height):
        self.modes = modes
        self.group = PLANES * modes
        self.rows = height // self.group
        self.quota = quota
        self.slots = quota * modes
        self.share = -(-terms // modes)
        self.fields = quota + self.share
        self.parts = self.fields + -(-2 * self.fields // self.rows)
        self.main = self.fields * self.rows
        self.block = self.parts * self.rows

    def coef(self, term):
        return term // self.share, self.quota + term % self.share

    def edge(self, i, side):
        at = 2 * i + side
        return self.fields + at // self.rows, at % self.rows


def vmem(count):
    return [pl.BlockSpec(memory_space=pltpu.VMEM)] * count


def smem(count):
    return [pl.BlockSpec(memory_space=pltpu.SMEM)] * count


def pack(field, mean, kl, mode, lay):
    kl_terms = kl.shape[0]
    width = field.shape[2]
    rows = lay.rows

    def kernel(mode_ref, field_ref, mean_ref, kl_ref, out_ref, mean_here, kl_here, sems):
        copies = [
            pltpu.make_async_copy(mean_ref, mean_here, sems.at[lay.group]),
            pltpu.make_async_copy(kl_ref, kl_here, sems.at[lay.group + 1]),
        ]
        for j in range(lay.group):
            copies.append(
                pltpu.make_async_copy(
                    field_ref.at[:, pl.ds(j * rows, rows), :],
                    out_ref.at[j, pl.ds(0, lay.quota)],
                    sems.at[j],
                )
            )
        for copy in copies:
            copy.start()
        copies[0].wait()
        copies[1].wait()
        for i in range(lay.share):
            term = mode_ref[0] * lay.share + i
            value = jnp.where(
                term == 0, mean_here[0], kl_here[jnp.clip(term - 1, 0, kl_terms - 1)]
            )
            for j in range(lay.group):
                out_ref[j, lay.quota + i] = value[j * rows : (j + 1) * rows]
        for copy in copies[2:]:
            copy.wait()
        none = jnp.zeros((1, width), jnp.float32)
        for j in range(lay.group):
            for i in range(lay.fields):
                low = out_ref[j - 1, i, rows - 1 :] if j > 0 else none
                high = out_ref[j + 1, i, :1] if j < lay.group - 1 else none
                for side, value in enumerate((low, high)):
                    part, line = lay.edge(i, side)
                    out_ref[j, part, line : line + 1] = value
            part, line = lay.edge(lay.fields, 0)
            if part < lay.parts:
                out_ref[j, part, line:] = jnp.zeros((rows - line, width), jnp.float32)

    return pl.pallas_call(
        kernel,
        out_shape=jax.ShapeDtypeStruct((lay.group, lay.parts, rows, width), jnp.float32),
        in_specs=smem(1) + [pl.BlockSpec(memory_space=pl.ANY)] * 3,
        out_specs=vmem(1)[0],
        scratch_shapes=[
            pltpu.VMEM(mean.shape, jnp.float32),
            pltpu.VMEM(kl.shape, jnp.float32),
            pltpu.SemaphoreType.DMA((lay.group + 2,)),
        ],
        compiler_params=pltpu.CompilerParams(vmem_limit_bytes=VMEM_LIMIT),
        name="pack",
    )(mode, field, mean, kl)


def coupling_lists(pattern, coupling, slot_mode):
    masked = (coupling * pattern.astype(jnp.float32))[1:]
    terms, modes = masked.shape[0], masked.shape[1]
    number = jnp.arange(modes, dtype=jnp.int32)
    one_hot = (slot_mode[:, None] == number[None, :]).astype(jnp.float32)
    coupled = jnp.einsum(
        "sa,kab,tb->kst", one_hot, masked, one_hot, precision=lax.Precision.HIGHEST
    )
    there = coupled != 0.0
    column = number[None, None, :]
    first = jnp.min(jnp.where(there, column, modes), 2)
    last = jnp.max(jnp.where(there, column, -1), 2)
    active = first < modes
    earlier = column < number[None, :, None]
    rank = jnp.sum(jnp.where(active[:, None, :] & earlier, 1, 0), 2)
    place = jnp.arange(ACTIVE, dtype=jnp.int32)[None, :, None]
    chosen = active[:, None, :] & (rank[:, None, :] == place)
    sources = jnp.sum(jnp.where(chosen, column, 0), 2)

    base = ACTIVE * jnp.arange(terms, dtype=jnp.int32)[:, None]
    products, factors, valid = [], [], []
    for chosen_t, is_valid in ((first, active), (last, last > first)):
        before = active[:, None, :] & (column < chosen_t[:, :, None])
        products.append(base + jnp.sum(jnp.where(before, 1, 0), 2))
        factors.append(jnp.sum(jnp.where(column == chosen_t[:, :, None], coupled, 0.0), 2))
        valid.append(is_valid)
    products = jnp.concatenate(products, 0)
    factors = jnp.concatenate(factors, 0)
    valid = jnp.concatenate(valid, 0)
    index = jnp.arange(2 * terms, dtype=jnp.int32)
    order = index[None, :] < index[:, None]
    rank = jnp.sum(jnp.where(valid[None] & order[:, :, None], 1, 0), 1)
    place = jnp.arange(MOST, dtype=jnp.int32)[:, None, None]
    chosen = valid[None] & (rank[None] == place)
    take = jnp.sum(jnp.where(chosen, products[None], 0), 1)
    factor = jnp.sum(jnp.where(chosen, factors[None], 0.0), 1)
    return sources.reshape(-1), take.T.reshape(-1), factor.T.reshape(-1)


def gather_products(s, take_ref, factor_ref, product_ref, p, total):
    for n in range(MOST):
        e = s * MOST + n
        total = total + factor_ref[e] * product_ref[take_ref[e], p]
    return total


def inner(gathered, lists, terms, lay):
    rows = lay.rows
    width = gathered.shape[2]
    full = (rows, width)

    def kernel(source_ref, take_ref, factor_ref, g_ref, out_ref, near_ref, product_ref):
        lane = lax.broadcasted_iota(jnp.int32, full, 1)
        line = lax.broadcasted_iota(jnp.int32, full, 0)

        def neighbours(p, block, i):
            at = block * lay.block
            here = g_ref[p, pl.ds(at + i * rows, rows), :]
            low = g_ref[p, pl.ds(at + lay.main + 2 * i, 1), :]
            high = g_ref[p, pl.ds(at + lay.main + 2 * i + 1, 1), :]
            right = pltpu.roll(here, width - 1, 1)
            left = pltpu.roll(here, 1, 1)
            above = jnp.where(line == rows - 1, high, pltpu.roll(here, rows - 1, 0))
            below = jnp.where(line == 0, low, pltpu.roll(here, 1, 0))
            return here, right, left, above, below

        for block in range(lay.modes):

            def spread(i, carry, block=block):
                for p in range(PLANES):
                    for n, value in enumerate(neighbours(p, block, i)):
                        near_ref[block * lay.quota + i, p, n] = value
                return carry

            lax.fori_loop(0, lay.quota, spread, 0, unroll=UNROLL)

        def operator_of(term):
            block, i = lay.coef(term)
            weights = []
            centres = []
            for p in range(PLANES):
                here, right, left, above, below = neighbours(p, block, i)
                right = jnp.where(lane == width - 1, 0.0, right)
                left = jnp.where(lane == 0, 0.0, left)
                faces = [0.5 * (here + n) for n in (right, left, above, below)]
                centres.append(here)
                diagonal = faces[0] + faces[1] + faces[2] + faces[3] + 0.5 * here
                faces[0] = jnp.where(lane == width - 1, 0.0, faces[0])
                faces[1] = jnp.where(lane == 0, 0.0, faces[1])
                weights.append([diagonal] + [-f for f in faces])
            between = 0.5 * (centres[0] + centres[1])
            for p in range(PLANES):
                weights[p][0] = weights[p][0] + between

            def operator(t, p):
                total = weights[p][0] * near_ref[t, p, 0]
                for n in range(1, 5):
                    total = total + weights[p][n] * near_ref[t, p, n]
                return total - between * near_ref[t, 1 - p, 0]

            return operator

        for term in range(1, terms):
            operator = operator_of(term)

            def apply(n, carry, operator=operator, term=term):
                e = (term - 1) * ACTIVE + n
                t = source_ref[e]
                for p in range(PLANES):
                    product_ref[e, p] = operator(t, p)
                return carry

            lax.fori_loop(0, ACTIVE, apply, 0, unroll=UNROLL)

        operator = operator_of(0)

        def collect(s, carry):
            for p in range(PLANES):
                out_ref[p, s] = gather_products(
                    s, take_ref, factor_ref, product_ref, p, operator(s, p)
                )
            return carry

        lax.fori_loop(0, lay.slots, collect, 0, unroll=UNROLL)

    return pl.pallas_call(
        kernel,
        out_shape=jax.ShapeDtypeStruct((PLANES, lay.slots, rows, width), jnp.float32),
        in_specs=smem(3) + vmem(1),
        out_specs=vmem(1)[0],
        scratch_shapes=[
            pltpu.VMEM((lay.slots, PLANES, 5, rows, width), jnp.float32),
            pltpu.VMEM(((terms - 1) * ACTIVE, PLANES, rows, width), jnp.float32),
        ],
        compiler_params=pltpu.CompilerParams(vmem_limit_bytes=VMEM_LIMIT),
        name="inner",
    )(*lists, gathered)


def outer(gathered, below, above, partial, lists, terms, lay):
    rows = lay.rows
    width = gathered.shape[2]

    def kernel(
        source_ref, take_ref, factor_ref, g_ref, below_ref, above_ref, part_ref, out_ref, product_ref
    ):
        far_refs = (below_ref, above_ref)

        def operator_of(term):
            block, i = lay.coef(term)
            weights = []
            for p in range(PLANES):
                here = g_ref[p, pl.ds(block * lay.block + i * rows, rows), :]
                far = far_refs[p][pl.ds(block * lay.main + i * rows, rows), :]
                weights.append((0.5 * far, 0.5 * (here + far)))

            def operator(t, p):
                block = t // lay.quota
                i = t - block * lay.quota
                near_at = pl.multiple_of(block * lay.block + i * rows, 8)
                far_at = pl.multiple_of(block * lay.main + i * rows, 8)
                here = g_ref[p, pl.ds(near_at, rows), :]
                far = far_refs[p][pl.ds(far_at, rows), :]
                return weights[p][0] * here - weights[p][1] * far

            return operator

        for term in range(1, terms):
            operator = operator_of(term)

            def apply(n, carry, operator=operator, term=term):
                e = (term - 1) * ACTIVE + n
                t = source_ref[e]
                for p in range(PLANES):
                    product_ref[e, p] = operator(t, p)
                return carry

            lax.fori_loop(0, ACTIVE, apply, 0, unroll=UNROLL)

        operator = operator_of(0)

        def collect(s, carry):
            for p in range(PLANES):
                out_ref[p, s] = gather_products(
                    s, take_ref, factor_ref, product_ref, p, part_ref[p, s] + operator(s, p)
                )
            return carry

        lax.fori_loop(0, lay.slots, collect, 0, unroll=UNROLL)

    return pl.pallas_call(
        kernel,
        out_shape=jax.ShapeDtypeStruct((PLANES, lay.slots, rows, width), jnp.float32),
        in_specs=smem(3) + vmem(4),
        out_specs=vmem(1)[0],
        scratch_shapes=[pltpu.VMEM(((terms - 1) * ACTIVE, PLANES, rows, width), jnp.float32)],
        compiler_params=pltpu.CompilerParams(vmem_limit_bytes=VMEM_LIMIT),
        name="outer",
    )(*lists, gathered, below, above, partial)


def on_device(chaos_field, mean_field, kl_fields, pattern, coupling, slot_mode):
    spaces, modes = lax.axis_size("space"), lax.axis_size("mode")
    quota, _, height, width = chaos_field.shape
    terms = kl_fields.shape[0] + 1
    lay = Layout(quota, terms, modes, height)
    groups = [
        list(range(start, start + lay.group)) for start in range(0, spaces * modes, lay.group)
    ]

    def exchange(blocks):
        return lax.all_to_all(
            blocks, ("space", "mode"), 0, 0, axis_index_groups=groups, tiled=True
        )

    mode = lax.axis_index("mode").astype(jnp.int32).reshape(1)
    blocks = pack(chaos_field[:, 0], mean_field, kl_fields[:, 0], mode, lay)
    lists = coupling_lists(pattern, coupling, slot_mode)
    gathered = exchange(blocks.reshape(lay.group, lay.block, width))

    main = gathered.reshape(PLANES, modes, lay.block, width)[:, :, : lay.main]
    main = main.reshape(PLANES, modes * lay.main, width)
    up = [(i, i + PLANES) for i in range(spaces - PLANES)]
    down = [(target, source) for source, target in up]
    below = lax.ppermute(main[PLANES - 1], "space", up)
    above = lax.ppermute(main[0], "space", down)

    planes = gathered.reshape(PLANES, modes * lay.block, width)
    partial = inner(planes, lists, terms, lay)
    total = outer(planes, below, above, partial, lists, terms, lay)

    back = exchange(total.reshape(lay.group, quota * lay.rows, width))
    back = back.reshape(lay.group, quota, lay.rows, width).transpose(1, 0, 2, 3)
    return back.reshape(chaos_field.shape)


def solution(mesh):
    in_specs = (
        P("mode", "space", None, None),
        P("space", None, None),
        P(None, "space", None, None),
        P(),
        P(),
        P(),
    )
    out_specs = P("mode", "space", None, None)
    return jax.shard_map(
        on_device, mesh=mesh, in_specs=in_specs, out_specs=out_specs, check_vma=False
    )
```

time: 89.6 us -> 86 us (0.960)
  Pallas kernels: 25.4 us -> 14.4 us
  waiting for transfers between devices: 23.8 us -> 31.4 us
  other arithmetic: 2.39 us -> 0.91 us
    pallas_call x3, Pallas kernels: 25.4 us -> 14.4 us  [the longest x1 6.47 us: inner(): pl.pallas_call(kernel, out_shape=jax.ShapeDtypeStruct((PLANES, lay.slots,...]
    ppermute x1, waiting for transfers between devices: 0.01 us -> 7.83 us  [on_device(): below = lax.ppermute(main[PLANES - 1], 'space', up)]
    reduce_sum x6, other arithmetic: 1.78 us -> 0.66 us  [the longest x1 0.24 us: coupling_lists(): products.append(base + jnp.sum(jnp.where(before, 1, 0), 2))]
    unnamed x12 -> x14, local copies, waits for them, and re-layouts: 3.18 us -> 3.58 us
  transfers between devices with their start and end apart: 3 -> 3, of which waited for: 2 -> 3; matrix products, arithmetic and copies ran while one was open for 3% -> 3% of each run, Pallas kernels for 16% -> 8%
where the time goes in v2:
time: 86 us; the launch traced here: 85.6 us
  waiting for transfers between devices  31.4 us (37%)
  blocking collectives  21.5 us (25%)
  Pallas kernels  14.4 us (17%)
  starting transfers between devices  10.1 us (12%)
  local copies, waits for them, and re-layouts  6.49 us (8%)
  other arithmetic  0.91 us (1%)
    all_to_all x1, blocking collectives, exchange(): lax.all_to_all(blocks, ('space', 'mode'), 0, 0, axis_index_groups=groups,...  21.5 us
    all_to_all x1, waiting for transfers between devices, exchange(): lax.all_to_all(blocks, ('space', 'mode'), 0, 0, axis_index_groups=groups,...  19.5 us
    ppermute x1, waiting for transfers between devices, on_device(): below = lax.ppermute(main[PLANES - 1], 'space', up)  7.83 us
    pallas_call x1, Pallas kernels, inner(): pl.pallas_call(kernel, out_shape=jax.ShapeDtypeStruct((PLANES, lay.slots,...  6.47 us
    pallas_call x1, Pallas kernels, outer(): pl.pallas_call(kernel, out_shape=jax.ShapeDtypeStruct((PLANES, lay.slots,...  6.05 us
    all_to_all x1, starting transfers between devices, exchange(): lax.all_to_all(blocks, ('space', 'mode'), 0, 0, axis_index_groups=groups,...  5.31 us
    ppermute x1, waiting for transfers between devices, on_device(): above = lax.ppermute(main[0], 'space', down)  4.05 us
    unnamed x14, local copies, waits for them, and re-layouts  3.58 us
  transfers between devices with their start and end apart: 3, of which 3 were waited for; matrix products, arithmetic and copies ran while one was open for 3% of the time, Pallas kernels for 8%

profile of v2, /device:TPU:0, one launch (start us, length us, event | category | flops | bytes accessed | tf_op | source)
XLA Modules:
  0.0 85.6 jit_solution(3476403521663588865)
XLA Ops:
  0.0 0.0 copy-start
  0.0 1.3 %copy-done = f32[21,1,128,128]{3,2,1,0:T(8,128)S(1)} copy-done((f32[21,1,128,128]{3,2,1,0:T(8,128)S(1)}, f32[21,1,128,128]{3,2,1,0:T(8,128)}, u32[]{:S(2)}) %copy-start) | copy-done | bytes 1376280
  1.3 0.0 copy-start.1
  1.3 1.0 %copy-done.1 = f32[6,1,128,128]{3,2,1,0:T(8,128)S(1)} copy-done((f32[6,1,128,128]{3,2,1,0:T(8,128)S(1)}, f32[6,1,128,128]{3,2,1,0:T(8,128)}, u32[]{:S(2)}) %copy-start.1) | copy-done | bytes 393240
  2.3 0.0 copy-start.2
  2.3 0.8 copy-done.2
  3.2 1.9 %pack.1 = f32[8,26,16,128]{3,2,1,0:T(8,128)} custom-call(s32[1]{0:T(128)} %bitcast.3.mode_ref, f32[21,128,128]{2,1,0:T(8,128)S(1)} %bitcast.26, f32[1,128,128]{2,1,0:T(8,128)S(1)} %copy-done.2, f32[6,128,128]{2,1,0:T(8,128)S(1)} %bitcast.27), custom_call_target="tpu_custom_call" | custom-call | tf_op jit(solution)/shard_map/pack/pallas_call | solution.py:87
  5.0 0.0 copy-start.3
  5.1 0.0 copy-start.4
  5.1 0.0 copy-start.5
  5.1 5.3 %all-to-all-start = ((f32[8,416,128]{2,1,0:T(8,128)}), f32[8,416,128]{2,1,0:T(8,128)S(1)}, u32[]{:S(2)}, u32[]{:S(2)}) async-start(f32[8,416,128]{2,1,0:T(8,128)} %bitcast.6), calls=%async_computation | async-start | bytes 3407872 | tf_op jit(solution)/shard_map/all_to_all | solution.py:313
  10.4 0.0 copy-done.3
  10.4 0.2 copy.9
  10.6 0.0 copy-done.4
  10.6 0.2 copy.10
  10.8 0.0 copy-done.5
  10.8 0.4 fusion
  11.2 0.3 fusion.10
  11.5 0.1 fusion.6
  11.7 0.2 select_reduce_fusion.3
  11.9 0.2 select_reduce_fusion.5
  12.1 0.1 reshape.74.source_ref
  12.2 0.1 select_reduce_fusion.6
  12.3 0.1 select_reduce_fusion.1
  12.4 19.5 %all-to-all-done = f32[8,416,128]{2,1,0:T(8,128)S(1)} async-done(((f32[8,416,128]{2,1,0:T(8,128)}), f32[8,416,128]{2,1,0:T(8,128)S(1)}, u32[]{:S(2)}, u32[]{:S(2)}) %all-to-all-start) | async-done | bytes 1703968 | tf_op jit(solution)/shard_map/all_to_all | solution.py:313
  31.9 1.2 %fusion.18 = (f32[1,4,368,128]{3,2,1,0:T(8,128)}, f32[1,4,368,128]{3,2,1,0:T(8,128)}) fusion(f32[2,4,416,128]{3,2,1,0:T(8,128)S(1)} %bitcast.22), kind=kLoop, calls=%fused_computation.43 | loop fusion | bytes 3014656 | tf_op jit(solution)/shard_map/slice | solution.py:327
  33.1 3.5 %collective-permute-start = (f32[1472,128]{1,0:T(8,128)}, f32[1472,128]{1,0:T(8,128)S(1)}, u32[]{:S(2)}, u32[]{:S(2)}) collective-permute-start(f32[1472,128]{1,0:T(8,128)} %bitcast.9), channel_id=1, source_target_pairs={{0,8},{4,12},{8,16},{12,20},{16,24},{20,28},{1,9},{5,13},{9,17},{1... | collective-permute-start | bytes 2261000 | tf_op jit(solution)/shard_map/ppermute | solution.py:326
  36.6 1.3 %collective-permute-start.1 = (f32[1472,128]{1,0:T(8,128)}, f32[1472,128]{1,0:T(8,128)S(1)}, u32[]{:S(2)}, u32[]{:S(2)}) collective-permute-start(f32[1472,128]{1,0:T(8,128)} %bitcast.10), channel_id=1, source_target_pairs={{8,0},{12,4},{16,8},{20,12},{24,16},{28,20},{9,1},{13,5},{17,9},{2... | collective-permute-start | bytes 2261000 | tf_op jit(solution)/shard_map/ppermute | solution.py:327
  38.0 0.1 copy.12
  38.1 0.1 reshape.76.factor_ref
  38.2 0.1 broadcast_add_fusion.1
  38.3 0.1 copy.11
  38.4 0.1 reshape.75.take_ref
  38.5 6.5 %inner.1.part_ref = f32[2,84,16,128]{3,2,1,0:T(8,128)S(1)} custom-call(s32[294]{0:T(512)S(1)} %reshape.74.source_ref, s32[672]{0:T(1024)S(1)} %reshape.75.take_ref, f32[672]{0:T(1024)S(1)} %reshape.76.factor_ref, f32[2,1664,128]{2,1,0:T(8,128)S(1)} %bitcast.23), custom_call_target="tpu_custom_call" | custom-call | tf_op jit(solution)/shard_map/inner/pallas_call | solution.py:227
  44.9 7.8 %collective-permute-done.below_ref = f32[1472,128]{1,0:T(8,128)S(1)} collective-permute-done((f32[1472,128]{1,0:T(8,128)}, f32[1472,128]{1,0:T(8,128)S(1)}, u32[]{:S(2)}, u32[]{:S(2)}) %collective-permute-start) | collective-permute-done | bytes 753696 | tf_op jit(solution)/shard_map/ppermute | solution.py:326
  52.8 4.1 %collective-permute-done.1.above_ref = f32[1472,128]{1,0:T(8,128)S(1)} collective-permute-done((f32[1472,128]{1,0:T(8,128)}, f32[1472,128]{1,0:T(8,128)S(1)}, u32[]{:S(2)}, u32[]{:S(2)}) %collective-permute-start.1) | collective-permute-done | bytes 753696 | tf_op jit(solution)/shard_map/ppermute | solution.py:327
  56.8 6.0 %outer.1 = f32[2,84,16,128]{3,2,1,0:T(8,128)S(1)} custom-call(s32[294]{0:T(512)S(1)} %reshape.74.source_ref, s32[672]{0:T(1024)S(1)} %reshape.75.take_ref, f32[672]{0:T(1024)S(1)} %reshape.76.factor_ref, f32[2,1664,128]{2,1,0:T(8,128)S(1)} %bitcast.24, f32[1472,128]{1,0:T(8,128)S(1)} %collective-permute-done.below_ref, ...), custom_call_target="tpu_custom_call" | custom-call | tf_op jit(solution)/shard_map/outer/pallas_call | solution.py:292
  62.9 21.5 %all_to_all.10 = f32[8,336,128]{2,1,0:T(8,128)S(1)} all-to-all(f32[8,336,128]{2,1,0:T(8,128)S(1)} %bitcast.25), channel_id=1, replica_groups={{0,1,2,3,4,5,6,7},{8,9,10,11,12,13,14,15},{16,17,18,19,20,21,22,23},{24..., dimensions={0} | all-to-all | bytes 2752512 | tf_op jit(solution)/shard_map/all_to_all | solution.py:313
  84.3 1.2 %copy.13 = f32[8,21,16,128]{3,2,0,1:T(8,128)} copy(f32[8,21,16,128]{3,2,1,0:T(8,128)S(1)} %bitcast.28) | data formatting | bytes 2752512 | tf_op jit(solution)/shard_map/reshape | solution.py:334
  (9 shorter events, 0.1 us)
Async XLA Ops:
  0.0 1.3 %copy-start = (f32[21,1,128,128]{3,2,1,0:T(8,128)S(1)}, f32[21,1,128,128]{3,2,1,0:T(8,128)}, u32[]{:S(2)}) copy-start(f32[21,1,128,128]{3,2,1,0:T(8,128)} %param.6) | copy-start | bytes 4128772
  1.3 1.0 %copy-start.1 = (f32[6,1,128,128]{3,2,1,0:T(8,128)S(1)}, f32[6,1,128,128]{3,2,1,0:T(8,128)}, u32[]{:S(2)}) copy-start(f32[6,1,128,128]{3,2,1,0:T(8,128)} %param.8) | copy-start | bytes 1179652
  2.3 0.8 copy-start.2
  5.0 5.4 %copy-start.3 = (s32[7,84,84]{2,1,0:T(8,128)S(1)}, s32[7,84,84]{2,1,0:T(8,128)}, u32[]{:S(2)}) copy-start(s32[7,84,84]{2,1,0:T(8,128)} %param.9) | copy-start | bytes 592708
  5.1 5.5 %copy-start.4 = (f32[7,84,84]{2,1,0:T(8,128)S(1)}, f32[7,84,84]{2,1,0:T(8,128)}, u32[]{:S(2)}) copy-start(f32[7,84,84]{2,1,0:T(8,128)} %param.10) | copy-start | bytes 592708
  5.1 5.7 %copy-start.5 = (s32[84]{0:T(128)S(1)}, s32[84]{0:T(128)}, u32[]{:S(2)}) copy-start(s32[84]{0:T(128)} %param.11) | copy-start | bytes 1012
  5.1 26.8 %all-to-all-start = ((f32[8,416,128]{2,1,0:T(8,128)}), f32[8,416,128]{2,1,0:T(8,128)S(1)}, u32[]{:S(2)}, u32[]{:S(2)}) async-start(f32[8,416,128]{2,1,0:T(8,128)} %bitcast.6), calls=%async_computation | async-start | bytes 3407872 | tf_op jit(solution)/shard_map/all_to_all | solution.py:313
  33.1 19.7 %collective-permute-start = (f32[1472,128]{1,0:T(8,128)}, f32[1472,128]{1,0:T(8,128)S(1)}, u32[]{:S(2)}, u32[]{:S(2)}) collective-permute-start(f32[1472,128]{1,0:T(8,128)} %bitcast.9), channel_id=1, source_target_pairs={{0,8},{4,12},{8,16},{12,20},{16,24},{20,28},{1,9},{5,13},{9,17},{1... | collective-permute-start | bytes 2261000 | tf_op jit(solution)/shard_map/ppermute | solution.py:326
  36.6 20.2 %collective-permute-start.1 = (f32[1472,128]{1,0:T(8,128)}, f32[1472,128]{1,0:T(8,128)S(1)}, u32[]{:S(2)}, u32[]{:S(2)}) collective-permute-start(f32[1472,128]{1,0:T(8,128)} %bitcast.10), channel_id=1, source_target_pairs={{8,0},{12,4},{16,8},{20,12},{24,16},{28,20},{9,1},{13,5},{17,9},{2... | collective-permute-start | bytes 2261000 | tf_op jit(solution)/shard_map/ppermute | solution.py:327

commit v3 on v2

--- a/solution.py
+++ b/solution.py
@@ -9,6 +9,7 @@
 PLANES = 2
 ACTIVE = 49
 MOST = 8
+CHUNKS = 2
 UNROLL = 7
 
 
@@ -16,7 +17,7 @@
     def __init__(self, quota, terms, modes, height):
         self.modes = modes
         self.group = PLANES * modes
-        self.rows = height // self.group
+        self.rows = height // (CHUNKS * self.group)
         self.quota = quota
         self.slots = quota * modes
         self.share = -(-terms // modes)
@@ -41,42 +42,59 @@
     return [pl.BlockSpec(memory_space=pltpu.SMEM)] * count
 
 
-def pack(field, mean, kl, mode, lay):
+def pack(field, mean, kl, mode, chunk, lay):
     kl_terms = kl.shape[0]
-    width = field.shape[2]
+    height, width = field.shape[1:]
     rows = lay.rows
-
-    def kernel(mode_ref, field_ref, mean_ref, kl_ref, out_ref, mean_here, kl_here, sems):
-        copies = [
-            pltpu.make_async_copy(mean_ref, mean_here, sems.at[lay.group]),
-            pltpu.make_async_copy(kl_ref, kl_here, sems.at[lay.group + 1]),
+    start = chunk * lay.group * rows
+    end = start + lay.group * rows
+    before, after = start > 0, end < height
+
+    def kernel(mode_ref, field_ref, mean_ref, kl_ref, out_ref, mean_here, kl_here, low_here, high_here, sems):
+        def copy(source, target, n):
+            made = pltpu.make_async_copy(source, target, sems.at[n])
+            made.start()
+            return made
+
+        coefs = [copy(mean_ref, mean_here, lay.group), copy(kl_ref, kl_here, lay.group + 1)]
+        fields = [
+            copy(
+                field_ref.at[:, pl.ds(start + j * rows, rows), :],
+                out_ref.at[j, pl.ds(0, lay.quota)],
+                j,
+            )
+            for j in range(lay.group)
         ]
-        for j in range(lay.group):
-            copies.append(
-                pltpu.make_async_copy(
-                    field_ref.at[:, pl.ds(j * rows, rows), :],
-                    out_ref.at[j, pl.ds(0, lay.quota)],
-                    sems.at[j],
-                )
-            )
-        for copy in copies:
-            copy.start()
-        copies[0].wait()
-        copies[1].wait()
+        if before:
+            fields.append(copy(field_ref.at[:, pl.ds(start - 8, 8), :], low_here, lay.group + 2))
+        if after:
+            fields.append(copy(field_ref.at[:, pl.ds(end, 8), :], high_here, lay.group + 3))
+        for made in coefs:
+            made.wait()
+        values = []
         for i in range(lay.share):
             term = mode_ref[0] * lay.share + i
             value = jnp.where(
                 term == 0, mean_here[0], kl_here[jnp.clip(term - 1, 0, kl_terms - 1)]
             )
+            values.append(value)
             for j in range(lay.group):
-                out_ref[j, lay.quota + i] = value[j * rows : (j + 1) * rows]
-        for copy in copies[2:]:
-            copy.wait()
+                out_ref[j, lay.quota + i] = value[start + j * rows : start + (j + 1) * rows]
+        for made in fields:
+            made.wait()
         none = jnp.zeros((1, width), jnp.float32)
         for j in range(lay.group):
             for i in range(lay.fields):
-                low = out_ref[j - 1, i, rows - 1 :] if j > 0 else none
-                high = out_ref[j + 1, i, :1] if j < lay.group - 1 else none
+                own = i < lay.quota
+                low, high = none, none
+                if j > 0:
+                    low = out_ref[j - 1, i, rows - 1 :]
+                elif before:
+                    low = low_here[i, 7:] if own else values[i - lay.quota][start - 1 : start]
+                if j < lay.group - 1:
+                    high = out_ref[j + 1, i, :1]
+                elif after:
+                    high = high_here[i, :1] if own else values[i - lay.quota][end : end + 1]
                 for side, value in enumerate((low, high)):
                     part, line = lay.edge(i, side)
                     out_ref[j, part, line : line + 1] = value
@@ -87,19 +105,48 @@
     return pl.pallas_call(
         kernel,
         out_shape=jax.ShapeDtypeStruct((lay.group, lay.parts, rows, width), jnp.float32),
-        in_specs=smem(1) + [pl.BlockSpec(memory_space=pl.ANY)] * 3,
+        in_specs=smem(1) + [pl.BlockSpec(memory_space=pltpu.HBM)] * 3,
         out_specs=vmem(1)[0],
         scratch_shapes=[
             pltpu.VMEM(mean.shape, jnp.float32),
             pltpu.VMEM(kl.shape, jnp.float32),
-            pltpu.SemaphoreType.DMA((lay.group + 2,)),
+            pltpu.VMEM((lay.quota, 8, width), jnp.float32),
+            pltpu.VMEM((lay.quota, 8, width), jnp.float32),
+            pltpu.SemaphoreType.DMA((lay.group + 4,)),
         ],
         compiler_params=pltpu.CompilerParams(vmem_limit_bytes=VMEM_LIMIT),
         name="pack",
     )(mode, field, mean, kl)
 
 
-def coupling_lists(pattern, coupling, slot_mode):
+def unpack(parts, shape, lay):
+    rows = lay.rows
+
+    def kernel(*refs):
+        part_refs, out_ref, sems = refs[:-2], refs[-2], refs[-1]
+        copies = []
+        for c, part_ref in enumerate(part_refs):
+            for j in range(lay.group):
+                n = c * lay.group + j
+                made = pltpu.make_async_copy(
+                    part_ref.at[j], out_ref.at[:, pl.ds(n * rows, rows), :], sems.at[n]
+                )
+                made.start()
+                copies.append(made)
+        for made in copies:
+            made.wait()
+
+    return pl.pallas_call(
+        kernel,
+        out_shape=jax.ShapeDtypeStruct(shape, jnp.float32),
+        in_specs=[pl.BlockSpec(memory_space=pl.ANY)] * len(parts),
+        out_specs=pl.BlockSpec(memory_space=pl.ANY),
+        scratch_shapes=[pltpu.SemaphoreType.DMA((CHUNKS * lay.group,))],
+        name="unpack",
+    )(*parts)
+
+
+def coupling_lists(pattern, coupling, slot_mode, lay):
     masked = (coupling * pattern.astype(jnp.float32))[1:]
     terms, modes = masked.shape[0], masked.shape[1]
     number = jnp.arange(modes, dtype=jnp.int32)
@@ -135,7 +182,13 @@
     chosen = valid[None] & (rank[None] == place)
     take = jnp.sum(jnp.where(chosen, products[None], 0), 1)
     factor = jnp.sum(jnp.where(chosen, factors[None], 0.0), 1)
-    return sources.reshape(-1), take.T.reshape(-1), factor.T.reshape(-1)
+    sources = sources.reshape(-1)
+    block = jnp.zeros_like(sources)
+    for n in range(1, lay.modes):
+        block = block + jnp.where(sources >= n * lay.quota, 1, 0)
+    far = sources * lay.rows + block * (lay.main - lay.quota * lay.rows)
+    near = far + block * (lay.block - lay.main)
+    return sources, near, far, take.T.reshape(-1), factor.T.reshape(-1)
 
 
 def gather_products(s, take_ref, factor_ref, product_ref, p, total):
@@ -235,7 +288,7 @@
         ],
         compiler_params=pltpu.CompilerParams(vmem_limit_bytes=VMEM_LIMIT),
         name="inner",
-    )(*lists, gathered)
+    )(lists[0], *lists[3:], gathered)
 
 
 def outer(gathered, below, above, partial, lists, terms, lay):
@@ -243,26 +296,22 @@
     width = gathered.shape[2]
 
     def kernel(
-        source_ref, take_ref, factor_ref, g_ref, below_ref, above_ref, part_ref, out_ref, product_ref
+        near_ref, far_ref, take_ref, factor_ref, g_ref, below_ref, above_ref, part_ref, out_ref, product_ref
     ):
-        far_refs = (below_ref, above_ref)
+        other_refs = (below_ref, above_ref)
 
         def operator_of(term):
             block, i = lay.coef(term)
             weights = []
             for p in range(PLANES):
                 here = g_ref[p, pl.ds(block * lay.block + i * rows, rows), :]
-                far = far_refs[p][pl.ds(block * lay.main + i * rows, rows), :]
-                weights.append((0.5 * far, 0.5 * (here + far)))
-
-            def operator(t, p):
-                block = t // lay.quota
-                i = t - block * lay.quota
-                near_at = pl.multiple_of(block * lay.block + i * rows, 8)
-                far_at = pl.multiple_of(block * lay.main + i * rows, 8)
-                here = g_ref[p, pl.ds(near_at, rows), :]
-                far = far_refs[p][pl.ds(far_at, rows), :]
-                return weights[p][0] * here - weights[p][1] * far
+                other = other_refs[p][pl.ds(block * lay.main + i * rows, rows), :]
+                weights.append((0.5 * other, 0.5 * (here + other)))
+
+            def operator(near, far, p):
+                here = g_ref[p, pl.ds(pl.multiple_of(near, 8), rows), :]
+                other = other_refs[p][pl.ds(pl.multiple_of(far, 8), rows), :]
+                return weights[p][0] * here - weights[p][1] * other
 
             return operator
 
@@ -271,33 +320,36 @@
 
             def apply(n, carry, operator=operator, term=term):
                 e = (term - 1) * ACTIVE + n
-                t = source_ref[e]
+                near, far = near_ref[e], far_ref[e]
                 for p in range(PLANES):
-                    product_ref[e, p] = operator(t, p)
+                    product_ref[e, p] = operator(near, far, p)
                 return carry
 
             lax.fori_loop(0, ACTIVE, apply, 0, unroll=UNROLL)
 
         operator = operator_of(0)
-
-        def collect(s, carry):
-            for p in range(PLANES):
-                out_ref[p, s] = gather_products(
-                    s, take_ref, factor_ref, product_ref, p, part_ref[p, s] + operator(s, p)
-                )
-            return carry
-
-        lax.fori_loop(0, lay.slots, collect, 0, unroll=UNROLL)
+        for block in range(lay.modes):
+
+            def collect(i, carry, block=block):
+                s = block * lay.quota + i
+                near = block * lay.block + i * rows
+                far = block * lay.main + i * rows
+                for p in range(PLANES):
+                    total = part_ref[p, s] + operator(near, far, p)
+                    out_ref[p, s] = gather_products(s, take_ref, factor_ref, product_ref, p, total)
+                return carry
+
+            lax.fori_loop(0, lay.quota, collect, 0, unroll=UNROLL)
 
     return pl.pallas_call(
         kernel,
         out_shape=jax.ShapeDtypeStruct((PLANES, lay.slots, rows, width), jnp.float32),
-        in_specs=smem(3) + vmem(4),
+        in_specs=smem(4) + vmem(4),
         out_specs=vmem(1)[0],
         scratch_shapes=[pltpu.VMEM(((terms - 1) * ACTIVE, PLANES, rows, width), jnp.float32)],
         compiler_params=pltpu.CompilerParams(vmem_limit_bytes=VMEM_LIMIT),
         name="outer",
-    )(*lists, gathered, below, above, partial)
+    )(*lists[1:], gathered, below, above, partial)
 
 
 def on_device(chaos_field, mean_field, kl_fields, pattern, coupling, slot_mode):
@@ -315,24 +367,27 @@
         )
 
     mode = lax.axis_index("mode").astype(jnp.int32).reshape(1)
-    blocks = pack(chaos_field[:, 0], mean_field, kl_fields[:, 0], mode, lay)
-    lists = coupling_lists(pattern, coupling, slot_mode)
-    gathered = exchange(blocks.reshape(lay.group, lay.block, width))
-
-    main = gathered.reshape(PLANES, modes, lay.block, width)[:, :, : lay.main]
-    main = main.reshape(PLANES, modes * lay.main, width)
     up = [(i, i + PLANES) for i in range(spaces - PLANES)]
     down = [(target, source) for source, target in up]
-    below = lax.ppermute(main[PLANES - 1], "space", up)
-    above = lax.ppermute(main[0], "space", down)
-
-    planes = gathered.reshape(PLANES, modes * lay.block, width)
-    partial = inner(planes, lists, terms, lay)
-    total = outer(planes, below, above, partial, lists, terms, lay)
-
-    back = exchange(total.reshape(lay.group, quota * lay.rows, width))
-    back = back.reshape(lay.group, quota, lay.rows, width).transpose(1, 0, 2, 3)
-    return back.reshape(chaos_field.shape)
+    field, kl = chaos_field[:, 0], kl_fields[:, 0]
+
+    gathered = []
+    for chunk in range(CHUNKS):
+        blocks = pack(field, mean_field, kl, mode, chunk, lay)
+        gathered.append(exchange(blocks.reshape(lay.group, lay.block, width)))
+    lists = coupling_lists(pattern, coupling, slot_mode, lay)
+    parts = []
+    for chunk in range(CHUNKS):
+        main = gathered[chunk].reshape(PLANES, modes, lay.block, width)[:, :, : lay.main]
+        main = main.reshape(PLANES, modes * lay.main, width)
+        below = lax.ppermute(main[PLANES - 1], "space", up)
+        above = lax.ppermute(main[0], "space", down)
+        planes = gathered[chunk].reshape(PLANES, modes * lay.block, width)
+        partial = inner(planes, lists, terms, lay)
+        total = outer(planes, below, above, partial, lists, terms, lay)
+        back = exchange(total.reshape(lay.group, quota * lay.rows, width))
+        parts.append(back.reshape(lay.group, quota, lay.rows, width))
+    return unpack(parts, field.shape, lay).reshape(chaos_field.shape)
 
 
 def solution(mesh):

time: 86 us -> 130 us (1.51)
  Pallas kernels: 14.4 us -> 63.9 us
  starting transfers between devices: 10.1 us -> 22.3 us
  waiting for transfers between devices: 31.4 us -> 21.9 us
  blocking collectives: 21.5 us -> 14.9 us
  local copies, waits for them, and re-layouts: 6.49 us -> 4.15 us
    pallas_call x0 -> x1, Pallas kernels: none -> 42.9 us  [unpack(): pl.pallas_call(kernel, out_shape=jax.ShapeDtypeStruct(shape, jnp.float32)...]
    all_to_all x1 -> x3, waiting for transfers between devices: 19.5 us -> 9.91 us  [exchange(): lax.all_to_all(blocks, ('space', 'mode'), 0, 0, axis_index_groups=groups,...]
    all_to_all x1 -> x3, starting transfers between devices: 5.31 us -> 12.7 us  [exchange(): lax.all_to_all(blocks, ('space', 'mode'), 0, 0, axis_index_groups=groups,...]
    all_to_all x1, blocking collectives: 21.5 us -> 14.9 us  [exchange(): lax.all_to_all(blocks, ('space', 'mode'), 0, 0, axis_index_groups=groups,...]
    ppermute x1 -> x2, waiting for transfers between devices: 4.05 us -> 8.27 us  [on_device(): above = lax.ppermute(main[0], 'space', down)]
    ppermute x1 -> x2, waiting for transfers between devices: 7.83 us -> 3.74 us  [on_device(): below = lax.ppermute(main[PLANES - 1], 'space', up)]
    pallas_call x1 -> x2, Pallas kernels: 6.47 us -> 10.4 us  [inner(): pl.pallas_call(kernel, out_shape=jax.ShapeDtypeStruct((PLANES, lay.slots,...]
    ppermute x1 -> x2, starting transfers between devices: 3.52 us -> 6.99 us  [on_device(): below = lax.ppermute(main[PLANES - 1], 'space', up)]
  transfers between devices with their start and end apart: 3 -> 7, of which waited for: 3 -> 5; matrix products, arithmetic and copies ran while one was open for 3% -> 2% of each run, Pallas kernels for 8% -> 15%
where the time goes in v3:
time: 130 us; the launch traced here: 129 us
  Pallas kernels  63.9 us (49%)
  starting transfers between devices  22.3 us (17%)
  waiting for transfers between devices  21.9 us (17%)
  blocking collectives  14.9 us (11%)
  local copies, waits for them, and re-layouts  4.15 us (3%)
    pallas_call x1, Pallas kernels, unpack(): pl.pallas_call(kernel, out_shape=jax.ShapeDtypeStruct(shape, jnp.float32)...  42.9 us
    all_to_all x1, blocking collectives, exchange(): lax.all_to_all(blocks, ('space', 'mode'), 0, 0, axis_index_groups=groups,...  14.9 us
    all_to_all x3, starting transfers between devices, exchange(): lax.all_to_all(blocks, ('space', 'mode'), 0, 0, axis_index_groups=groups,...  12.7 us
    pallas_call x2, Pallas kernels, inner(): pl.pallas_call(kernel, out_shape=jax.ShapeDtypeStruct((PLANES, lay.slots,...  10.4 us
    all_to_all x3, waiting for transfers between devices, exchange(): lax.all_to_all(blocks, ('space', 'mode'), 0, 0, axis_index_groups=groups,...  9.91 us
    ppermute x2, waiting for transfers between devices, on_device(): above = lax.ppermute(main[0], 'space', down)  8.27 us
    pallas_call x2, Pallas kernels, outer(): pl.pallas_call(kernel, out_shape=jax.ShapeDtypeStruct((PLANES, lay.slots,...  7.51 us
    ppermute x2, starting transfers between devices, on_device(): below = lax.ppermute(main[PLANES - 1], 'space', up)  6.99 us
  transfers between devices with their start and end apart: 7, of which 5 were waited for; matrix products, arithmetic and copies ran while one was open for 2% of the time, Pallas kernels for 15%

profile of v3, /device:TPU:0, one launch (start us, length us, event | category | flops | bytes accessed | tf_op | source)
XLA Modules:
  0.0 129.1 jit_solution(11922733669215590952)
XLA Ops:
  0.0 0.0 copy-start
  0.0 1.3 %copy-done = f32[21,1,128,128]{3,2,1,0:T(8,128)S(1)} copy-done((f32[21,1,128,128]{3,2,1,0:T(8,128)S(1)}, f32[21,1,128,128]{3,2,1,0:T(8,128)}, u32[]{:S(2)}) %copy-start) | copy-done | bytes 1376280
  1.3 0.0 copy-start.2
  1.3 1.0 copy-done.2
  2.3 0.0 copy-start.4
  2.3 0.8 copy-done.4
  3.2 1.6 %pack.3 = f32[8,29,8,128]{3,2,1,0:T(8,128)} custom-call(s32[1]{0:T(128)} %bitcast.3.mode_ref, f32[21,128,128]{2,1,0:T(8,128)S(1)} %bitcast.35, f32[1,128,128]{2,1,0:T(8,128)S(1)} %copy-done.4, f32[6,128,128]{2,1,0:T(8,128)S(1)} %bitcast.38), custom_call_target="tpu_custom_call" | custom-call | tf_op jit(solution)/shard_map/pack/pallas_call | solution.py:105
  4.7 0.0 copy-start.1
  4.7 0.0 copy-start.3
  4.8 0.0 copy-start.5
  4.8 5.3 %all-to-all-start.2 = ((f32[8,232,128]{2,1,0:T(8,128)}), f32[8,232,128]{2,1,0:T(8,128)S(1)}, u32[]{:S(2)}, u32[]{:S(2)}) async-start(f32[8,232,128]{2,1,0:T(8,128)} %bitcast.13), calls=%async_computation.2 | async-start | bytes 1900544 | tf_op jit(solution)/shard_map/all_to_all | solution.py:365
  10.1 0.0 copy-done.1
  10.1 0.0 copy-done.3
  10.1 0.0 copy-done.5
  10.1 0.0 copy-start.7
  10.1 0.0 copy-start.8
  10.2 0.0 copy-start.9
  10.2 1.6 %pack.2 = f32[8,29,8,128]{3,2,1,0:T(8,128)} custom-call(s32[1]{0:T(128)} %bitcast.3.mode_ref, f32[21,128,128]{2,1,0:T(8,128)S(1)} %bitcast.36, f32[1,128,128]{2,1,0:T(8,128)S(1)} %copy-done.5, f32[6,128,128]{2,1,0:T(8,128)S(1)} %bitcast.39), custom_call_target="tpu_custom_call" | custom-call | tf_op jit(solution)/shard_map/pack/pallas_call | solution.py:105
  11.8 0.0 copy-done.7
  11.8 0.2 copy.9
  12.0 0.0 copy-done.8
  12.0 0.2 copy.10
  12.2 0.0 copy-done.9
  12.2 0.4 fusion
  12.5 0.3 fusion.10
  12.9 0.1 fusion.6
  13.0 0.1 select_reduce_fusion.1
  13.2 0.1 select_reduce_fusion.6
  13.3 0.2 select_reduce_fusion.3
  13.5 0.1 broadcast_add_fusion.1
  13.6 9.9 %all-to-all-done.2 = f32[8,232,128]{2,1,0:T(8,128)S(1)} async-done(((f32[8,232,128]{2,1,0:T(8,128)}), f32[8,232,128]{2,1,0:T(8,128)S(1)}, u32[]{:S(2)}, u32[]{:S(2)}) %all-to-all-start.2) | async-done | bytes 950304 | tf_op jit(solution)/shard_map/all_to_all | solution.py:365
  23.5 3.6 %all-to-all-start = ((f32[8,232,128]{2,1,0:T(8,128)}), f32[8,232,128]{2,1,0:T(8,128)S(1)}, u32[]{:S(2)}, u32[]{:S(2)}) async-start(f32[8,232,128]{2,1,0:T(8,128)} %bitcast.6), calls=%async_computation | async-start | bytes 1900544 | tf_op jit(solution)/shard_map/all_to_all | solution.py:365
  27.1 0.2 select_reduce_fusion.5
  27.3 0.1 fusion.18
  27.3 3.5 %collective-permute-start.2 = (f32[736,128]{1,0:T(8,128)S(1)}, f32[736,128]{1,0:T(8,128)S(1)}, u32[]{:S(2)}, u32[]{:S(2)}) collective-permute-start(f32[736,128]{1,0:T(8,128)S(1)} %bitcast.43), channel_id=1, source_target_pairs={{0,8},{4,12},{8,16},{12,20},{16,24},{20,28},{1,9},{5,13},{9,17},{1... | collective-permute-start | bytes 1130504 | tf_op jit(solution)/shard_map/ppermute | solution.py:383
  30.8 1.3 %collective-permute-start.3 = (f32[736,128]{1,0:T(8,128)S(1)}, f32[736,128]{1,0:T(8,128)S(1)}, u32[]{:S(2)}, u32[]{:S(2)}) collective-permute-start(f32[736,128]{1,0:T(8,128)S(1)} %bitcast.42), channel_id=1, source_target_pairs={{8,0},{12,4},{16,8},{20,12},{24,16},{28,20},{9,1},{13,5},{17,9},{2... | collective-permute-start | bytes 1130504 | tf_op jit(solution)/shard_map/ppermute | solution.py:384
  32.2 0.1 reshape.94.source_ref
  32.2 0.1 copy.12
  32.3 0.1 reshape.96.factor_ref
  32.4 0.1 copy.11
  32.6 0.1 reshape.95.take_ref
  32.7 5.2 %inner.3.part_ref = f32[2,84,8,128]{3,2,1,0:T(8,128)S(1)} custom-call(s32[294]{0:T(512)S(1)} %reshape.94.source_ref, s32[672]{0:T(1024)S(1)} %reshape.95.take_ref, f32[672]{0:T(1024)S(1)} %reshape.96.factor_ref, f32[2,928,128]{2,1,0:T(8,128)S(1)} %bitcast.30), custom_call_target="tpu_custom_call" | custom-call | tf_op jit(solution)/shard_map/inner/pallas_call | solution.py:280
  37.8 1.6 %collective-permute-done.2.below_ref = f32[736,128]{1,0:T(8,128)S(1)} collective-permute-done((f32[736,128]{1,0:T(8,128)S(1)}, f32[736,128]{1,0:T(8,128)S(1)}, u32[]{:S(2)}, u32[]{:S(2)}) %collective-permute-start.2) | collective-permute-done | bytes 376864 | tf_op jit(solution)/shard_map/ppermute | solution.py:383
  39.4 4.1 %collective-permute-done.3.above_ref = f32[736,128]{1,0:T(8,128)S(1)} collective-permute-done((f32[736,128]{1,0:T(8,128)S(1)}, f32[736,128]{1,0:T(8,128)S(1)}, u32[]{:S(2)}, u32[]{:S(2)}) %collective-permute-start.3) | collective-permute-done | bytes 376864 | tf_op jit(solution)/shard_map/ppermute | solution.py:384
  43.5 4.2 %outer.3 = f32[2,84,8,128]{3,2,1,0:T(8,128)} custom-call(s32[294]{0:T(512)S(1)} %get-tuple-element.19.near_ref, s32[294]{0:T(512)S(1)} %get-tuple-element.18.far_ref, s32[672]{0:T(1024)S(1)} %reshape.95.take_ref, f32[672]{0:T(1024)S(1)} %reshape.96.factor_ref, f32[2,928,128]{2,1,0:T(8,128)S(1)} %bitcast.31, f32[736,128]{1,0:T(8,128)S(1)} %collective-permute-done.2.below_ref, ...), custom_call_target="tpu_custom_call" | custom-call | tf_op jit(solution)/shard_map/outer/pallas_call | solution.py:344
  47.7 0.0 all-to-all-done
  47.7 3.8 %all-to-all-start.3 = ((f32[8,168,128]{2,1,0:T(8,128)}), f32[8,168,128]{2,1,0:T(8,128)S(1)}, u32[]{:S(2)}, u32[]{:S(2)}) async-start(f32[8,168,128]{2,1,0:T(8,128)} %bitcast.18), calls=%async_computation.3 | async-start | bytes 1376256 | tf_op jit(solution)/shard_map/all_to_all | solution.py:365
  51.6 3.5 %collective-permute-start = (f32[736,128]{1,0:T(8,128)S(1)}, f32[736,128]{1,0:T(8,128)S(1)}, u32[]{:S(2)}, u32[]{:S(2)}) collective-permute-start(f32[736,128]{1,0:T(8,128)S(1)} %bitcast.45), channel_id=1, source_target_pairs={{0,8},{4,12},{8,16},{12,20},{16,24},{20,28},{1,9},{5,13},{9,17},{1... | collective-permute-start | bytes 1130504 | tf_op jit(solution)/shard_map/ppermute | solution.py:383
  55.1 1.3 %collective-permute-start.1 = (f32[736,128]{1,0:T(8,128)S(1)}, f32[736,128]{1,0:T(8,128)S(1)}, u32[]{:S(2)}, u32[]{:S(2)}) collective-permute-start(f32[736,128]{1,0:T(8,128)S(1)} %bitcast.44), channel_id=1, source_target_pairs={{8,0},{12,4},{16,8},{20,12},{24,16},{28,20},{9,1},{13,5},{17,9},{2... | collective-permute-start | bytes 1130504 | tf_op jit(solution)/shard_map/ppermute | solution.py:384
  56.4 5.2 %inner.2.part_ref = f32[2,84,8,128]{3,2,1,0:T(8,128)S(1)} custom-call(s32[294]{0:T(512)S(1)} %reshape.94.source_ref, s32[672]{0:T(1024)S(1)} %reshape.95.take_ref, f32[672]{0:T(1024)S(1)} %reshape.96.factor_ref, f32[2,928,128]{2,1,0:T(8,128)S(1)} %bitcast.33), custom_call_target="tpu_custom_call" | custom-call | tf_op jit(solution)/shard_map/inner/pallas_call | solution.py:280
  61.6 2.2 %collective-permute-done.below_ref = f32[736,128]{1,0:T(8,128)S(1)} collective-permute-done((f32[736,128]{1,0:T(8,128)S(1)}, f32[736,128]{1,0:T(8,128)S(1)}, u32[]{:S(2)}, u32[]{:S(2)}) %collective-permute-start) | collective-permute-done | bytes 376864 | tf_op jit(solution)/shard_map/ppermute | solution.py:383
  63.8 4.1 %collective-permute-done.1.above_ref = f32[736,128]{1,0:T(8,128)S(1)} collective-permute-done((f32[736,128]{1,0:T(8,128)S(1)}, f32[736,128]{1,0:T(8,128)S(1)}, u32[]{:S(2)}, u32[]{:S(2)}) %collective-permute-start.1) | collective-permute-done | bytes 376864 | tf_op jit(solution)/shard_map/ppermute | solution.py:384
  67.9 3.3 %outer.2 = f32[2,84,8,128]{3,2,1,0:T(8,128)S(1)} custom-call(s32[294]{0:T(512)S(1)} %get-tuple-element.19.near_ref, s32[294]{0:T(512)S(1)} %get-tuple-element.18.far_ref, s32[672]{0:T(1024)S(1)} %reshape.95.take_ref, f32[672]{0:T(1024)S(1)} %reshape.96.factor_ref, f32[2,928,128]{2,1,0:T(8,128)S(1)} %bitcast.34, ...), custom_call_target="tpu_custom_call" | custom-call | tf_op jit(solution)/shard_map/outer/pallas_call | solution.py:344
  71.2 0.0 all-to-all-done.3
  71.3 0.0 copy-start.6
  71.3 14.9 %all_to_all.20 = f32[8,168,128]{2,1,0:T(8,128)} all-to-all(f32[8,168,128]{2,1,0:T(8,128)S(1)} %bitcast.37), channel_id=1, replica_groups={{0,1,2,3,4,5,6,7},{8,9,10,11,12,13,14,15},{16,17,18,19,20,21,22,23},{24..., dimensions={0} | all-to-all | bytes 1376256 | tf_op jit(solution)/shard_map/all_to_all | solution.py:365
  86.2 0.0 copy-done.6
  86.2 42.9 %unpack.1 = f32[21,128,128]{2,1,0:T(8,128)} custom-call(f32[8,21,8,128]{3,2,1,0:T(8,128)} %bitcast.41, f32[8,21,8,128]{3,2,1,0:T(8,128)} %bitcast.40), custom_call_target="tpu_custom_call" | custom-call | tf_op jit(solution)/shard_map/unpack/pallas_call | solution.py:139
  (11 shorter events, 0.2 us)
Async XLA Ops:
  0.0 1.3 %copy-start = (f32[21,1,128,128]{3,2,1,0:T(8,128)S(1)}, f32[21,1,128,128]{3,2,1,0:T(8,128)}, u32[]{:S(2)}) copy-start(f32[21,1,128,128]{3,2,1,0:T(8,128)} %param.6) | copy-start | bytes 4128772
  1.3 1.0 copy-start.2
  2.3 0.8 copy-start.4
  4.7 5.4 %copy-start.1 = (f32[21,1,128,128]{3,2,1,0:T(8,128)S(1)}, f32[21,1,128,128]{3,2,1,0:T(8,128)}, u32[]{:S(2)}) copy-start(f32[21,1,128,128]{3,2,1,0:T(8,128)} %param.6) | copy-start | bytes 4128772
  4.7 5.4 %copy-start.3 = (f32[6,1,128,128]{3,2,1,0:T(8,128)S(1)}, f32[6,1,128,128]{3,2,1,0:T(8,128)}, u32[]{:S(2)}) copy-start(f32[6,1,128,128]{3,2,1,0:T(8,128)} %param.8) | copy-start | bytes 1179652
  4.8 5.4 %copy-start.5 = (f32[1,128,128]{2,1,0:T(8,128)S(1)}, f32[1,128,128]{2,1,0:T(8,128)}, u32[]{:S(2)}) copy-start(f32[1,128,128]{2,1,0:T(8,128)} %mean_ref.3) | copy-start | bytes 196612
  4.8 18.7 %all-to-all-start.2 = ((f32[8,232,128]{2,1,0:T(8,128)}), f32[8,232,128]{2,1,0:T(8,128)S(1)}, u32[]{:S(2)}, u32[]{:S(2)}) async-start(f32[8,232,128]{2,1,0:T(8,128)} %bitcast.13), calls=%async_computation.2 | async-start | bytes 1900544 | tf_op jit(solution)/shard_map/all_to_all | solution.py:365
  10.1 1.6 %copy-start.7 = (s32[7,84,84]{2,1,0:T(8,128)S(1)}, s32[7,84,84]{2,1,0:T(8,128)}, u32[]{:S(2)}) copy-start(s32[7,84,84]{2,1,0:T(8,128)} %param.9) | copy-start | bytes 592708
  10.1 1.8 %copy-start.8 = (f32[7,84,84]{2,1,0:T(8,128)S(1)}, f32[7,84,84]{2,1,0:T(8,128)}, u32[]{:S(2)}) copy-start(f32[7,84,84]{2,1,0:T(8,128)} %param.10) | copy-start | bytes 592708
  10.2 2.0 %copy-start.9 = (s32[84]{0:T(128)S(1)}, s32[84]{0:T(128)}, u32[]{:S(2)}) copy-start(s32[84]{0:T(128)} %param.11) | copy-start | bytes 1012
  23.5 24.2 %all-to-all-start = ((f32[8,232,128]{2,1,0:T(8,128)}), f32[8,232,128]{2,1,0:T(8,128)S(1)}, u32[]{:S(2)}, u32[]{:S(2)}) async-start(f32[8,232,128]{2,1,0:T(8,128)} %bitcast.6), calls=%async_computation | async-start | bytes 1900544 | tf_op jit(solution)/shard_map/all_to_all | solution.py:365
  27.3 12.1 %collective-permute-start.2 = (f32[736,128]{1,0:T(8,128)S(1)}, f32[736,128]{1,0:T(8,128)S(1)}, u32[]{:S(2)}, u32[]{:S(2)}) collective-permute-start(f32[736,128]{1,0:T(8,128)S(1)} %bitcast.43), channel_id=1, source_target_pairs={{0,8},{4,12},{8,16},{12,20},{16,24},{20,28},{1,9},{5,13},{9,17},{1... | collective-permute-start | bytes 1130504 | tf_op jit(solution)/shard_map/ppermute | solution.py:383
  30.8 12.7 %collective-permute-start.3 = (f32[736,128]{1,0:T(8,128)S(1)}, f32[736,128]{1,0:T(8,128)S(1)}, u32[]{:S(2)}, u32[]{:S(2)}) collective-permute-start(f32[736,128]{1,0:T(8,128)S(1)} %bitcast.42), channel_id=1, source_target_pairs={{8,0},{12,4},{16,8},{20,12},{24,16},{28,20},{9,1},{13,5},{17,9},{2... | collective-permute-start | bytes 1130504 | tf_op jit(solution)/shard_map/ppermute | solution.py:384
  47.7 23.5 %all-to-all-start.3 = ((f32[8,168,128]{2,1,0:T(8,128)}), f32[8,168,128]{2,1,0:T(8,128)S(1)}, u32[]{:S(2)}, u32[]{:S(2)}) async-start(f32[8,168,128]{2,1,0:T(8,128)} %bitcast.18), calls=%async_computation.3 | async-start | bytes 1376256 | tf_op jit(solution)/shard_map/all_to_all | solution.py:365
  51.6 12.1 %collective-permute-start = (f32[736,128]{1,0:T(8,128)S(1)}, f32[736,128]{1,0:T(8,128)S(1)}, u32[]{:S(2)}, u32[]{:S(2)}) collective-permute-start(f32[736,128]{1,0:T(8,128)S(1)} %bitcast.45), channel_id=1, source_target_pairs={{0,8},{4,12},{8,16},{12,20},{16,24},{20,28},{1,9},{5,13},{9,17},{1... | collective-permute-start | bytes 1130504 | tf_op jit(solution)/shard_map/ppermute | solution.py:383
  55.1 12.8 %collective-permute-start.1 = (f32[736,128]{1,0:T(8,128)S(1)}, f32[736,128]{1,0:T(8,128)S(1)}, u32[]{:S(2)}, u32[]{:S(2)}) collective-permute-start(f32[736,128]{1,0:T(8,128)S(1)} %bitcast.44), channel_id=1, source_target_pairs={{8,0},{12,4},{16,8},{20,12},{24,16},{28,20},{9,1},{13,5},{17,9},{2... | collective-permute-start | bytes 1130504 | tf_op jit(solution)/shard_map/ppermute | solution.py:384
  71.3 14.9 %copy-start.6 = (f32[8,168,128]{2,1,0:T(8,128)}, f32[8,168,128]{2,1,0:T(8,128)S(1)}, u32[]{:S(2)}) copy-start(f32[8,168,128]{2,1,0:T(8,128)S(1)} %all-to-all-done.3) | copy-start | bytes 2064388

commit v4 on v2

v4 whole, which is shorter than its diff:
```python
import jax
import jax.numpy as jnp
from jax import lax
from jax.experimental import pallas as pl
from jax.experimental.pallas import tpu as pltpu
from jax.sharding import PartitionSpec as P

VMEM_LIMIT = 40 * 1024 * 1024
PACK_LIMIT = 60 * 1024 * 1024
PLANES = 2
ACTIVE = 49
MOST = 8
UNROLL = 7


class Layout:
    def __init__(self, quota, terms, modes, height, width):
        self.modes = modes
        self.group = PLANES * modes
        self.rows = height // self.group
        self.width = width
        self.terms = terms
        self.quota = quota
        self.slots = quota * modes
        self.share = -(-terms // modes)
        self.fields = quota + self.share
        self.main = self.fields * self.rows
        edges = -(-2 * self.fields // 8) * 8
        self.piece = self.main + edges
        self.places = self.fields * modes

    def origin(self, j, r):
        other = jnp.bitwise_xor(j, r)
        plane = other // self.modes
        return plane, other - plane * self.modes

    def place(self, block, i):
        return jnp.where(
            i < self.quota,
            block * self.quota + i,
            self.slots + block * self.share + (i - self.quota),
        )


def vmem(count):
    return [pl.BlockSpec(memory_space=pltpu.VMEM)] * count


def smem(count):
    return [pl.BlockSpec(memory_space=pltpu.SMEM)] * count


def pack(field, mean, kl, j, lay):
    kl_terms = kl.shape[0]
    rows, width = lay.rows, lay.width
    height = field.shape[1]

    def kernel(j_ref, field_ref, mean_ref, kl_ref, *refs):
        out_refs, (stage_ref, mean_here, kl_here, sems) = refs[: lay.group], refs[lay.group :]
        copies = [
            pltpu.make_async_copy(field_ref, stage_ref.at[pl.ds(0, lay.quota)], sems.at[0]),
            pltpu.make_async_copy(mean_ref, mean_here, sems.at[1]),
            pltpu.make_async_copy(kl_ref, kl_here, sems.at[2]),
        ]
        for made in copies:
            made.start()
        me = j_ref[0]
        mode = lax.rem(me, lay.modes)
        copies[1].wait()
        copies[2].wait()
        for i in range(lay.share):
            term = mode * lay.share + i
            other = kl_here[jnp.clip(term - 1, 0, kl_terms - 1)]
            stage_ref[lay.quota + i] = jnp.where(term == 0, mean_here[0], other)
        copies[0].wait()
        for r in range(lay.group):
            other = jnp.bitwise_xor(me, r)
            start = pl.multiple_of(other * rows, 8)
            lower = jnp.maximum(start - 1, 0)
            upper = jnp.minimum(start + rows, height - 1)
            for i in range(lay.fields):
                out_refs[r][i * rows : (i + 1) * rows, :] = stage_ref[i, pl.ds(start, rows), :]
                low = stage_ref[i, pl.ds(lower, 1), :]
                high = stage_ref[i, pl.ds(upper, 1), :]
                at = lay.main + 2 * i
                out_refs[r][at : at + 1, :] = jnp.where(other == 0, 0.0, low)
                out_refs[r][at + 1 : at + 2, :] = jnp.where(other == lay.group - 1, 0.0, high)
            spare = lay.piece - lay.main - 2 * lay.fields
            if spare:
                out_refs[r][lay.piece - spare :, :] = jnp.zeros((spare, width), jnp.float32)

    return pl.pallas_call(
        kernel,
        out_shape=[jax.ShapeDtypeStruct((lay.piece, width), jnp.float32)] * lay.group,
        in_specs=smem(1) + [pl.BlockSpec(memory_space=pltpu.HBM)] * 3,
        out_specs=vmem(lay.group),
        scratch_shapes=[
            pltpu.VMEM((lay.fields, height, width), jnp.float32),
            pltpu.VMEM(mean.shape, jnp.float32),
            pltpu.VMEM(kl.shape, jnp.float32),
            pltpu.SemaphoreType.DMA((3,)),
        ],
        compiler_params=pltpu.CompilerParams(vmem_limit_bytes=PACK_LIMIT),
        name="pack",
    )(j, field, mean, kl)


def unpack(pieces, j, shape, lay):
    rows = lay.rows

    def kernel(j_ref, *refs):
        piece_refs, out_ref, sems = refs[:-2], refs[-2], refs[-1]
        copies = []
        for r, piece_ref in enumerate(piece_refs):
            start = pl.multiple_of(jnp.bitwise_xor(j_ref[0], r) * rows, 8)
            made = pltpu.make_async_copy(
                piece_ref, out_ref.at[:, pl.ds(start, rows), :], sems.at[r]
            )
            made.start()
            copies.append(made)
        for made in copies:
            made.wait()

    return pl.pallas_call(
        kernel,
        out_shape=jax.ShapeDtypeStruct(shape, jnp.float32),
        in_specs=smem(1) + vmem(lay.group),
        out_specs=pl.BlockSpec(memory_space=pltpu.HBM),
        scratch_shapes=[pltpu.SemaphoreType.DMA((lay.group,))],
        compiler_params=pltpu.CompilerParams(vmem_limit_bytes=VMEM_LIMIT),
        name="unpack",
    )(j, *pieces)


def coupling_lists(pattern, coupling, slot_mode):
    masked = (coupling * pattern.astype(jnp.float32))[1:]
    terms, modes = masked.shape[0], masked.shape[1]
    number = jnp.arange(modes, dtype=jnp.int32)
    one_hot = (slot_mode[:, None] == number[None, :]).astype(jnp.float32)
    coupled = jnp.einsum(
        "sa,kab,tb->kst", one_hot, masked, one_hot, precision=lax.Precision.HIGHEST
    )
    there = coupled != 0.0
    column = number[None, None, :]
    first = jnp.min(jnp.where(there, column, modes), 2)
    last = jnp.max(jnp.where(there, column, -1), 2)
    active = first < modes
    earlier = column < number[None, :, None]
    rank = jnp.sum(jnp.where(active[:, None, :] & earlier, 1, 0), 2)
    place = jnp.arange(ACTIVE, dtype=jnp.int32)[None, :, None]
    chosen = active[:, None, :] & (rank[:, None, :] == place)
    sources = jnp.sum(jnp.where(chosen, column, 0), 2)

    base = ACTIVE * jnp.arange(terms, dtype=jnp.int32)[:, None]
    products, factors, valid = [], [], []
    for chosen_t, is_valid in ((first, active), (last, last > first)):
        before = active[:, None, :] & (column < chosen_t[:, :, None])
        products.append(base + jnp.sum(jnp.where(before, 1, 0), 2))
        factors.append(jnp.sum(jnp.where(column == chosen_t[:, :, None], coupled, 0.0), 2))
        valid.append(is_valid)
    products = jnp.concatenate(products, 0)
    factors = jnp.concatenate(factors, 0)
    valid = jnp.concatenate(valid, 0)
    index = jnp.arange(2 * terms, dtype=jnp.int32)
    order = index[None, :] < index[:, None]
    rank = jnp.sum(jnp.where(valid[None] & order[:, :, None], 1, 0), 1)
    place = jnp.arange(MOST, dtype=jnp.int32)[:, None, None]
    chosen = valid[None] & (rank[None] == place)
    take = jnp.sum(jnp.where(chosen, products[None], 0), 1)
    factor = jnp.sum(jnp.where(chosen, factors[None], 0.0), 1)
    return sources.reshape(-1), take.T.reshape(-1), factor.T.reshape(-1)


def gather_products(s, take_ref, factor_ref, product_ref, where, total):
    for n in range(MOST):
        e = s * MOST + n
        total = total + factor_ref[e] * product_ref[(take_ref[e], *where)]
    return total


def inner(pieces, lists, j, lay):
    rows, width = lay.rows, lay.width
    full = (rows, width)

    def kernel(j_ref, source_ref, take_ref, factor_ref, *refs):
        piece_refs, (out_ref, centre_ref, near_ref, product_ref) = refs[: lay.group], refs[lay.group :]
        lane = lax.broadcasted_iota(jnp.int32, full, 1)
        line = lax.broadcasted_iota(jnp.int32, full, 0)

        for r in range(lay.group):
            plane, block = lay.origin(j_ref[0], r)

            def spread(i, carry, piece_ref=piece_refs[r], plane=plane, block=block):
                here = piece_ref[pl.ds(i * rows, rows), :]
                low = piece_ref[pl.ds(lay.main + 2 * i, 1), :]
                high = piece_ref[pl.ds(lay.main + 2 * i + 1, 1), :]
                at = lay.place(block, i)
                centre_ref[at, plane] = here
                near_ref[at, plane, 0] = pltpu.roll(here, width - 1, 1)
                near_ref[at, plane, 1] = pltpu.roll(here, 1, 1)
                near_ref[at, plane, 2] = jnp.where(
                    line == rows - 1, high, pltpu.roll(here, rows - 1, 0)
                )
                near_ref[at, plane, 3] = jnp.where(line == 0, low, pltpu.roll(here, 1, 0))
                return carry

            lax.fori_loop(0, lay.fields, spread, 0, unroll=UNROLL)

        def operator_of(term):
            at = lay.slots + term
            weights = []
            centres = []
            for p in range(PLANES):
                here = centre_ref[at, p]
                beside = [near_ref[at, p, n] for n in range(4)]
                beside[0] = jnp.where(lane == width - 1, 0.0, beside[0])
                beside[1] = jnp.where(lane == 0, 0.0, beside[1])
                faces = [0.5 * (here + n) for n in beside]
                centres.append(here)
                diagonal = faces[0] + faces[1] + faces[2] + faces[3] + 0.5 * here
                faces[0] = jnp.where(lane == width - 1, 0.0, faces[0])
                faces[1] = jnp.where(lane == 0, 0.0, faces[1])
                weights.append([diagonal] + [-f for f in faces])
            between = 0.5 * (centres[0] + centres[1])
            for p in range(PLANES):
                weights[p][0] = weights[p][0] + between

            def operator(t, p):
                total = weights[p][0] * centre_ref[t, p]
                for n in range(4):
                    total = total + weights[p][n + 1] * near_ref[t, p, n]
                return total - between * centre_ref[t, 1 - p]

            return operator

        for term in range(1, lay.terms):
            operator = operator_of(term)

            def apply(n, carry, operator=operator, term=term):
                e = (term - 1) * ACTIVE + n
                t = source_ref[e]
                for p in range(PLANES):
                    product_ref[e, p] = operator(t, p)
                return carry

            lax.fori_loop(0, ACTIVE, apply, 0, unroll=UNROLL)

        operator = operator_of(0)

        def collect(s, carry):
            for p in range(PLANES):
                out_ref[s, p] = gather_products(
                    s, take_ref, factor_ref, product_ref, (p,), operator(s, p)
                )
            return carry

        lax.fori_loop(0, lay.slots, collect, 0, unroll=UNROLL)

    return pl.pallas_call(
        kernel,
        out_shape=[
            jax.ShapeDtypeStruct((lay.slots, PLANES, rows, width), jnp.float32),
            jax.ShapeDtypeStruct((lay.places, PLANES, rows, width), jnp.float32),
        ],
        in_specs=smem(4) + vmem(lay.group),
        out_specs=vmem(2),
        scratch_shapes=[
            pltpu.VMEM((lay.places, PLANES, 4, rows, width), jnp.float32),
            pltpu.VMEM(((lay.terms - 1) * ACTIVE, PLANES, rows, width), jnp.float32),
        ],
        compiler_params=pltpu.CompilerParams(vmem_limit_bytes=VMEM_LIMIT),
        name="inner",
    )(j, *lists, *pieces)


def outer(centre, partial, halos, lists, j, crossing, lay):
    rows, width = lay.rows, lay.width
    first = lay.modes if crossing else 0

    def kernel(j_ref, source_ref, take_ref, factor_ref, centre_ref, part_ref, *refs):
        halo_refs, refs = refs[: len(halos)], refs[len(halos) :]
        out_refs, (far_ref, product_ref) = refs[: lay.modes], refs[lay.modes :]
        plane, _ = lay.origin(j_ref[0], first)
        n = 0
        for halo_ref in halo_refs:
            for at in range(halo_ref.shape[0]):
                _, block = lay.origin(j_ref[0], n)
                n += 1

                def spread(i, carry, halo_ref=halo_ref, at=at, block=block):
                    far_ref[lay.place(block, i)] = halo_ref[at, pl.ds(i * rows, rows), :]
                    return carry

                lax.fori_loop(0, lay.fields, spread, 0, unroll=UNROLL)

        def operator_of(term):
            at = lay.slots + term
            far = far_ref[at]
            half, whole = 0.5 * far, 0.5 * (centre_ref[at, plane] + far)
            return lambda t: half * centre_ref[t, plane] - whole * far_ref[t]

        for term in range(1, lay.terms):
            operator = operator_of(term)

            def apply(n, carry, operator=operator, term=term):
                e = (term - 1) * ACTIVE + n
                product_ref[e] = operator(source_ref[e])
                return carry

            lax.fori_loop(0, ACTIVE, apply, 0, unroll=UNROLL)

        operator = operator_of(0)
        for n in range(lay.modes):
            _, block = lay.origin(j_ref[0], first + n)

            def collect(i, carry, out_ref=out_refs[n], block=block):
                s = block * lay.quota + i
                total = part_ref[s, plane] + operator(s)
                out_ref[i] = gather_products(s, take_ref, factor_ref, product_ref, (), total)
                return carry

            lax.fori_loop(0, lay.quota, collect, 0, unroll=UNROLL)

    return pl.pallas_call(
        kernel,
        out_shape=[jax.ShapeDtypeStruct((lay.quota, rows, width), jnp.float32)] * lay.modes,
        in_specs=smem(4) + vmem(2 + len(halos)),
        out_specs=vmem(lay.modes),
        scratch_shapes=[
            pltpu.VMEM((lay.places, rows, width), jnp.float32),
            pltpu.VMEM(((lay.terms - 1) * ACTIVE, rows, width), jnp.float32),
        ],
        compiler_params=pltpu.CompilerParams(vmem_limit_bytes=VMEM_LIMIT),
        name="outer_crossing" if crossing else "outer_own",
    )(j, *lists, centre, partial, *halos)


def on_device(chaos_field, mean_field, kl_fields, pattern, coupling, slot_mode):
    spaces, modes = lax.axis_size("space"), lax.axis_size("mode")
    quota, _, height, width = chaos_field.shape
    terms = kl_fields.shape[0] + 1
    lay = Layout(quota, terms, modes, height, width)
    axes = ("space", "mode")
    devices = spaces * modes
    space = lax.axis_index("space").astype(jnp.int32)
    mode = lax.axis_index("mode").astype(jnp.int32)
    j = (lax.rem(space, PLANES) * modes + mode).reshape(1)

    def swap(piece, r):
        if r == 0:
            return piece
        return lax.ppermute(piece, axes, [(d, d ^ r) for d in range(devices)])

    def shift(pieces, crossing):
        pairs = []
        for d in range(devices):
            upper = (d // modes) % PLANES == (0 if crossing else 1)
            other = d + lay.group if upper else d - lay.group
            if 0 <= other < devices:
                pairs.append((d, other))
        main = jnp.stack([piece[: lay.main] for piece in pieces])
        return lax.ppermute(main, axes, pairs)

    sent = pack(chaos_field[:, 0], mean_field, kl_fields[:, 0], j, lay)
    pieces = [swap(piece, r) for r, piece in enumerate(sent)]
    half = modes + modes // 2
    far_own = shift(pieces[:modes], False)
    far_first = shift(pieces[modes:half], True)
    far_second = shift(pieces[half:], True)
    lists = coupling_lists(pattern, coupling, slot_mode)
    partial, centre = inner(pieces, lists, j, lay)
    crossing = outer(centre, partial, [far_own], lists, j, True, lay)
    own = outer(centre, partial, [far_first, far_second], lists, j, False, lay)
    back = [swap(piece, r) for r, piece in enumerate(own + crossing)]
    return unpack(back, j, (quota, height, width), lay).reshape(chaos_field.shape)


def solution(mesh):
    in_specs = (
        P("mode", "space", None, None),
        P("space", None, None),
        P(None, "space", None, None),
        P(),
        P(),
        P(),
    )
    out_specs = P("mode", "space", None, None)
    return jax.shard_map(
        on_device, mesh=mesh, in_specs=in_specs, out_specs=out_specs, check_vma=False
    )
```

time: 86 us -> 72.4 us (0.84)
  blocking collectives: 21.5 us -> 0 us
  starting transfers between devices: 10.1 us -> 22.8 us
  waiting for transfers between devices: 31.4 us -> 24.6 us
  local copies, waits for them, and re-layouts: 6.49 us -> 1.65 us
  Pallas kernels: 14.4 us -> 18.1 us
  other arithmetic: 0.91 us -> 3.95 us
    all_to_all x1 -> x0, blocking collectives: 21.5 us -> none  [exchange(): lax.all_to_all(blocks, ('space', 'mode'), 0, 0, axis_index_groups=groups,...]
    all_to_all x1 -> x0, waiting for transfers between devices: 19.5 us -> none  [exchange(): lax.all_to_all(blocks, ('space', 'mode'), 0, 0, axis_index_groups=groups,...]
    ppermute x2 -> x17, starting transfers between devices: 4.81 us -> 22.8 us  [the longest x14 14.1 us: swap(): return lax.ppermute(piece, axes, [(d, d ^ r) for d in range(devices)])]
    ppermute x2 -> x17, waiting for transfers between devices: 11.9 us -> 24.6 us  [the longest x14 24.6 us: swap(): return lax.ppermute(piece, axes, [(d, d ^ r) for d in range(devices)])]
    all_to_all x1 -> x0, starting transfers between devices: 5.31 us -> none  [exchange(): lax.all_to_all(blocks, ('space', 'mode'), 0, 0, axis_index_groups=groups,...]
    pallas_call x3 -> x5, Pallas kernels: 14.4 us -> 18.1 us  [the longest x1 8.19 us: inner(): pl.pallas_call(kernel, out_shape=[jax.ShapeDtypeStruct((lay.slots, PLANES...]
    unnamed x14, local copies, waits for them, and re-layouts: 3.58 us -> 0.41 us
    another operation x0 -> x3, other arithmetic: none -> 2.46 us  [shift(): main = jnp.stack([piece[:lay.main] for piece in pieces])]
  transfers between devices with their start and end apart: 3 -> 17, of which waited for: 3 -> 7; matrix products, arithmetic and copies ran while one was open for 3% -> 9% of each run, Pallas kernels for 8% -> 19%
where the time goes in v4:
time: 72.4 us; the launch traced here: 72.1 us
  waiting for transfers between devices  24.6 us (34%)
  starting transfers between devices  22.8 us (31%)
  Pallas kernels  18.1 us (25%)
  other arithmetic  3.95 us (5%)
  local copies, waits for them, and re-layouts  1.65 us (2%)
    ppermute x14, waiting for transfers between devices, swap(): return lax.ppermute(piece, axes, [(d, d ^ r) for d in range(devices)])  24.6 us
    ppermute x14, starting transfers between devices, swap(): return lax.ppermute(piece, axes, [(d, d ^ r) for d in range(devices)])  14.1 us
    ppermute x3, starting transfers between devices, shift(): return lax.ppermute(main, axes, pairs)  8.64 us
    pallas_call x1, Pallas kernels, inner(): pl.pallas_call(kernel, out_shape=[jax.ShapeDtypeStruct((lay.slots, PLANES...  8.19 us
    pallas_call x2, Pallas kernels, outer(): pl.pallas_call(kernel, out_shape=[jax.ShapeDtypeStruct((lay.quota, rows,...  5.8 us
    pallas_call x1, Pallas kernels, pack(): pl.pallas_call(kernel, out_shape=[jax.ShapeDtypeStruct((lay.piece, width)...  3.01 us
    another operation x3, other arithmetic, shift(): main = jnp.stack([piece[:lay.main] for piece in pieces])  2.46 us
  transfers between devices with their start and end apart: 17, of which 7 were waited for; matrix products, arithmetic and copies ran while one was open for 9% of the time, Pallas kernels for 19%

profile of v4, /device:TPU:0, one launch (start us, length us, event | category | flops | bytes accessed | tf_op | source)
XLA Modules:
  0.0 72.1 jit_solution(13215158813486632444)
XLA Ops:
  0.0 3.0 %pack.1 = (f32[416,128]{1,0:T(8,128)}, f32[416,128]{1,0:T(8,128)}, f32[416,128]{1,0:T(8,128)}, f32[416,128]{1,0:T(8,128)}, f32[416,128]{1,0:T(8,128)}, /*index=5...) custom-call(s32[1]{0:T(128)} %bitcast.j_ref, f32[21,128,128]{2,1,0:T(8,128)} %bitcast.31, ...), custom_call_target="tpu_custom_call" | custom-call | tf_op jit(solution)/shard_map/pack/pallas_call | solution.py:92
  3.0 0.5 collective-permute-start
  3.5 2.6 %collective-permute-start.1 = (f32[416,128]{1,0:T(8,128)}, f32[416,128]{1,0:T(8,128)S(1)}, u32[]{:S(2)}, u32[]{:S(2)}) collective-permute-start(f32[416,128]{1,0:T(8,128)} %get-tuple-element.25), channel_id=1, source_target_pairs={{0,2},{1,3},{2,0},{3,1},{4,6},{5,7},{6,4},{7,5},{8,10},{9,11},{10,... | collective-permute-start | bytes 638984 | tf_op jit(solution)/shard_map/ppermute | solution.py:352
  6.1 0.1 collective-permute-start.2
  6.2 1.7 %collective-permute-start.3 = (f32[416,128]{1,0:T(8,128)}, f32[416,128]{1,0:T(8,128)S(1)}, u32[]{:S(2)}, u32[]{:S(2)}) collective-permute-start(f32[416,128]{1,0:T(8,128)} %get-tuple-element.27), channel_id=1, source_target_pairs={{0,4},{1,5},{2,6},{3,7},{4,0},{5,1},{6,2},{7,3},{8,12},{9,13},{10,... | collective-permute-start | bytes 638984 | tf_op jit(solution)/shard_map/ppermute | solution.py:352
  7.9 0.0 collective-permute-start.4
  8.0 0.0 copy-done.1
  8.0 0.0 copy-start
  8.0 0.2 copy.10
  8.2 0.0 copy-done.2
  8.2 0.0 copy-start.4
  8.2 0.0 copy-start.5
  8.2 0.2 copy.9
  8.4 0.0 copy-done.3
  8.4 0.4 fusion
  8.8 0.3 fusion.10
  9.1 0.1 fusion.6
  9.2 0.2 select_reduce_fusion.3
  9.5 0.2 select_reduce_fusion.5
  9.7 0.1 broadcast_add_fusion.1
  9.8 0.1 select_reduce_fusion.6
  9.9 7.9 %collective-permute-done.4.refs_5_ = f32[416,128]{1,0:T(8,128)S(1)} collective-permute-done((f32[416,128]{1,0:T(8,128)}, f32[416,128]{1,0:T(8,128)S(1)}, u32[]{:S(2)}, u32[]{:S(2)}) %collective-permute-start.4) | collective-permute-done | bytes 213024 | tf_op jit(solution)/shard_map/ppermute | solution.py:352
  17.8 2.7 %collective-permute-start.5 = (f32[416,128]{1,0:T(8,128)S(1)}, f32[416,128]{1,0:T(8,128)S(1)}, u32[]{:S(2)}, u32[]{:S(2)}) collective-permute-start(f32[416,128]{1,0:T(8,128)S(1)} %copy-done.4), channel_id=1, source_target_pairs={{0,6},{1,7},{2,4},{3,5},{4,2},{5,3},{6,0},{7,1},{8,14},{9,15},{10,... | collective-permute-start | bytes 638984 | tf_op jit(solution)/shard_map/ppermute | solution.py:352
  20.6 0.0 collective-permute-done.3.refs_4_
  20.6 0.1 collective-permute-start.6
  20.7 0.8 %pad_maximum_fusion.1 = f32[2,368,128]{2,1,0:T(8,128)} fusion(f32[1,368,128]{2,1,0:T(8,128)S(1)} %slice_bitcast_fusion.5, f32[1,368,128]{2,1,0:T(8,128)S(1)} %slice_bitcast_fusion.6), kind=kLoop, calls=%fused_computation.1 | loop fusion | flops 94208 | bytes 753664 | tf_op jit(solution)/shard_map/stack | solution.py:361
  21.5 0.0 collective-permute-done.2.refs_3_
  21.5 3.7 %collective-permute-start.7 = (f32[2,368,128]{2,1,0:T(8,128)}, f32[2,368,128]{2,1,0:T(8,128)S(1)}, u32[]{:S(2)}, u32[]{:S(2)}) collective-permute-start(f32[2,368,128]{2,1,0:T(8,128)} %pad_maximum_fusion.1), channel_id=1, source_target_pairs={{0,8},{1,9},{2,10},{3,11},{8,16},{9,17},{10,18},{11,19},{12,4},{13... | collective-permute-start | bytes 1130504 | tf_op jit(solution)/shard_map/ppermute | solution.py:362
  25.2 0.0 collective-permute-done.1.refs_2_
  25.3 0.0 collective-permute-done.refs_1_
  25.3 0.9 %pad_maximum_fusion = f32[4,368,128]{2,1,0:T(8,128)} fusion(f32[1,368,128]{2,1,0:T(8,128)S(1)} %slice_bitcast_fusion, f32[1,368,128]{2,1,0:T(8,128)S(1)} %slice_bitcast_fusion.1, f32[1,368,128]{2,1,0:T(8,128)S(1)} %slice_bitcast_fusion.2, f32[1,368,128]{2,1,0:T(8,128)S(1)} %slice_bitcast_fusion.7), kind=kLoop, calls=%fused_computation | loop fusion | flops 565248 | bytes 1507328 | tf_op jit(solution)/shard_map/stack | solution.py:361
  26.2 1.3 %collective-permute-start.12 = (f32[4,368,128]{2,1,0:T(8,128)}, f32[4,368,128]{2,1,0:T(8,128)S(1)}, u32[]{:S(2)}, u32[]{:S(2)}) collective-permute-start(f32[4,368,128]{2,1,0:T(8,128)} %pad_maximum_fusion), channel_id=1, source_target_pairs={{4,12},{5,13},{6,14},{7,15},{8,0},{9,1},{10,2},{11,3},{12,20},{13,... | collective-permute-start | bytes 2261000 | tf_op jit(solution)/shard_map/ppermute | solution.py:362
  27.5 3.0 %collective-permute-done.6.refs_7_ = f32[416,128]{1,0:T(8,128)S(1)} collective-permute-done((f32[416,128]{1,0:T(8,128)S(1)}, f32[416,128]{1,0:T(8,128)S(1)}, u32[]{:S(2)}, u32[]{:S(2)}) %collective-permute-start.6) | collective-permute-done | bytes 213024 | tf_op jit(solution)/shard_map/ppermute | solution.py:352
  30.6 0.0 collective-permute-done.5.refs_6_
  30.6 0.8 %pad_maximum_fusion.2 = f32[2,368,128]{2,1,0:T(8,128)} fusion(f32[1,368,128]{2,1,0:T(8,128)S(1)} %slice_bitcast_fusion.3, f32[1,368,128]{2,1,0:T(8,128)S(1)} %slice_bitcast_fusion.4), kind=kLoop, calls=%fused_computation.2 | loop fusion | flops 94208 | bytes 753664 | tf_op jit(solution)/shard_map/stack | solution.py:361
  31.4 3.6 %collective-permute-start.8 = (f32[2,368,128]{2,1,0:T(8,128)}, f32[2,368,128]{2,1,0:T(8,128)S(1)}, u32[]{:S(2)}, u32[]{:S(2)}) collective-permute-start(f32[2,368,128]{2,1,0:T(8,128)} %pad_maximum_fusion.2), channel_id=1, source_target_pairs={{0,8},{1,9},{2,10},{3,11},{8,16},{9,17},{10,18},{11,19},{12,4},{13... | collective-permute-start | bytes 1130504 | tf_op jit(solution)/shard_map/ppermute | solution.py:362
  35.0 0.6 select_reduce_fusion.8
  35.6 0.1 reshape.55.source_ref
  35.7 0.8 %copy.11 = s32[84,8]{1,0:T(8,128)S(1)} copy(s32[84,8]{0,1:T(8,128)} %bitcast.33) | data formatting | bytes 5376 | tf_op jit(solution)/shard_map/transpose | solution.py:171
  36.5 0.1 reshape.56.take_ref
  36.6 0.1 select_reduce_fusion.1
  36.7 0.1 copy.12
  36.8 0.1 reshape.57.factor_ref
  36.9 8.2 %inner.1 = (f32[84,2,16,128]{3,2,1,0:T(8,128)S(1)}, f32[92,2,16,128]{3,2,1,0:T(8,128)S(1)}) custom-call(s32[1]{0:T(128)} %bitcast.j_ref, s32[294]{0:T(512)S(1)} %reshape.55.source_ref, s32[672]{0:T(1024)S(1)} %reshape.56.take_ref, f32[672]{0:T(1024)S(1)} %reshape.57.factor_ref, f32[416,128]{1,0:T(8,128)S(1)} %copy-done, ...), custom_call_target="tpu_custom_call" | custom-call | tf_op jit(solution)/shard_map/inner/pallas_call | solution.py:259
  45.1 0.0 collective-permute-done.7.refs_0_
  45.1 0.0 collective-permute-done.8.refs_1_
  45.1 2.9 %outer_own.1 = (f32[21,16,128]{2,1,0:T(8,128)S(1)}, f32[21,16,128]{2,1,0:T(8,128)S(1)}, f32[21,16,128]{2,1,0:T(8,128)S(1)}, f32[21,16,128]{2,1,0:T(8,128)S(1)}) custom-call(s32[1]{0:T(128)} %bitcast.j_ref, s32[294]{0:T(512)S(1)} %reshape.55.source_ref, s32[672]{0:T(1024)S(1)} %reshape.56.take_ref, f32[672]{0:T(1024)S(1)} %reshape.57.factor_ref, ...), custom_call_target="tpu_custom_call" | custom-call | tf_op jit(solution)/shard_map/outer_own/pallas_call | solution.py:324
  48.0 0.1 collective-permute-start.9
  48.1 1.6 %collective-permute-start.10 = (f32[21,16,128]{2,1,0:T(8,128)S(1)}, f32[21,16,128]{2,1,0:T(8,128)S(1)}, u32[]{:S(2)}, u32[]{:S(2)}) collective-permute-start(f32[21,16,128]{2,1,0:T(8,128)S(1)} %get-tuple-element.35), channel_id=1, source_target_pairs={{0,2},{1,3},{2,0},{3,1},{4,6},{5,7},{6,4},{7,5},{8,10},{9,11},{10,... | collective-permute-start | bytes 516104 | tf_op jit(solution)/shard_map/ppermute | solution.py:352
  49.7 0.3 collective-permute-start.11
  50.0 0.0 collective-permute-done.12.refs_0_
  50.0 2.9 %outer_crossing.1 = (f32[21,16,128]{2,1,0:T(8,128)S(1)}, f32[21,16,128]{2,1,0:T(8,128)S(1)}, f32[21,16,128]{2,1,0:T(8,128)S(1)}, f32[21,16,128]{2,1,0:T(8,128)S(1)}) custom-call(s32[1]{0:T(128)} %bitcast.j_ref, s32[294]{0:T(512)S(1)} %reshape.55.source_ref, s32[672]{0:T(1024)S(1)} %reshape.56.take_ref, f32[672]{0:T(1024)S(1)} %reshape.57.factor_ref, ...), custom_call_target="tpu_custom_call" | custom-call | tf_op jit(solution)/shard_map/outer_crossing/pallas_call | solution.py:324
  52.9 1.0 %collective-permute-start.13 = (f32[21,16,128]{2,1,0:T(8,128)S(1)}, f32[21,16,128]{2,1,0:T(8,128)S(1)}, u32[]{:S(2)}, u32[]{:S(2)}) collective-permute-start(f32[21,16,128]{2,1,0:T(8,128)S(1)} %get-tuple-element.37), channel_id=1, source_target_pairs={{0,4},{1,5},{2,6},{3,7},{4,0},{5,1},{6,2},{7,3},{8,12},{9,13},{10,... | collective-permute-start | bytes 516104 | tf_op jit(solution)/shard_map/ppermute | solution.py:352
  53.9 0.8 %collective-permute-start.14 = (f32[21,16,128]{2,1,0:T(8,128)S(1)}, f32[21,16,128]{2,1,0:T(8,128)S(1)}, u32[]{:S(2)}, u32[]{:S(2)}) collective-permute-start(f32[21,16,128]{2,1,0:T(8,128)S(1)} %get-tuple-element.38), channel_id=1, source_target_pairs={{0,5},{1,4},{2,7},{3,6},{4,1},{5,0},{6,3},{7,2},{8,13},{9,12},{10,... | collective-permute-start | bytes 516104 | tf_op jit(solution)/shard_map/ppermute | solution.py:352
  54.6 0.0 collective-permute-done.9.refs_1_
  54.6 1.9 %collective-permute-start.15 = (f32[21,16,128]{2,1,0:T(8,128)S(1)}, f32[21,16,128]{2,1,0:T(8,128)S(1)}, u32[]{:S(2)}, u32[]{:S(2)}) collective-permute-start(f32[21,16,128]{2,1,0:T(8,128)S(1)} %get-tuple-element.39), channel_id=1, source_target_pairs={{0,6},{1,7},{2,4},{3,5},{4,2},{5,3},{6,0},{7,1},{8,14},{9,15},{10,... | collective-permute-start | bytes 516104 | tf_op jit(solution)/shard_map/ppermute | solution.py:352
  56.5 0.0 collective-permute-done.10.refs_2_
  56.5 0.8 %collective-permute-start.16 = (f32[21,16,128]{2,1,0:T(8,128)S(1)}, f32[21,16,128]{2,1,0:T(8,128)S(1)}, u32[]{:S(2)}, u32[]{:S(2)}) collective-permute-start(f32[21,16,128]{2,1,0:T(8,128)S(1)} %get-tuple-element.40), channel_id=1, source_target_pairs={{0,7},{1,6},{2,5},{3,4},{4,3},{5,2},{6,1},{7,0},{8,15},{9,14},{10,... | collective-permute-start | bytes 516104 | tf_op jit(solution)/shard_map/ppermute | solution.py:352
  57.3 0.8 %collective-permute-done.11.refs_3_ = f32[21,16,128]{2,1,0:T(8,128)S(1)} collective-permute-done((f32[21,16,128]{2,1,0:T(8,128)S(1)}, f32[21,16,128]{2,1,0:T(8,128)S(1)}, u32[]{:S(2)}, u32[]{:S(2)}) %collective-permute-start.11) | collective-permute-done | bytes 172064 | tf_op jit(solution)/shard_map/ppermute | solution.py:352
  58.1 2.0 %collective-permute-done.13.refs_4_ = f32[21,16,128]{2,1,0:T(8,128)S(1)} collective-permute-done((f32[21,16,128]{2,1,0:T(8,128)S(1)}, f32[21,16,128]{2,1,0:T(8,128)S(1)}, u32[]{:S(2)}, u32[]{:S(2)}) %collective-permute-start.13) | collective-permute-done | bytes 172064 | tf_op jit(solution)/shard_map/ppermute | solution.py:352
  60.1 2.6 %collective-permute-done.14.refs_5_ = f32[21,16,128]{2,1,0:T(8,128)S(1)} collective-permute-done((f32[21,16,128]{2,1,0:T(8,128)S(1)}, f32[21,16,128]{2,1,0:T(8,128)S(1)}, u32[]{:S(2)}, u32[]{:S(2)}) %collective-permute-start.14) | collective-permute-done | bytes 172064 | tf_op jit(solution)/shard_map/ppermute | solution.py:352
  62.7 5.8 %collective-permute-done.15.refs_6_ = f32[21,16,128]{2,1,0:T(8,128)S(1)} collective-permute-done((f32[21,16,128]{2,1,0:T(8,128)S(1)}, f32[21,16,128]{2,1,0:T(8,128)S(1)}, u32[]{:S(2)}, u32[]{:S(2)}) %collective-permute-start.15) | collective-permute-done | bytes 172064 | tf_op jit(solution)/shard_map/ppermute | solution.py:352
  68.4 2.6 %collective-permute-done.16.refs_7_ = f32[21,16,128]{2,1,0:T(8,128)S(1)} collective-permute-done((f32[21,16,128]{2,1,0:T(8,128)S(1)}, f32[21,16,128]{2,1,0:T(8,128)S(1)}, u32[]{:S(2)}, u32[]{:S(2)}) %collective-permute-start.16) | collective-permute-done | bytes 172064 | tf_op jit(solution)/shard_map/ppermute | solution.py:352
  71.0 1.1 %unpack.1 = f32[21,128,128]{2,1,0:T(8,128)} custom-call(s32[1]{0:T(128)} %bitcast.j_ref, f32[21,16,128]{2,1,0:T(8,128)S(1)} %get-tuple-element.33.refs_0_, f32[21,16,128]{2,1,0:T(8,128)S(1)} %collective-permute-done.9.refs_1_, f32[21,16,128]{2,1,0:T(8,128)S(1)} %collective-permute-done.10.refs_2_, f32[21,16,128]{2,1,0:T(8,128)S(1)} %collective-permute-done.11.refs_3_, ...), custom_call_target="tpu_custom_call" | custom-call | tf_op jit(solution)/shard_map/unpack/pallas_call | solution.py:124
  (22 shorter events, 0.2 us)
Async XLA Ops:
  0.0 8.0 %copy-start.1 = (f32[7,84,84]{2,1,0:T(8,128)S(1)}, f32[7,84,84]{2,1,0:T(8,128)}, u32[]{:S(2)}) copy-start(f32[7,84,84]{2,1,0:T(8,128)} %param.10) | copy-start | bytes 592708
  0.0 8.2 %copy-start.2 = (s32[7,84,84]{2,1,0:T(8,128)S(1)}, s32[7,84,84]{2,1,0:T(8,128)}, u32[]{:S(2)}) copy-start(s32[7,84,84]{2,1,0:T(8,128)} %param.9) | copy-start | bytes 592708
  0.0 8.4 %copy-start.3 = (s32[84]{0:T(128)S(1)}, s32[84]{0:T(128)}, u32[]{:S(2)}) copy-start(s32[84]{0:T(128)} %param.11) | copy-start | bytes 1012
  3.0 22.3 %collective-permute-start = (f32[416,128]{1,0:T(8,128)}, f32[416,128]{1,0:T(8,128)S(1)}, u32[]{:S(2)}, u32[]{:S(2)}) collective-permute-start(f32[416,128]{1,0:T(8,128)} %get-tuple-element.24), channel_id=1, source_target_pairs={{0,1},{1,0},{2,3},{3,2},{4,5},{5,4},{6,7},{7,6},{8,9},{9,8},{10,11... | collective-permute-start | bytes 638984 | tf_op jit(solution)/shard_map/ppermute | solution.py:352
  3.5 21.7 %collective-permute-start.1 = (f32[416,128]{1,0:T(8,128)}, f32[416,128]{1,0:T(8,128)S(1)}, u32[]{:S(2)}, u32[]{:S(2)}) collective-permute-start(f32[416,128]{1,0:T(8,128)} %get-tuple-element.25), channel_id=1, source_target_pairs={{0,2},{1,3},{2,0},{3,1},{4,6},{5,7},{6,4},{7,5},{8,10},{9,11},{10,... | collective-permute-start | bytes 638984 | tf_op jit(solution)/shard_map/ppermute | solution.py:352
  6.1 15.4 %collective-permute-start.2 = (f32[416,128]{1,0:T(8,128)}, f32[416,128]{1,0:T(8,128)S(1)}, u32[]{:S(2)}, u32[]{:S(2)}) collective-permute-start(f32[416,128]{1,0:T(8,128)} %get-tuple-element.26), channel_id=1, source_target_pairs={{0,3},{1,2},{2,1},{3,0},{4,7},{5,6},{6,5},{7,4},{8,11},{9,10},{10,... | collective-permute-start | bytes 638984 | tf_op jit(solution)/shard_map/ppermute | solution.py:352
  6.2 14.4 %collective-permute-start.3 = (f32[416,128]{1,0:T(8,128)}, f32[416,128]{1,0:T(8,128)S(1)}, u32[]{:S(2)}, u32[]{:S(2)}) collective-permute-start(f32[416,128]{1,0:T(8,128)} %get-tuple-element.27), channel_id=1, source_target_pairs={{0,4},{1,5},{2,6},{3,7},{4,0},{5,1},{6,2},{7,3},{8,12},{9,13},{10,... | collective-permute-start | bytes 638984 | tf_op jit(solution)/shard_map/ppermute | solution.py:352
  7.9 9.9 %collective-permute-start.4 = (f32[416,128]{1,0:T(8,128)}, f32[416,128]{1,0:T(8,128)S(1)}, u32[]{:S(2)}, u32[]{:S(2)}) collective-permute-start(f32[416,128]{1,0:T(8,128)} %get-tuple-element.28), channel_id=1, source_target_pairs={{0,5},{1,4},{2,7},{3,6},{4,1},{5,0},{6,3},{7,2},{8,13},{9,12},{10,... | collective-permute-start | bytes 638984 | tf_op jit(solution)/shard_map/ppermute | solution.py:352
  8.0 1.9 %copy-start = (f32[416,128]{1,0:T(8,128)S(1)}, f32[416,128]{1,0:T(8,128)}, u32[]{:S(2)}) copy-start(f32[416,128]{1,0:T(8,128)} %get-tuple-element.23.refs_0_) | copy-start | bytes 638980
  8.2 9.6 %copy-start.4 = (f32[416,128]{1,0:T(8,128)S(1)}, f32[416,128]{1,0:T(8,128)}, u32[]{:S(2)}) copy-start(f32[416,128]{1,0:T(8,128)} %get-tuple-element.29) | copy-start | bytes 638980
  8.2 12.4 %copy-start.5 = (f32[416,128]{1,0:T(8,128)S(1)}, f32[416,128]{1,0:T(8,128)}, u32[]{:S(2)}) copy-start(f32[416,128]{1,0:T(8,128)} %get-tuple-element.30) | copy-start | bytes 638980
  17.8 12.7 %collective-permute-start.5 = (f32[416,128]{1,0:T(8,128)S(1)}, f32[416,128]{1,0:T(8,128)S(1)}, u32[]{:S(2)}, u32[]{:S(2)}) collective-permute-start(f32[416,128]{1,0:T(8,128)S(1)} %copy-done.4), channel_id=1, source_target_pairs={{0,6},{1,7},{2,4},{3,5},{4,2},{5,3},{6,0},{7,1},{8,14},{9,15},{10,... | collective-permute-start | bytes 638984 | tf_op jit(solution)/shard_map/ppermute | solution.py:352
  20.6 9.9 %collective-permute-start.6 = (f32[416,128]{1,0:T(8,128)S(1)}, f32[416,128]{1,0:T(8,128)S(1)}, u32[]{:S(2)}, u32[]{:S(2)}) collective-permute-start(f32[416,128]{1,0:T(8,128)S(1)} %copy-done.5), channel_id=1, source_target_pairs={{0,7},{1,6},{2,5},{3,4},{4,3},{5,2},{6,1},{7,0},{8,15},{9,14},{10,... | collective-permute-start | bytes 638984 | tf_op jit(solution)/shard_map/ppermute | solution.py:352
  21.5 23.6 %collective-permute-start.7 = (f32[2,368,128]{2,1,0:T(8,128)}, f32[2,368,128]{2,1,0:T(8,128)S(1)}, u32[]{:S(2)}, u32[]{:S(2)}) collective-permute-start(f32[2,368,128]{2,1,0:T(8,128)} %pad_maximum_fusion.1), channel_id=1, source_target_pairs={{0,8},{1,9},{2,10},{3,11},{8,16},{9,17},{10,18},{11,19},{12,4},{13... | collective-permute-start | bytes 1130504 | tf_op jit(solution)/shard_map/ppermute | solution.py:362
  26.2 23.7 %collective-permute-start.12 = (f32[4,368,128]{2,1,0:T(8,128)}, f32[4,368,128]{2,1,0:T(8,128)S(1)}, u32[]{:S(2)}, u32[]{:S(2)}) collective-permute-start(f32[4,368,128]{2,1,0:T(8,128)} %pad_maximum_fusion), channel_id=1, source_target_pairs={{4,12},{5,13},{6,14},{7,15},{8,0},{9,1},{10,2},{11,3},{12,20},{13,... | collective-permute-start | bytes 2261000 | tf_op jit(solution)/shard_map/ppermute | solution.py:362
  31.4 13.7 %collective-permute-start.8 = (f32[2,368,128]{2,1,0:T(8,128)}, f32[2,368,128]{2,1,0:T(8,128)S(1)}, u32[]{:S(2)}, u32[]{:S(2)}) collective-permute-start(f32[2,368,128]{2,1,0:T(8,128)} %pad_maximum_fusion.2), channel_id=1, source_target_pairs={{0,8},{1,9},{2,10},{3,11},{8,16},{9,17},{10,18},{11,19},{12,4},{13... | collective-permute-start | bytes 1130504 | tf_op jit(solution)/shard_map/ppermute | solution.py:362
  48.0 6.6 %collective-permute-start.9 = (f32[21,16,128]{2,1,0:T(8,128)S(1)}, f32[21,16,128]{2,1,0:T(8,128)S(1)}, u32[]{:S(2)}, u32[]{:S(2)}) collective-permute-start(f32[21,16,128]{2,1,0:T(8,128)S(1)} %get-tuple-element.34), channel_id=1, source_target_pairs={{0,1},{1,0},{2,3},{3,2},{4,5},{5,4},{6,7},{7,6},{8,9},{9,8},{10,11... | collective-permute-start | bytes 516104 | tf_op jit(solution)/shard_map/ppermute | solution.py:352
  48.1 8.4 %collective-permute-start.10 = (f32[21,16,128]{2,1,0:T(8,128)S(1)}, f32[21,16,128]{2,1,0:T(8,128)S(1)}, u32[]{:S(2)}, u32[]{:S(2)}) collective-permute-start(f32[21,16,128]{2,1,0:T(8,128)S(1)} %get-tuple-element.35), channel_id=1, source_target_pairs={{0,2},{1,3},{2,0},{3,1},{4,6},{5,7},{6,4},{7,5},{8,10},{9,11},{10,... | collective-permute-start | bytes 516104 | tf_op jit(solution)/shard_map/ppermute | solution.py:352
  49.7 8.4 %collective-permute-start.11 = (f32[21,16,128]{2,1,0:T(8,128)S(1)}, f32[21,16,128]{2,1,0:T(8,128)S(1)}, u32[]{:S(2)}, u32[]{:S(2)}) collective-permute-start(f32[21,16,128]{2,1,0:T(8,128)S(1)} %get-tuple-element.36), channel_id=1, source_target_pairs={{0,3},{1,2},{2,1},{3,0},{4,7},{5,6},{6,5},{7,4},{8,11},{9,10},{10,... | collective-permute-start | bytes 516104 | tf_op jit(solution)/shard_map/ppermute | solution.py:352
  52.9 7.3 %collective-permute-start.13 = (f32[21,16,128]{2,1,0:T(8,128)S(1)}, f32[21,16,128]{2,1,0:T(8,128)S(1)}, u32[]{:S(2)}, u32[]{:S(2)}) collective-permute-start(f32[21,16,128]{2,1,0:T(8,128)S(1)} %get-tuple-element.37), channel_id=1, source_target_pairs={{0,4},{1,5},{2,6},{3,7},{4,0},{5,1},{6,2},{7,3},{8,12},{9,13},{10,... | collective-permute-start | bytes 516104 | tf_op jit(solution)/shard_map/ppermute | solution.py:352
  53.9 8.8 %collective-permute-start.14 = (f32[21,16,128]{2,1,0:T(8,128)S(1)}, f32[21,16,128]{2,1,0:T(8,128)S(1)}, u32[]{:S(2)}, u32[]{:S(2)}) collective-permute-start(f32[21,16,128]{2,1,0:T(8,128)S(1)} %get-tuple-element.38), channel_id=1, source_target_pairs={{0,5},{1,4},{2,7},{3,6},{4,1},{5,0},{6,3},{7,2},{8,13},{9,12},{10,... | collective-permute-start | bytes 516104 | tf_op jit(solution)/shard_map/ppermute | solution.py:352
  54.6 13.8 %collective-permute-start.15 = (f32[21,16,128]{2,1,0:T(8,128)S(1)}, f32[21,16,128]{2,1,0:T(8,128)S(1)}, u32[]{:S(2)}, u32[]{:S(2)}) collective-permute-start(f32[21,16,128]{2,1,0:T(8,128)S(1)} %get-tuple-element.39), channel_id=1, source_target_pairs={{0,6},{1,7},{2,4},{3,5},{4,2},{5,3},{6,0},{7,1},{8,14},{9,15},{10,... | collective-permute-start | bytes 516104 | tf_op jit(solution)/shard_map/ppermute | solution.py:352
  56.5 14.5 %collective-permute-start.16 = (f32[21,16,128]{2,1,0:T(8,128)S(1)}, f32[21,16,128]{2,1,0:T(8,128)S(1)}, u32[]{:S(2)}, u32[]{:S(2)}) collective-permute-start(f32[21,16,128]{2,1,0:T(8,128)S(1)} %get-tuple-element.40), channel_id=1, source_target_pairs={{0,7},{1,6},{2,5},{3,4},{4,3},{5,2},{6,1},{7,0},{8,15},{9,14},{10,... | collective-permute-start | bytes 516104 | tf_op jit(solution)/shard_map/ppermute | solution.py:352

commit v5 on v4

v5 whole, which is shorter than its diff:
```python
import jax
import jax.numpy as jnp
from jax import lax
from jax.experimental import pallas as pl
from jax.experimental.pallas import tpu as pltpu
from jax.sharding import PartitionSpec as P

VMEM_LIMIT = 40 * 1024 * 1024
PACK_LIMIT = 60 * 1024 * 1024
PLANES = 2
ACTIVE = 49
MOST = 8
UNROLL = 7


class Layout:
    def __init__(self, quota, terms, modes, height, width):
        self.modes = modes
        self.group = PLANES * modes
        self.rows = height // self.group
        self.width = width
        self.terms = terms
        self.quota = quota
        self.slots = quota * modes
        self.share = -(-terms // modes)
        self.fields = quota + self.share
        self.main = self.fields * self.rows
        edges = -(-2 * self.fields // 8) * 8
        self.piece = self.main + edges
        self.places = self.fields * modes

    def place(self, block, i):
        if i < self.quota:
            return block * self.quota + i
        return self.slots + block * self.share + (i - self.quota)

    def term_place(self, term, mode):
        block = jnp.bitwise_xor(term // self.share, mode)
        return self.slots + block * self.share + term % self.share


def vmem(count):
    return [pl.BlockSpec(memory_space=pltpu.VMEM)] * count


def smem(count):
    return [pl.BlockSpec(memory_space=pltpu.SMEM)] * count


def pack(field, mean, kl, j, crossing, lay):
    kl_terms = kl.shape[0]
    rows, width = lay.rows, lay.width
    height = field.shape[1]
    first = lay.modes if crossing else 0

    def kernel(j_ref, field_ref, mean_ref, kl_ref, *refs):
        out_refs, (stage_ref, mean_here, kl_here, sems) = refs[: lay.modes], refs[lay.modes :]
        copies = [
            pltpu.make_async_copy(field_ref, stage_ref.at[pl.ds(0, lay.quota)], sems.at[0]),
            pltpu.make_async_copy(mean_ref, mean_here, sems.at[1]),
            pltpu.make_async_copy(kl_ref, kl_here, sems.at[2]),
        ]
        for made in copies:
            made.start()
        me = j_ref[0]
        mode = lax.rem(me, lay.modes)
        copies[1].wait()
        copies[2].wait()
        for i in range(lay.share):
            term = mode * lay.share + i
            other = kl_here[jnp.clip(term - 1, 0, kl_terms - 1)]
            stage_ref[lay.quota + i] = jnp.where(term == 0, mean_here[0], other)
        copies[0].wait()
        for n, out_ref in enumerate(out_refs):
            other = jnp.bitwise_xor(me, first + n)
            start = pl.multiple_of(other * rows, 8)
            lower = jnp.maximum(start - 1, 0)
            upper = jnp.minimum(start + rows, height - 1)
            keep_low = jnp.where(other == 0, 0.0, 1.0)
            keep_high = jnp.where(other == lay.group - 1, 0.0, 1.0)
            for i in range(lay.fields):
                out_ref[i * rows : (i + 1) * rows, :] = stage_ref[i, pl.ds(start, rows), :]
                at = lay.main + 2 * i
                out_ref[at : at + 1, :] = stage_ref[i, pl.ds(lower, 1), :] * keep_low
                out_ref[at + 1 : at + 2, :] = stage_ref[i, pl.ds(upper, 1), :] * keep_high
            spare = lay.piece - lay.main - 2 * lay.fields
            if spare:
                out_ref[lay.piece - spare :, :] = jnp.zeros((spare, width), jnp.float32)

    return pl.pallas_call(
        kernel,
        out_shape=[jax.ShapeDtypeStruct((lay.piece, width), jnp.float32)] * lay.modes,
        in_specs=smem(1) + [pl.BlockSpec(memory_space=pltpu.HBM)] * 3,
        out_specs=vmem(lay.modes),
        scratch_shapes=[
            pltpu.VMEM((lay.fields, height, width), jnp.float32),
            pltpu.VMEM(mean.shape, jnp.float32),
            pltpu.VMEM(kl.shape, jnp.float32),
            pltpu.SemaphoreType.DMA((3,)),
        ],
        compiler_params=pltpu.CompilerParams(vmem_limit_bytes=PACK_LIMIT),
        name="pack_crossing" if crossing else "pack_own",
    )(j, field, mean, kl)


def unpack(pieces, j, shape, lay):
    rows = lay.rows

    def kernel(j_ref, *refs):
        piece_refs, out_ref, sems = refs[:-2], refs[-2], refs[-1]
        copies = []
        for r, piece_ref in zip(pieces, piece_refs):
            start = pl.multiple_of(jnp.bitwise_xor(j_ref[0], r) * rows, 8)
            made = pltpu.make_async_copy(
                piece_ref, out_ref.at[:, pl.ds(start, rows), :], sems.at[r]
            )
            made.start()
            copies.append(made)
        for made in copies:
            made.wait()

    return pl.pallas_call(
        kernel,
        out_shape=jax.ShapeDtypeStruct(shape, jnp.float32),
        in_specs=smem(1) + vmem(lay.group),
        out_specs=pl.BlockSpec(memory_space=pltpu.HBM),
        scratch_shapes=[pltpu.SemaphoreType.DMA((lay.group,))],
        compiler_params=pltpu.CompilerParams(vmem_limit_bytes=VMEM_LIMIT),
        name="unpack",
    )(j, *pieces.values())


def coupling_lists(pattern, coupling, slot_mode):
    masked = (coupling * pattern.astype(jnp.float32))[1:]
    terms, modes = masked.shape[0], masked.shape[1]
    number = jnp.arange(modes, dtype=jnp.int32)
    one_hot = (slot_mode[:, None] == number[None, :]).astype(jnp.float32)
    coupled = jnp.einsum(
        "sa,kab,tb->kst", one_hot, masked, one_hot, precision=lax.Precision.HIGHEST
    )
    there = coupled != 0.0
    column = number[None, None, :]
    first = jnp.min(jnp.where(there, column, modes), 2)
    last = jnp.max(jnp.where(there, column, -1), 2)
    active = first < modes
    earlier = column < number[None, :, None]
    rank = jnp.sum(jnp.where(active[:, None, :] & earlier, 1, 0), 2)
    place = jnp.arange(ACTIVE, dtype=jnp.int32)[None, :, None]
    chosen = active[:, None, :] & (rank[:, None, :] == place)
    sources = jnp.sum(jnp.where(chosen, column, 0), 2)

    base = ACTIVE * jnp.arange(terms, dtype=jnp.int32)[:, None]
    products, factors, valid = [], [], []
    for chosen_t, is_valid in ((first, active), (last, last > first)):
        before = active[:, None, :] & (column < chosen_t[:, :, None])
        products.append(base + jnp.sum(jnp.where(before, 1, 0), 2))
        factors.append(jnp.sum(jnp.where(column == chosen_t[:, :, None], coupled, 0.0), 2))
        valid.append(is_valid)
    products = jnp.concatenate(products, 0)
    factors = jnp.concatenate(factors, 0)
    valid = jnp.concatenate(valid, 0)
    index = jnp.arange(2 * terms, dtype=jnp.int32)
    order = index[None, :] < index[:, None]
    rank = jnp.sum(jnp.where(valid[None] & order[:, :, None], 1, 0), 1)
    place = jnp.arange(MOST, dtype=jnp.int32)[:, None, None]
    chosen = valid[None] & (rank[None] == place)
    take = jnp.sum(jnp.where(chosen, products[None], 0), 1)
    factor = jnp.sum(jnp.where(chosen, factors[None], 0.0), 1)
    return sources.reshape(-1), take.T.reshape(-1), factor.T.reshape(-1)


def gather_products(s, take_ref, factor_ref, product_ref, total):
    for n in range(MOST):
        e = s * MOST + n
        total = total + factor_ref[e] * product_ref[take_ref[e]]
    return total


def inner(pieces, others, lists, j, name, lay):
    rows, width = lay.rows, lay.width
    full = (rows, width)

    def kernel(j_ref, source_ref, take_ref, factor_ref, *refs):
        piece_refs, refs = refs[: lay.modes], refs[lay.modes :]
        other_refs, refs = refs[: lay.modes], refs[lay.modes :]
        out_ref, centre_ref, near_ref, beyond_ref, product_ref = refs
        lane = lax.broadcasted_iota(jnp.int32, full, 1)
        line = lax.broadcasted_iota(jnp.int32, full, 0)
        mode = lax.rem(j_ref[0], lay.modes)

        for block in range(lay.modes):

            def spread(i, at, piece_ref=piece_refs[block], other_ref=other_refs[block]):
                here = piece_ref[pl.ds(i * rows, rows), :]
                low = piece_ref[pl.ds(lay.main + 2 * i, 1), :]
                high = piece_ref[pl.ds(lay.main + 2 * i + 1, 1), :]
                centre_ref[at] = here
                beyond_ref[at] = other_ref[pl.ds(i * rows, rows), :]
                near_ref[at, 0] = pltpu.roll(here, width - 1, 1)
                near_ref[at, 1] = pltpu.roll(here, 1, 1)
                near_ref[at, 2] = jnp.where(line == rows - 1, high, pltpu.roll(here, rows - 1, 0))
                near_ref[at, 3] = jnp.where(line == 0, low, pltpu.roll(here, 1, 0))

            def spread_slot(i, carry, spread=spread, block=block):
                spread(i, block * lay.quota + i)
                return carry

            lax.fori_loop(0, lay.quota, spread_slot, 0, unroll=UNROLL)
            for i in range(lay.quota, lay.fields):
                spread(i, lay.place(block, i))

        def operator_of(term):
            at = lay.term_place(term, mode)
            here = centre_ref[at]
            beside = [near_ref[at, n] for n in range(4)]
            beside[0] = jnp.where(lane == width - 1, 0.0, beside[0])
            beside[1] = jnp.where(lane == 0, 0.0, beside[1])
            faces = [0.5 * (here + n) for n in beside]
            between = 0.5 * (here + beyond_ref[at])
            diagonal = faces[0] + faces[1] + faces[2] + faces[3] + between + 0.5 * here
            faces[0] = jnp.where(lane == width - 1, 0.0, faces[0])
            faces[1] = jnp.where(lane == 0, 0.0, faces[1])

            def operator(t):
                total = diagonal * centre_ref[t] - between * beyond_ref[t]
                for n in range(4):
                    total = total - faces[n] * near_ref[t, n]
                return total

            return operator

        for term in range(1, lay.terms):
            operator = operator_of(term)

            def apply(n, carry, operator=operator, term=term):
                e = (term - 1) * ACTIVE + n
                product_ref[e] = operator(source_ref[e])
                return carry

            lax.fori_loop(0, ACTIVE, apply, 0, unroll=UNROLL)

        operator = operator_of(0)

        def collect(s, carry):
            out_ref[s] = gather_products(s, take_ref, factor_ref, product_ref, operator(s))
            return carry

        lax.fori_loop(0, lay.slots, collect, 0, unroll=UNROLL)

    return pl.pallas_call(
        kernel,
        out_shape=[
            jax.ShapeDtypeStruct((lay.slots, rows, width), jnp.float32),
            jax.ShapeDtypeStruct((lay.places, rows, width), jnp.float32),
        ],
        in_specs=smem(4) + vmem(2 * lay.modes),
        out_specs=vmem(2),
        scratch_shapes=[
            pltpu.VMEM((lay.places, 4, rows, width), jnp.float32),
            pltpu.VMEM((lay.places, rows, width), jnp.float32),
            pltpu.VMEM(((lay.terms - 1) * ACTIVE, rows, width), jnp.float32),
        ],
        compiler_params=pltpu.CompilerParams(vmem_limit_bytes=VMEM_LIMIT),
        name=name,
    )(j, *lists, *pieces, *others)


def outer(centre, partial, halos, lists, j, name, lay):
    rows, width = lay.rows, lay.width

    def kernel(j_ref, source_ref, take_ref, factor_ref, centre_ref, part_ref, *refs):
        halo_refs, refs = refs[: len(halos)], refs[len(halos) :]
        out_refs, (far_ref, product_ref) = refs[: lay.modes], refs[lay.modes :]
        mode = lax.rem(j_ref[0], lay.modes)
        block = 0
        for halo_ref in halo_refs:
            for n in range(halo_ref.shape[0]):

                def spread_slot(i, carry, halo_ref=halo_ref, n=n, block=block):
                    far_ref[block * lay.quota + i] = halo_ref[n, pl.ds(i * rows, rows), :]
                    return carry

                lax.fori_loop(0, lay.quota, spread_slot, 0, unroll=UNROLL)
                for i in range(lay.quota, lay.fields):
                    far_ref[lay.place(block, i)] = halo_ref[n, i * rows : (i + 1) * rows, :]
                block += 1

        def operator_of(term):
            at = lay.term_place(term, mode)
            far = far_ref[at]
            half, whole = 0.5 * far, 0.5 * (centre_ref[at] + far)
            return lambda t: half * centre_ref[t] - whole * far_ref[t]

        for term in range(1, lay.terms):
            operator = operator_of(term)

            def apply(n, carry, operator=operator, term=term):
                e = (term - 1) * ACTIVE + n
                product_ref[e] = operator(source_ref[e])
                return carry

            lax.fori_loop(0, ACTIVE, apply, 0, unroll=UNROLL)

        operator = operator_of(0)
        for block in range(lay.modes):

            def collect(i, carry, out_ref=out_refs[block], block=block):
                s = block * lay.quota + i
                total = part_ref[s] + operator(s)
                out_ref[i] = gather_products(s, take_ref, factor_ref, product_ref, total)
                return carry

            lax.fori_loop(0, lay.quota, collect, 0, unroll=UNROLL)

    return pl.pallas_call(
        kernel,
        out_shape=[jax.ShapeDtypeStruct((lay.quota, rows, width), jnp.float32)] * lay.modes,
        in_specs=smem(4) + vmem(2 + len(halos)),
        out_specs=vmem(lay.modes),
        scratch_shapes=[
            pltpu.VMEM((lay.places, rows, width), jnp.float32),
            pltpu.VMEM(((lay.terms - 1) * ACTIVE, rows, width), jnp.float32),
        ],
        compiler_params=pltpu.CompilerParams(vmem_limit_bytes=VMEM_LIMIT),
        name=name,
    )(j, *lists, centre, partial, *halos)


def after(value, *done):
    return lax.optimization_barrier((value, *done))[0]


def on_device(chaos_field, mean_field, kl_fields, pattern, coupling, slot_mode):
    spaces, modes = lax.axis_size("space"), lax.axis_size("mode")
    quota, _, height, width = chaos_field.shape
    terms = kl_fields.shape[0] + 1
    lay = Layout(quota, terms, modes, height, width)
    axes = ("space", "mode")
    devices = spaces * modes
    space = lax.axis_index("space").astype(jnp.int32)
    mode = lax.axis_index("mode").astype(jnp.int32)
    j = (lax.rem(space, PLANES) * modes + mode).reshape(1)

    def swap(piece, r):
        if r == 0:
            return piece
        return lax.ppermute(piece, axes, [(d, d ^ r) for d in range(devices)])

    def shift(pieces, crossing):
        pairs = []
        for d in range(devices):
            upper = (d // modes) % PLANES == (0 if crossing else 1)
            other = d + lay.group if upper else d - lay.group
            if 0 <= other < devices:
                pairs.append((d, other))
        main = jnp.stack([piece[: lay.main] for piece in pieces])
        return lax.ppermute(main, axes, pairs)

    field, kl = chaos_field[:, 0], kl_fields[:, 0]
    sent = [None] * lay.group
    sent[modes:] = pack(field, mean_field, kl, j, True, lay)
    sent[:modes] = pack(field, mean_field, kl, after(j, *sent[modes:]), False, lay)
    pieces = sent[:1] + [None] * (lay.group - 1)
    half = modes + modes // 2
    early = [r for r in range(modes, half)] + [r for r in range(1, modes)]
    for r in early:
        pieces[r] = swap(sent[r], r)
    for r in range(half, lay.group):
        pieces[r] = swap(after(sent[r], pieces[r - half + 1]), r)
    number = jnp.arange(modes, dtype=jnp.int32)
    mine = jnp.bitwise_xor(number, mode)[:, None, None] == number[None, :, None]
    slot_mode = jnp.sum(jnp.where(mine, slot_mode.reshape(1, modes, quota), 0), 1).reshape(-1)
    lists = coupling_lists(pattern, coupling, slot_mode)
    pieces[modes] = after(pieces[modes], *lists)
    far_own = shift(pieces[:modes], False)
    far_first = shift(pieces[modes:half], True)
    far_second = shift(pieces[half:], True)

    part, centre = inner(pieces[modes:], pieces[:modes], lists, j, "inner_crossing", lay)
    own_part, own_centre = inner(pieces[:modes], pieces[modes:], lists, j, "inner_own", lay)
    crossing = outer(centre, part, [far_own], lists, j, "outer_crossing", lay)
    own_part = after(own_part, *crossing)
    own = outer(own_centre, own_part, [far_first, far_second], lists, j, "outer_own", lay)
    back = {modes + n: swap(piece, modes + n) for n, piece in enumerate(crossing)}
    back.update({n: swap(piece, n) for n, piece in enumerate(own)})
    return unpack(back, j, (quota, height, width), lay).reshape(chaos_field.shape)


def solution(mesh):
    in_specs = (
        P("mode", "space", None, None),
        P("space", None, None),
        P(None, "space", None, None),
        P(),
        P(),
        P(),
    )
    out_specs = P("mode", "space", None, None)
    return jax.shard_map(
        on_device, mesh=mesh, in_specs=in_specs, out_specs=out_specs, check_vma=False
    )
```

time: 72.4 us -> 79.9 us (1.10)
  waiting for transfers between devices: 24.6 us -> 32.4 us
  other arithmetic: 3.95 us -> 1.18 us
  Pallas kernels: 18.1 us -> 19.6 us
  starting transfers between devices: 22.8 us -> 24.3 us
    ppermute x3, waiting for transfers between devices: 0.01 us -> 7.37 us  [shift(): return lax.ppermute(main, axes, pairs)]
    another operation x3, other arithmetic: 2.46 us -> 0.11 us  [shift(): main = jnp.stack([piece[:lay.main] for piece in pieces])]
    pallas_call x1 -> x2, Pallas kernels: 3.01 us -> 5.08 us  [pack(): pl.pallas_call(kernel, out_shape=[jax.ShapeDtypeStruct((lay.piece, width)...]
    ppermute x14, starting transfers between devices: 14.1 us -> 15 us  [swap(): return lax.ppermute(piece, axes, [(d, d ^ r) for d in range(devices)])]
    pallas_call x2, Pallas kernels: 5.8 us -> 4.97 us  [outer(): pl.pallas_call(kernel, out_shape=[jax.ShapeDtypeStruct((lay.quota, rows,...]
    pallas_call x1 -> x2, Pallas kernels: 8.19 us -> 8.38 us  [inner(): pl.pallas_call(kernel, out_shape=[jax.ShapeDtypeStruct((lay.slots, rows,...]
  transfers between devices with their start and end apart: 17 -> 17, of which waited for: 7 -> 7; matrix products, arithmetic and copies ran while one was open for 9% -> 4% of each run, Pallas kernels for 19% -> 20%
where the time goes in v5:
time: 79.9 us; the launch traced here: 79.7 us
  waiting for transfers between devices  32.4 us (41%)
  starting transfers between devices  24.3 us (30%)
  Pallas kernels  19.6 us (25%)
  other arithmetic  1.18 us (1%)
  local copies, waits for them, and re-layouts  1.14 us (1%)
    ppermute x14, waiting for transfers between devices, swap(): return lax.ppermute(piece, axes, [(d, d ^ r) for d in range(devices)])  25 us
    ppermute x14, starting transfers between devices, swap(): return lax.ppermute(piece, axes, [(d, d ^ r) for d in range(devices)])  15 us
    ppermute x3, starting transfers between devices, shift(): return lax.ppermute(main, axes, pairs)  9.33 us
    pallas_call x2, Pallas kernels, inner(): pl.pallas_call(kernel, out_shape=[jax.ShapeDtypeStruct((lay.slots, rows,...  8.38 us
    ppermute x3, waiting for transfers between devices, shift(): return lax.ppermute(main, axes, pairs)  7.37 us
    pallas_call x2, Pallas kernels, pack(): pl.pallas_call(kernel, out_shape=[jax.ShapeDtypeStruct((lay.piece, width)...  5.08 us
    pallas_call x2, Pallas kernels, outer(): pl.pallas_call(kernel, out_shape=[jax.ShapeDtypeStruct((lay.quota, rows,...  4.97 us
  transfers between devices with their start and end apart: 17, of which 7 were waited for; matrix products, arithmetic and copies ran while one was open for 4% of the time, Pallas kernels for 20%

profile of v5, /device:TPU:0, one launch (start us, length us, event | category | flops | bytes accessed | tf_op | source)
XLA Modules:
  0.0 79.7 jit_solution(6526797641881906809)
XLA Ops:
  0.0 2.5 %pack_crossing.1 = (f32[416,128]{1,0:T(8,128)}, f32[416,128]{1,0:T(8,128)}, f32[416,128]{1,0:T(8,128)}, f32[416,128]{1,0:T(8,128)}) custom-call(s32[1]{0:T(128)} %bitcast.j_ref, f32[21,128,128]{2,1,0:T(8,128)} %bitcast.31, f32[1,128,128]{2,1,0:T(8,128)} %mean_ref.3, f32[6,128,128]{2,1,0:T(8,128)} %bitcast.33), custom_call_target="tpu_custom_call" | custom-call | tf_op jit(solution)/shard_map/pack_crossing/pallas_call | solution.py:90
  2.5 0.0 copy-start.1
  2.5 0.0 copy-start.2
  2.6 3.0 %collective-permute-start = (f32[416,128]{1,0:T(8,128)}, f32[416,128]{1,0:T(8,128)S(1)}, u32[]{:S(2)}, u32[]{:S(2)}) collective-permute-start(f32[416,128]{1,0:T(8,128)} %get-tuple-element.30), channel_id=1, source_target_pairs={{0,4},{1,5},{2,6},{3,7},{4,0},{5,1},{6,2},{7,3},{8,12},{9,13},{10,... | collective-permute-start | bytes 638984 | tf_op jit(solution)/shard_map/ppermute | solution.py:347
  5.6 0.0 collective-permute-start.1
  5.6 2.6 %pack_own.1 = (f32[416,128]{1,0:T(8,128)}, f32[416,128]{1,0:T(8,128)}, f32[416,128]{1,0:T(8,128)}, f32[416,128]{1,0:T(8,128)}) custom-call(s32[1]{0:T(128)} %bitcast.j_ref, f32[21,128,128]{2,1,0:T(8,128)} %bitcast.32, f32[1,128,128]{2,1,0:T(8,128)} %mean_ref.3, f32[6,128,128]{2,1,0:T(8,128)} %bitcast.34), custom_call_target="tpu_custom_call" | custom-call | tf_op jit(solution)/shard_map/pack_own/pallas_call | solution.py:90
  8.1 0.3 collective-permute-start.2
  8.4 2.0 %collective-permute-start.4 = (f32[416,128]{1,0:T(8,128)}, f32[416,128]{1,0:T(8,128)S(1)}, u32[]{:S(2)}, u32[]{:S(2)}) collective-permute-start(f32[416,128]{1,0:T(8,128)} %get-tuple-element.38), channel_id=1, source_target_pairs={{0,2},{1,3},{2,0},{3,1},{4,6},{5,7},{6,4},{7,5},{8,10},{9,11},{10,... | collective-permute-start | bytes 638984 | tf_op jit(solution)/shard_map/ppermute | solution.py:347
  10.4 0.0 collective-permute-start.6
  10.4 0.2 copy.10
  10.6 0.2 copy.9
  10.8 0.0 copy-start.4
  10.8 0.1 broadcast_in_dim.135
  10.9 0.1 iota_compare_fusion.9
  11.0 0.1 select_reduce_fusion.9
  11.1 0.1 eq.38
  11.2 0.3 fusion
  11.5 0.3 fusion.10
  11.9 0.1 fusion.6
  12.0 0.2 select_reduce_fusion.3
  12.3 0.2 select_reduce_fusion.5
  12.4 0.1 reshape.85.source_ref
  12.5 0.1 broadcast_add_fusion.1
  12.6 0.1 select_reduce_fusion.6
  12.8 0.1 copy.11
  12.9 0.1 reshape.86.take_ref
  13.0 0.1 select_reduce_fusion.1
  13.1 0.1 copy.12
  13.2 0.1 reshape.87.factor_ref
  13.3 0.0 collective-permute-done.refs_0_.refs_4_
  13.3 0.0 collective-permute-done.2.refs_5_.refs_1_
  13.3 2.4 %collective-permute-start.3 = (f32[416,128]{1,0:T(8,128)S(1)}, f32[416,128]{1,0:T(8,128)S(1)}, u32[]{:S(2)}, u32[]{:S(2)}) collective-permute-start(f32[416,128]{1,0:T(8,128)S(1)} %copy-done.4), channel_id=1, source_target_pairs={{0,6},{1,7},{2,4},{3,5},{4,2},{5,3},{6,0},{7,1},{8,14},{9,15},{10,... | collective-permute-start | bytes 638984 | tf_op jit(solution)/shard_map/ppermute | solution.py:347
  15.8 0.9 %collective-permute-done.4.refs_6_.refs_2_ = f32[416,128]{1,0:T(8,128)S(1)} collective-permute-done((f32[416,128]{1,0:T(8,128)}, f32[416,128]{1,0:T(8,128)S(1)}, u32[]{:S(2)}, u32[]{:S(2)}) %collective-permute-start.4) | collective-permute-done | bytes 213024 | tf_op jit(solution)/shard_map/ppermute | solution.py:347
  16.7 0.9 %collective-permute-start.5 = (f32[416,128]{1,0:T(8,128)S(1)}, f32[416,128]{1,0:T(8,128)S(1)}, u32[]{:S(2)}, u32[]{:S(2)}) collective-permute-start(f32[416,128]{1,0:T(8,128)S(1)} %copy-done.5), channel_id=1, source_target_pairs={{0,7},{1,6},{2,5},{3,4},{4,3},{5,2},{6,1},{7,0},{8,15},{9,14},{10,... | collective-permute-start | bytes 638984 | tf_op jit(solution)/shard_map/ppermute | solution.py:347
  17.6 11.6 %collective-permute-done.6.refs_7_.refs_3_ = f32[416,128]{1,0:T(8,128)S(1)} collective-permute-done((f32[416,128]{1,0:T(8,128)}, f32[416,128]{1,0:T(8,128)S(1)}, u32[]{:S(2)}, u32[]{:S(2)}) %collective-permute-start.6) | collective-permute-done | bytes 213024 | tf_op jit(solution)/shard_map/ppermute | solution.py:347
  29.2 0.1 pad_maximum_fusion
  29.2 1.3 %collective-permute-start.7 = (f32[4,368,128]{2,1,0:T(8,128)S(1)}, f32[4,368,128]{2,1,0:T(8,128)S(1)}, u32[]{:S(2)}, u32[]{:S(2)}) collective-permute-start(f32[4,368,128]{2,1,0:T(8,128)S(1)} %pad_maximum_fusion), channel_id=1, source_target_pairs={{4,12},{5,13},{6,14},{7,15},{8,0},{9,1},{10,2},{11,3},{12,20},{13,... | collective-permute-start | bytes 2261000 | tf_op jit(solution)/shard_map/ppermute | solution.py:357
  30.6 0.0 collective-permute-done.1.refs_1_.refs_5_
  30.6 4.6 %collective-permute-start.12 = (f32[2,368,128]{2,1,0:T(8,128)S(1)}, f32[2,368,128]{2,1,0:T(8,128)S(1)}, u32[]{:S(2)}, u32[]{:S(2)}) collective-permute-start(f32[2,368,128]{2,1,0:T(8,128)S(1)} %pad_maximum_fusion.1), channel_id=1, source_target_pairs={{0,8},{1,9},{2,10},{3,11},{8,16},{9,17},{10,18},{11,19},{12,4},{13... | collective-permute-start | bytes 1130504 | tf_op jit(solution)/shard_map/ppermute | solution.py:357
  35.2 0.0 collective-permute-done.5.refs_3_.refs_7_
  35.2 0.0 collective-permute-done.3.refs_2_.refs_6_
  35.3 3.5 %collective-permute-start.13 = (f32[2,368,128]{2,1,0:T(8,128)S(1)}, f32[2,368,128]{2,1,0:T(8,128)S(1)}, u32[]{:S(2)}, u32[]{:S(2)}) collective-permute-start(f32[2,368,128]{2,1,0:T(8,128)S(1)} %pad_maximum_fusion.2), channel_id=1, source_target_pairs={{0,8},{1,9},{2,10},{3,11},{8,16},{9,17},{10,18},{11,19},{12,4},{13... | collective-permute-start | bytes 1130504 | tf_op jit(solution)/shard_map/ppermute | solution.py:357
  38.8 4.2 %inner_crossing.1 = (f32[84,16,128]{2,1,0:T(8,128)S(1)}, f32[92,16,128]{2,1,0:T(8,128)S(1)}) custom-call(s32[1]{0:T(128)} %bitcast.j_ref, s32[294]{0:T(512)S(1)} %reshape.85.source_ref, s32[672]{0:T(1024)S(1)} %reshape.86.take_ref, f32[672]{0:T(1024)S(1)} %reshape.87.factor_ref, f32[416,128]{1,0:T(8,128)S(1)} %collective-permute-done.refs_0_.refs_4_, ...), custom_call_target="tpu_custom_call" | custom-call | tf_op jit(solution)/shard_map/inner_crossing/pallas_call | solution.py:250
  43.0 7.4 %collective-permute-done.7.refs_0_ = f32[4,368,128]{2,1,0:T(8,128)S(1)} collective-permute-done((f32[4,368,128]{2,1,0:T(8,128)S(1)}, f32[4,368,128]{2,1,0:T(8,128)S(1)}, u32[]{:S(2)}, u32[]{:S(2)}) %collective-permute-start.7) | collective-permute-done | bytes 753696 | tf_op jit(solution)/shard_map/ppermute | solution.py:357
  50.4 2.5 %outer_crossing.1 = (f32[21,16,128]{2,1,0:T(8,128)S(1)}, f32[21,16,128]{2,1,0:T(8,128)S(1)}, f32[21,16,128]{2,1,0:T(8,128)S(1)}, f32[21,16,128]{2,1,0:T(8,128)S(1)}) custom-call(s32[1]{0:T(128)} %bitcast.j_ref, s32[294]{0:T(512)S(1)} %reshape.85.source_ref, s32[672]{0:T(1024)S(1)} %reshape.86.take_ref, f32[672]{0:T(1024)S(1)} %reshape.87.factor_ref, ...), custom_call_target="tpu_custom_call" | custom-call | tf_op jit(solution)/shard_map/outer_crossing/pallas_call | solution.py:315
  52.8 0.8 %collective-permute-start.8 = (f32[21,16,128]{2,1,0:T(8,128)S(1)}, f32[21,16,128]{2,1,0:T(8,128)S(1)}, u32[]{:S(2)}, u32[]{:S(2)}) collective-permute-start(f32[21,16,128]{2,1,0:T(8,128)S(1)} %get-tuple-element.44), channel_id=1, source_target_pairs={{0,4},{1,5},{2,6},{3,7},{4,0},{5,1},{6,2},{7,3},{8,12},{9,13},{10,... | collective-permute-start | bytes 516104 | tf_op jit(solution)/shard_map/ppermute | solution.py:347
  53.7 0.3 collective-permute-start.9
  54.0 4.2 %inner_own.1 = (f32[84,16,128]{2,1,0:T(8,128)S(1)}, f32[92,16,128]{2,1,0:T(8,128)S(1)}) custom-call(s32[1]{0:T(128)} %bitcast.j_ref, s32[294]{0:T(512)S(1)} %reshape.85.source_ref, s32[672]{0:T(1024)S(1)} %reshape.86.take_ref, f32[672]{0:T(1024)S(1)} %reshape.87.factor_ref, f32[416,128]{1,0:T(8,128)S(1)} %copy-done, ...), custom_call_target="tpu_custom_call" | custom-call | tf_op jit(solution)/shard_map/inner_own/pallas_call | solution.py:250
  58.1 2.2 %collective-permute-start.10 = (f32[21,16,128]{2,1,0:T(8,128)S(1)}, f32[21,16,128]{2,1,0:T(8,128)S(1)}, u32[]{:S(2)}, u32[]{:S(2)}) collective-permute-start(f32[21,16,128]{2,1,0:T(8,128)S(1)} %get-tuple-element.46), channel_id=1, source_target_pairs={{0,6},{1,7},{2,4},{3,5},{4,2},{5,3},{6,0},{7,1},{8,14},{9,15},{10,... | collective-permute-start | bytes 516104 | tf_op jit(solution)/shard_map/ppermute | solution.py:347
  60.3 0.0 collective-permute-done.12.refs_0_
  60.3 1.2 %collective-permute-start.11 = (f32[21,16,128]{2,1,0:T(8,128)S(1)}, f32[21,16,128]{2,1,0:T(8,128)S(1)}, u32[]{:S(2)}, u32[]{:S(2)}) collective-permute-start(f32[21,16,128]{2,1,0:T(8,128)S(1)} %get-tuple-element.47), channel_id=1, source_target_pairs={{0,7},{1,6},{2,5},{3,4},{4,3},{5,2},{6,1},{7,0},{8,15},{9,14},{10,... | collective-permute-start | bytes 516104 | tf_op jit(solution)/shard_map/ppermute | solution.py:347
  61.6 0.0 collective-permute-done.13.refs_1_
  61.6 2.5 %outer_own.1 = (f32[21,16,128]{2,1,0:T(8,128)S(1)}, f32[21,16,128]{2,1,0:T(8,128)S(1)}, f32[21,16,128]{2,1,0:T(8,128)S(1)}, f32[21,16,128]{2,1,0:T(8,128)S(1)}) custom-call(s32[1]{0:T(128)} %bitcast.j_ref, s32[294]{0:T(512)S(1)} %reshape.85.source_ref, s32[672]{0:T(1024)S(1)} %reshape.86.take_ref, f32[672]{0:T(1024)S(1)} %reshape.87.factor_ref, ...), custom_call_target="tpu_custom_call" | custom-call | tf_op jit(solution)/shard_map/outer_own/pallas_call | solution.py:315
  64.1 0.1 collective-permute-start.14
  64.1 0.0 collective-permute-done.8.refs_0_
  64.2 1.8 %collective-permute-start.15 = (f32[21,16,128]{2,1,0:T(8,128)S(1)}, f32[21,16,128]{2,1,0:T(8,128)S(1)}, u32[]{:S(2)}, u32[]{:S(2)}) collective-permute-start(f32[21,16,128]{2,1,0:T(8,128)S(1)} %get-tuple-element.53), channel_id=1, source_target_pairs={{0,2},{1,3},{2,0},{3,1},{4,6},{5,7},{6,4},{7,5},{8,10},{9,11},{10,... | collective-permute-start | bytes 516104 | tf_op jit(solution)/shard_map/ppermute | solution.py:347
  65.9 0.0 collective-permute-done.9.refs_1_
  65.9 0.1 collective-permute-start.16
  66.0 2.6 %collective-permute-done.10.refs_2_ = f32[21,16,128]{2,1,0:T(8,128)S(1)} collective-permute-done((f32[21,16,128]{2,1,0:T(8,128)S(1)}, f32[21,16,128]{2,1,0:T(8,128)S(1)}, u32[]{:S(2)}, u32[]{:S(2)}) %collective-permute-start.10) | collective-permute-done | bytes 172064 | tf_op jit(solution)/shard_map/ppermute | solution.py:347
  68.6 1.7 %collective-permute-done.11.refs_3_ = f32[21,16,128]{2,1,0:T(8,128)S(1)} collective-permute-done((f32[21,16,128]{2,1,0:T(8,128)S(1)}, f32[21,16,128]{2,1,0:T(8,128)S(1)}, u32[]{:S(2)}, u32[]{:S(2)}) %collective-permute-start.11) | collective-permute-done | bytes 172064 | tf_op jit(solution)/shard_map/ppermute | solution.py:347
  70.3 0.0 collective-permute-done.14.refs_5_
  70.3 4.6 %collective-permute-done.15.refs_6_ = f32[21,16,128]{2,1,0:T(8,128)S(1)} collective-permute-done((f32[21,16,128]{2,1,0:T(8,128)S(1)}, f32[21,16,128]{2,1,0:T(8,128)S(1)}, u32[]{:S(2)}, u32[]{:S(2)}) %collective-permute-start.15) | collective-permute-done | bytes 172064 | tf_op jit(solution)/shard_map/ppermute | solution.py:347
  74.9 3.6 %collective-permute-done.16.refs_7_ = f32[21,16,128]{2,1,0:T(8,128)S(1)} collective-permute-done((f32[21,16,128]{2,1,0:T(8,128)S(1)}, f32[21,16,128]{2,1,0:T(8,128)S(1)}, u32[]{:S(2)}, u32[]{:S(2)}) %collective-permute-start.16) | collective-permute-done | bytes 172064 | tf_op jit(solution)/shard_map/ppermute | solution.py:347
  78.5 1.1 %unpack.1 = f32[21,128,128]{2,1,0:T(8,128)} custom-call(s32[1]{0:T(128)} %bitcast.j_ref, f32[21,16,128]{2,1,0:T(8,128)S(1)} %collective-permute-done.8.refs_0_, f32[21,16,128]{2,1,0:T(8,128)S(1)} %collective-permute-done.9.refs_1_, f32[21,16,128]{2,1,0:T(8,128)S(1)} %collective-permute-done.10.refs_2_, f32[21,16,128]{2,1,0:T(8,128)S(1)} %collective-permute-done.11.refs_3_, ...), custom_call_target="tpu_custom_call" | custom-call | tf_op jit(solution)/shard_map/unpack/pallas_call | solution.py:122
  (29 shorter events, 0.3 us)
Async XLA Ops:
  2.5 7.9 %copy-start.1 = (f32[7,84,84]{2,1,0:T(8,128)S(1)}, f32[7,84,84]{2,1,0:T(8,128)}, u32[]{:S(2)}) copy-start(f32[7,84,84]{2,1,0:T(8,128)} %param.10) | copy-start | bytes 592708
  2.5 8.1 %copy-start.2 = (s32[7,84,84]{2,1,0:T(8,128)S(1)}, s32[7,84,84]{2,1,0:T(8,128)}, u32[]{:S(2)}) copy-start(s32[7,84,84]{2,1,0:T(8,128)} %param.9) | copy-start | bytes 592708
  2.6 10.8 %collective-permute-start = (f32[416,128]{1,0:T(8,128)}, f32[416,128]{1,0:T(8,128)S(1)}, u32[]{:S(2)}, u32[]{:S(2)}) collective-permute-start(f32[416,128]{1,0:T(8,128)} %get-tuple-element.30), channel_id=1, source_target_pairs={{0,4},{1,5},{2,6},{3,7},{4,0},{5,1},{6,2},{7,3},{8,12},{9,13},{10,... | collective-permute-start | bytes 638984 | tf_op jit(solution)/shard_map/ppermute | solution.py:347
  5.6 25.0 %collective-permute-start.1 = (f32[416,128]{1,0:T(8,128)}, f32[416,128]{1,0:T(8,128)S(1)}, u32[]{:S(2)}, u32[]{:S(2)}) collective-permute-start(f32[416,128]{1,0:T(8,128)} %get-tuple-element.32), channel_id=1, source_target_pairs={{0,5},{1,4},{2,7},{3,6},{4,1},{5,0},{6,3},{7,2},{8,13},{9,12},{10,... | collective-permute-start | bytes 638984 | tf_op jit(solution)/shard_map/ppermute | solution.py:347
  5.6 5.3 %copy-start.3 = (s32[84]{0:T(128)S(1)}, s32[84]{0:T(128)}, u32[]{:S(2)}) copy-start(s32[84]{0:T(128)} %param.11) | copy-start | bytes 1012
  8.1 5.2 %collective-permute-start.2 = (f32[416,128]{1,0:T(8,128)}, f32[416,128]{1,0:T(8,128)S(1)}, u32[]{:S(2)}, u32[]{:S(2)}) collective-permute-start(f32[416,128]{1,0:T(8,128)} %get-tuple-element.36), channel_id=1, source_target_pairs={{0,1},{1,0},{2,3},{3,2},{4,5},{5,4},{6,7},{7,6},{8,9},{9,8},{10,11... | collective-permute-start | bytes 638984 | tf_op jit(solution)/shard_map/ppermute | solution.py:347
  8.4 8.3 %collective-permute-start.4 = (f32[416,128]{1,0:T(8,128)}, f32[416,128]{1,0:T(8,128)S(1)}, u32[]{:S(2)}, u32[]{:S(2)}) collective-permute-start(f32[416,128]{1,0:T(8,128)} %get-tuple-element.38), channel_id=1, source_target_pairs={{0,2},{1,3},{2,0},{3,1},{4,6},{5,7},{6,4},{7,5},{8,10},{9,11},{10,... | collective-permute-start | bytes 638984 | tf_op jit(solution)/shard_map/ppermute | solution.py:347
  10.4 18.8 %collective-permute-start.6 = (f32[416,128]{1,0:T(8,128)}, f32[416,128]{1,0:T(8,128)S(1)}, u32[]{:S(2)}, u32[]{:S(2)}) collective-permute-start(f32[416,128]{1,0:T(8,128)} %get-tuple-element.41), channel_id=1, source_target_pairs={{0,3},{1,2},{2,1},{3,0},{4,7},{5,6},{6,5},{7,4},{8,11},{9,10},{10,... | collective-permute-start | bytes 638984 | tf_op jit(solution)/shard_map/ppermute | solution.py:347
  10.6 2.7 %copy-start = (f32[416,128]{1,0:T(8,128)S(1)}, f32[416,128]{1,0:T(8,128)}, u32[]{:S(2)}) copy-start(f32[416,128]{1,0:T(8,128)} %get-tuple-element.40.refs_4_.refs_0_) | copy-start | bytes 638980
  10.8 2.5 %copy-start.4 = (f32[416,128]{1,0:T(8,128)S(1)}, f32[416,128]{1,0:T(8,128)}, u32[]{:S(2)}) copy-start(f32[416,128]{1,0:T(8,128)} %get-tuple-element.37) | copy-start | bytes 638980
  10.8 5.8 %copy-start.5 = (f32[416,128]{1,0:T(8,128)S(1)}, f32[416,128]{1,0:T(8,128)}, u32[]{:S(2)}) copy-start(f32[416,128]{1,0:T(8,128)} %get-tuple-element.39) | copy-start | bytes 638980
  13.3 21.9 %collective-permute-start.3 = (f32[416,128]{1,0:T(8,128)S(1)}, f32[416,128]{1,0:T(8,128)S(1)}, u32[]{:S(2)}, u32[]{:S(2)}) collective-permute-start(f32[416,128]{1,0:T(8,128)S(1)} %copy-done.4), channel_id=1, source_target_pairs={{0,6},{1,7},{2,4},{3,5},{4,2},{5,3},{6,0},{7,1},{8,14},{9,15},{10,... | collective-permute-start | bytes 638984 | tf_op jit(solution)/shard_map/ppermute | solution.py:347
  16.7 18.5 %collective-permute-start.5 = (f32[416,128]{1,0:T(8,128)S(1)}, f32[416,128]{1,0:T(8,128)S(1)}, u32[]{:S(2)}, u32[]{:S(2)}) collective-permute-start(f32[416,128]{1,0:T(8,128)S(1)} %copy-done.5), channel_id=1, source_target_pairs={{0,7},{1,6},{2,5},{3,4},{4,3},{5,2},{6,1},{7,0},{8,15},{9,14},{10,... | collective-permute-start | bytes 638984 | tf_op jit(solution)/shard_map/ppermute | solution.py:347
  29.2 21.1 %collective-permute-start.7 = (f32[4,368,128]{2,1,0:T(8,128)S(1)}, f32[4,368,128]{2,1,0:T(8,128)S(1)}, u32[]{:S(2)}, u32[]{:S(2)}) collective-permute-start(f32[4,368,128]{2,1,0:T(8,128)S(1)} %pad_maximum_fusion), channel_id=1, source_target_pairs={{4,12},{5,13},{6,14},{7,15},{8,0},{9,1},{10,2},{11,3},{12,20},{13,... | collective-permute-start | bytes 2261000 | tf_op jit(solution)/shard_map/ppermute | solution.py:357
  30.6 29.7 %collective-permute-start.12 = (f32[2,368,128]{2,1,0:T(8,128)S(1)}, f32[2,368,128]{2,1,0:T(8,128)S(1)}, u32[]{:S(2)}, u32[]{:S(2)}) collective-permute-start(f32[2,368,128]{2,1,0:T(8,128)S(1)} %pad_maximum_fusion.1), channel_id=1, source_target_pairs={{0,8},{1,9},{2,10},{3,11},{8,16},{9,17},{10,18},{11,19},{12,4},{13... | collective-permute-start | bytes 1130504 | tf_op jit(solution)/shard_map/ppermute | solution.py:357
  35.3 26.3 %collective-permute-start.13 = (f32[2,368,128]{2,1,0:T(8,128)S(1)}, f32[2,368,128]{2,1,0:T(8,128)S(1)}, u32[]{:S(2)}, u32[]{:S(2)}) collective-permute-start(f32[2,368,128]{2,1,0:T(8,128)S(1)} %pad_maximum_fusion.2), channel_id=1, source_target_pairs={{0,8},{1,9},{2,10},{3,11},{8,16},{9,17},{10,18},{11,19},{12,4},{13... | collective-permute-start | bytes 1130504 | tf_op jit(solution)/shard_map/ppermute | solution.py:357
  52.8 11.3 %collective-permute-start.8 = (f32[21,16,128]{2,1,0:T(8,128)S(1)}, f32[21,16,128]{2,1,0:T(8,128)S(1)}, u32[]{:S(2)}, u32[]{:S(2)}) collective-permute-start(f32[21,16,128]{2,1,0:T(8,128)S(1)} %get-tuple-element.44), channel_id=1, source_target_pairs={{0,4},{1,5},{2,6},{3,7},{4,0},{5,1},{6,2},{7,3},{8,12},{9,13},{10,... | collective-permute-start | bytes 516104 | tf_op jit(solution)/shard_map/ppermute | solution.py:347
  53.7 12.2 %collective-permute-start.9 = (f32[21,16,128]{2,1,0:T(8,128)S(1)}, f32[21,16,128]{2,1,0:T(8,128)S(1)}, u32[]{:S(2)}, u32[]{:S(2)}) collective-permute-start(f32[21,16,128]{2,1,0:T(8,128)S(1)} %get-tuple-element.45), channel_id=1, source_target_pairs={{0,5},{1,4},{2,7},{3,6},{4,1},{5,0},{6,3},{7,2},{8,13},{9,12},{10,... | collective-permute-start | bytes 516104 | tf_op jit(solution)/shard_map/ppermute | solution.py:347
  58.1 10.5 %collective-permute-start.10 = (f32[21,16,128]{2,1,0:T(8,128)S(1)}, f32[21,16,128]{2,1,0:T(8,128)S(1)}, u32[]{:S(2)}, u32[]{:S(2)}) collective-permute-start(f32[21,16,128]{2,1,0:T(8,128)S(1)} %get-tuple-element.46), channel_id=1, source_target_pairs={{0,6},{1,7},{2,4},{3,5},{4,2},{5,3},{6,0},{7,1},{8,14},{9,15},{10,... | collective-permute-start | bytes 516104 | tf_op jit(solution)/shard_map/ppermute | solution.py:347
  60.3 10.0 %collective-permute-start.11 = (f32[21,16,128]{2,1,0:T(8,128)S(1)}, f32[21,16,128]{2,1,0:T(8,128)S(1)}, u32[]{:S(2)}, u32[]{:S(2)}) collective-permute-start(f32[21,16,128]{2,1,0:T(8,128)S(1)} %get-tuple-element.47), channel_id=1, source_target_pairs={{0,7},{1,6},{2,5},{3,4},{4,3},{5,2},{6,1},{7,0},{8,15},{9,14},{10,... | collective-permute-start | bytes 516104 | tf_op jit(solution)/shard_map/ppermute | solution.py:347
  64.1 6.3 %collective-permute-start.14 = (f32[21,16,128]{2,1,0:T(8,128)S(1)}, f32[21,16,128]{2,1,0:T(8,128)S(1)}, u32[]{:S(2)}, u32[]{:S(2)}) collective-permute-start(f32[21,16,128]{2,1,0:T(8,128)S(1)} %get-tuple-element.52), channel_id=1, source_target_pairs={{0,1},{1,0},{2,3},{3,2},{4,5},{5,4},{6,7},{7,6},{8,9},{9,8},{10,11... | collective-permute-start | bytes 516104 | tf_op jit(solution)/shard_map/ppermute | solution.py:347
  64.2 10.8 %collective-permute-start.15 = (f32[21,16,128]{2,1,0:T(8,128)S(1)}, f32[21,16,128]{2,1,0:T(8,128)S(1)}, u32[]{:S(2)}, u32[]{:S(2)}) collective-permute-start(f32[21,16,128]{2,1,0:T(8,128)S(1)} %get-tuple-element.53), channel_id=1, source_target_pairs={{0,2},{1,3},{2,0},{3,1},{4,6},{5,7},{6,4},{7,5},{8,10},{9,11},{10,... | collective-permute-start | bytes 516104 | tf_op jit(solution)/shard_map/ppermute | solution.py:347
  65.9 12.6 %collective-permute-start.16 = (f32[21,16,128]{2,1,0:T(8,128)S(1)}, f32[21,16,128]{2,1,0:T(8,128)S(1)}, u32[]{:S(2)}, u32[]{:S(2)}) collective-permute-start(f32[21,16,128]{2,1,0:T(8,128)S(1)} %get-tuple-element.54), channel_id=1, source_target_pairs={{0,3},{1,2},{2,1},{3,0},{4,7},{5,6},{6,5},{7,4},{8,11},{9,10},{10,... | collective-permute-start | bytes 516104 | tf_op jit(solution)/shard_map/ppermute | solution.py:347

commit v6 on v5

v6 whole, which is shorter than its diff:
```python
import jax
import jax.numpy as jnp
from jax import lax
from jax.experimental import pallas as pl
from jax.experimental.pallas import tpu as pltpu
from jax.sharding import PartitionSpec as P

VMEM_LIMIT = 40 * 1024 * 1024
PACK_LIMIT = 60 * 1024 * 1024
PLANES = 2
ACTIVE = 49
MOST = 8
UNROLL = 7


class Layout:
    def __init__(self, quota, terms, modes, height, width):
        self.modes = modes
        self.group = PLANES * modes
        self.rows = height // self.group
        self.width = width
        self.terms = terms
        self.quota = quota
        self.slots = quota * modes
        self.share = -(-terms // modes)
        self.fields = quota + self.share
        self.main = self.fields * self.rows
        self.parts = self.fields + -(-2 * self.fields // self.rows)
        self.piece = self.parts * self.rows
        self.places = self.fields * modes

    def edge(self, i):
        return self.fields + 2 * i // self.rows, 2 * i % self.rows

    def place(self, block, i):
        if i < self.quota:
            return block * self.quota + i
        return self.slots + block * self.share + (i - self.quota)

    def term_place(self, term, mode):
        block = jnp.bitwise_xor(term // self.share, mode)
        return self.slots + block * self.share + term % self.share


def vmem(count):
    return [pl.BlockSpec(memory_space=pltpu.VMEM)] * count


def smem(count):
    return [pl.BlockSpec(memory_space=pltpu.SMEM)] * count


def pack(field, mean, kl, j, crossing, lay):
    kl_terms = kl.shape[0]
    rows, width, modes, quota = lay.rows, lay.width, lay.modes, lay.quota
    half = modes * rows
    tile = 8

    def kernel(j_ref, field_ref, mean_ref, kl_ref, *refs):
        out_refs, (stage_ref, past_ref, in_sems, out_sems) = refs[:modes], refs[modes:]
        plane = j_ref[0] // modes
        mode = j_ref[0] - plane * modes
        side = 1 - plane if crossing else plane
        start = side * half
        beside = pl.multiple_of(half - side * tile, tile)

        def load(n, begin=True):
            if n < modes:
                at, target = pl.ds(pl.multiple_of(start + n * rows, tile), rows), stage_ref.at[n]
            else:
                at, target = pl.ds(beside, tile), past_ref
            copies = [
                pltpu.make_async_copy(
                    field_ref.at[:, at, :], target.at[pl.ds(0, quota)], in_sems.at[n, 0]
                )
            ]
            if begin:
                copies[0].start()
            for i in range(lay.share):
                term = mode * lay.share + i
                into, sem = target.at[quota + i], in_sems.at[n, 1 + i]
                if not begin:
                    copies.append(pltpu.make_async_copy(mean_ref.at[0, at, :], into, sem))
                    continue

                @pl.when(term == 0)
                def _():
                    pltpu.make_async_copy(mean_ref.at[0, at, :], into, sem).start()

                @pl.when(term > 0)
                def _():
                    source = kl_ref.at[jnp.clip(term - 1, 0, kl_terms - 1), at, :]
                    pltpu.make_async_copy(source, into, sem).start()

            return copies

        for n in range(modes + 1):
            load(n)
        for n in range(modes + 1):
            for made in load(n, begin=False):
                made.wait()
        low_there = jnp.where(side == 0, 0.0, 1.0)
        high_there = jnp.where(side == PLANES - 1, 0.0, 1.0)
        for n in range(modes):
            for i in range(lay.fields):
                if n > 0:
                    low = stage_ref[n - 1, i, rows - 1 :]
                else:
                    low = past_ref[i, tile - 1 :] * low_there
                if n < modes - 1:
                    high = stage_ref[n + 1, i, :1]
                else:
                    high = past_ref[i, :1] * high_there
                part, line = lay.edge(i)
                stage_ref[n, part, line : line + 1] = low
                stage_ref[n, part, line + 1 : line + 2] = high
            part, line = lay.edge(lay.fields)
            if part < lay.parts:
                stage_ref[n, part, line:] = jnp.zeros((rows - line, width), jnp.float32)
        copies = []
        for n, out_ref in enumerate(out_refs):
            source = stage_ref.at[jnp.bitwise_xor(mode, n)]
            made = pltpu.make_async_copy(source, out_ref, out_sems.at[n])
            made.start()
            copies.append(made)
        for made in copies:
            made.wait()

    shape = (lay.parts, rows, width)
    sent = pl.pallas_call(
        kernel,
        out_shape=[jax.ShapeDtypeStruct(shape, jnp.float32)] * modes,
        in_specs=smem(1) + [pl.BlockSpec(memory_space=pltpu.HBM)] * 3,
        out_specs=[pl.BlockSpec(memory_space=pltpu.HBM)] * modes,
        scratch_shapes=[
            pltpu.VMEM((modes, *shape), jnp.float32),
            pltpu.VMEM((lay.fields, tile, width), jnp.float32),
            pltpu.SemaphoreType.DMA((modes + 1, 1 + lay.share)),
            pltpu.SemaphoreType.DMA((modes,)),
        ],
        compiler_params=pltpu.CompilerParams(vmem_limit_bytes=PACK_LIMIT),
        name="pack_crossing" if crossing else "pack_own",
    )(j, field, mean, kl)
    return [piece.reshape(lay.piece, width) for piece in sent]


def unpack(pieces, j, shape, lay):
    rows = lay.rows

    def kernel(j_ref, *refs):
        piece_refs, out_ref, sems = refs[:-2], refs[-2], refs[-1]
        copies = []
        for r, piece_ref in zip(pieces, piece_refs):
            start = pl.multiple_of(jnp.bitwise_xor(j_ref[0], r) * rows, 8)
            made = pltpu.make_async_copy(
                piece_ref, out_ref.at[:, pl.ds(start, rows), :], sems.at[r]
            )
            made.start()
            copies.append(made)
        for made in copies:
            made.wait()

    return pl.pallas_call(
        kernel,
        out_shape=jax.ShapeDtypeStruct(shape, jnp.float32),
        in_specs=smem(1) + vmem(lay.group),
        out_specs=pl.BlockSpec(memory_space=pltpu.HBM),
        scratch_shapes=[pltpu.SemaphoreType.DMA((lay.group,))],
        compiler_params=pltpu.CompilerParams(vmem_limit_bytes=VMEM_LIMIT),
        name="unpack",
    )(j, *pieces.values())


def coupling_lists(pattern, coupling, slot_mode):
    masked = (coupling * pattern.astype(jnp.float32))[1:]
    terms, modes = masked.shape[0], masked.shape[1]
    number = jnp.arange(modes, dtype=jnp.int32)
    one_hot = (slot_mode[:, None] == number[None, :]).astype(jnp.float32)
    coupled = jnp.einsum(
        "sa,kab,tb->kst", one_hot, masked, one_hot, precision=lax.Precision.HIGHEST
    )
    there = coupled != 0.0
    column = number[None, None, :]
    first = jnp.min(jnp.where(there, column, modes), 2)
    last = jnp.max(jnp.where(there, column, -1), 2)
    active = first < modes
    earlier = column < number[None, :, None]
    rank = jnp.sum(jnp.where(active[:, None, :] & earlier, 1, 0), 2)
    place = jnp.arange(ACTIVE, dtype=jnp.int32)[None, :, None]
    chosen = active[:, None, :] & (rank[:, None, :] == place)
    sources = jnp.sum(jnp.where(chosen, column, 0), 2)

    base = ACTIVE * jnp.arange(terms, dtype=jnp.int32)[:, None]
    products, factors, valid = [], [], []
    for chosen_t, is_valid in ((first, active), (last, last > first)):
        before = active[:, None, :] & (column < chosen_t[:, :, None])
        products.append(base + jnp.sum(jnp.where(before, 1, 0), 2))
        factors.append(jnp.sum(jnp.where(column == chosen_t[:, :, None], coupled, 0.0), 2))
        valid.append(is_valid)
    products = jnp.concatenate(products, 0)
    factors = jnp.concatenate(factors, 0)
    valid = jnp.concatenate(valid, 0)
    index = jnp.arange(2 * terms, dtype=jnp.int32)
    order = index[None, :] < index[:, None]
    rank = jnp.sum(jnp.where(valid[None] & order[:, :, None], 1, 0), 1)
    place = jnp.arange(MOST, dtype=jnp.int32)[:, None, None]
    chosen = valid[None] & (rank[None] == place)
    take = jnp.sum(jnp.where(chosen, products[None], 0), 1)
    factor = jnp.sum(jnp.where(chosen, factors[None], 0.0), 1)
    return sources.reshape(-1), take.T.reshape(-1), factor.T.reshape(-1)


def gather_products(s, take_ref, factor_ref, product_ref, total):
    for n in range(MOST):
        e = s * MOST + n
        total = total + factor_ref[e] * product_ref[take_ref[e]]
    return total


def stencil(pieces, others, halos, lists, j, name, lay):
    rows, width = lay.rows, lay.width
    full = (rows, width)

    def kernel(j_ref, source_ref, take_ref, factor_ref, *refs):
        piece_refs, refs = refs[: lay.modes], refs[lay.modes :]
        other_refs, refs = refs[: lay.modes], refs[lay.modes :]
        halo_refs, refs = refs[: len(halos)], refs[len(halos) :]
        out_refs, (near_ref, product_ref) = refs[: lay.modes], refs[lay.modes :]
        lane = lax.broadcasted_iota(jnp.int32, full, 1)
        line = lax.broadcasted_iota(jnp.int32, full, 0)
        mode = lax.rem(j_ref[0], lay.modes)
        halo_parts = [(ref, n) for ref in halo_refs for n in range(ref.shape[0])]

        for block in range(lay.modes):

            def spread(i, at, block=block):
                piece_ref = piece_refs[block]
                halo_ref, n = halo_parts[block]
                here = piece_ref[pl.ds(i * rows, rows), :]
                low = piece_ref[pl.ds(lay.main + 2 * i, 1), :]
                high = piece_ref[pl.ds(lay.main + 2 * i + 1, 1), :]
                near_ref[at, 0] = here
                near_ref[at, 1] = pltpu.roll(here, width - 1, 1)
                near_ref[at, 2] = pltpu.roll(here, 1, 1)
                near_ref[at, 3] = jnp.where(line == rows - 1, high, pltpu.roll(here, rows - 1, 0))
                near_ref[at, 4] = jnp.where(line == 0, low, pltpu.roll(here, 1, 0))
                near_ref[at, 5] = other_refs[block][pl.ds(i * rows, rows), :]
                near_ref[at, 6] = halo_ref[n, pl.ds(i * rows, rows), :]

            def spread_slot(i, carry, spread=spread, block=block):
                spread(i, block * lay.quota + i)
                return carry

            lax.fori_loop(0, lay.quota, spread_slot, 0, unroll=UNROLL)
            for i in range(lay.quota, lay.fields):
                spread(i, lay.place(block, i))

        def operator_of(term):
            at = lay.term_place(term, mode)
            here, right, left, *rest = [near_ref[at, n] for n in range(7)]
            right = jnp.where(lane == width - 1, 0.0, right)
            left = jnp.where(lane == 0, 0.0, left)
            faces = [0.5 * (here + n) for n in (right, left, *rest)]
            diagonal = faces[0] + faces[1] + faces[2] + faces[3] + faces[4] + faces[5]
            faces[0] = jnp.where(lane == width - 1, 0.0, faces[0])
            faces[1] = jnp.where(lane == 0, 0.0, faces[1])

            def operator(t):
                total = diagonal * near_ref[t, 0]
                for n, face in enumerate(faces):
                    total = total - face * near_ref[t, n + 1]
                return total

            return operator

        for term in range(1, lay.terms):
            operator = operator_of(term)

            def apply(n, carry, operator=operator, term=term):
                e = (term - 1) * ACTIVE + n
                product_ref[e] = operator(source_ref[e])
                return carry

            lax.fori_loop(0, ACTIVE, apply, 0, unroll=UNROLL)

        operator = operator_of(0)
        for block in range(lay.modes):

            def collect(i, carry, out_ref=out_refs[block], block=block):
                s = block * lay.quota + i
                out_ref[i] = gather_products(s, take_ref, factor_ref, product_ref, operator(s))
                return carry

            lax.fori_loop(0, lay.quota, collect, 0, unroll=UNROLL)

    return pl.pallas_call(
        kernel,
        out_shape=[jax.ShapeDtypeStruct((lay.quota, rows, width), jnp.float32)] * lay.modes,
        in_specs=smem(4) + vmem(2 * lay.modes + len(halos)),
        out_specs=vmem(lay.modes),
        scratch_shapes=[
            pltpu.VMEM((lay.places, 7, rows, width), jnp.float32),
            pltpu.VMEM(((lay.terms - 1) * ACTIVE, rows, width), jnp.float32),
        ],
        compiler_params=pltpu.CompilerParams(vmem_limit_bytes=VMEM_LIMIT),
        name=name,
    )(j, *lists, *pieces, *others, *halos)


def after(value, *done):
    return lax.optimization_barrier((value, *done))[0]


def on_device(chaos_field, mean_field, kl_fields, pattern, coupling, slot_mode):
    spaces, modes = lax.axis_size("space"), lax.axis_size("mode")
    quota, _, height, width = chaos_field.shape
    terms = kl_fields.shape[0] + 1
    lay = Layout(quota, terms, modes, height, width)
    axes = ("space", "mode")
    devices = spaces * modes
    space = lax.axis_index("space").astype(jnp.int32)
    mode = lax.axis_index("mode").astype(jnp.int32)
    j = (lax.rem(space, PLANES) * modes + mode).reshape(1)

    def swap(piece, r):
        if r == 0:
            return piece
        return lax.ppermute(piece, axes, [(d, d ^ r) for d in range(devices)])

    def shift(pieces, crossing):
        pairs = []
        for d in range(devices):
            upper = (d // modes) % PLANES == (0 if crossing else 1)
            other = d + lay.group if upper else d - lay.group
            if 0 <= other < devices:
                pairs.append((d, other))
        main = jnp.stack([piece[: lay.main] for piece in pieces])
        return lax.ppermute(main, axes, pairs)

    field, kl = chaos_field[:, 0], kl_fields[:, 0]
    sent = [None] * lay.group
    sent[:modes] = pack(field, mean_field, kl, j, False, lay)
    sent[modes:] = pack(field, mean_field, kl, after(j, *sent[:modes]), True, lay)
    half = modes // 2
    pieces = sent[:1] + [None] * (lay.group - 1)
    for r in [*range(half, modes), *range(1, half), *range(modes, modes + half)]:
        pieces[r] = swap(sent[r], r)
    for r in range(modes + half, lay.group):
        pieces[r] = swap(after(sent[r], *pieces[half:modes]), r)
    number = jnp.arange(modes, dtype=jnp.int32)
    mine = jnp.bitwise_xor(number, mode)[:, None, None] == number[None, :, None]
    slot_mode = jnp.sum(jnp.where(mine, slot_mode.reshape(1, modes, quota), 0), 1).reshape(-1)
    lists = coupling_lists(pattern, coupling, slot_mode)
    pieces[half] = after(pieces[half], *lists)
    own_halo = shift(pieces[:modes], False)
    halos = [shift(pieces[r : r + half], True) for r in (modes, modes + half)]

    own, crossing = pieces[:modes], pieces[modes:]
    crossing_out = stencil(crossing, own, [own_halo], lists, j, "stencil_crossing", lay)
    own_j = after(j, *crossing_out)
    own_out = stencil(own, crossing, halos, lists, own_j, "stencil_own", lay)
    back = {}
    for n in [*range(half, modes), *range(half)]:
        back[modes + n] = swap(crossing_out[n], modes + n)
    for n in [*range(half, modes), *range(half)]:
        back[n] = swap(own_out[n], n)
    return unpack(back, j, (quota, height, width), lay).reshape(chaos_field.shape)


def solution(mesh):
    in_specs = (
        P("mode", "space", None, None),
        P("space", None, None),
        P(None, "space", None, None),
        P(),
        P(),
        P(),
    )
    out_specs = P("mode", "space", None, None)
    return jax.shard_map(
        on_device, mesh=mesh, in_specs=in_specs, out_specs=out_specs, check_vma=False
    )
```

time: 79.9 us -> 60.6 us (0.76)
  waiting for transfers between devices: 32.4 us -> 16.2 us
  Pallas kernels: 19.6 us -> 14.8 us
  starting transfers between devices: 24.3 us -> 25.9 us
    ppermute x14, waiting for transfers between devices: 25 us -> 14.4 us  [swap(): return lax.ppermute(piece, axes, [(d, d ^ r) for d in range(devices)])]
    ppermute x3, waiting for transfers between devices: 7.37 us -> 1.82 us  [shift(): return lax.ppermute(main, axes, pairs)]
    pallas_call x6 -> x4, Pallas kernels: 18.4 us -> 13.7 us  [the longest x2 8.77 us: stencil(): pl.pallas_call(kernel, out_shape=[jax.ShapeDtypeStruct((lay.quota, rows,...]
    ppermute x14, starting transfers between devices: 15 us -> 17.7 us  [swap(): return lax.ppermute(piece, axes, [(d, d ^ r) for d in range(devices)])]
    ppermute x3, starting transfers between devices: 9.33 us -> 8.21 us  [shift(): return lax.ppermute(main, axes, pairs)]
  transfers between devices with their start and end apart: 17 -> 17, of which waited for: 7 -> 7; matrix products, arithmetic and copies ran while one was open for 4% -> 5% of each run, Pallas kernels for 20% -> 19%
where the time goes in v6:
time: 60.6 us; the launch traced here: 60.2 us
  starting transfers between devices  25.9 us (43%)
  waiting for transfers between devices  16.2 us (27%)
  Pallas kernels  14.8 us (24%)
  other arithmetic  1.19 us (2%)
  local copies, waits for them, and re-layouts  1.15 us (2%)
  matrix products  0.69 us (1%)
    ppermute x14, starting transfers between devices, swap(): return lax.ppermute(piece, axes, [(d, d ^ r) for d in range(devices)])  17.7 us
    ppermute x14, waiting for transfers between devices, swap(): return lax.ppermute(piece, axes, [(d, d ^ r) for d in range(devices)])  14.4 us
    pallas_call x2, Pallas kernels, stencil(): pl.pallas_call(kernel, out_shape=[jax.ShapeDtypeStruct((lay.quota, rows,...  8.77 us
    ppermute x3, starting transfers between devices, shift(): return lax.ppermute(main, axes, pairs)  8.21 us
    pallas_call x2, Pallas kernels, pack(): pl.pallas_call(kernel, out_shape=[jax.ShapeDtypeStruct(shape, jnp.float32...  4.9 us
    ppermute x3, waiting for transfers between devices, shift(): return lax.ppermute(main, axes, pairs)  1.82 us
  transfers between devices with their start and end apart: 17, of which 7 were waited for; matrix products, arithmetic and copies ran while one was open for 5% of the time, Pallas kernels for 19%

profile of v6, /device:TPU:0, one launch (start us, length us, event | category | flops | bytes accessed | tf_op | source)
XLA Modules:
  0.0 60.2 jit_solution(5462510895711035193)
XLA Ops:
  0.0 2.5 %pack_own.1 = (f32[26,16,128]{2,1,0:T(8,128)}, f32[26,16,128]{2,1,0:T(8,128)}, f32[26,16,128]{2,1,0:T(8,128)}, f32[26,16,128]{2,1,0:T(8,128)}) custom-call(s32[1]{0:T(128)} %bitcast.j_ref, f32[21,128,128]{2,1,0:T(8,128)} %bitcast.40, f32[1,128,128]{2,1,0:T(8,128)} %mean_ref.3, f32[6,128,128]{2,1,0:T(8,128)} %bitcast.42), custom_call_target="tpu_custom_call" | custom-call | tf_op jit(solution)/shard_map/pack_own/pallas_call | solution.py:130
  2.5 0.0 copy-start
  2.5 0.0 copy-start.3
  2.5 0.0 copy-start.1
  2.5 3.0 %collective-permute-start.2 = (f32[416,128]{1,0:T(8,128)}, f32[416,128]{1,0:T(8,128)S(1)}, u32[]{:S(2)}, u32[]{:S(2)}) collective-permute-start(f32[416,128]{1,0:T(8,128)} %bitcast.53), channel_id=1, source_target_pairs={{0,2},{1,3},{2,0},{3,1},{4,6},{5,7},{6,4},{7,5},{8,10},{9,11},{10,... | collective-permute-start | bytes 638984 | tf_op jit(solution)/shard_map/ppermute | solution.py:328
  5.5 0.0 collective-permute-start.6
  5.5 0.2 collective-permute-start.3
  5.7 2.4 %pack_crossing.1 = (f32[26,16,128]{2,1,0:T(8,128)}, f32[26,16,128]{2,1,0:T(8,128)}, f32[26,16,128]{2,1,0:T(8,128)}, f32[26,16,128]{2,1,0:T(8,128)}) custom-call(s32[1]{0:T(128)} %bitcast.j_ref, f32[21,128,128]{2,1,0:T(8,128)} %bitcast.41, f32[1,128,128]{2,1,0:T(8,128)} %mean_ref.3, f32[6,128,128]{2,1,0:T(8,128)} %bitcast.43), custom_call_target="tpu_custom_call" | custom-call | tf_op jit(solution)/shard_map/pack_crossing/pallas_call | solution.py:130
  8.2 1.6 %collective-permute-start.1 = (f32[416,128]{1,0:T(8,128)}, f32[416,128]{1,0:T(8,128)S(1)}, u32[]{:S(2)}, u32[]{:S(2)}) collective-permute-start(f32[416,128]{1,0:T(8,128)} %bitcast.50), channel_id=1, source_target_pairs={{0,5},{1,4},{2,7},{3,6},{4,1},{5,0},{6,3},{7,2},{8,13},{9,12},{10,... | collective-permute-start | bytes 638984 | tf_op jit(solution)/shard_map/ppermute | solution.py:328
  9.8 0.5 collective-permute-start
  10.3 0.1 iota_compare_fusion.9
  10.4 0.0 copy-done.3
  10.4 0.1 broadcast_in_dim.135
  10.5 0.1 select_reduce_fusion.9
  10.6 0.1 eq.38
  10.6 0.2 copy.9
  10.8 0.0 copy-done.2
  10.8 0.2 copy.10
  11.0 0.4 fusion
  11.4 0.3 fusion.10
  11.7 0.1 fusion.6
  11.9 0.1 select_reduce_fusion.1
  12.0 0.2 select_reduce_fusion.3
  12.2 0.2 select_reduce_fusion.5
  12.4 0.1 reshape.111.source_ref
  12.5 0.1 select_reduce_fusion.6
  12.7 0.1 copy.12
  12.8 0.1 reshape.113.factor_ref
  12.9 0.1 broadcast_add_fusion.1
  13.0 0.1 copy.11
  13.1 0.1 reshape.112.take_ref
  13.2 0.0 collective-permute-done.2.refs_6_.refs_2_
  13.2 0.0 collective-permute-done.6.refs_5_.refs_1_
  13.2 1.7 %collective-permute-done.3.refs_7_.refs_3_ = f32[416,128]{1,0:T(8,128)S(1)} collective-permute-done((f32[416,128]{1,0:T(8,128)}, f32[416,128]{1,0:T(8,128)S(1)}, u32[]{:S(2)}, u32[]{:S(2)}) %collective-permute-start.3) | collective-permute-done | bytes 213024 | tf_op jit(solution)/shard_map/ppermute | solution.py:328
  14.9 0.1 pad_maximum_fusion
  15.0 1.3 %collective-permute-start.7 = (f32[4,368,128]{2,1,0:T(8,128)S(1)}, f32[4,368,128]{2,1,0:T(8,128)S(1)}, u32[]{:S(2)}, u32[]{:S(2)}) collective-permute-start(f32[4,368,128]{2,1,0:T(8,128)S(1)} %pad_maximum_fusion), channel_id=1, source_target_pairs={{4,12},{5,13},{6,14},{7,15},{8,0},{9,1},{10,2},{11,3},{12,20},{13,... | collective-permute-start | bytes 2261000 | tf_op jit(solution)/shard_map/ppermute | solution.py:338
  16.3 5.0 %collective-permute-start.5 = (f32[416,128]{1,0:T(8,128)S(1)}, f32[416,128]{1,0:T(8,128)S(1)}, u32[]{:S(2)}, u32[]{:S(2)}) collective-permute-start(f32[416,128]{1,0:T(8,128)S(1)} %bitcast.48), channel_id=1, source_target_pairs={{0,7},{1,6},{2,5},{3,4},{4,3},{5,2},{6,1},{7,0},{8,15},{9,14},{10,... | collective-permute-start | bytes 638984 | tf_op jit(solution)/shard_map/ppermute | solution.py:328
  21.4 0.0 collective-permute-start.4
  21.4 0.0 collective-permute-done.1.refs_1_.refs_5_
  21.4 0.0 collective-permute-done.refs_0_.refs_4_
  21.5 3.5 %collective-permute-start.12 = (f32[2,368,128]{2,1,0:T(8,128)S(1)}, f32[2,368,128]{2,1,0:T(8,128)S(1)}, u32[]{:S(2)}, u32[]{:S(2)}) collective-permute-start(f32[2,368,128]{2,1,0:T(8,128)S(1)} %pad_maximum_fusion.1), channel_id=1, source_target_pairs={{0,8},{1,9},{2,10},{3,11},{8,16},{9,17},{10,18},{11,19},{12,4},{13... | collective-permute-start | bytes 1130504 | tf_op jit(solution)/shard_map/ppermute | solution.py:338
  24.9 2.2 %collective-permute-done.5.refs_3_.refs_7_ = f32[416,128]{1,0:T(8,128)S(1)} collective-permute-done((f32[416,128]{1,0:T(8,128)S(1)}, f32[416,128]{1,0:T(8,128)S(1)}, u32[]{:S(2)}, u32[]{:S(2)}) %collective-permute-start.5) | collective-permute-done | bytes 213024 | tf_op jit(solution)/shard_map/ppermute | solution.py:328
  27.2 3.9 %collective-permute-done.4.refs_2_.refs_6_ = f32[416,128]{1,0:T(8,128)S(1)} collective-permute-done((f32[416,128]{1,0:T(8,128)S(1)}, f32[416,128]{1,0:T(8,128)S(1)}, u32[]{:S(2)}, u32[]{:S(2)}) %collective-permute-start.4) | collective-permute-done | bytes 213024 | tf_op jit(solution)/shard_map/ppermute | solution.py:328
  31.2 3.5 %collective-permute-start.13 = (f32[2,368,128]{2,1,0:T(8,128)S(1)}, f32[2,368,128]{2,1,0:T(8,128)S(1)}, u32[]{:S(2)}, u32[]{:S(2)}) collective-permute-start(f32[2,368,128]{2,1,0:T(8,128)S(1)} %pad_maximum_fusion.2), channel_id=1, source_target_pairs={{0,8},{1,9},{2,10},{3,11},{8,16},{9,17},{10,18},{11,19},{12,4},{13... | collective-permute-start | bytes 1130504 | tf_op jit(solution)/shard_map/ppermute | solution.py:338
  34.6 1.8 %collective-permute-done.7.refs_8_ = f32[4,368,128]{2,1,0:T(8,128)S(1)} collective-permute-done((f32[4,368,128]{2,1,0:T(8,128)S(1)}, f32[4,368,128]{2,1,0:T(8,128)S(1)}, u32[]{:S(2)}, u32[]{:S(2)}) %collective-permute-start.7) | collective-permute-done | bytes 753696 | tf_op jit(solution)/shard_map/ppermute | solution.py:338
  36.5 4.4 %stencil_crossing.1 = (f32[21,16,128]{2,1,0:T(8,128)S(1)}, f32[21,16,128]{2,1,0:T(8,128)S(1)}, f32[21,16,128]{2,1,0:T(8,128)S(1)}, f32[21,16,128]{2,1,0:T(8,128)S(1)}) custom-call(s32[1]{0:T(128)} %bitcast.j_ref, s32[294]{0:T(512)S(1)} %reshape.111.source_ref, s32[672]{0:T(1024)S(1)} %reshape.112.take_ref, f32[672]{0:T(1024)S(1)} %reshape.113.factor_ref, ...), custom_call_target="tpu_custom_call" | custom-call | tf_op jit(solution)/shard_map/stencil_crossing/pallas_call | solution.py:296
  40.8 1.1 %collective-permute-start.8 = (f32[21,16,128]{2,1,0:T(8,128)S(1)}, f32[21,16,128]{2,1,0:T(8,128)S(1)}, u32[]{:S(2)}, u32[]{:S(2)}) collective-permute-start(f32[21,16,128]{2,1,0:T(8,128)S(1)} %get-tuple-element.38), channel_id=1, source_target_pairs={{0,6},{1,7},{2,4},{3,5},{4,2},{5,3},{6,0},{7,1},{8,14},{9,15},{10,... | collective-permute-start | bytes 516104 | tf_op jit(solution)/shard_map/ppermute | solution.py:328
  42.0 1.1 %collective-permute-start.9 = (f32[21,16,128]{2,1,0:T(8,128)S(1)}, f32[21,16,128]{2,1,0:T(8,128)S(1)}, u32[]{:S(2)}, u32[]{:S(2)}) collective-permute-start(f32[21,16,128]{2,1,0:T(8,128)S(1)} %get-tuple-element.39), channel_id=1, source_target_pairs={{0,7},{1,6},{2,5},{3,4},{4,3},{5,2},{6,1},{7,0},{8,15},{9,14},{10,... | collective-permute-start | bytes 516104 | tf_op jit(solution)/shard_map/ppermute | solution.py:328
  43.1 0.9 %collective-permute-start.10 = (f32[21,16,128]{2,1,0:T(8,128)S(1)}, f32[21,16,128]{2,1,0:T(8,128)S(1)}, u32[]{:S(2)}, u32[]{:S(2)}) collective-permute-start(f32[21,16,128]{2,1,0:T(8,128)S(1)} %get-tuple-element.40), channel_id=1, source_target_pairs={{0,4},{1,5},{2,6},{3,7},{4,0},{5,1},{6,2},{7,3},{8,12},{9,13},{10,... | collective-permute-start | bytes 516104 | tf_op jit(solution)/shard_map/ppermute | solution.py:328
  44.0 0.0 collective-permute-done.12.refs_8_
  44.0 1.3 %collective-permute-start.11 = (f32[21,16,128]{2,1,0:T(8,128)S(1)}, f32[21,16,128]{2,1,0:T(8,128)S(1)}, u32[]{:S(2)}, u32[]{:S(2)}) collective-permute-start(f32[21,16,128]{2,1,0:T(8,128)S(1)} %get-tuple-element.41), channel_id=1, source_target_pairs={{0,5},{1,4},{2,7},{3,6},{4,1},{5,0},{6,3},{7,2},{8,13},{9,12},{10,... | collective-permute-start | bytes 516104 | tf_op jit(solution)/shard_map/ppermute | solution.py:328
  45.3 0.0 collective-permute-done.13.refs_9_
  45.3 4.4 %stencil_own.1 = (f32[21,16,128]{2,1,0:T(8,128)S(1)}, f32[21,16,128]{2,1,0:T(8,128)S(1)}, f32[21,16,128]{2,1,0:T(8,128)S(1)}, f32[21,16,128]{2,1,0:T(8,128)S(1)}) custom-call(s32[1]{0:T(128)} %bitcast.j_ref, s32[294]{0:T(512)S(1)} %reshape.111.source_ref, s32[672]{0:T(1024)S(1)} %reshape.112.take_ref, f32[672]{0:T(1024)S(1)} %reshape.113.factor_ref, ...), custom_call_target="tpu_custom_call" | custom-call | tf_op jit(solution)/shard_map/stencil_own/pallas_call | solution.py:296
  49.7 1.1 %collective-permute-start.14 = (f32[21,16,128]{2,1,0:T(8,128)S(1)}, f32[21,16,128]{2,1,0:T(8,128)S(1)}, u32[]{:S(2)}, u32[]{:S(2)}) collective-permute-start(f32[21,16,128]{2,1,0:T(8,128)S(1)} %get-tuple-element.43), channel_id=1, source_target_pairs={{0,2},{1,3},{2,0},{3,1},{4,6},{5,7},{6,4},{7,5},{8,10},{9,11},{10,... | collective-permute-start | bytes 516104 | tf_op jit(solution)/shard_map/ppermute | solution.py:328
  50.8 0.0 collective-permute-done.8.refs_0_
  50.8 0.2 collective-permute-start.15
  51.1 0.0 collective-permute-done.9.refs_1_
  51.1 1.5 %collective-permute-start.16 = (f32[21,16,128]{2,1,0:T(8,128)S(1)}, f32[21,16,128]{2,1,0:T(8,128)S(1)}, u32[]{:S(2)}, u32[]{:S(2)}) collective-permute-start(f32[21,16,128]{2,1,0:T(8,128)S(1)} %get-tuple-element.46), channel_id=1, source_target_pairs={{0,1},{1,0},{2,3},{3,2},{4,5},{5,4},{6,7},{7,6},{8,9},{9,8},{10,11... | collective-permute-start | bytes 516104 | tf_op jit(solution)/shard_map/ppermute | solution.py:328
  52.6 3.4 %collective-permute-done.10.refs_2_ = f32[21,16,128]{2,1,0:T(8,128)S(1)} collective-permute-done((f32[21,16,128]{2,1,0:T(8,128)S(1)}, f32[21,16,128]{2,1,0:T(8,128)S(1)}, u32[]{:S(2)}, u32[]{:S(2)}) %collective-permute-start.10) | collective-permute-done | bytes 172064 | tf_op jit(solution)/shard_map/ppermute | solution.py:328
  56.0 2.1 %collective-permute-done.11.refs_3_ = f32[21,16,128]{2,1,0:T(8,128)S(1)} collective-permute-done((f32[21,16,128]{2,1,0:T(8,128)S(1)}, f32[21,16,128]{2,1,0:T(8,128)S(1)}, u32[]{:S(2)}, u32[]{:S(2)}) %collective-permute-start.11) | collective-permute-done | bytes 172064 | tf_op jit(solution)/shard_map/ppermute | solution.py:328
  58.1 0.0 collective-permute-done.14.refs_4_
  58.1 1.0 %collective-permute-done.15.refs_5_ = f32[21,16,128]{2,1,0:T(8,128)S(1)} collective-permute-done((f32[21,16,128]{2,1,0:T(8,128)S(1)}, f32[21,16,128]{2,1,0:T(8,128)S(1)}, u32[]{:S(2)}, u32[]{:S(2)}) %collective-permute-start.15) | collective-permute-done | bytes 172064 | tf_op jit(solution)/shard_map/ppermute | solution.py:328
  59.1 0.0 collective-permute-done.16.refs_7_
  59.1 1.1 %unpack.1 = f32[21,128,128]{2,1,0:T(8,128)} custom-call(s32[1]{0:T(128)} %bitcast.j_ref, f32[21,16,128]{2,1,0:T(8,128)S(1)} %collective-permute-done.8.refs_0_, f32[21,16,128]{2,1,0:T(8,128)S(1)} %collective-permute-done.9.refs_1_, f32[21,16,128]{2,1,0:T(8,128)S(1)} %collective-permute-done.10.refs_2_, f32[21,16,128]{2,1,0:T(8,128)S(1)} %collective-permute-done.11.refs_3_, ...), custom_call_target="tpu_custom_call" | custom-call | tf_op jit(solution)/shard_map/unpack/pallas_call | solution.py:163
  (27 shorter events, 0.3 us)
Async XLA Ops:
  2.5 7.8 %copy-start = (f32[26,16,128]{2,1,0:T(8,128)S(1)}, f32[26,16,128]{2,1,0:T(8,128)}, u32[]{:S(2)}) copy-start(f32[26,16,128]{2,1,0:T(8,128)} %get-tuple-element.26) | copy-start | bytes 638980
  2.5 7.9 %copy-start.3 = (s32[84]{0:T(128)S(1)}, s32[84]{0:T(128)}, u32[]{:S(2)}) copy-start(s32[84]{0:T(128)} %param.11) | copy-start | bytes 1012
  2.5 8.2 %copy-start.1 = (s32[7,84,84]{2,1,0:T(8,128)S(1)}, s32[7,84,84]{2,1,0:T(8,128)}, u32[]{:S(2)}) copy-start(s32[7,84,84]{2,1,0:T(8,128)} %param.9) | copy-start | bytes 592708
  2.5 10.7 %collective-permute-start.2 = (f32[416,128]{1,0:T(8,128)}, f32[416,128]{1,0:T(8,128)S(1)}, u32[]{:S(2)}, u32[]{:S(2)}) collective-permute-start(f32[416,128]{1,0:T(8,128)} %bitcast.53), channel_id=1, source_target_pairs={{0,2},{1,3},{2,0},{3,1},{4,6},{5,7},{6,4},{7,5},{8,10},{9,11},{10,... | collective-permute-start | bytes 638984 | tf_op jit(solution)/shard_map/ppermute | solution.py:328
  5.5 7.7 %collective-permute-start.6 = (f32[416,128]{1,0:T(8,128)}, f32[416,128]{1,0:T(8,128)S(1)}, u32[]{:S(2)}, u32[]{:S(2)}) collective-permute-start(f32[416,128]{1,0:T(8,128)} %bitcast.52), channel_id=1, source_target_pairs={{0,1},{1,0},{2,3},{3,2},{4,5},{5,4},{6,7},{7,6},{8,9},{9,8},{10,11... | collective-permute-start | bytes 638984 | tf_op jit(solution)/shard_map/ppermute | solution.py:328
  5.5 9.4 %collective-permute-start.3 = (f32[416,128]{1,0:T(8,128)}, f32[416,128]{1,0:T(8,128)S(1)}, u32[]{:S(2)}, u32[]{:S(2)}) collective-permute-start(f32[416,128]{1,0:T(8,128)} %bitcast.51), channel_id=1, source_target_pairs={{0,3},{1,2},{2,1},{3,0},{4,7},{5,6},{6,5},{7,4},{8,11},{9,10},{10,... | collective-permute-start | bytes 638984 | tf_op jit(solution)/shard_map/ppermute | solution.py:328
  5.7 5.1 %copy-start.2 = (f32[7,84,84]{2,1,0:T(8,128)S(1)}, f32[7,84,84]{2,1,0:T(8,128)}, u32[]{:S(2)}) copy-start(f32[7,84,84]{2,1,0:T(8,128)} %param.10) | copy-start | bytes 592708
  8.2 13.2 %collective-permute-start.1 = (f32[416,128]{1,0:T(8,128)}, f32[416,128]{1,0:T(8,128)S(1)}, u32[]{:S(2)}, u32[]{:S(2)}) collective-permute-start(f32[416,128]{1,0:T(8,128)} %bitcast.50), channel_id=1, source_target_pairs={{0,5},{1,4},{2,7},{3,6},{4,1},{5,0},{6,3},{7,2},{8,13},{9,12},{10,... | collective-permute-start | bytes 638984 | tf_op jit(solution)/shard_map/ppermute | solution.py:328
  9.8 11.6 %collective-permute-start = (f32[416,128]{1,0:T(8,128)}, f32[416,128]{1,0:T(8,128)S(1)}, u32[]{:S(2)}, u32[]{:S(2)}) collective-permute-start(f32[416,128]{1,0:T(8,128)} %bitcast.49), channel_id=1, source_target_pairs={{0,4},{1,5},{2,6},{3,7},{4,0},{5,1},{6,2},{7,3},{8,12},{9,13},{10,... | collective-permute-start | bytes 638984 | tf_op jit(solution)/shard_map/ppermute | solution.py:328
  13.0 3.3 %copy-start.5 = (f32[26,16,128]{2,1,0:T(8,128)S(1)}, f32[26,16,128]{2,1,0:T(8,128)}, u32[]{:S(2)}) copy-start(f32[26,16,128]{2,1,0:T(8,128)} %get-tuple-element.35) | copy-start | bytes 638980
  13.0 8.4 %copy-start.4 = (f32[26,16,128]{2,1,0:T(8,128)S(1)}, f32[26,16,128]{2,1,0:T(8,128)}, u32[]{:S(2)}) copy-start(f32[26,16,128]{2,1,0:T(8,128)} %get-tuple-element.33) | copy-start | bytes 638980
  15.0 21.5 %collective-permute-start.7 = (f32[4,368,128]{2,1,0:T(8,128)S(1)}, f32[4,368,128]{2,1,0:T(8,128)S(1)}, u32[]{:S(2)}, u32[]{:S(2)}) collective-permute-start(f32[4,368,128]{2,1,0:T(8,128)S(1)} %pad_maximum_fusion), channel_id=1, source_target_pairs={{4,12},{5,13},{6,14},{7,15},{8,0},{9,1},{10,2},{11,3},{12,20},{13,... | collective-permute-start | bytes 2261000 | tf_op jit(solution)/shard_map/ppermute | solution.py:338
  16.3 10.9 %collective-permute-start.5 = (f32[416,128]{1,0:T(8,128)S(1)}, f32[416,128]{1,0:T(8,128)S(1)}, u32[]{:S(2)}, u32[]{:S(2)}) collective-permute-start(f32[416,128]{1,0:T(8,128)S(1)} %bitcast.48), channel_id=1, source_target_pairs={{0,7},{1,6},{2,5},{3,4},{4,3},{5,2},{6,1},{7,0},{8,15},{9,14},{10,... | collective-permute-start | bytes 638984 | tf_op jit(solution)/shard_map/ppermute | solution.py:328
  21.4 9.8 %collective-permute-start.4 = (f32[416,128]{1,0:T(8,128)S(1)}, f32[416,128]{1,0:T(8,128)S(1)}, u32[]{:S(2)}, u32[]{:S(2)}) collective-permute-start(f32[416,128]{1,0:T(8,128)S(1)} %bitcast.47), channel_id=1, source_target_pairs={{0,6},{1,7},{2,4},{3,5},{4,2},{5,3},{6,0},{7,1},{8,14},{9,15},{10,... | collective-permute-start | bytes 638984 | tf_op jit(solution)/shard_map/ppermute | solution.py:328
  21.5 22.6 %collective-permute-start.12 = (f32[2,368,128]{2,1,0:T(8,128)S(1)}, f32[2,368,128]{2,1,0:T(8,128)S(1)}, u32[]{:S(2)}, u32[]{:S(2)}) collective-permute-start(f32[2,368,128]{2,1,0:T(8,128)S(1)} %pad_maximum_fusion.1), channel_id=1, source_target_pairs={{0,8},{1,9},{2,10},{3,11},{8,16},{9,17},{10,18},{11,19},{12,4},{13... | collective-permute-start | bytes 1130504 | tf_op jit(solution)/shard_map/ppermute | solution.py:338
  31.2 14.1 %collective-permute-start.13 = (f32[2,368,128]{2,1,0:T(8,128)S(1)}, f32[2,368,128]{2,1,0:T(8,128)S(1)}, u32[]{:S(2)}, u32[]{:S(2)}) collective-permute-start(f32[2,368,128]{2,1,0:T(8,128)S(1)} %pad_maximum_fusion.2), channel_id=1, source_target_pairs={{0,8},{1,9},{2,10},{3,11},{8,16},{9,17},{10,18},{11,19},{12,4},{13... | collective-permute-start | bytes 1130504 | tf_op jit(solution)/shard_map/ppermute | solution.py:338
  40.8 10.0 %collective-permute-start.8 = (f32[21,16,128]{2,1,0:T(8,128)S(1)}, f32[21,16,128]{2,1,0:T(8,128)S(1)}, u32[]{:S(2)}, u32[]{:S(2)}) collective-permute-start(f32[21,16,128]{2,1,0:T(8,128)S(1)} %get-tuple-element.38), channel_id=1, source_target_pairs={{0,6},{1,7},{2,4},{3,5},{4,2},{5,3},{6,0},{7,1},{8,14},{9,15},{10,... | collective-permute-start | bytes 516104 | tf_op jit(solution)/shard_map/ppermute | solution.py:328
  42.0 9.1 %collective-permute-start.9 = (f32[21,16,128]{2,1,0:T(8,128)S(1)}, f32[21,16,128]{2,1,0:T(8,128)S(1)}, u32[]{:S(2)}, u32[]{:S(2)}) collective-permute-start(f32[21,16,128]{2,1,0:T(8,128)S(1)} %get-tuple-element.39), channel_id=1, source_target_pairs={{0,7},{1,6},{2,5},{3,4},{4,3},{5,2},{6,1},{7,0},{8,15},{9,14},{10,... | collective-permute-start | bytes 516104 | tf_op jit(solution)/shard_map/ppermute | solution.py:328
  43.1 12.9 %collective-permute-start.10 = (f32[21,16,128]{2,1,0:T(8,128)S(1)}, f32[21,16,128]{2,1,0:T(8,128)S(1)}, u32[]{:S(2)}, u32[]{:S(2)}) collective-permute-start(f32[21,16,128]{2,1,0:T(8,128)S(1)} %get-tuple-element.40), channel_id=1, source_target_pairs={{0,4},{1,5},{2,6},{3,7},{4,0},{5,1},{6,2},{7,3},{8,12},{9,13},{10,... | collective-permute-start | bytes 516104 | tf_op jit(solution)/shard_map/ppermute | solution.py:328
  44.0 14.0 %collective-permute-start.11 = (f32[21,16,128]{2,1,0:T(8,128)S(1)}, f32[21,16,128]{2,1,0:T(8,128)S(1)}, u32[]{:S(2)}, u32[]{:S(2)}) collective-permute-start(f32[21,16,128]{2,1,0:T(8,128)S(1)} %get-tuple-element.41), channel_id=1, source_target_pairs={{0,5},{1,4},{2,7},{3,6},{4,1},{5,0},{6,3},{7,2},{8,13},{9,12},{10,... | collective-permute-start | bytes 516104 | tf_op jit(solution)/shard_map/ppermute | solution.py:328
  49.7 8.4 %collective-permute-start.14 = (f32[21,16,128]{2,1,0:T(8,128)S(1)}, f32[21,16,128]{2,1,0:T(8,128)S(1)}, u32[]{:S(2)}, u32[]{:S(2)}) collective-permute-start(f32[21,16,128]{2,1,0:T(8,128)S(1)} %get-tuple-element.43), channel_id=1, source_target_pairs={{0,2},{1,3},{2,0},{3,1},{4,6},{5,7},{6,4},{7,5},{8,10},{9,11},{10,... | collective-permute-start | bytes 516104 | tf_op jit(solution)/shard_map/ppermute | solution.py:328
  50.8 8.3 %collective-permute-start.15 = (f32[21,16,128]{2,1,0:T(8,128)S(1)}, f32[21,16,128]{2,1,0:T(8,128)S(1)}, u32[]{:S(2)}, u32[]{:S(2)}) collective-permute-start(f32[21,16,128]{2,1,0:T(8,128)S(1)} %get-tuple-element.44), channel_id=1, source_target_pairs={{0,3},{1,2},{2,1},{3,0},{4,7},{5,6},{6,5},{7,4},{8,11},{9,10},{10,... | collective-permute-start | bytes 516104 | tf_op jit(solution)/shard_map/ppermute | solution.py:328
  51.1 8.0 %collective-permute-start.16 = (f32[21,16,128]{2,1,0:T(8,128)S(1)}, f32[21,16,128]{2,1,0:T(8,128)S(1)}, u32[]{:S(2)}, u32[]{:S(2)}) collective-permute-start(f32[21,16,128]{2,1,0:T(8,128)S(1)} %get-tuple-element.46), channel_id=1, source_target_pairs={{0,1},{1,0},{2,3},{3,2},{4,5},{5,4},{6,7},{7,6},{8,9},{9,8},{10,11... | collective-permute-start | bytes 516104 | tf_op jit(solution)/shard_map/ppermute | solution.py:328

commit v7 on v6

--- a/solution.py
+++ b/solution.py
@@ -6,11 +6,10 @@
 from jax.sharding import PartitionSpec as P
 
 VMEM_LIMIT = 40 * 1024 * 1024
-PACK_LIMIT = 60 * 1024 * 1024
 PLANES = 2
 ACTIVE = 49
 MOST = 8
-UNROLL = 7
+GROUP = 7
 
 
 class Layout:
@@ -57,7 +56,7 @@
     tile = 8
 
     def kernel(j_ref, field_ref, mean_ref, kl_ref, *refs):
-        out_refs, (stage_ref, past_ref, in_sems, out_sems) = refs[:modes], refs[modes:]
+        out_refs, (stage_ref, past_ref, in_sems) = refs[:modes], refs[modes:]
         plane = j_ref[0] // modes
         mode = j_ref[0] - plane * modes
         side = 1 - plane if crossing else plane
@@ -117,30 +116,25 @@
             part, line = lay.edge(lay.fields)
             if part < lay.parts:
                 stage_ref[n, part, line:] = jnp.zeros((rows - line, width), jnp.float32)
-        copies = []
         for n, out_ref in enumerate(out_refs):
-            source = stage_ref.at[jnp.bitwise_xor(mode, n)]
-            made = pltpu.make_async_copy(source, out_ref, out_sems.at[n])
-            made.start()
-            copies.append(made)
-        for made in copies:
-            made.wait()
+            to = jnp.bitwise_xor(mode, n)
+            for part in range(lay.parts):
+                out_ref[part] = stage_ref[to, part]
 
     shape = (lay.parts, rows, width)
     sent = pl.pallas_call(
         kernel,
-        out_shape=[jax.ShapeDtypeStruct(shape, jnp.float32)] * modes,
+        out_shape=[pltpu.VMEM(shape, jnp.float32)] * modes,
         in_specs=smem(1) + [pl.BlockSpec(memory_space=pltpu.HBM)] * 3,
-        out_specs=[pl.BlockSpec(memory_space=pltpu.HBM)] * modes,
+        out_specs=vmem(modes),
         scratch_shapes=[
             pltpu.VMEM((modes, *shape), jnp.float32),
             pltpu.VMEM((lay.fields, tile, width), jnp.float32),
             pltpu.SemaphoreType.DMA((modes + 1, 1 + lay.share)),
-            pltpu.SemaphoreType.DMA((modes,)),
         ],
-        compiler_params=pltpu.CompilerParams(vmem_limit_bytes=PACK_LIMIT),
+        compiler_params=pltpu.CompilerParams(vmem_limit_bytes=VMEM_LIMIT),
         name="pack_crossing" if crossing else "pack_own",
-    )(j, field, mean, kl)
+    )(j, *[pltpu.with_memory_space_constraint(x, pltpu.HBM) for x in (field, mean, kl)])
     return [piece.reshape(lay.piece, width) for piece in sent]
 
 
@@ -233,27 +227,32 @@
 
         for block in range(lay.modes):
 
-            def spread(i, at, block=block):
+            def spread(i, block=block):
                 piece_ref = piece_refs[block]
                 halo_ref, n = halo_parts[block]
                 here = piece_ref[pl.ds(i * rows, rows), :]
                 low = piece_ref[pl.ds(lay.main + 2 * i, 1), :]
                 high = piece_ref[pl.ds(lay.main + 2 * i + 1, 1), :]
-                near_ref[at, 0] = here
-                near_ref[at, 1] = pltpu.roll(here, width - 1, 1)
-                near_ref[at, 2] = pltpu.roll(here, 1, 1)
-                near_ref[at, 3] = jnp.where(line == rows - 1, high, pltpu.roll(here, rows - 1, 0))
-                near_ref[at, 4] = jnp.where(line == 0, low, pltpu.roll(here, 1, 0))
-                near_ref[at, 5] = other_refs[block][pl.ds(i * rows, rows), :]
-                near_ref[at, 6] = halo_ref[n, pl.ds(i * rows, rows), :]
-
-            def spread_slot(i, carry, spread=spread, block=block):
-                spread(i, block * lay.quota + i)
-                return carry
-
-            lax.fori_loop(0, lay.quota, spread_slot, 0, unroll=UNROLL)
+                return (
+                    here,
+                    pltpu.roll(here, width - 1, 1),
+                    pltpu.roll(here, 1, 1),
+                    jnp.where(line == rows - 1, high, pltpu.roll(here, rows - 1, 0)),
+                    jnp.where(line == 0, low, pltpu.roll(here, 1, 0)),
+                    other_refs[block][pl.ds(i * rows, rows), :],
+                    halo_ref[n, pl.ds(i * rows, rows), :],
+                )
+
+            def keep(at, values):
+                for n, value in enumerate(values):
+                    near_ref[at, n] = value
+
+            def keep_slot(i, values, block=block):
+                keep(block * lay.quota + i, values)
+
+            grouped(0, lay.quota, spread, keep_slot)
             for i in range(lay.quota, lay.fields):
-                spread(i, lay.place(block, i))
+                keep(lay.place(block, i), spread(i))
 
         def operator_of(term):
             at = lay.term_place(term, mode)
@@ -273,25 +272,29 @@
 
             return operator
 
+        def keep_product(e, value):
+            product_ref[e] = value
+
         for term in range(1, lay.terms):
             operator = operator_of(term)
-
-            def apply(n, carry, operator=operator, term=term):
-                e = (term - 1) * ACTIVE + n
-                product_ref[e] = operator(source_ref[e])
-                return carry
-
-            lax.fori_loop(0, ACTIVE, apply, 0, unroll=UNROLL)
+            grouped(
+                (term - 1) * ACTIVE,
+                ACTIVE,
+                lambda e, operator=operator: operator(source_ref[e]),
+                keep_product,
+            )
 
         operator = operator_of(0)
         for block in range(lay.modes):
 
-            def collect(i, carry, out_ref=out_refs[block], block=block):
+            def collect(i, block=block):
                 s = block * lay.quota + i
-                out_ref[i] = gather_products(s, take_ref, factor_ref, product_ref, operator(s))
-                return carry
-
-            lax.fori_loop(0, lay.quota, collect, 0, unroll=UNROLL)
+                return gather_products(s, take_ref, factor_ref, product_ref, operator(s))
+
+            def keep_out(i, value, out_ref=out_refs[block]):
+                out_ref[i] = value
+
+            grouped(0, lay.quota, collect, keep_out)
 
     return pl.pallas_call(
         kernel,
@@ -305,6 +308,19 @@
         compiler_params=pltpu.CompilerParams(vmem_limit_bytes=VMEM_LIMIT),
         name=name,
     )(j, *lists, *pieces, *others, *halos)
+
+
+def grouped(first, count, compute, store):
+    size = max(n for n in range(1, GROUP + 1) if count % n == 0)
+
+    def step(g, carry):
+        numbers = [first + g * size + n for n in range(size)]
+        values = [compute(n) for n in numbers]
+        for n, value in zip(numbers, values):
+            store(n, value)
+        return carry
+
+    lax.fori_loop(0, count // size, step, 0)
 
 
 def after(value, *done):
@@ -359,11 +375,12 @@
     crossing_out = stencil(crossing, own, [own_halo], lists, j, "stencil_crossing", lay)
     own_j = after(j, *crossing_out)
     own_out = stencil(own, crossing, halos, lists, own_j, "stencil_own", lay)
-    back = {}
-    for n in [*range(half, modes), *range(half)]:
-        back[modes + n] = swap(crossing_out[n], modes + n)
-    for n in [*range(half, modes), *range(half)]:
-        back[n] = swap(own_out[n], n)
+    out = [*own_out, *crossing_out]
+    for r in range(modes, modes + half):
+        out[r] = after(out[r], *own_out)
+    first = [*range(modes + half, lay.group)]
+    rest = [r + n for n in range(half) for r in (half, modes)] + [*range(half)]
+    back = {r: swap(out[r], r) for r in first + rest}
     return unpack(back, j, (quota, height, width), lay).reshape(chaos_field.shape)
 
 

time: 60.6 us -> 59.5 us (0.982)
  Pallas kernels: 14.8 us -> 13 us
  local copies, waits for them, and re-layouts: 1.15 us -> 2.78 us
  waiting for transfers between devices: 16.2 us -> 15.4 us
    pallas_call x2, Pallas kernels: 4.9 us -> 3.1 us  [pack(): pl.pallas_call(kernel, out_shape=[pltpu.VMEM(shape, jnp.float32)] * modes...]
    unnamed x14 -> x8, local copies, waits for them, and re-layouts: 0.42 us -> 1.37 us
    ppermute x14, waiting for transfers between devices: 14.4 us -> 13.6 us  [swap(): return lax.ppermute(piece, axes, [(d, d ^ r) for d in range(devices)])]
    slice x1, local copies, waits for them, and re-layouts: 0.01 us -> 0.69 us  [shift(): main = jnp.stack([piece[:lay.main] for piece in pieces])]
  transfers between devices with their start and end apart: 17 -> 17, of which waited for: 7 -> 7; matrix products, arithmetic and copies ran while one was open for 5% -> 8% of each run, Pallas kernels for 19% -> 17%
where the time goes in v7:
time: 59.5 us; the launch traced here: 59.2 us
  starting transfers between devices  25.9 us (44%)
  waiting for transfers between devices  15.4 us (26%)
  Pallas kernels  13 us (22%)
  local copies, waits for them, and re-layouts  2.78 us (5%)
  other arithmetic  1.18 us (2%)
  matrix products  0.69 us (1%)
    ppermute x14, starting transfers between devices, swap(): return lax.ppermute(piece, axes, [(d, d ^ r) for d in range(devices)])  17.7 us
    ppermute x14, waiting for transfers between devices, swap(): return lax.ppermute(piece, axes, [(d, d ^ r) for d in range(devices)])  13.6 us
    pallas_call x2, Pallas kernels, stencil(): pl.pallas_call(kernel, out_shape=[jax.ShapeDtypeStruct((lay.quota, rows,...  8.81 us
    ppermute x3, starting transfers between devices, shift(): return lax.ppermute(main, axes, pairs)  8.21 us
    pallas_call x2, Pallas kernels, pack(): pl.pallas_call(kernel, out_shape=[pltpu.VMEM(shape, jnp.float32)] * modes...  3.1 us
    ppermute x3, waiting for transfers between devices, shift(): return lax.ppermute(main, axes, pairs)  1.83 us
    unnamed x8, local copies, waits for them, and re-layouts  1.37 us
  transfers between devices with their start and end apart: 17, of which 7 were waited for; matrix products, arithmetic and copies ran while one was open for 8% of the time, Pallas kernels for 17%

profile of v7, /device:TPU:0, one launch (start us, length us, event | category | flops | bytes accessed | tf_op | source)
XLA Modules:
  0.0 59.2 jit_solution(1430904683487021100)
XLA Ops:
  0.0 1.5 %pack_own.1 = (f32[26,16,128]{2,1,0:T(8,128)S(1)}, f32[26,16,128]{2,1,0:T(8,128)S(1)}, f32[26,16,128]{2,1,0:T(8,128)S(1)}, f32[26,16,128]{2,1,0:T(8,128)S(1)}) custom-call(s32[1]{0:T(128)} %bitcast.j_ref, f32[21,128,128]{2,1,0:T(8,128)} %bitcast.47, f32[1,128,128]{2,1,0:T(8,128)} %mean_ref.3, f32[6,128,128]{2,1,0:T(8,128)} %bitcast.49), custom_call_target="tpu_custom_call" | custom-call | tf_op jit(solution)/shard_map/pack_own/pallas_call | solution.py:125
  1.6 0.0 copy-start.2
  1.6 0.0 copy-start.1
  1.6 3.0 %collective-permute-start.2 = (f32[416,128]{1,0:T(8,128)S(1)}, f32[416,128]{1,0:T(8,128)S(1)}, u32[]{:S(2)}, u32[]{:S(2)}) collective-permute-start(f32[416,128]{1,0:T(8,128)S(1)} %bitcast.46), channel_id=1, source_target_pairs={{0,2},{1,3},{2,0},{3,1},{4,6},{5,7},{6,4},{7,5},{8,10},{9,11},{10,... | collective-permute-start | bytes 638984 | tf_op jit(solution)/shard_map/ppermute | solution.py:344
  4.6 0.0 collective-permute-start.6
  4.6 0.2 collective-permute-start.3
  4.8 1.5 %pack_crossing.1 = (f32[26,16,128]{2,1,0:T(8,128)S(1)}, f32[26,16,128]{2,1,0:T(8,128)S(1)}, f32[26,16,128]{2,1,0:T(8,128)S(1)}, f32[26,16,128]{2,1,0:T(8,128)S(1)}) custom-call(s32[1]{0:T(128)} %bitcast.j_ref, f32[21,128,128]{2,1,0:T(8,128)} %bitcast.48, f32[1,128,128]{2,1,0:T(8,128)} %mean_ref.3, f32[6,128,128]{2,1,0:T(8,128)} %bitcast.50), custom_call_target="tpu_custom_call" | custom-call | tf_op jit(solution)/shard_map/pack_crossing/pallas_call | solution.py:125
  6.4 1.6 %collective-permute-start.1 = (f32[416,128]{1,0:T(8,128)S(1)}, f32[416,128]{1,0:T(8,128)S(1)}, u32[]{:S(2)}, u32[]{:S(2)}) collective-permute-start(f32[416,128]{1,0:T(8,128)S(1)} %bitcast.43), channel_id=1, source_target_pairs={{0,5},{1,4},{2,7},{3,6},{4,1},{5,0},{6,3},{7,2},{8,13},{9,12},{10,... | collective-permute-start | bytes 638984 | tf_op jit(solution)/shard_map/ppermute | solution.py:344
  8.0 0.5 collective-permute-start
  8.5 0.7 %slice.29 = f32[23,16,128]{2,1,0:T(8,128)} slice(f32[26,16,128]{2,1,0:T(8,128)S(1)} %get-tuple-element.28), slice={[0:23], [0:16], [0:128]} | slice | bytes 376832 | tf_op jit(solution)/shard_map/slice | solution.py:353
  9.1 0.1 iota_compare_fusion.9
  9.2 0.0 copy-done.2
  9.2 0.1 broadcast_in_dim.135
  9.3 0.1 select_reduce_fusion.9
  9.4 0.1 eq.38
  9.5 0.2 copy.9
  9.7 1.2 %copy.10 = f32[7,84,84]{1,2,0:T(8,128)S(1)} copy(f32[7,84,84]{2,1,0:T(8,128)} %param.10) | data formatting | bytes 395136 | tf_op args[4]
  10.8 0.3 fusion
  11.2 0.0 copy-start
  11.2 0.3 fusion.10
  11.6 0.1 fusion.6
  11.7 0.1 select_reduce_fusion.1
  11.8 0.2 select_reduce_fusion.3
  12.1 0.2 select_reduce_fusion.5
  12.2 0.1 reshape.111.source_ref
  12.3 0.1 select_reduce_fusion.6
  12.5 0.1 copy.12
  12.6 0.1 reshape.113.factor_ref
  12.7 0.1 broadcast_add_fusion.1
  12.8 0.1 copy.11
  12.9 0.1 reshape.112.take_ref
  13.0 0.0 collective-permute-done.2.refs_6_.refs_2_
  13.0 0.0 collective-permute-done.6.refs_5_.refs_1_
  13.0 0.7 %collective-permute-done.3.refs_7_.refs_3_ = f32[416,128]{1,0:T(8,128)S(1)} collective-permute-done((f32[416,128]{1,0:T(8,128)S(1)}, f32[416,128]{1,0:T(8,128)S(1)}, u32[]{:S(2)}, u32[]{:S(2)}) %collective-permute-start.3) | collective-permute-done | bytes 213024 | tf_op jit(solution)/shard_map/ppermute | solution.py:344
  13.7 0.1 pad_maximum_fusion
  13.8 1.3 %collective-permute-start.7 = (f32[4,368,128]{2,1,0:T(8,128)S(1)}, f32[4,368,128]{2,1,0:T(8,128)S(1)}, u32[]{:S(2)}, u32[]{:S(2)}) collective-permute-start(f32[4,368,128]{2,1,0:T(8,128)S(1)} %pad_maximum_fusion), channel_id=1, source_target_pairs={{4,12},{5,13},{6,14},{7,15},{8,0},{9,1},{10,2},{11,3},{12,20},{13,... | collective-permute-start | bytes 2261000 | tf_op jit(solution)/shard_map/ppermute | solution.py:354
  15.1 5.1 %collective-permute-start.5 = (f32[416,128]{1,0:T(8,128)S(1)}, f32[416,128]{1,0:T(8,128)S(1)}, u32[]{:S(2)}, u32[]{:S(2)}) collective-permute-start(f32[416,128]{1,0:T(8,128)S(1)} %bitcast.41), channel_id=1, source_target_pairs={{0,7},{1,6},{2,5},{3,4},{4,3},{5,2},{6,1},{7,0},{8,15},{9,14},{10,... | collective-permute-start | bytes 638984 | tf_op jit(solution)/shard_map/ppermute | solution.py:344
  20.2 0.0 collective-permute-start.4
  20.2 0.0 collective-permute-done.1.refs_1_.refs_5_
  20.2 0.0 collective-permute-done.refs_0_.refs_4_
  20.3 3.5 %collective-permute-start.10 = (f32[2,368,128]{2,1,0:T(8,128)S(1)}, f32[2,368,128]{2,1,0:T(8,128)S(1)}, u32[]{:S(2)}, u32[]{:S(2)}) collective-permute-start(f32[2,368,128]{2,1,0:T(8,128)S(1)} %pad_maximum_fusion.1), channel_id=1, source_target_pairs={{0,8},{1,9},{2,10},{3,11},{8,16},{9,17},{10,18},{11,19},{12,4},{13... | collective-permute-start | bytes 1130504 | tf_op jit(solution)/shard_map/ppermute | solution.py:354
  23.8 2.3 %collective-permute-done.5.refs_3_.refs_7_ = f32[416,128]{1,0:T(8,128)S(1)} collective-permute-done((f32[416,128]{1,0:T(8,128)S(1)}, f32[416,128]{1,0:T(8,128)S(1)}, u32[]{:S(2)}, u32[]{:S(2)}) %collective-permute-start.5) | collective-permute-done | bytes 213024 | tf_op jit(solution)/shard_map/ppermute | solution.py:344
  26.1 3.9 %collective-permute-done.4.refs_2_.refs_6_ = f32[416,128]{1,0:T(8,128)S(1)} collective-permute-done((f32[416,128]{1,0:T(8,128)S(1)}, f32[416,128]{1,0:T(8,128)S(1)}, u32[]{:S(2)}, u32[]{:S(2)}) %collective-permute-start.4) | collective-permute-done | bytes 213024 | tf_op jit(solution)/shard_map/ppermute | solution.py:344
  30.0 3.5 %collective-permute-start.11 = (f32[2,368,128]{2,1,0:T(8,128)S(1)}, f32[2,368,128]{2,1,0:T(8,128)S(1)}, u32[]{:S(2)}, u32[]{:S(2)}) collective-permute-start(f32[2,368,128]{2,1,0:T(8,128)S(1)} %pad_maximum_fusion.2), channel_id=1, source_target_pairs={{0,8},{1,9},{2,10},{3,11},{8,16},{9,17},{10,18},{11,19},{12,4},{13... | collective-permute-start | bytes 1130504 | tf_op jit(solution)/shard_map/ppermute | solution.py:354
  33.5 1.8 %collective-permute-done.7.refs_8_ = f32[4,368,128]{2,1,0:T(8,128)S(1)} collective-permute-done((f32[4,368,128]{2,1,0:T(8,128)S(1)}, f32[4,368,128]{2,1,0:T(8,128)S(1)}, u32[]{:S(2)}, u32[]{:S(2)}) %collective-permute-start.7) | collective-permute-done | bytes 753696 | tf_op jit(solution)/shard_map/ppermute | solution.py:354
  35.3 4.4 %stencil_crossing.1 = (f32[21,16,128]{2,1,0:T(8,128)S(1)}, f32[21,16,128]{2,1,0:T(8,128)S(1)}, f32[21,16,128]{2,1,0:T(8,128)S(1)}, f32[21,16,128]{2,1,0:T(8,128)S(1)}) custom-call(s32[1]{0:T(128)} %bitcast.j_ref, s32[294]{0:T(512)S(1)} %reshape.111.source_ref, s32[672]{0:T(1024)S(1)} %reshape.112.take_ref, f32[672]{0:T(1024)S(1)} %reshape.113.factor_ref, ...), custom_call_target="tpu_custom_call" | custom-call | tf_op jit(solution)/shard_map/stencil_crossing/pallas_call | solution.py:299
  39.7 1.2 %collective-permute-start.8 = (f32[21,16,128]{2,1,0:T(8,128)S(1)}, f32[21,16,128]{2,1,0:T(8,128)S(1)}, u32[]{:S(2)}, u32[]{:S(2)}) collective-permute-start(f32[21,16,128]{2,1,0:T(8,128)S(1)} %get-tuple-element.40), channel_id=1, source_target_pairs={{0,6},{1,7},{2,4},{3,5},{4,2},{5,3},{6,0},{7,1},{8,14},{9,15},{10,... | collective-permute-start | bytes 516104 | tf_op jit(solution)/shard_map/ppermute | solution.py:344
  40.9 1.2 %collective-permute-start.9 = (f32[21,16,128]{2,1,0:T(8,128)S(1)}, f32[21,16,128]{2,1,0:T(8,128)S(1)}, u32[]{:S(2)}, u32[]{:S(2)}) collective-permute-start(f32[21,16,128]{2,1,0:T(8,128)S(1)} %get-tuple-element.41), channel_id=1, source_target_pairs={{0,7},{1,6},{2,5},{3,4},{4,3},{5,2},{6,1},{7,0},{8,15},{9,14},{10,... | collective-permute-start | bytes 516104 | tf_op jit(solution)/shard_map/ppermute | solution.py:344
  42.1 0.0 collective-permute-done.10.refs_8_
  42.1 0.0 collective-permute-done.11.refs_9_
  42.1 4.4 %stencil_own.1 = (f32[21,16,128]{2,1,0:T(8,128)S(1)}, f32[21,16,128]{2,1,0:T(8,128)S(1)}, f32[21,16,128]{2,1,0:T(8,128)S(1)}, f32[21,16,128]{2,1,0:T(8,128)S(1)}) custom-call(s32[1]{0:T(128)} %bitcast.j_ref, s32[294]{0:T(512)S(1)} %reshape.111.source_ref, s32[672]{0:T(1024)S(1)} %reshape.112.take_ref, f32[672]{0:T(1024)S(1)} %reshape.113.factor_ref, ...), custom_call_target="tpu_custom_call" | custom-call | tf_op jit(solution)/shard_map/stencil_own/pallas_call | solution.py:299
  46.5 1.2 %collective-permute-start.12 = (f32[21,16,128]{2,1,0:T(8,128)S(1)}, f32[21,16,128]{2,1,0:T(8,128)S(1)}, u32[]{:S(2)}, u32[]{:S(2)}) collective-permute-start(f32[21,16,128]{2,1,0:T(8,128)S(1)} %get-tuple-element.45), channel_id=1, source_target_pairs={{0,2},{1,3},{2,0},{3,1},{4,6},{5,7},{6,4},{7,5},{8,10},{9,11},{10,... | collective-permute-start | bytes 516104 | tf_op jit(solution)/shard_map/ppermute | solution.py:344
  47.7 1.5 %collective-permute-start.13 = (f32[21,16,128]{2,1,0:T(8,128)S(1)}, f32[21,16,128]{2,1,0:T(8,128)S(1)}, u32[]{:S(2)}, u32[]{:S(2)}) collective-permute-start(f32[21,16,128]{2,1,0:T(8,128)S(1)} %get-tuple-element.49), channel_id=1, source_target_pairs={{0,4},{1,5},{2,6},{3,7},{4,0},{5,1},{6,2},{7,3},{8,12},{9,13},{10,... | collective-permute-start | bytes 516104 | tf_op jit(solution)/shard_map/ppermute | solution.py:344
  49.2 0.2 collective-permute-start.15
  49.5 0.0 collective-permute-done.8.refs_0_
  49.5 0.4 collective-permute-start.16
  49.9 0.0 collective-permute-done.9.refs_1_
  49.9 1.5 %collective-permute-start.14 = (f32[21,16,128]{2,1,0:T(8,128)S(1)}, f32[21,16,128]{2,1,0:T(8,128)S(1)}, u32[]{:S(2)}, u32[]{:S(2)}) collective-permute-start(f32[21,16,128]{2,1,0:T(8,128)S(1)} %get-tuple-element.48), channel_id=1, source_target_pairs={{0,3},{1,2},{2,1},{3,0},{4,7},{5,6},{6,5},{7,4},{8,11},{9,10},{10,... | collective-permute-start | bytes 516104 | tf_op jit(solution)/shard_map/ppermute | solution.py:344
  51.4 3.6 %collective-permute-done.13.refs_3_ = f32[21,16,128]{2,1,0:T(8,128)S(1)} collective-permute-done((f32[21,16,128]{2,1,0:T(8,128)S(1)}, f32[21,16,128]{2,1,0:T(8,128)S(1)}, u32[]{:S(2)}, u32[]{:S(2)}) %collective-permute-start.13) | collective-permute-done | bytes 172064 | tf_op jit(solution)/shard_map/ppermute | solution.py:344
  54.9 2.6 %collective-permute-done.15.refs_5_ = f32[21,16,128]{2,1,0:T(8,128)S(1)} collective-permute-done((f32[21,16,128]{2,1,0:T(8,128)S(1)}, f32[21,16,128]{2,1,0:T(8,128)S(1)}, u32[]{:S(2)}, u32[]{:S(2)}) %collective-permute-start.15) | collective-permute-done | bytes 172064 | tf_op jit(solution)/shard_map/ppermute | solution.py:344
  57.5 0.0 collective-permute-done.12.refs_2_
  57.5 0.0 collective-permute-done.16.refs_7_
  57.5 0.6 collective-permute-done.14.refs_4_
  58.1 1.1 %unpack.1 = f32[21,128,128]{2,1,0:T(8,128)} custom-call(s32[1]{0:T(128)} %bitcast.j_ref, f32[21,16,128]{2,1,0:T(8,128)S(1)} %collective-permute-done.8.refs_0_, f32[21,16,128]{2,1,0:T(8,128)S(1)} %collective-permute-done.9.refs_1_, f32[21,16,128]{2,1,0:T(8,128)S(1)} %collective-permute-done.12.refs_2_, f32[21,16,128]{2,1,0:T(8,128)S(1)} %collective-permute-done.13.refs_3_, ...), custom_call_target="tpu_custom_call" | custom-call | tf_op jit(solution)/shard_map/unpack/pallas_call | solution.py:157
  (21 shorter events, 0.3 us)
Async XLA Ops:
  1.6 7.7 %copy-start.2 = (s32[84]{0:T(128)S(1)}, s32[84]{0:T(128)}, u32[]{:S(2)}) copy-start(s32[84]{0:T(128)} %param.11) | copy-start | bytes 1012
  1.6 7.9 %copy-start.1 = (s32[7,84,84]{2,1,0:T(8,128)S(1)}, s32[7,84,84]{2,1,0:T(8,128)}, u32[]{:S(2)}) copy-start(s32[7,84,84]{2,1,0:T(8,128)} %param.9) | copy-start | bytes 592708
  1.6 11.4 %collective-permute-start.2 = (f32[416,128]{1,0:T(8,128)S(1)}, f32[416,128]{1,0:T(8,128)S(1)}, u32[]{:S(2)}, u32[]{:S(2)}) collective-permute-start(f32[416,128]{1,0:T(8,128)S(1)} %bitcast.46), channel_id=1, source_target_pairs={{0,2},{1,3},{2,0},{3,1},{4,6},{5,7},{6,4},{7,5},{8,10},{9,11},{10,... | collective-permute-start | bytes 638984 | tf_op jit(solution)/shard_map/ppermute | solution.py:344
  4.6 8.4 %collective-permute-start.6 = (f32[416,128]{1,0:T(8,128)S(1)}, f32[416,128]{1,0:T(8,128)S(1)}, u32[]{:S(2)}, u32[]{:S(2)}) collective-permute-start(f32[416,128]{1,0:T(8,128)S(1)} %bitcast.45), channel_id=1, source_target_pairs={{0,1},{1,0},{2,3},{3,2},{4,5},{5,4},{6,7},{7,6},{8,9},{9,8},{10,11... | collective-permute-start | bytes 638984 | tf_op jit(solution)/shard_map/ppermute | solution.py:344
  4.6 9.1 %collective-permute-start.3 = (f32[416,128]{1,0:T(8,128)S(1)}, f32[416,128]{1,0:T(8,128)S(1)}, u32[]{:S(2)}, u32[]{:S(2)}) collective-permute-start(f32[416,128]{1,0:T(8,128)S(1)} %bitcast.44), channel_id=1, source_target_pairs={{0,3},{1,2},{2,1},{3,0},{4,7},{5,6},{6,5},{7,4},{8,11},{9,10},{10,... | collective-permute-start | bytes 638984 | tf_op jit(solution)/shard_map/ppermute | solution.py:344
  6.4 13.9 %collective-permute-start.1 = (f32[416,128]{1,0:T(8,128)S(1)}, f32[416,128]{1,0:T(8,128)S(1)}, u32[]{:S(2)}, u32[]{:S(2)}) collective-permute-start(f32[416,128]{1,0:T(8,128)S(1)} %bitcast.43), channel_id=1, source_target_pairs={{0,5},{1,4},{2,7},{3,6},{4,1},{5,0},{6,3},{7,2},{8,13},{9,12},{10,... | collective-permute-start | bytes 638984 | tf_op jit(solution)/shard_map/ppermute | solution.py:344
  8.0 12.3 %collective-permute-start = (f32[416,128]{1,0:T(8,128)S(1)}, f32[416,128]{1,0:T(8,128)S(1)}, u32[]{:S(2)}, u32[]{:S(2)}) collective-permute-start(f32[416,128]{1,0:T(8,128)S(1)} %bitcast.42), channel_id=1, source_target_pairs={{0,4},{1,5},{2,6},{3,7},{4,0},{5,1},{6,2},{7,3},{8,12},{9,13},{10,... | collective-permute-start | bytes 638984 | tf_op jit(solution)/shard_map/ppermute | solution.py:344
  11.2 2.5 %copy-start = (f32[23,16,128]{2,1,0:T(8,128)S(1)}, f32[23,16,128]{2,1,0:T(8,128)}, u32[]{:S(2)}) copy-start(f32[23,16,128]{2,1,0:T(8,128)} %slice.29) | copy-start | bytes 565252
  13.8 21.6 %collective-permute-start.7 = (f32[4,368,128]{2,1,0:T(8,128)S(1)}, f32[4,368,128]{2,1,0:T(8,128)S(1)}, u32[]{:S(2)}, u32[]{:S(2)}) collective-permute-start(f32[4,368,128]{2,1,0:T(8,128)S(1)} %pad_maximum_fusion), channel_id=1, source_target_pairs={{4,12},{5,13},{6,14},{7,15},{8,0},{9,1},{10,2},{11,3},{12,20},{13,... | collective-permute-start | bytes 2261000 | tf_op jit(solution)/shard_map/ppermute | solution.py:354
  15.1 11.0 %collective-permute-start.5 = (f32[416,128]{1,0:T(8,128)S(1)}, f32[416,128]{1,0:T(8,128)S(1)}, u32[]{:S(2)}, u32[]{:S(2)}) collective-permute-start(f32[416,128]{1,0:T(8,128)S(1)} %bitcast.41), channel_id=1, source_target_pairs={{0,7},{1,6},{2,5},{3,4},{4,3},{5,2},{6,1},{7,0},{8,15},{9,14},{10,... | collective-permute-start | bytes 638984 | tf_op jit(solution)/shard_map/ppermute | solution.py:344
  20.2 9.8 %collective-permute-start.4 = (f32[416,128]{1,0:T(8,128)S(1)}, f32[416,128]{1,0:T(8,128)S(1)}, u32[]{:S(2)}, u32[]{:S(2)}) collective-permute-start(f32[416,128]{1,0:T(8,128)S(1)} %bitcast.40), channel_id=1, source_target_pairs={{0,6},{1,7},{2,4},{3,5},{4,2},{5,3},{6,0},{7,1},{8,14},{9,15},{10,... | collective-permute-start | bytes 638984 | tf_op jit(solution)/shard_map/ppermute | solution.py:344
  20.3 21.8 %collective-permute-start.10 = (f32[2,368,128]{2,1,0:T(8,128)S(1)}, f32[2,368,128]{2,1,0:T(8,128)S(1)}, u32[]{:S(2)}, u32[]{:S(2)}) collective-permute-start(f32[2,368,128]{2,1,0:T(8,128)S(1)} %pad_maximum_fusion.1), channel_id=1, source_target_pairs={{0,8},{1,9},{2,10},{3,11},{8,16},{9,17},{10,18},{11,19},{12,4},{13... | collective-permute-start | bytes 1130504 | tf_op jit(solution)/shard_map/ppermute | solution.py:354
  30.0 12.1 %collective-permute-start.11 = (f32[2,368,128]{2,1,0:T(8,128)S(1)}, f32[2,368,128]{2,1,0:T(8,128)S(1)}, u32[]{:S(2)}, u32[]{:S(2)}) collective-permute-start(f32[2,368,128]{2,1,0:T(8,128)S(1)} %pad_maximum_fusion.2), channel_id=1, source_target_pairs={{0,8},{1,9},{2,10},{3,11},{8,16},{9,17},{10,18},{11,19},{12,4},{13... | collective-permute-start | bytes 1130504 | tf_op jit(solution)/shard_map/ppermute | solution.py:354
  39.7 9.7 %collective-permute-start.8 = (f32[21,16,128]{2,1,0:T(8,128)S(1)}, f32[21,16,128]{2,1,0:T(8,128)S(1)}, u32[]{:S(2)}, u32[]{:S(2)}) collective-permute-start(f32[21,16,128]{2,1,0:T(8,128)S(1)} %get-tuple-element.40), channel_id=1, source_target_pairs={{0,6},{1,7},{2,4},{3,5},{4,2},{5,3},{6,0},{7,1},{8,14},{9,15},{10,... | collective-permute-start | bytes 516104 | tf_op jit(solution)/shard_map/ppermute | solution.py:344
  40.9 9.0 %collective-permute-start.9 = (f32[21,16,128]{2,1,0:T(8,128)S(1)}, f32[21,16,128]{2,1,0:T(8,128)S(1)}, u32[]{:S(2)}, u32[]{:S(2)}) collective-permute-start(f32[21,16,128]{2,1,0:T(8,128)S(1)} %get-tuple-element.41), channel_id=1, source_target_pairs={{0,7},{1,6},{2,5},{3,4},{4,3},{5,2},{6,1},{7,0},{8,15},{9,14},{10,... | collective-permute-start | bytes 516104 | tf_op jit(solution)/shard_map/ppermute | solution.py:344
  46.5 11.0 %collective-permute-start.12 = (f32[21,16,128]{2,1,0:T(8,128)S(1)}, f32[21,16,128]{2,1,0:T(8,128)S(1)}, u32[]{:S(2)}, u32[]{:S(2)}) collective-permute-start(f32[21,16,128]{2,1,0:T(8,128)S(1)} %get-tuple-element.45), channel_id=1, source_target_pairs={{0,2},{1,3},{2,0},{3,1},{4,6},{5,7},{6,4},{7,5},{8,10},{9,11},{10,... | collective-permute-start | bytes 516104 | tf_op jit(solution)/shard_map/ppermute | solution.py:344
  47.7 7.2 %collective-permute-start.13 = (f32[21,16,128]{2,1,0:T(8,128)S(1)}, f32[21,16,128]{2,1,0:T(8,128)S(1)}, u32[]{:S(2)}, u32[]{:S(2)}) collective-permute-start(f32[21,16,128]{2,1,0:T(8,128)S(1)} %get-tuple-element.49), channel_id=1, source_target_pairs={{0,4},{1,5},{2,6},{3,7},{4,0},{5,1},{6,2},{7,3},{8,12},{9,13},{10,... | collective-permute-start | bytes 516104 | tf_op jit(solution)/shard_map/ppermute | solution.py:344
  49.2 8.3 %collective-permute-start.15 = (f32[21,16,128]{2,1,0:T(8,128)S(1)}, f32[21,16,128]{2,1,0:T(8,128)S(1)}, u32[]{:S(2)}, u32[]{:S(2)}) collective-permute-start(f32[21,16,128]{2,1,0:T(8,128)S(1)} %get-tuple-element.50), channel_id=1, source_target_pairs={{0,5},{1,4},{2,7},{3,6},{4,1},{5,0},{6,3},{7,2},{8,13},{9,12},{10,... | collective-permute-start | bytes 516104 | tf_op jit(solution)/shard_map/ppermute | solution.py:344
  49.5 8.1 %collective-permute-start.16 = (f32[21,16,128]{2,1,0:T(8,128)S(1)}, f32[21,16,128]{2,1,0:T(8,128)S(1)}, u32[]{:S(2)}, u32[]{:S(2)}) collective-permute-start(f32[21,16,128]{2,1,0:T(8,128)S(1)} %get-tuple-element.47), channel_id=1, source_target_pairs={{0,1},{1,0},{2,3},{3,2},{4,5},{5,4},{6,7},{7,6},{8,9},{9,8},{10,11... | collective-permute-start | bytes 516104 | tf_op jit(solution)/shard_map/ppermute | solution.py:344
  49.9 8.2 %collective-permute-start.14 = (f32[21,16,128]{2,1,0:T(8,128)S(1)}, f32[21,16,128]{2,1,0:T(8,128)S(1)}, u32[]{:S(2)}, u32[]{:S(2)}) collective-permute-start(f32[21,16,128]{2,1,0:T(8,128)S(1)} %get-tuple-element.48), channel_id=1, source_target_pairs={{0,3},{1,2},{2,1},{3,0},{4,7},{5,6},{6,5},{7,4},{8,11},{9,10},{10,... | collective-permute-start | bytes 516104 | tf_op jit(solution)/shard_map/ppermute | solution.py:344

commit v8 on v7

--- a/solution.py
+++ b/solution.py
@@ -49,35 +49,26 @@
     return [pl.BlockSpec(memory_space=pltpu.SMEM)] * count
 
 
-def pack(field, mean, kl, j, crossing, lay):
+def pack(field, mean, kl, j, lay):
     kl_terms = kl.shape[0]
-    rows, width, modes, quota = lay.rows, lay.width, lay.modes, lay.quota
-    half = modes * rows
-    tile = 8
+    rows, width, quota = lay.rows, lay.width, lay.quota
 
     def kernel(j_ref, field_ref, mean_ref, kl_ref, *refs):
-        out_refs, (stage_ref, past_ref, in_sems) = refs[:modes], refs[modes:]
-        plane = j_ref[0] // modes
-        mode = j_ref[0] - plane * modes
-        side = 1 - plane if crossing else plane
-        start = side * half
-        beside = pl.multiple_of(half - side * tile, tile)
+        out_refs, (stage_ref, sems) = refs[: lay.group], refs[lay.group :]
+        mode = lax.rem(j_ref[0], lay.modes)
 
         def load(n, begin=True):
-            if n < modes:
-                at, target = pl.ds(pl.multiple_of(start + n * rows, tile), rows), stage_ref.at[n]
-            else:
-                at, target = pl.ds(beside, tile), past_ref
+            at, target = pl.ds(n * rows, rows), stage_ref.at[n]
             copies = [
                 pltpu.make_async_copy(
-                    field_ref.at[:, at, :], target.at[pl.ds(0, quota)], in_sems.at[n, 0]
+                    field_ref.at[:, at, :], target.at[pl.ds(0, quota)], sems.at[n, 0]
                 )
             ]
             if begin:
                 copies[0].start()
             for i in range(lay.share):
                 term = mode * lay.share + i
-                into, sem = target.at[quota + i], in_sems.at[n, 1 + i]
+                into, sem = target.at[quota + i], sems.at[n, 1 + i]
                 if not begin:
                     copies.append(pltpu.make_async_copy(mean_ref.at[0, at, :], into, sem))
                     continue
@@ -93,47 +84,39 @@
 
             return copies
 
-        for n in range(modes + 1):
+        for n in range(lay.group):
             load(n)
-        for n in range(modes + 1):
+        for n in range(lay.group):
             for made in load(n, begin=False):
                 made.wait()
-        low_there = jnp.where(side == 0, 0.0, 1.0)
-        high_there = jnp.where(side == PLANES - 1, 0.0, 1.0)
-        for n in range(modes):
+        none = jnp.zeros((1, width), jnp.float32)
+        for n in range(lay.group):
             for i in range(lay.fields):
-                if n > 0:
-                    low = stage_ref[n - 1, i, rows - 1 :]
-                else:
-                    low = past_ref[i, tile - 1 :] * low_there
-                if n < modes - 1:
-                    high = stage_ref[n + 1, i, :1]
-                else:
-                    high = past_ref[i, :1] * high_there
                 part, line = lay.edge(i)
+                low = stage_ref[n - 1, i, rows - 1 :] if n > 0 else none
+                high = stage_ref[n + 1, i, :1] if n < lay.group - 1 else none
                 stage_ref[n, part, line : line + 1] = low
                 stage_ref[n, part, line + 1 : line + 2] = high
             part, line = lay.edge(lay.fields)
             if part < lay.parts:
                 stage_ref[n, part, line:] = jnp.zeros((rows - line, width), jnp.float32)
-        for n, out_ref in enumerate(out_refs):
-            to = jnp.bitwise_xor(mode, n)
+        for r, out_ref in enumerate(out_refs):
+            to = jnp.bitwise_xor(j_ref[0], r)
             for part in range(lay.parts):
                 out_ref[part] = stage_ref[to, part]
 
     shape = (lay.parts, rows, width)
     sent = pl.pallas_call(
         kernel,
-        out_shape=[pltpu.VMEM(shape, jnp.float32)] * modes,
+        out_shape=[pltpu.VMEM(shape, jnp.float32)] * lay.group,
         in_specs=smem(1) + [pl.BlockSpec(memory_space=pltpu.HBM)] * 3,
-        out_specs=vmem(modes),
+        out_specs=vmem(lay.group),
         scratch_shapes=[
-            pltpu.VMEM((modes, *shape), jnp.float32),
-            pltpu.VMEM((lay.fields, tile, width), jnp.float32),
-            pltpu.SemaphoreType.DMA((modes + 1, 1 + lay.share)),
+            pltpu.VMEM((lay.group, *shape), jnp.float32),
+            pltpu.SemaphoreType.DMA((lay.group, 1 + lay.share)),
         ],
         compiler_params=pltpu.CompilerParams(vmem_limit_bytes=VMEM_LIMIT),
-        name="pack_crossing" if crossing else "pack_own",
+        name="pack",
     )(j, *[pltpu.with_memory_space_constraint(x, pltpu.HBM) for x in (field, mean, kl)])
     return [piece.reshape(lay.piece, width) for piece in sent]
 
@@ -354,27 +337,29 @@
         return lax.ppermute(main, axes, pairs)
 
     field, kl = chaos_field[:, 0], kl_fields[:, 0]
-    sent = [None] * lay.group
-    sent[:modes] = pack(field, mean_field, kl, j, False, lay)
-    sent[modes:] = pack(field, mean_field, kl, after(j, *sent[:modes]), True, lay)
+    sent = pack(field, mean_field, kl, j, lay)
     half = modes // 2
     pieces = sent[:1] + [None] * (lay.group - 1)
-    for r in [*range(half, modes), *range(1, half), *range(modes, modes + half)]:
+    for r in [modes, half, *range(1, half), *range(half + 1, modes)]:
         pieces[r] = swap(sent[r], r)
+    for r in range(modes + 1, modes + half):
+        pieces[r] = swap(after(sent[r], *pieces[1:half]), r)
+    halos = [shift(pieces[:1], False)]
     for r in range(modes + half, lay.group):
-        pieces[r] = swap(after(sent[r], *pieces[half:modes]), r)
+        pieces[r] = swap(after(sent[r], *pieces[half : modes + half], halos[0]), r)
     number = jnp.arange(modes, dtype=jnp.int32)
     mine = jnp.bitwise_xor(number, mode)[:, None, None] == number[None, :, None]
     slot_mode = jnp.sum(jnp.where(mine, slot_mode.reshape(1, modes, quota), 0), 1).reshape(-1)
-    lists = coupling_lists(pattern, coupling, slot_mode)
-    pieces[half] = after(pieces[half], *lists)
-    own_halo = shift(pieces[:modes], False)
-    halos = [shift(pieces[r : r + half], True) for r in (modes, modes + half)]
+    lists = coupling_lists(pattern, coupling, after(slot_mode, pieces[modes + 1]))
+    pieces[modes + half] = after(pieces[modes + half], *lists)
+    halos.append(shift(pieces[1:modes], False))
+    halos.append(shift(pieces[modes : modes + half], True))
+    halos.append(shift(pieces[modes + half :], True))
 
     own, crossing = pieces[:modes], pieces[modes:]
-    crossing_out = stencil(crossing, own, [own_halo], lists, j, "stencil_crossing", lay)
+    crossing_out = stencil(crossing, own, halos[:2], lists, j, "stencil_crossing", lay)
     own_j = after(j, *crossing_out)
-    own_out = stencil(own, crossing, halos, lists, own_j, "stencil_own", lay)
+    own_out = stencil(own, crossing, halos[2:], lists, own_j, "stencil_own", lay)
     out = [*own_out, *crossing_out]
     for r in range(modes, modes + half):
         out[r] = after(out[r], *own_out)

time: 59.5 us -> 62.6 us (1.052)
  starting transfers between devices: 25.9 us -> 27.5 us
  Pallas kernels: 13 us -> 11.9 us
  waiting for transfers between devices: 15.4 us -> 16.5 us
  other arithmetic: 1.18 us -> 1.98 us
  local copies, waits for them, and re-layouts: 2.78 us -> 3.44 us
    ppermute x3 -> x4, starting transfers between devices: 8.21 us -> 9.81 us  [shift(): return lax.ppermute(main, axes, pairs)]
    pallas_call x2 -> x1, Pallas kernels: 3.1 us -> 1.97 us  [pack(): pl.pallas_call(kernel, out_shape=[pltpu.VMEM(shape, jnp.float32)] * lay.g...]
    ppermute x14, waiting for transfers between devices: 13.6 us -> 14.6 us  [swap(): return lax.ppermute(piece, axes, [(d, d ^ r) for d in range(devices)])]
    another operation x3, other arithmetic: 0.11 us -> 0.9 us  [shift(): main = jnp.stack([piece[:lay.main] for piece in pieces])]
    another operation x7, local copies, waits for them, and re-layouts: 0.1 us -> 0.77 us  [shift(): main = jnp.stack([piece[:lay.main] for piece in pieces])]
    ppermute x3 -> x4, waiting for transfers between devices: 1.83 us -> 1.82 us  [shift(): return lax.ppermute(main, axes, pairs)]
  transfers between devices with their start and end apart: 17 -> 18, of which waited for: 7 -> 5; matrix products, arithmetic and copies ran while one was open for 8% -> 10% of each run, Pallas kernels for 17% -> 14%
where the time goes in v8:
time: 62.6 us; the launch traced here: 62.3 us
  starting transfers between devices  27.5 us (44%)
  waiting for transfers between devices  16.5 us (26%)
  Pallas kernels  11.9 us (19%)
  local copies, waits for them, and re-layouts  3.44 us (5%)
  other arithmetic  1.98 us (3%)
  matrix products  0.67 us (1%)
    ppermute x14, starting transfers between devices, swap(): return lax.ppermute(piece, axes, [(d, d ^ r) for d in range(devices)])  17.7 us
    ppermute x14, waiting for transfers between devices, swap(): return lax.ppermute(piece, axes, [(d, d ^ r) for d in range(devices)])  14.6 us
    ppermute x4, starting transfers between devices, shift(): return lax.ppermute(main, axes, pairs)  9.81 us
    pallas_call x2, Pallas kernels, stencil(): pl.pallas_call(kernel, out_shape=[jax.ShapeDtypeStruct((lay.quota, rows,...  8.82 us
    pallas_call x1, Pallas kernels, pack(): pl.pallas_call(kernel, out_shape=[pltpu.VMEM(shape, jnp.float32)] * lay.g...  1.97 us
    ppermute x4, waiting for transfers between devices, shift(): return lax.ppermute(main, axes, pairs)  1.82 us
    unnamed x8, local copies, waits for them, and re-layouts  1.37 us
  transfers between devices with their start and end apart: 18, of which 5 were waited for; matrix products, arithmetic and copies ran while one was open for 10% of the time, Pallas kernels for 14%

profile of v8, /device:TPU:0, one launch (start us, length us, event | category | flops | bytes accessed | tf_op | source)
XLA Modules:
  0.0 62.3 jit_solution(13193106203118423078)
XLA Ops:
  0.0 2.0 %pack.1 = (f32[26,16,128]{2,1,0:T(8,128)S(1)}, f32[26,16,128]{2,1,0:T(8,128)S(1)}, f32[26,16,128]{2,1,0:T(8,128)S(1)}, f32[26,16,128]{2,1,0:T(8,128)S(1)}, f32[2...) custom-call(s32[1]{0:T(128)} %bitcast.j_ref, ...), custom_call_target="tpu_custom_call" | custom-call | tf_op jit(solution)/shard_map/pack/pallas_call | solution.py:109
  2.0 0.5 collective-permute-start
  2.5 2.6 %collective-permute-start.2 = (f32[416,128]{1,0:T(8,128)S(1)}, f32[416,128]{1,0:T(8,128)S(1)}, u32[]{:S(2)}, u32[]{:S(2)}) collective-permute-start(f32[416,128]{1,0:T(8,128)S(1)} %bitcast.43), channel_id=1, source_target_pairs={{0,4},{1,5},{2,6},{3,7},{4,0},{5,1},{6,2},{7,3},{8,12},{9,13},{10,... | collective-permute-start | bytes 638984 | tf_op jit(solution)/shard_map/ppermute | solution.py:327
  5.1 1.5 %collective-permute-start.3 = (f32[416,128]{1,0:T(8,128)S(1)}, f32[416,128]{1,0:T(8,128)S(1)}, u32[]{:S(2)}, u32[]{:S(2)}) collective-permute-start(f32[416,128]{1,0:T(8,128)S(1)} %bitcast.44), channel_id=1, source_target_pairs={{0,2},{1,3},{2,0},{3,1},{4,6},{5,7},{6,4},{7,5},{8,10},{9,11},{10,... | collective-permute-start | bytes 638984 | tf_op jit(solution)/shard_map/ppermute | solution.py:327
  6.6 0.0 collective-permute-start.4
  6.6 0.7 %slice.29 = f32[23,16,128]{2,1,0:T(8,128)} slice(f32[26,16,128]{2,1,0:T(8,128)S(1)} %get-tuple-element.37), slice={[0:23], [0:16], [0:128]} | slice | bytes 376832 | tf_op jit(solution)/shard_map/slice | solution.py:336
  7.3 1.3 %collective-permute-start.5 = (f32[1,368,128]{2,1,0:T(8,128)}, f32[1,368,128]{2,1,0:T(8,128)S(1)}, u32[]{:S(2)}, u32[]{:S(2)}) collective-permute-start(f32[1,368,128]{2,1,0:T(8,128)} %bitcast.12), channel_id=1, source_target_pairs={{4,12},{5,13},{6,14},{7,15},{8,0},{9,1},{10,2},{11,3},{12,20},{13,... | collective-permute-start | bytes 565256 | tf_op jit(solution)/shard_map/ppermute | solution.py:337
  8.6 0.1 iota_compare_fusion.9
  8.7 0.0 copy-done.2
  8.7 0.1 broadcast_in_dim.136
  8.8 0.1 select_reduce_fusion.9
  8.9 0.1 reshape.114
  9.0 0.0 copy-done.1
  9.0 0.2 copy.10
  9.2 1.2 %copy.9 = s32[7,84,84]{1,2,0:T(8,128)S(1)} copy(s32[7,84,84]{2,1,0:T(8,128)} %param.9) | data formatting | bytes 395136 | tf_op args[3]
  10.3 0.0 collective-permute-done.refs_5_.refs_1_
  10.4 2.7 %collective-permute-start.1 = (f32[416,128]{1,0:T(8,128)S(1)}, f32[416,128]{1,0:T(8,128)S(1)}, u32[]{:S(2)}, u32[]{:S(2)}) collective-permute-start(f32[416,128]{1,0:T(8,128)S(1)} %bitcast.42), channel_id=1, source_target_pairs={{0,5},{1,4},{2,7},{3,6},{4,1},{5,0},{6,3},{7,2},{8,13},{9,12},{10,... | collective-permute-start | bytes 638984 | tf_op jit(solution)/shard_map/ppermute | solution.py:327
  13.1 3.1 %collective-permute-done.4.refs_7_.refs_3_ = f32[416,128]{1,0:T(8,128)S(1)} collective-permute-done((f32[416,128]{1,0:T(8,128)S(1)}, f32[416,128]{1,0:T(8,128)S(1)}, u32[]{:S(2)}, u32[]{:S(2)}) %collective-permute-start.4) | collective-permute-done | bytes 213024 | tf_op jit(solution)/shard_map/ppermute | solution.py:327
  16.2 0.0 collective-permute-done.3.refs_6_.refs_2_
  16.2 0.8 %pad_maximum_fusion = f32[3,368,128]{2,1,0:T(8,128)} fusion(f32[1,368,128]{2,1,0:T(8,128)S(1)} %slice_bitcast_fusion.3, f32[1,368,128]{2,1,0:T(8,128)S(1)} %slice_bitcast_fusion.4, f32[1,368,128]{2,1,0:T(8,128)S(1)} %slice_bitcast_fusion.5), kind=kLoop, calls=%fused_computation | loop fusion | flops 282624 | bytes 1130496 | tf_op jit(solution)/shard_map/stack | solution.py:336
  17.1 1.3 %collective-permute-start.8 = (f32[3,368,128]{2,1,0:T(8,128)}, f32[3,368,128]{2,1,0:T(8,128)S(1)}, u32[]{:S(2)}, u32[]{:S(2)}) collective-permute-start(f32[3,368,128]{2,1,0:T(8,128)} %pad_maximum_fusion), channel_id=1, source_target_pairs={{4,12},{5,13},{6,14},{7,15},{8,0},{9,1},{10,2},{11,3},{12,20},{13,... | collective-permute-start | bytes 1695752 | tf_op jit(solution)/shard_map/ppermute | solution.py:337
  18.4 0.0 collective-permute-done.2.refs_0_.refs_4_
  18.4 0.7 %slice_bitcast_fusion.2 = f32[1,368,128]{2,1,0:T(8,128)} fusion(f32[416,128]{1,0:T(8,128)S(1)} %collective-permute-done.2.refs_0_.refs_4_), kind=kLoop, calls=%fused_computation.25 | loop fusion | bytes 376832 | tf_op jit(solution)/shard_map/stack | solution.py:336
  19.1 0.0 collective-permute-done.5.refs_8_
  19.1 0.0 collective-permute-done.1.refs_1_.refs_5_
  19.1 3.9 %collective-permute-start.7 = (f32[416,128]{1,0:T(8,128)S(1)}, f32[416,128]{1,0:T(8,128)S(1)}, u32[]{:S(2)}, u32[]{:S(2)}) collective-permute-start(f32[416,128]{1,0:T(8,128)S(1)} %bitcast.40), channel_id=1, source_target_pairs={{0,7},{1,6},{2,5},{3,4},{4,3},{5,2},{6,1},{7,0},{8,15},{9,14},{10,... | collective-permute-start | bytes 638984 | tf_op jit(solution)/shard_map/ppermute | solution.py:327
  23.0 0.0 collective-permute-start.6
  23.0 0.3 fusion
  23.4 0.3 fusion.10
  23.7 0.1 fusion.6
  23.8 0.1 select_reduce_fusion.1
  24.0 0.1 select_reduce_fusion.6
  24.1 0.1 copy.12
  24.2 0.1 reshape.119.factor_ref
  24.3 0.2 select_reduce_fusion.3
  24.6 0.1 broadcast_add_fusion.1
  24.7 0.1 copy.11
  24.8 0.1 reshape.118.take_ref
  24.9 0.2 select_reduce_fusion.5
  25.1 0.1 reshape.117.source_ref
  25.2 3.8 %collective-permute-start.11 = (f32[2,368,128]{2,1,0:T(8,128)S(1)}, f32[2,368,128]{2,1,0:T(8,128)S(1)}, u32[]{:S(2)}, u32[]{:S(2)}) collective-permute-start(f32[2,368,128]{2,1,0:T(8,128)S(1)} %pad_maximum_fusion.1), channel_id=1, source_target_pairs={{0,8},{1,9},{2,10},{3,11},{8,16},{9,17},{10,18},{11,19},{12,4},{13... | collective-permute-start | bytes 1130504 | tf_op jit(solution)/shard_map/ppermute | solution.py:337
  29.0 4.4 %collective-permute-done.6.refs_2_.refs_6_ = f32[416,128]{1,0:T(8,128)S(1)} collective-permute-done((f32[416,128]{1,0:T(8,128)S(1)}, f32[416,128]{1,0:T(8,128)S(1)}, u32[]{:S(2)}, u32[]{:S(2)}) %collective-permute-start.6) | collective-permute-done | bytes 213024 | tf_op jit(solution)/shard_map/ppermute | solution.py:327
  33.4 0.0 collective-permute-done.7.refs_3_.refs_7_
  33.5 3.5 %collective-permute-start.12 = (f32[2,368,128]{2,1,0:T(8,128)S(1)}, f32[2,368,128]{2,1,0:T(8,128)S(1)}, u32[]{:S(2)}, u32[]{:S(2)}) collective-permute-start(f32[2,368,128]{2,1,0:T(8,128)S(1)} %pad_maximum_fusion.2), channel_id=1, source_target_pairs={{0,8},{1,9},{2,10},{3,11},{8,16},{9,17},{10,18},{11,19},{12,4},{13... | collective-permute-start | bytes 1130504 | tf_op jit(solution)/shard_map/ppermute | solution.py:337
  37.0 0.0 collective-permute-done.8.refs_9_
  37.0 4.4 %stencil_crossing.1 = (f32[21,16,128]{2,1,0:T(8,128)S(1)}, f32[21,16,128]{2,1,0:T(8,128)S(1)}, f32[21,16,128]{2,1,0:T(8,128)S(1)}, f32[21,16,128]{2,1,0:T(8,128)S(1)}) custom-call(s32[1]{0:T(128)} %bitcast.j_ref, s32[294]{0:T(512)S(1)} %reshape.117.source_ref, s32[672]{0:T(1024)S(1)} %reshape.118.take_ref, f32[672]{0:T(1024)S(1)} %reshape.119.factor_ref, ...), custom_call_target="tpu_custom_call" | custom-call | tf_op jit(solution)/shard_map/stencil_crossing/pallas_call | solution.py:282
  41.4 0.1 collective-permute-start.10
  41.5 1.8 %collective-permute-start.9 = (f32[21,16,128]{2,1,0:T(8,128)S(1)}, f32[21,16,128]{2,1,0:T(8,128)S(1)}, u32[]{:S(2)}, u32[]{:S(2)}) collective-permute-start(f32[21,16,128]{2,1,0:T(8,128)S(1)} %get-tuple-element.42), channel_id=1, source_target_pairs={{0,6},{1,7},{2,4},{3,5},{4,2},{5,3},{6,0},{7,1},{8,14},{9,15},{10,... | collective-permute-start | bytes 516104 | tf_op jit(solution)/shard_map/ppermute | solution.py:327
  43.3 0.0 collective-permute-done.11.refs_8_
  43.3 1.8 %collective-permute-done.12.refs_9_ = f32[2,368,128]{2,1,0:T(8,128)S(1)} collective-permute-done((f32[2,368,128]{2,1,0:T(8,128)S(1)}, f32[2,368,128]{2,1,0:T(8,128)S(1)}, u32[]{:S(2)}, u32[]{:S(2)}) %collective-permute-start.12) | collective-permute-done | bytes 376864 | tf_op jit(solution)/shard_map/ppermute | solution.py:337
  45.1 4.4 %stencil_own.1 = (f32[21,16,128]{2,1,0:T(8,128)S(1)}, f32[21,16,128]{2,1,0:T(8,128)S(1)}, f32[21,16,128]{2,1,0:T(8,128)S(1)}, f32[21,16,128]{2,1,0:T(8,128)S(1)}) custom-call(s32[1]{0:T(128)} %bitcast.j_ref, s32[294]{0:T(512)S(1)} %reshape.117.source_ref, s32[672]{0:T(1024)S(1)} %reshape.118.take_ref, f32[672]{0:T(1024)S(1)} %reshape.119.factor_ref, ...), custom_call_target="tpu_custom_call" | custom-call | tf_op jit(solution)/shard_map/stencil_own/pallas_call | solution.py:282
  49.5 1.3 %collective-permute-start.13 = (f32[21,16,128]{2,1,0:T(8,128)S(1)}, f32[21,16,128]{2,1,0:T(8,128)S(1)}, u32[]{:S(2)}, u32[]{:S(2)}) collective-permute-start(f32[21,16,128]{2,1,0:T(8,128)S(1)} %get-tuple-element.47), channel_id=1, source_target_pairs={{0,2},{1,3},{2,0},{3,1},{4,6},{5,7},{6,4},{7,5},{8,10},{9,11},{10,... | collective-permute-start | bytes 516104 | tf_op jit(solution)/shard_map/ppermute | solution.py:327
  50.8 0.9 %collective-permute-start.16 = (f32[21,16,128]{2,1,0:T(8,128)S(1)}, f32[21,16,128]{2,1,0:T(8,128)S(1)}, u32[]{:S(2)}, u32[]{:S(2)}) collective-permute-start(f32[21,16,128]{2,1,0:T(8,128)S(1)} %get-tuple-element.52), channel_id=1, source_target_pairs={{0,5},{1,4},{2,7},{3,6},{4,1},{5,0},{6,3},{7,2},{8,13},{9,12},{10,... | collective-permute-start | bytes 516104 | tf_op jit(solution)/shard_map/ppermute | solution.py:327
  51.7 1.7 %collective-permute-start.14 = (f32[21,16,128]{2,1,0:T(8,128)S(1)}, f32[21,16,128]{2,1,0:T(8,128)S(1)}, u32[]{:S(2)}, u32[]{:S(2)}) collective-permute-start(f32[21,16,128]{2,1,0:T(8,128)S(1)} %get-tuple-element.51), channel_id=1, source_target_pairs={{0,4},{1,5},{2,6},{3,7},{4,0},{5,1},{6,2},{7,3},{8,12},{9,13},{10,... | collective-permute-start | bytes 516104 | tf_op jit(solution)/shard_map/ppermute | solution.py:327
  53.4 0.0 collective-permute-done.10.refs_1_
  53.4 0.2 collective-permute-start.15
  53.6 0.0 collective-permute-done.9.refs_0_
  53.6 0.4 collective-permute-start.17
  54.1 2.3 %collective-permute-done.16.refs_5_ = f32[21,16,128]{2,1,0:T(8,128)S(1)} collective-permute-done((f32[21,16,128]{2,1,0:T(8,128)S(1)}, f32[21,16,128]{2,1,0:T(8,128)S(1)}, u32[]{:S(2)}, u32[]{:S(2)}) %collective-permute-start.16) | collective-permute-done | bytes 172064 | tf_op jit(solution)/shard_map/ppermute | solution.py:327
  56.3 4.8 %collective-permute-done.14.refs_3_ = f32[21,16,128]{2,1,0:T(8,128)S(1)} collective-permute-done((f32[21,16,128]{2,1,0:T(8,128)S(1)}, f32[21,16,128]{2,1,0:T(8,128)S(1)}, u32[]{:S(2)}, u32[]{:S(2)}) %collective-permute-start.14) | collective-permute-done | bytes 172064 | tf_op jit(solution)/shard_map/ppermute | solution.py:327
  61.2 0.0 collective-permute-done.13.refs_2_
  61.2 0.0 collective-permute-done.15.refs_4_
  61.2 0.0 collective-permute-done.17.refs_7_
  61.2 1.1 %unpack.1 = f32[21,128,128]{2,1,0:T(8,128)} custom-call(s32[1]{0:T(128)} %bitcast.j_ref, f32[21,16,128]{2,1,0:T(8,128)S(1)} %collective-permute-done.9.refs_0_, f32[21,16,128]{2,1,0:T(8,128)S(1)} %collective-permute-done.10.refs_1_, f32[21,16,128]{2,1,0:T(8,128)S(1)} %collective-permute-done.13.refs_2_, f32[21,16,128]{2,1,0:T(8,128)S(1)} %collective-permute-done.14.refs_3_, ...), custom_call_target="tpu_custom_call" | custom-call | tf_op jit(solution)/shard_map/unpack/pallas_call | solution.py:140
  (22 shorter events, 0.3 us)
Async XLA Ops:
  0.0 8.7 %copy-start.2 = (s32[84]{0:T(128)S(1)}, s32[84]{0:T(128)}, u32[]{:S(2)}) copy-start(s32[84]{0:T(128)} %param.11) | copy-start | bytes 1012
  0.0 9.0 %copy-start.1 = (f32[7,84,84]{2,1,0:T(8,128)S(1)}, f32[7,84,84]{2,1,0:T(8,128)}, u32[]{:S(2)}) copy-start(f32[7,84,84]{2,1,0:T(8,128)} %param.10) | copy-start | bytes 592708
  2.0 8.4 %collective-permute-start = (f32[416,128]{1,0:T(8,128)S(1)}, f32[416,128]{1,0:T(8,128)S(1)}, u32[]{:S(2)}, u32[]{:S(2)}) collective-permute-start(f32[416,128]{1,0:T(8,128)S(1)} %bitcast.46), channel_id=1, source_target_pairs={{0,1},{1,0},{2,3},{3,2},{4,5},{5,4},{6,7},{7,6},{8,9},{9,8},{10,11... | collective-permute-start | bytes 638984 | tf_op jit(solution)/shard_map/ppermute | solution.py:327
  2.5 15.9 %collective-permute-start.2 = (f32[416,128]{1,0:T(8,128)S(1)}, f32[416,128]{1,0:T(8,128)S(1)}, u32[]{:S(2)}, u32[]{:S(2)}) collective-permute-start(f32[416,128]{1,0:T(8,128)S(1)} %bitcast.43), channel_id=1, source_target_pairs={{0,4},{1,5},{2,6},{3,7},{4,0},{5,1},{6,2},{7,3},{8,12},{9,13},{10,... | collective-permute-start | bytes 638984 | tf_op jit(solution)/shard_map/ppermute | solution.py:327
  5.1 11.1 %collective-permute-start.3 = (f32[416,128]{1,0:T(8,128)S(1)}, f32[416,128]{1,0:T(8,128)S(1)}, u32[]{:S(2)}, u32[]{:S(2)}) collective-permute-start(f32[416,128]{1,0:T(8,128)S(1)} %bitcast.44), channel_id=1, source_target_pairs={{0,2},{1,3},{2,0},{3,1},{4,6},{5,7},{6,4},{7,5},{8,10},{9,11},{10,... | collective-permute-start | bytes 638984 | tf_op jit(solution)/shard_map/ppermute | solution.py:327
  6.6 9.6 %collective-permute-start.4 = (f32[416,128]{1,0:T(8,128)S(1)}, f32[416,128]{1,0:T(8,128)S(1)}, u32[]{:S(2)}, u32[]{:S(2)}) collective-permute-start(f32[416,128]{1,0:T(8,128)S(1)} %bitcast.45), channel_id=1, source_target_pairs={{0,3},{1,2},{2,1},{3,0},{4,7},{5,6},{6,5},{7,4},{8,11},{9,10},{10,... | collective-permute-start | bytes 638984 | tf_op jit(solution)/shard_map/ppermute | solution.py:327
  7.3 11.8 %collective-permute-start.5 = (f32[1,368,128]{2,1,0:T(8,128)}, f32[1,368,128]{2,1,0:T(8,128)S(1)}, u32[]{:S(2)}, u32[]{:S(2)}) collective-permute-start(f32[1,368,128]{2,1,0:T(8,128)} %bitcast.12), channel_id=1, source_target_pairs={{4,12},{5,13},{6,14},{7,15},{8,0},{9,1},{10,2},{11,3},{12,20},{13,... | collective-permute-start | bytes 565256 | tf_op jit(solution)/shard_map/ppermute | solution.py:337
  10.4 8.7 %collective-permute-start.1 = (f32[416,128]{1,0:T(8,128)S(1)}, f32[416,128]{1,0:T(8,128)S(1)}, u32[]{:S(2)}, u32[]{:S(2)}) collective-permute-start(f32[416,128]{1,0:T(8,128)S(1)} %bitcast.42), channel_id=1, source_target_pairs={{0,5},{1,4},{2,7},{3,6},{4,1},{5,0},{6,3},{7,2},{8,13},{9,12},{10,... | collective-permute-start | bytes 638984 | tf_op jit(solution)/shard_map/ppermute | solution.py:327
  17.1 19.9 %collective-permute-start.8 = (f32[3,368,128]{2,1,0:T(8,128)}, f32[3,368,128]{2,1,0:T(8,128)S(1)}, u32[]{:S(2)}, u32[]{:S(2)}) collective-permute-start(f32[3,368,128]{2,1,0:T(8,128)} %pad_maximum_fusion), channel_id=1, source_target_pairs={{4,12},{5,13},{6,14},{7,15},{8,0},{9,1},{10,2},{11,3},{12,20},{13,... | collective-permute-start | bytes 1695752 | tf_op jit(solution)/shard_map/ppermute | solution.py:337
  19.1 14.3 %collective-permute-start.7 = (f32[416,128]{1,0:T(8,128)S(1)}, f32[416,128]{1,0:T(8,128)S(1)}, u32[]{:S(2)}, u32[]{:S(2)}) collective-permute-start(f32[416,128]{1,0:T(8,128)S(1)} %bitcast.40), channel_id=1, source_target_pairs={{0,7},{1,6},{2,5},{3,4},{4,3},{5,2},{6,1},{7,0},{8,15},{9,14},{10,... | collective-permute-start | bytes 638984 | tf_op jit(solution)/shard_map/ppermute | solution.py:327
  23.0 10.4 %collective-permute-start.6 = (f32[416,128]{1,0:T(8,128)S(1)}, f32[416,128]{1,0:T(8,128)S(1)}, u32[]{:S(2)}, u32[]{:S(2)}) collective-permute-start(f32[416,128]{1,0:T(8,128)S(1)} %bitcast.41), channel_id=1, source_target_pairs={{0,6},{1,7},{2,4},{3,5},{4,2},{5,3},{6,0},{7,1},{8,14},{9,15},{10,... | collective-permute-start | bytes 638984 | tf_op jit(solution)/shard_map/ppermute | solution.py:327
  23.4 1.8 %copy-start = (f32[1,368,128]{2,1,0:T(8,128)S(1)}, f32[1,368,128]{2,1,0:T(8,128)}, u32[]{:S(2)}) copy-start(f32[1,368,128]{2,1,0:T(8,128)} %slice_bitcast_fusion.2) | copy-start | bytes 565252
  25.2 18.1 %collective-permute-start.11 = (f32[2,368,128]{2,1,0:T(8,128)S(1)}, f32[2,368,128]{2,1,0:T(8,128)S(1)}, u32[]{:S(2)}, u32[]{:S(2)}) collective-permute-start(f32[2,368,128]{2,1,0:T(8,128)S(1)} %pad_maximum_fusion.1), channel_id=1, source_target_pairs={{0,8},{1,9},{2,10},{3,11},{8,16},{9,17},{10,18},{11,19},{12,4},{13... | collective-permute-start | bytes 1130504 | tf_op jit(solution)/shard_map/ppermute | solution.py:337
  33.5 11.6 %collective-permute-start.12 = (f32[2,368,128]{2,1,0:T(8,128)S(1)}, f32[2,368,128]{2,1,0:T(8,128)S(1)}, u32[]{:S(2)}, u32[]{:S(2)}) collective-permute-start(f32[2,368,128]{2,1,0:T(8,128)S(1)} %pad_maximum_fusion.2), channel_id=1, source_target_pairs={{0,8},{1,9},{2,10},{3,11},{8,16},{9,17},{10,18},{11,19},{12,4},{13... | collective-permute-start | bytes 1130504 | tf_op jit(solution)/shard_map/ppermute | solution.py:337
  41.4 12.1 %collective-permute-start.10 = (f32[21,16,128]{2,1,0:T(8,128)S(1)}, f32[21,16,128]{2,1,0:T(8,128)S(1)}, u32[]{:S(2)}, u32[]{:S(2)}) collective-permute-start(f32[21,16,128]{2,1,0:T(8,128)S(1)} %get-tuple-element.43), channel_id=1, source_target_pairs={{0,7},{1,6},{2,5},{3,4},{4,3},{5,2},{6,1},{7,0},{8,15},{9,14},{10,... | collective-permute-start | bytes 516104 | tf_op jit(solution)/shard_map/ppermute | solution.py:327
  41.5 12.2 %collective-permute-start.9 = (f32[21,16,128]{2,1,0:T(8,128)S(1)}, f32[21,16,128]{2,1,0:T(8,128)S(1)}, u32[]{:S(2)}, u32[]{:S(2)}) collective-permute-start(f32[21,16,128]{2,1,0:T(8,128)S(1)} %get-tuple-element.42), channel_id=1, source_target_pairs={{0,6},{1,7},{2,4},{3,5},{4,2},{5,3},{6,0},{7,1},{8,14},{9,15},{10,... | collective-permute-start | bytes 516104 | tf_op jit(solution)/shard_map/ppermute | solution.py:327
  49.5 11.7 %collective-permute-start.13 = (f32[21,16,128]{2,1,0:T(8,128)S(1)}, f32[21,16,128]{2,1,0:T(8,128)S(1)}, u32[]{:S(2)}, u32[]{:S(2)}) collective-permute-start(f32[21,16,128]{2,1,0:T(8,128)S(1)} %get-tuple-element.47), channel_id=1, source_target_pairs={{0,2},{1,3},{2,0},{3,1},{4,6},{5,7},{6,4},{7,5},{8,10},{9,11},{10,... | collective-permute-start | bytes 516104 | tf_op jit(solution)/shard_map/ppermute | solution.py:327
  50.8 5.5 %collective-permute-start.16 = (f32[21,16,128]{2,1,0:T(8,128)S(1)}, f32[21,16,128]{2,1,0:T(8,128)S(1)}, u32[]{:S(2)}, u32[]{:S(2)}) collective-permute-start(f32[21,16,128]{2,1,0:T(8,128)S(1)} %get-tuple-element.52), channel_id=1, source_target_pairs={{0,5},{1,4},{2,7},{3,6},{4,1},{5,0},{6,3},{7,2},{8,13},{9,12},{10,... | collective-permute-start | bytes 516104 | tf_op jit(solution)/shard_map/ppermute | solution.py:327
  51.7 9.5 %collective-permute-start.14 = (f32[21,16,128]{2,1,0:T(8,128)S(1)}, f32[21,16,128]{2,1,0:T(8,128)S(1)}, u32[]{:S(2)}, u32[]{:S(2)}) collective-permute-start(f32[21,16,128]{2,1,0:T(8,128)S(1)} %get-tuple-element.51), channel_id=1, source_target_pairs={{0,4},{1,5},{2,6},{3,7},{4,0},{5,1},{6,2},{7,3},{8,12},{9,13},{10,... | collective-permute-start | bytes 516104 | tf_op jit(solution)/shard_map/ppermute | solution.py:327
  53.4 7.7 %collective-permute-start.15 = (f32[21,16,128]{2,1,0:T(8,128)S(1)}, f32[21,16,128]{2,1,0:T(8,128)S(1)}, u32[]{:S(2)}, u32[]{:S(2)}) collective-permute-start(f32[21,16,128]{2,1,0:T(8,128)S(1)} %get-tuple-element.50), channel_id=1, source_target_pairs={{0,3},{1,2},{2,1},{3,0},{4,7},{5,6},{6,5},{7,4},{8,11},{9,10},{10,... | collective-permute-start | bytes 516104 | tf_op jit(solution)/shard_map/ppermute | solution.py:327
  53.6 7.5 %collective-permute-start.17 = (f32[21,16,128]{2,1,0:T(8,128)S(1)}, f32[21,16,128]{2,1,0:T(8,128)S(1)}, u32[]{:S(2)}, u32[]{:S(2)}) collective-permute-start(f32[21,16,128]{2,1,0:T(8,128)S(1)} %get-tuple-element.49), channel_id=1, source_target_pairs={{0,1},{1,0},{2,3},{3,2},{4,5},{5,4},{6,7},{7,6},{8,9},{9,8},{10,11... | collective-permute-start | bytes 516104 | tf_op jit(solution)/shard_map/ppermute | solution.py:327

commit v9 on v8

--- a/solution.py
+++ b/solution.py
@@ -340,21 +340,18 @@
     sent = pack(field, mean_field, kl, j, lay)
     half = modes // 2
     pieces = sent[:1] + [None] * (lay.group - 1)
-    for r in [modes, half, *range(1, half), *range(half + 1, modes)]:
+    for r in [half, modes, *range(half + 1, modes), *range(modes + 1, modes + half), *range(1, half)]:
         pieces[r] = swap(sent[r], r)
-    for r in range(modes + 1, modes + half):
-        pieces[r] = swap(after(sent[r], *pieces[1:half]), r)
     halos = [shift(pieces[:1], False)]
     for r in range(modes + half, lay.group):
-        pieces[r] = swap(after(sent[r], *pieces[half : modes + half], halos[0]), r)
+        pieces[r] = swap(after(sent[r], *pieces[half:modes], halos[0]), r)
     number = jnp.arange(modes, dtype=jnp.int32)
     mine = jnp.bitwise_xor(number, mode)[:, None, None] == number[None, :, None]
     slot_mode = jnp.sum(jnp.where(mine, slot_mode.reshape(1, modes, quota), 0), 1).reshape(-1)
-    lists = coupling_lists(pattern, coupling, after(slot_mode, pieces[modes + 1]))
+    lists = coupling_lists(pattern, coupling, after(slot_mode, pieces[modes]))
     pieces[modes + half] = after(pieces[modes + half], *lists)
     halos.append(shift(pieces[1:modes], False))
-    halos.append(shift(pieces[modes : modes + half], True))
-    halos.append(shift(pieces[modes + half :], True))
+    halos += [shift(pieces[r : r + half], True) for r in (modes, modes + half)]
 
     own, crossing = pieces[:modes], pieces[modes:]
     crossing_out = stencil(crossing, own, halos[:2], lists, j, "stencil_crossing", lay)

time: 62.6 us -> 60.8 us (0.971)
  other arithmetic: 1.98 us -> 1.17 us
  local copies, waits for them, and re-layouts: 3.44 us -> 2.77 us
    ppermute x4, waiting for transfers between devices: 1.82 us -> 5.39 us  [shift(): return lax.ppermute(main, axes, pairs)]
    ppermute x14, waiting for transfers between devices: 14.6 us -> 11.1 us  [swap(): return lax.ppermute(piece, axes, [(d, d ^ r) for d in range(devices)])]
    ppermute x14, starting transfers between devices: 17.7 us -> 15.8 us  [swap(): return lax.ppermute(piece, axes, [(d, d ^ r) for d in range(devices)])]
    ppermute x4, starting transfers between devices: 9.81 us -> 11.3 us  [shift(): return lax.ppermute(main, axes, pairs)]
    another operation x3, other arithmetic: 0.9 us -> 0.09 us  [shift(): main = jnp.stack([piece[:lay.main] for piece in pieces])]
    another operation x7, local copies, waits for them, and re-layouts: 0.77 us -> 0.1 us  [shift(): main = jnp.stack([piece[:lay.main] for piece in pieces])]
    unnamed x8 -> x6, local copies, waits for them, and re-layouts: 1.37 us -> 1.36 us
  transfers between devices with their start and end apart: 18 -> 18, of which waited for: 5 -> 8; matrix products, arithmetic and copies ran while one was open for 10% -> 8% of each run, Pallas kernels for 14% -> 15%
where the time goes in v9:
time: 60.8 us; the launch traced here: 60.5 us
  starting transfers between devices  27.2 us (45%)
  waiting for transfers between devices  16.5 us (27%)
  Pallas kernels  12 us (20%)
  local copies, waits for them, and re-layouts  2.77 us (5%)
  other arithmetic  1.17 us (2%)
  matrix products  0.68 us (1%)
    ppermute x14, starting transfers between devices, swap(): return lax.ppermute(piece, axes, [(d, d ^ r) for d in range(devices)])  15.8 us
    ppermute x4, starting transfers between devices, shift(): return lax.ppermute(main, axes, pairs)  11.3 us
    ppermute x14, waiting for transfers between devices, swap(): return lax.ppermute(piece, axes, [(d, d ^ r) for d in range(devices)])  11.1 us
    pallas_call x2, Pallas kernels, stencil(): pl.pallas_call(kernel, out_shape=[jax.ShapeDtypeStruct((lay.quota, rows,...  8.84 us
    ppermute x4, waiting for transfers between devices, shift(): return lax.ppermute(main, axes, pairs)  5.39 us
    pallas_call x1, Pallas kernels, pack(): pl.pallas_call(kernel, out_shape=[pltpu.VMEM(shape, jnp.float32)] * lay.g...  1.97 us
    unnamed x6, local copies, waits for them, and re-layouts  1.36 us
  transfers between devices with their start and end apart: 18, of which 8 were waited for; matrix products, arithmetic and copies ran while one was open for 8% of the time, Pallas kernels for 15%

profile of v9, /device:TPU:0, one launch (start us, length us, event | category | flops | bytes accessed | tf_op | source)
XLA Modules:
  0.0 60.5 jit_solution(18298166616818406104)
XLA Ops:
  0.0 0.0 copy-start.1
  0.0 0.0 copy-start
  0.0 2.0 %pack.1 = (f32[26,16,128]{2,1,0:T(8,128)S(1)}, f32[26,16,128]{2,1,0:T(8,128)S(1)}, f32[26,16,128]{2,1,0:T(8,128)S(1)}, f32[26,16,128]{2,1,0:T(8,128)S(1)}, f32[2...) custom-call(s32[1]{0:T(128)} %bitcast.j_ref, ...), custom_call_target="tpu_custom_call" | custom-call | tf_op jit(solution)/shard_map/pack/pallas_call | solution.py:109
  2.0 3.0 %collective-permute-start = (f32[416,128]{1,0:T(8,128)S(1)}, f32[416,128]{1,0:T(8,128)S(1)}, u32[]{:S(2)}, u32[]{:S(2)}) collective-permute-start(f32[416,128]{1,0:T(8,128)S(1)} %bitcast.46), channel_id=1, source_target_pairs={{0,4},{1,5},{2,6},{3,7},{4,0},{5,1},{6,2},{7,3},{8,12},{9,13},{10,... | collective-permute-start | bytes 638984 | tf_op jit(solution)/shard_map/ppermute | solution.py:327
  5.0 1.5 %collective-permute-start.2 = (f32[416,128]{1,0:T(8,128)S(1)}, f32[416,128]{1,0:T(8,128)S(1)}, u32[]{:S(2)}, u32[]{:S(2)}) collective-permute-start(f32[416,128]{1,0:T(8,128)S(1)} %bitcast.45), channel_id=1, source_target_pairs={{0,2},{1,3},{2,0},{3,1},{4,6},{5,7},{6,4},{7,5},{8,10},{9,11},{10,... | collective-permute-start | bytes 638984 | tf_op jit(solution)/shard_map/ppermute | solution.py:327
  6.5 0.0 collective-permute-start.3
  6.5 0.7 %slice.29 = f32[23,16,128]{2,1,0:T(8,128)} slice(f32[26,16,128]{2,1,0:T(8,128)S(1)} %get-tuple-element.34), slice={[0:23], [0:16], [0:128]} | slice | bytes 376832 | tf_op jit(solution)/shard_map/slice | solution.py:336
  7.2 1.3 %collective-permute-start.4 = (f32[1,368,128]{2,1,0:T(8,128)}, f32[1,368,128]{2,1,0:T(8,128)S(1)}, u32[]{:S(2)}, u32[]{:S(2)}) collective-permute-start(f32[1,368,128]{2,1,0:T(8,128)} %bitcast.11), channel_id=1, source_target_pairs={{4,12},{5,13},{6,14},{7,15},{8,0},{9,1},{10,2},{11,3},{12,20},{13,... | collective-permute-start | bytes 565256 | tf_op jit(solution)/shard_map/ppermute | solution.py:337
  8.5 0.7 %collective-permute-start.7 = (f32[416,128]{1,0:T(8,128)S(1)}, f32[416,128]{1,0:T(8,128)S(1)}, u32[]{:S(2)}, u32[]{:S(2)}) collective-permute-start(f32[416,128]{1,0:T(8,128)S(1)} %bitcast.43), channel_id=1, source_target_pairs={{0,1},{1,0},{2,3},{3,2},{4,5},{5,4},{6,7},{7,6},{8,9},{9,8},{10,11... | collective-permute-start | bytes 638984 | tf_op jit(solution)/shard_map/ppermute | solution.py:327
  9.2 0.1 iota_compare_fusion.9
  9.3 0.0 copy-done.1
  9.3 0.1 broadcast_in_dim.136
  9.4 0.1 select_reduce_fusion.9
  9.4 0.1 reshape.114
  9.5 0.0 copy-done
  9.5 0.2 copy.10
  9.7 1.2 %copy.9 = s32[7,84,84]{1,2,0:T(8,128)S(1)} copy(s32[7,84,84]{2,1,0:T(8,128)} %param.9) | data formatting | bytes 395136 | tf_op args[3]
  10.9 0.0 collective-permute-done.refs_0_.refs_4_
  10.9 2.3 %collective-permute-start.1 = (f32[416,128]{1,0:T(8,128)S(1)}, f32[416,128]{1,0:T(8,128)S(1)}, u32[]{:S(2)}, u32[]{:S(2)}) collective-permute-start(f32[416,128]{1,0:T(8,128)S(1)} %bitcast.42), channel_id=1, source_target_pairs={{0,5},{1,4},{2,7},{3,6},{4,1},{5,0},{6,3},{7,2},{8,13},{9,12},{10,... | collective-permute-start | bytes 638984 | tf_op jit(solution)/shard_map/ppermute | solution.py:327
  13.2 0.3 fusion
  13.6 0.3 fusion.10
  13.9 0.1 fusion.6
  14.0 0.1 select_reduce_fusion.1
  14.2 0.1 select_reduce_fusion.6
  14.3 0.1 copy.12
  14.4 0.1 reshape.118.factor_ref
  14.5 0.2 select_reduce_fusion.3
  14.8 0.1 broadcast_add_fusion.1
  14.9 0.1 copy.11
  15.0 0.1 reshape.117.take_ref
  15.1 0.2 select_reduce_fusion.5
  15.2 0.1 reshape.116.source_ref
  15.3 1.2 %collective-permute-done.4.refs_8_ = f32[1,368,128]{2,1,0:T(8,128)S(1)} collective-permute-done((f32[1,368,128]{2,1,0:T(8,128)}, f32[1,368,128]{2,1,0:T(8,128)S(1)}, u32[]{:S(2)}, u32[]{:S(2)}) %collective-permute-start.4) | collective-permute-done | bytes 188448 | tf_op jit(solution)/shard_map/ppermute | solution.py:337
  16.6 0.0 collective-permute-done.2.refs_6_.refs_2_
  16.6 0.0 collective-permute-done.3.refs_7_.refs_3_
  16.6 0.2 collective-permute-start.5
  16.7 2.0 %collective-permute-start.6 = (f32[416,128]{1,0:T(8,128)S(1)}, f32[416,128]{1,0:T(8,128)S(1)}, u32[]{:S(2)}, u32[]{:S(2)}) collective-permute-start(f32[416,128]{1,0:T(8,128)S(1)} %bitcast.40), channel_id=1, source_target_pairs={{0,7},{1,6},{2,5},{3,4},{4,3},{5,2},{6,1},{7,0},{8,15},{9,14},{10,... | collective-permute-start | bytes 638984 | tf_op jit(solution)/shard_map/ppermute | solution.py:327
  18.7 0.0 collective-permute-done.7.refs_5_.refs_1_
  18.8 1.3 %collective-permute-start.8 = (f32[3,368,128]{2,1,0:T(8,128)S(1)}, f32[3,368,128]{2,1,0:T(8,128)S(1)}, u32[]{:S(2)}, u32[]{:S(2)}) collective-permute-start(f32[3,368,128]{2,1,0:T(8,128)S(1)} %pad_maximum_fusion), channel_id=1, source_target_pairs={{4,12},{5,13},{6,14},{7,15},{8,0},{9,1},{10,2},{11,3},{12,20},{13,... | collective-permute-start | bytes 1695752 | tf_op jit(solution)/shard_map/ppermute | solution.py:337
  20.1 0.0 collective-permute-done.1.refs_1_.refs_5_
  20.2 4.6 %collective-permute-start.11 = (f32[2,368,128]{2,1,0:T(8,128)S(1)}, f32[2,368,128]{2,1,0:T(8,128)S(1)}, u32[]{:S(2)}, u32[]{:S(2)}) collective-permute-start(f32[2,368,128]{2,1,0:T(8,128)S(1)} %pad_maximum_fusion.1), channel_id=1, source_target_pairs={{0,8},{1,9},{2,10},{3,11},{8,16},{9,17},{10,18},{11,19},{12,4},{13... | collective-permute-start | bytes 1130504 | tf_op jit(solution)/shard_map/ppermute | solution.py:337
  24.8 0.8 %collective-permute-done.5.refs_2_.refs_6_ = f32[416,128]{1,0:T(8,128)S(1)} collective-permute-done((f32[416,128]{1,0:T(8,128)S(1)}, f32[416,128]{1,0:T(8,128)S(1)}, u32[]{:S(2)}, u32[]{:S(2)}) %collective-permute-start.5) | collective-permute-done | bytes 213024 | tf_op jit(solution)/shard_map/ppermute | solution.py:327
  25.6 2.3 %collective-permute-done.6.refs_3_.refs_7_ = f32[416,128]{1,0:T(8,128)S(1)} collective-permute-done((f32[416,128]{1,0:T(8,128)S(1)}, f32[416,128]{1,0:T(8,128)S(1)}, u32[]{:S(2)}, u32[]{:S(2)}) %collective-permute-start.6) | collective-permute-done | bytes 213024 | tf_op jit(solution)/shard_map/ppermute | solution.py:327
  28.0 4.2 %collective-permute-start.12 = (f32[2,368,128]{2,1,0:T(8,128)S(1)}, f32[2,368,128]{2,1,0:T(8,128)S(1)}, u32[]{:S(2)}, u32[]{:S(2)}) collective-permute-start(f32[2,368,128]{2,1,0:T(8,128)S(1)} %pad_maximum_fusion.2), channel_id=1, source_target_pairs={{0,8},{1,9},{2,10},{3,11},{8,16},{9,17},{10,18},{11,19},{12,4},{13... | collective-permute-start | bytes 1130504 | tf_op jit(solution)/shard_map/ppermute | solution.py:337
  32.2 4.2 %collective-permute-done.8.refs_9_ = f32[3,368,128]{2,1,0:T(8,128)S(1)} collective-permute-done((f32[3,368,128]{2,1,0:T(8,128)S(1)}, f32[3,368,128]{2,1,0:T(8,128)S(1)}, u32[]{:S(2)}, u32[]{:S(2)}) %collective-permute-start.8) | collective-permute-done | bytes 565280 | tf_op jit(solution)/shard_map/ppermute | solution.py:337
  36.3 4.4 %stencil_crossing.1 = (f32[21,16,128]{2,1,0:T(8,128)S(1)}, f32[21,16,128]{2,1,0:T(8,128)S(1)}, f32[21,16,128]{2,1,0:T(8,128)S(1)}, f32[21,16,128]{2,1,0:T(8,128)S(1)}) custom-call(s32[1]{0:T(128)} %bitcast.j_ref, s32[294]{0:T(512)S(1)} %reshape.116.source_ref, s32[672]{0:T(1024)S(1)} %reshape.117.take_ref, f32[672]{0:T(1024)S(1)} %reshape.118.factor_ref, ...), custom_call_target="tpu_custom_call" | custom-call | tf_op jit(solution)/shard_map/stencil_crossing/pallas_call | solution.py:282
  40.7 0.1 collective-permute-start.10
  40.8 2.6 %collective-permute-start.9 = (f32[21,16,128]{2,1,0:T(8,128)S(1)}, f32[21,16,128]{2,1,0:T(8,128)S(1)}, u32[]{:S(2)}, u32[]{:S(2)}) collective-permute-start(f32[21,16,128]{2,1,0:T(8,128)S(1)} %get-tuple-element.40), channel_id=1, source_target_pairs={{0,6},{1,7},{2,4},{3,5},{4,2},{5,3},{6,0},{7,1},{8,14},{9,15},{10,... | collective-permute-start | bytes 516104 | tf_op jit(solution)/shard_map/ppermute | solution.py:327
  43.4 0.0 collective-permute-done.11.refs_8_
  43.4 0.0 collective-permute-done.12.refs_9_
  43.4 4.4 %stencil_own.1 = (f32[21,16,128]{2,1,0:T(8,128)S(1)}, f32[21,16,128]{2,1,0:T(8,128)S(1)}, f32[21,16,128]{2,1,0:T(8,128)S(1)}, f32[21,16,128]{2,1,0:T(8,128)S(1)}) custom-call(s32[1]{0:T(128)} %bitcast.j_ref, s32[294]{0:T(512)S(1)} %reshape.116.source_ref, s32[672]{0:T(1024)S(1)} %reshape.117.take_ref, f32[672]{0:T(1024)S(1)} %reshape.118.factor_ref, ...), custom_call_target="tpu_custom_call" | custom-call | tf_op jit(solution)/shard_map/stencil_own/pallas_call | solution.py:282
  47.8 0.7 %collective-permute-start.13 = (f32[21,16,128]{2,1,0:T(8,128)S(1)}, f32[21,16,128]{2,1,0:T(8,128)S(1)}, u32[]{:S(2)}, u32[]{:S(2)}) collective-permute-start(f32[21,16,128]{2,1,0:T(8,128)S(1)} %get-tuple-element.45), channel_id=1, source_target_pairs={{0,2},{1,3},{2,0},{3,1},{4,6},{5,7},{6,4},{7,5},{8,10},{9,11},{10,... | collective-permute-start | bytes 516104 | tf_op jit(solution)/shard_map/ppermute | solution.py:327
  48.5 0.0 collective-permute-start.16
  48.5 1.9 %collective-permute-start.14 = (f32[21,16,128]{2,1,0:T(8,128)S(1)}, f32[21,16,128]{2,1,0:T(8,128)S(1)}, u32[]{:S(2)}, u32[]{:S(2)}) collective-permute-start(f32[21,16,128]{2,1,0:T(8,128)S(1)} %get-tuple-element.49), channel_id=1, source_target_pairs={{0,4},{1,5},{2,6},{3,7},{4,0},{5,1},{6,2},{7,3},{8,12},{9,13},{10,... | collective-permute-start | bytes 516104 | tf_op jit(solution)/shard_map/ppermute | solution.py:327
  50.4 0.0 collective-permute-done.10.refs_1_
  50.4 1.0 %collective-permute-start.15 = (f32[21,16,128]{2,1,0:T(8,128)S(1)}, f32[21,16,128]{2,1,0:T(8,128)S(1)}, u32[]{:S(2)}, u32[]{:S(2)}) collective-permute-start(f32[21,16,128]{2,1,0:T(8,128)S(1)} %get-tuple-element.48), channel_id=1, source_target_pairs={{0,3},{1,2},{2,1},{3,0},{4,7},{5,6},{6,5},{7,4},{8,11},{9,10},{10,... | collective-permute-start | bytes 516104 | tf_op jit(solution)/shard_map/ppermute | solution.py:327
  51.4 0.8 %collective-permute-done.9.refs_0_ = f32[21,16,128]{2,1,0:T(8,128)S(1)} collective-permute-done((f32[21,16,128]{2,1,0:T(8,128)S(1)}, f32[21,16,128]{2,1,0:T(8,128)S(1)}, u32[]{:S(2)}, u32[]{:S(2)}) %collective-permute-start.9) | collective-permute-done | bytes 172064 | tf_op jit(solution)/shard_map/ppermute | solution.py:327
  52.2 0.0 collective-permute-start.17
  52.2 2.6 %collective-permute-done.16.refs_5_ = f32[21,16,128]{2,1,0:T(8,128)S(1)} collective-permute-done((f32[21,16,128]{2,1,0:T(8,128)S(1)}, f32[21,16,128]{2,1,0:T(8,128)S(1)}, u32[]{:S(2)}, u32[]{:S(2)}) %collective-permute-start.16) | collective-permute-done | bytes 172064 | tf_op jit(solution)/shard_map/ppermute | solution.py:327
  54.8 4.1 %collective-permute-done.14.refs_3_ = f32[21,16,128]{2,1,0:T(8,128)S(1)} collective-permute-done((f32[21,16,128]{2,1,0:T(8,128)S(1)}, f32[21,16,128]{2,1,0:T(8,128)S(1)}, u32[]{:S(2)}, u32[]{:S(2)}) %collective-permute-start.14) | collective-permute-done | bytes 172064 | tf_op jit(solution)/shard_map/ppermute | solution.py:327
  58.9 0.0 collective-permute-done.13.refs_2_
  58.9 0.5 collective-permute-done.15.refs_4_
  59.4 0.0 collective-permute-done.17.refs_7_
  59.4 1.1 %unpack.1 = f32[21,128,128]{2,1,0:T(8,128)} custom-call(s32[1]{0:T(128)} %bitcast.j_ref, f32[21,16,128]{2,1,0:T(8,128)S(1)} %collective-permute-done.9.refs_0_, f32[21,16,128]{2,1,0:T(8,128)S(1)} %collective-permute-done.10.refs_1_, f32[21,16,128]{2,1,0:T(8,128)S(1)} %collective-permute-done.13.refs_2_, f32[21,16,128]{2,1,0:T(8,128)S(1)} %collective-permute-done.14.refs_3_, ...), custom_call_target="tpu_custom_call" | custom-call | tf_op jit(solution)/shard_map/unpack/pallas_call | solution.py:140
  (20 shorter events, 0.3 us)
Async XLA Ops:
  0.0 9.3 %copy-start.1 = (s32[84]{0:T(128)S(1)}, s32[84]{0:T(128)}, u32[]{:S(2)}) copy-start(s32[84]{0:T(128)} %param.11) | copy-start | bytes 1012
  0.0 9.5 %copy-start = (f32[7,84,84]{2,1,0:T(8,128)S(1)}, f32[7,84,84]{2,1,0:T(8,128)}, u32[]{:S(2)}) copy-start(f32[7,84,84]{2,1,0:T(8,128)} %param.10) | copy-start | bytes 592708
  2.0 8.9 %collective-permute-start = (f32[416,128]{1,0:T(8,128)S(1)}, f32[416,128]{1,0:T(8,128)S(1)}, u32[]{:S(2)}, u32[]{:S(2)}) collective-permute-start(f32[416,128]{1,0:T(8,128)S(1)} %bitcast.46), channel_id=1, source_target_pairs={{0,4},{1,5},{2,6},{3,7},{4,0},{5,1},{6,2},{7,3},{8,12},{9,13},{10,... | collective-permute-start | bytes 638984 | tf_op jit(solution)/shard_map/ppermute | solution.py:327
  5.0 11.6 %collective-permute-start.2 = (f32[416,128]{1,0:T(8,128)S(1)}, f32[416,128]{1,0:T(8,128)S(1)}, u32[]{:S(2)}, u32[]{:S(2)}) collective-permute-start(f32[416,128]{1,0:T(8,128)S(1)} %bitcast.45), channel_id=1, source_target_pairs={{0,2},{1,3},{2,0},{3,1},{4,6},{5,7},{6,4},{7,5},{8,10},{9,11},{10,... | collective-permute-start | bytes 638984 | tf_op jit(solution)/shard_map/ppermute | solution.py:327
  6.5 10.0 %collective-permute-start.3 = (f32[416,128]{1,0:T(8,128)S(1)}, f32[416,128]{1,0:T(8,128)S(1)}, u32[]{:S(2)}, u32[]{:S(2)}) collective-permute-start(f32[416,128]{1,0:T(8,128)S(1)} %bitcast.44), channel_id=1, source_target_pairs={{0,3},{1,2},{2,1},{3,0},{4,7},{5,6},{6,5},{7,4},{8,11},{9,10},{10,... | collective-permute-start | bytes 638984 | tf_op jit(solution)/shard_map/ppermute | solution.py:327
  7.2 9.3 %collective-permute-start.4 = (f32[1,368,128]{2,1,0:T(8,128)}, f32[1,368,128]{2,1,0:T(8,128)S(1)}, u32[]{:S(2)}, u32[]{:S(2)}) collective-permute-start(f32[1,368,128]{2,1,0:T(8,128)} %bitcast.11), channel_id=1, source_target_pairs={{4,12},{5,13},{6,14},{7,15},{8,0},{9,1},{10,2},{11,3},{12,20},{13,... | collective-permute-start | bytes 565256 | tf_op jit(solution)/shard_map/ppermute | solution.py:337
  8.5 10.2 %collective-permute-start.7 = (f32[416,128]{1,0:T(8,128)S(1)}, f32[416,128]{1,0:T(8,128)S(1)}, u32[]{:S(2)}, u32[]{:S(2)}) collective-permute-start(f32[416,128]{1,0:T(8,128)S(1)} %bitcast.43), channel_id=1, source_target_pairs={{0,1},{1,0},{2,3},{3,2},{4,5},{5,4},{6,7},{7,6},{8,9},{9,8},{10,11... | collective-permute-start | bytes 638984 | tf_op jit(solution)/shard_map/ppermute | solution.py:327
  10.9 9.2 %collective-permute-start.1 = (f32[416,128]{1,0:T(8,128)S(1)}, f32[416,128]{1,0:T(8,128)S(1)}, u32[]{:S(2)}, u32[]{:S(2)}) collective-permute-start(f32[416,128]{1,0:T(8,128)S(1)} %bitcast.42), channel_id=1, source_target_pairs={{0,5},{1,4},{2,7},{3,6},{4,1},{5,0},{6,3},{7,2},{8,13},{9,12},{10,... | collective-permute-start | bytes 638984 | tf_op jit(solution)/shard_map/ppermute | solution.py:327
  16.6 9.0 %collective-permute-start.5 = (f32[416,128]{1,0:T(8,128)S(1)}, f32[416,128]{1,0:T(8,128)S(1)}, u32[]{:S(2)}, u32[]{:S(2)}) collective-permute-start(f32[416,128]{1,0:T(8,128)S(1)} %bitcast.41), channel_id=1, source_target_pairs={{0,6},{1,7},{2,4},{3,5},{4,2},{5,3},{6,0},{7,1},{8,14},{9,15},{10,... | collective-permute-start | bytes 638984 | tf_op jit(solution)/shard_map/ppermute | solution.py:327
  16.7 11.2 %collective-permute-start.6 = (f32[416,128]{1,0:T(8,128)S(1)}, f32[416,128]{1,0:T(8,128)S(1)}, u32[]{:S(2)}, u32[]{:S(2)}) collective-permute-start(f32[416,128]{1,0:T(8,128)S(1)} %bitcast.40), channel_id=1, source_target_pairs={{0,7},{1,6},{2,5},{3,4},{4,3},{5,2},{6,1},{7,0},{8,15},{9,14},{10,... | collective-permute-start | bytes 638984 | tf_op jit(solution)/shard_map/ppermute | solution.py:327
  18.8 17.5 %collective-permute-start.8 = (f32[3,368,128]{2,1,0:T(8,128)S(1)}, f32[3,368,128]{2,1,0:T(8,128)S(1)}, u32[]{:S(2)}, u32[]{:S(2)}) collective-permute-start(f32[3,368,128]{2,1,0:T(8,128)S(1)} %pad_maximum_fusion), channel_id=1, source_target_pairs={{4,12},{5,13},{6,14},{7,15},{8,0},{9,1},{10,2},{11,3},{12,20},{13,... | collective-permute-start | bytes 1695752 | tf_op jit(solution)/shard_map/ppermute | solution.py:337
  20.2 23.2 %collective-permute-start.11 = (f32[2,368,128]{2,1,0:T(8,128)S(1)}, f32[2,368,128]{2,1,0:T(8,128)S(1)}, u32[]{:S(2)}, u32[]{:S(2)}) collective-permute-start(f32[2,368,128]{2,1,0:T(8,128)S(1)} %pad_maximum_fusion.1), channel_id=1, source_target_pairs={{0,8},{1,9},{2,10},{3,11},{8,16},{9,17},{10,18},{11,19},{12,4},{13... | collective-permute-start | bytes 1130504 | tf_op jit(solution)/shard_map/ppermute | solution.py:337
  28.0 15.5 %collective-permute-start.12 = (f32[2,368,128]{2,1,0:T(8,128)S(1)}, f32[2,368,128]{2,1,0:T(8,128)S(1)}, u32[]{:S(2)}, u32[]{:S(2)}) collective-permute-start(f32[2,368,128]{2,1,0:T(8,128)S(1)} %pad_maximum_fusion.2), channel_id=1, source_target_pairs={{0,8},{1,9},{2,10},{3,11},{8,16},{9,17},{10,18},{11,19},{12,4},{13... | collective-permute-start | bytes 1130504 | tf_op jit(solution)/shard_map/ppermute | solution.py:337
  40.7 9.7 %collective-permute-start.10 = (f32[21,16,128]{2,1,0:T(8,128)S(1)}, f32[21,16,128]{2,1,0:T(8,128)S(1)}, u32[]{:S(2)}, u32[]{:S(2)}) collective-permute-start(f32[21,16,128]{2,1,0:T(8,128)S(1)} %get-tuple-element.41), channel_id=1, source_target_pairs={{0,7},{1,6},{2,5},{3,4},{4,3},{5,2},{6,1},{7,0},{8,15},{9,14},{10,... | collective-permute-start | bytes 516104 | tf_op jit(solution)/shard_map/ppermute | solution.py:327
  40.8 11.4 %collective-permute-start.9 = (f32[21,16,128]{2,1,0:T(8,128)S(1)}, f32[21,16,128]{2,1,0:T(8,128)S(1)}, u32[]{:S(2)}, u32[]{:S(2)}) collective-permute-start(f32[21,16,128]{2,1,0:T(8,128)S(1)} %get-tuple-element.40), channel_id=1, source_target_pairs={{0,6},{1,7},{2,4},{3,5},{4,2},{5,3},{6,0},{7,1},{8,14},{9,15},{10,... | collective-permute-start | bytes 516104 | tf_op jit(solution)/shard_map/ppermute | solution.py:327
  47.8 11.0 %collective-permute-start.13 = (f32[21,16,128]{2,1,0:T(8,128)S(1)}, f32[21,16,128]{2,1,0:T(8,128)S(1)}, u32[]{:S(2)}, u32[]{:S(2)}) collective-permute-start(f32[21,16,128]{2,1,0:T(8,128)S(1)} %get-tuple-element.45), channel_id=1, source_target_pairs={{0,2},{1,3},{2,0},{3,1},{4,6},{5,7},{6,4},{7,5},{8,10},{9,11},{10,... | collective-permute-start | bytes 516104 | tf_op jit(solution)/shard_map/ppermute | solution.py:327
  48.5 6.3 %collective-permute-start.16 = (f32[21,16,128]{2,1,0:T(8,128)S(1)}, f32[21,16,128]{2,1,0:T(8,128)S(1)}, u32[]{:S(2)}, u32[]{:S(2)}) collective-permute-start(f32[21,16,128]{2,1,0:T(8,128)S(1)} %get-tuple-element.50), channel_id=1, source_target_pairs={{0,5},{1,4},{2,7},{3,6},{4,1},{5,0},{6,3},{7,2},{8,13},{9,12},{10,... | collective-permute-start | bytes 516104 | tf_op jit(solution)/shard_map/ppermute | solution.py:327
  48.5 10.4 %collective-permute-start.14 = (f32[21,16,128]{2,1,0:T(8,128)S(1)}, f32[21,16,128]{2,1,0:T(8,128)S(1)}, u32[]{:S(2)}, u32[]{:S(2)}) collective-permute-start(f32[21,16,128]{2,1,0:T(8,128)S(1)} %get-tuple-element.49), channel_id=1, source_target_pairs={{0,4},{1,5},{2,6},{3,7},{4,0},{5,1},{6,2},{7,3},{8,12},{9,13},{10,... | collective-permute-start | bytes 516104 | tf_op jit(solution)/shard_map/ppermute | solution.py:327
  50.4 8.9 %collective-permute-start.15 = (f32[21,16,128]{2,1,0:T(8,128)S(1)}, f32[21,16,128]{2,1,0:T(8,128)S(1)}, u32[]{:S(2)}, u32[]{:S(2)}) collective-permute-start(f32[21,16,128]{2,1,0:T(8,128)S(1)} %get-tuple-element.48), channel_id=1, source_target_pairs={{0,3},{1,2},{2,1},{3,0},{4,7},{5,6},{6,5},{7,4},{8,11},{9,10},{10,... | collective-permute-start | bytes 516104 | tf_op jit(solution)/shard_map/ppermute | solution.py:327
  52.2 7.2 %collective-permute-start.17 = (f32[21,16,128]{2,1,0:T(8,128)S(1)}, f32[21,16,128]{2,1,0:T(8,128)S(1)}, u32[]{:S(2)}, u32[]{:S(2)}) collective-permute-start(f32[21,16,128]{2,1,0:T(8,128)S(1)} %get-tuple-element.47), channel_id=1, source_target_pairs={{0,1},{1,0},{2,3},{3,2},{4,5},{5,4},{6,7},{7,6},{8,9},{9,8},{10,11... | collective-permute-start | bytes 516104 | tf_op jit(solution)/shard_map/ppermute | solution.py:327

commit v10 on v9

--- a/solution.py
+++ b/solution.py
@@ -7,6 +7,7 @@
 
 VMEM_LIMIT = 40 * 1024 * 1024
 PLANES = 2
+CORES = 2
 ACTIVE = 49
 MOST = 8
 GROUP = 7
@@ -54,7 +55,7 @@
     rows, width, quota = lay.rows, lay.width, lay.quota
 
     def kernel(j_ref, field_ref, mean_ref, kl_ref, *refs):
-        out_refs, (stage_ref, sems) = refs[: lay.group], refs[lay.group :]
+        out_refs, (halo_ref, stage_ref, sems) = refs[: lay.group], refs[lay.group :]
         mode = lax.rem(j_ref[0], lay.modes)
 
         def load(n, begin=True):
@@ -104,13 +105,16 @@
             to = jnp.bitwise_xor(j_ref[0], r)
             for part in range(lay.parts):
                 out_ref[part] = stage_ref[to, part]
+                if r < CORES and part < lay.fields:
+                    halo_ref[r, part] = stage_ref[to, part]
 
     shape = (lay.parts, rows, width)
-    sent = pl.pallas_call(
+    *sent, halo = pl.pallas_call(
         kernel,
-        out_shape=[pltpu.VMEM(shape, jnp.float32)] * lay.group,
+        out_shape=[pltpu.VMEM(shape, jnp.float32)] * lay.group
+        + [pltpu.VMEM((CORES, lay.fields, rows, width), jnp.float32)],
         in_specs=smem(1) + [pl.BlockSpec(memory_space=pltpu.HBM)] * 3,
-        out_specs=vmem(lay.group),
+        out_specs=vmem(lay.group + 1),
         scratch_shapes=[
             pltpu.VMEM((lay.group, *shape), jnp.float32),
             pltpu.SemaphoreType.DMA((lay.group, 1 + lay.share)),
@@ -118,7 +122,8 @@
         compiler_params=pltpu.CompilerParams(vmem_limit_bytes=VMEM_LIMIT),
         name="pack",
     )(j, *[pltpu.with_memory_space_constraint(x, pltpu.HBM) for x in (field, mean, kl)])
-    return [piece.reshape(lay.piece, width) for piece in sent]
+    sent = [piece.reshape(lay.piece, width) for piece in sent]
+    return sent, halo.reshape(CORES, lay.main, width)
 
 
 def unpack(pieces, j, shape, lay):
@@ -326,37 +331,40 @@
             return piece
         return lax.ppermute(piece, axes, [(d, d ^ r) for d in range(devices)])
 
-    def shift(pieces, crossing):
+    def shift(fields, crossing):
         pairs = []
         for d in range(devices):
             upper = (d // modes) % PLANES == (0 if crossing else 1)
             other = d + lay.group if upper else d - lay.group
             if 0 <= other < devices:
                 pairs.append((d, other))
-        main = jnp.stack([piece[: lay.main] for piece in pieces])
-        return lax.ppermute(main, axes, pairs)
+        return lax.ppermute(fields, axes, pairs)
+
+    def mains(pieces):
+        return jnp.stack([piece[: lay.main] for piece in pieces])
 
     field, kl = chaos_field[:, 0], kl_fields[:, 0]
-    sent = pack(field, mean_field, kl, j, lay)
+    sent, chip_rows = pack(field, mean_field, kl, j, lay)
     half = modes // 2
     pieces = sent[:1] + [None] * (lay.group - 1)
-    for r in [half, modes, *range(half + 1, modes), *range(modes + 1, modes + half), *range(1, half)]:
+    for r in [half, *range(half + 1, modes), *range(modes, modes + half), *range(1, half)]:
         pieces[r] = swap(sent[r], r)
-    halos = [shift(pieces[:1], False)]
-    for r in range(modes + half, lay.group):
-        pieces[r] = swap(after(sent[r], *pieces[half:modes], halos[0]), r)
+    chip_halo = shift(chip_rows, False)
+    first, last = modes + half, lay.group - 1
+    pieces[first] = swap(after(sent[first], *pieces[half:first]), first)
+    pieces[last] = swap(after(sent[last], *pieces[half:first]), last)
     number = jnp.arange(modes, dtype=jnp.int32)
     mine = jnp.bitwise_xor(number, mode)[:, None, None] == number[None, :, None]
     slot_mode = jnp.sum(jnp.where(mine, slot_mode.reshape(1, modes, quota), 0), 1).reshape(-1)
-    lists = coupling_lists(pattern, coupling, after(slot_mode, pieces[modes]))
-    pieces[modes + half] = after(pieces[modes + half], *lists)
-    halos.append(shift(pieces[1:modes], False))
-    halos += [shift(pieces[r : r + half], True) for r in (modes, modes + half)]
+    lists = coupling_lists(pattern, coupling, after(slot_mode, chip_halo))
+    pieces[first] = after(pieces[first], *lists)
+    own_halos = [chip_halo[:1], swap(chip_halo[1:], 1), shift(mains(pieces[half:modes]), False)]
+    crossing_halos = [shift(mains(pieces[r : r + half]), True) for r in (modes, first)]
 
     own, crossing = pieces[:modes], pieces[modes:]
-    crossing_out = stencil(crossing, own, halos[:2], lists, j, "stencil_crossing", lay)
+    crossing_out = stencil(crossing, own, own_halos, lists, j, "stencil_crossing", lay)
     own_j = after(j, *crossing_out)
-    own_out = stencil(own, crossing, halos[2:], lists, own_j, "stencil_own", lay)
+    own_out = stencil(own, crossing, crossing_halos, lists, own_j, "stencil_own", lay)
     out = [*own_out, *crossing_out]
     for r in range(modes, modes + half):
         out[r] = after(out[r], *own_out)

time: 60.8 us -> 61.8 us (1.016)
  waiting for transfers between devices: 16.5 us -> 13.5 us
  local copies, waits for them, and re-layouts: 2.77 us -> 4.79 us
  other arithmetic: 1.17 us -> 2.63 us
    ppermute x4, waiting for transfers between devices: 5.39 us -> 0.48 us  [shift(): return lax.ppermute(fields, axes, pairs)]
    ppermute x14 -> x15, waiting for transfers between devices: 11.1 us -> 13 us  [swap(): return lax.ppermute(piece, axes, [(d, d ^ r) for d in range(devices)])]
    unnamed x6, local copies, waits for them, and re-layouts: 1.36 us -> 3.05 us
    another operation x3, other arithmetic: 0.09 us -> 1.56 us  [mains(): return jnp.stack([piece[:lay.main] for piece in pieces])]
    ppermute x14 -> x15, starting transfers between devices: 15.8 us -> 17 us  [swap(): return lax.ppermute(piece, axes, [(d, d ^ r) for d in range(devices)])]
  transfers between devices with their start and end apart: 18 -> 19, of which waited for: 8 -> 7; matrix products, arithmetic and copies ran while one was open for 8% -> 13% of each run, Pallas kernels for 15% -> 14%
where the time goes in v10:
time: 61.8 us; the launch traced here: 61.5 us
  starting transfers between devices  27.7 us (45%)
  waiting for transfers between devices  13.5 us (22%)
  Pallas kernels  11.9 us (19%)
  local copies, waits for them, and re-layouts  4.79 us (8%)
  other arithmetic  2.63 us (4%)
  matrix products  0.68 us (1%)
    ppermute x15, starting transfers between devices, swap(): return lax.ppermute(piece, axes, [(d, d ^ r) for d in range(devices)])  17 us
    ppermute x15, waiting for transfers between devices, swap(): return lax.ppermute(piece, axes, [(d, d ^ r) for d in range(devices)])  13 us
    ppermute x4, starting transfers between devices, shift(): return lax.ppermute(fields, axes, pairs)  10.8 us
    pallas_call x2, Pallas kernels, stencil(): pl.pallas_call(kernel, out_shape=[jax.ShapeDtypeStruct((lay.quota, rows,...  8.82 us
    unnamed x6, local copies, waits for them, and re-layouts  3.05 us
    pallas_call x1, Pallas kernels, pack(): pl.pallas_call(kernel, out_shape=[pltpu.VMEM(shape, jnp.float32)] * lay.g...  1.97 us
    another operation x3, other arithmetic, mains(): return jnp.stack([piece[:lay.main] for piece in pieces])  1.56 us
  transfers between devices with their start and end apart: 19, of which 7 were waited for; matrix products, arithmetic and copies ran while one was open for 13% of the time, Pallas kernels for 14%

profile of v10, /device:TPU:0, one launch (start us, length us, event | category | flops | bytes accessed | tf_op | source)
XLA Modules:
  0.0 61.5 jit_solution(9150811146715132285)
XLA Ops:
  0.0 2.0 %pack.1 = (f32[26,16,128]{2,1,0:T(8,128)S(1)}, f32[26,16,128]{2,1,0:T(8,128)S(1)}, f32[26,16,128]{2,1,0:T(8,128)S(1)}, f32[26,16,128]{2,1,0:T(8,128)S(1)}, f32[2...) custom-call(s32[1]{0:T(128)} %bitcast.j_ref, ...), custom_call_target="tpu_custom_call" | custom-call | tf_op jit(solution)/shard_map/pack/pallas_call | solution.py:112
  2.0 3.0 %collective-permute-start.1 = (f32[416,128]{1,0:T(8,128)S(1)}, f32[416,128]{1,0:T(8,128)S(1)}, u32[]{:S(2)}, u32[]{:S(2)}) collective-permute-start(f32[416,128]{1,0:T(8,128)S(1)} %bitcast.45), channel_id=1, source_target_pairs={{0,4},{1,5},{2,6},{3,7},{4,0},{5,1},{6,2},{7,3},{8,12},{9,13},{10,... | collective-permute-start | bytes 638984 | tf_op jit(solution)/shard_map/ppermute | solution.py:332
  5.0 0.0 collective-permute-start.2
  5.0 1.5 %collective-permute-start.3 = (f32[416,128]{1,0:T(8,128)S(1)}, f32[416,128]{1,0:T(8,128)S(1)}, u32[]{:S(2)}, u32[]{:S(2)}) collective-permute-start(f32[416,128]{1,0:T(8,128)S(1)} %bitcast.43), channel_id=1, source_target_pairs={{0,2},{1,3},{2,0},{3,1},{4,6},{5,7},{6,4},{7,5},{8,10},{9,11},{10,... | collective-permute-start | bytes 638984 | tf_op jit(solution)/shard_map/ppermute | solution.py:332
  6.5 0.3 collective-permute-start.4
  6.8 1.3 %collective-permute-start = (f32[2,368,128]{2,1,0:T(8,128)S(1)}, f32[2,368,128]{2,1,0:T(8,128)}, u32[]{:S(2)}, u32[]{:S(2)}) collective-permute-start(f32[2,368,128]{2,1,0:T(8,128)S(1)} %bitcast.38), channel_id=1, source_target_pairs={{4,12},{5,13},{6,14},{7,15},{8,0},{9,1},{10,2},{11,3},{12,20},{13,... | collective-permute-start | bytes 1130504 | tf_op jit(solution)/shard_map/ppermute | solution.py:341
  8.1 0.1 iota_compare_fusion.9
  8.2 0.1 broadcast_in_dim.136
  8.3 0.1 select_reduce_fusion.9
  8.4 0.1 reshape.115
  8.4 1.2 %copy.10 = f32[7,84,84]{1,2,0:T(8,128)S(1)} copy(f32[7,84,84]{2,1,0:T(8,128)} %param.10) | data formatting | bytes 395136 | tf_op args[4]
  9.6 1.9 %copy.9 = s32[7,84,84]{1,2,0:T(8,128)} copy(s32[7,84,84]{2,1,0:T(8,128)} %param.9) | data formatting | bytes 395136 | tf_op args[3]
  11.5 0.0 collective-permute-done.1.refs_0_.refs_4_
  11.5 0.4 collective-permute-start.7
  11.9 2.1 %collective-permute-done.2.refs_1_.refs_5_ = f32[416,128]{1,0:T(8,128)S(1)} collective-permute-done((f32[416,128]{1,0:T(8,128)S(1)}, f32[416,128]{1,0:T(8,128)S(1)}, u32[]{:S(2)}, u32[]{:S(2)}) %collective-permute-start.2) | collective-permute-done | bytes 213024 | tf_op jit(solution)/shard_map/ppermute | solution.py:332
  14.1 0.0 collective-permute-done.3.refs_6_.refs_2_
  14.1 2.6 %collective-permute-done.4.refs_7_.refs_3_ = f32[416,128]{1,0:T(8,128)S(1)} collective-permute-done((f32[416,128]{1,0:T(8,128)S(1)}, f32[416,128]{1,0:T(8,128)S(1)}, u32[]{:S(2)}, u32[]{:S(2)}) %collective-permute-start.4) | collective-permute-done | bytes 213024 | tf_op jit(solution)/shard_map/ppermute | solution.py:332
  16.7 2.9 %collective-permute-start.6 = (f32[416,128]{1,0:T(8,128)S(1)}, f32[416,128]{1,0:T(8,128)S(1)}, u32[]{:S(2)}, u32[]{:S(2)}) collective-permute-start(f32[416,128]{1,0:T(8,128)S(1)} %bitcast.40), channel_id=1, source_target_pairs={{0,7},{1,6},{2,5},{3,4},{4,3},{5,2},{6,1},{7,0},{8,15},{9,14},{10,... | collective-permute-start | bytes 638984 | tf_op jit(solution)/shard_map/ppermute | solution.py:332
  19.5 0.4 collective-permute-start.5
  19.9 0.8 %pad_maximum_fusion = f32[2,368,128]{2,1,0:T(8,128)} fusion(f32[1,368,128]{2,1,0:T(8,128)S(1)} %slice_bitcast_fusion.3, f32[1,368,128]{2,1,0:T(8,128)S(1)} %slice_bitcast_fusion.4), kind=kLoop, calls=%fused_computation | loop fusion | flops 94208 | bytes 753664 | tf_op jit(solution)/shard_map/stack | solution.py:344
  20.7 1.3 %collective-permute-start.9 = (f32[2,368,128]{2,1,0:T(8,128)}, f32[2,368,128]{2,1,0:T(8,128)S(1)}, u32[]{:S(2)}, u32[]{:S(2)}) collective-permute-start(f32[2,368,128]{2,1,0:T(8,128)} %pad_maximum_fusion), channel_id=1, source_target_pairs={{4,12},{5,13},{6,14},{7,15},{8,0},{9,1},{10,2},{11,3},{12,20},{13,... | collective-permute-start | bytes 1130504 | tf_op jit(solution)/shard_map/ppermute | solution.py:341
  22.0 0.8 %pad_maximum_fusion.1 = f32[2,368,128]{2,1,0:T(8,128)} fusion(f32[1,368,128]{2,1,0:T(8,128)S(1)} %slice_bitcast_fusion.1, f32[1,368,128]{2,1,0:T(8,128)S(1)} %slice_bitcast_fusion.2), kind=kLoop, calls=%fused_computation.1 | loop fusion | flops 94208 | bytes 753664 | tf_op jit(solution)/shard_map/stack | solution.py:344
  22.8 0.0 collective-permute-done
  22.8 4.6 %collective-permute-start.12 = (f32[2,368,128]{2,1,0:T(8,128)}, f32[2,368,128]{2,1,0:T(8,128)S(1)}, u32[]{:S(2)}, u32[]{:S(2)}) collective-permute-start(f32[2,368,128]{2,1,0:T(8,128)} %pad_maximum_fusion.1), channel_id=1, source_target_pairs={{0,8},{1,9},{2,10},{3,11},{8,16},{9,17},{10,18},{11,19},{12,4},{13... | collective-permute-start | bytes 1130504 | tf_op jit(solution)/shard_map/ppermute | solution.py:341
  27.4 0.3 fusion
  27.7 0.3 fusion.10
  28.1 0.1 fusion.6
  28.2 0.1 select_reduce_fusion.1
  28.3 0.1 select_reduce_fusion.6
  28.5 0.1 copy.12
  28.6 0.1 reshape.119.factor_ref
  28.7 0.2 select_reduce_fusion.3
  28.9 0.1 broadcast_add_fusion.1
  29.0 0.1 copy.11
  29.1 0.1 reshape.118.take_ref
  29.2 0.2 select_reduce_fusion.5
  29.4 0.1 reshape.117.source_ref
  29.5 0.4 collective-permute-done.5.refs_2_.refs_6_
  29.9 0.0 collective-permute-done.6.refs_3_.refs_7_
  30.0 3.7 %collective-permute-start.13 = (f32[2,368,128]{2,1,0:T(8,128)S(1)}, f32[2,368,128]{2,1,0:T(8,128)S(1)}, u32[]{:S(2)}, u32[]{:S(2)}) collective-permute-start(f32[2,368,128]{2,1,0:T(8,128)S(1)} %pad_maximum_fusion.2), channel_id=1, source_target_pairs={{0,8},{1,9},{2,10},{3,11},{8,16},{9,17},{10,18},{11,19},{12,4},{13... | collective-permute-start | bytes 1130504 | tf_op jit(solution)/shard_map/ppermute | solution.py:341
  33.7 1.0 %fusion.18 = (f32[1,368,128]{2,1,0:T(8,128)S(1)}, f32[1,368,128]{2,1,0:T(8,128)S(1)}) fusion(f32[2,368,128]{2,1,0:T(8,128)} %collective-permute-done), kind=kLoop, calls=%fused_computation.55 | loop fusion | bytes 753664 | tf_op jit(solution)/shard_map/slice | solution.py:361
  34.7 0.1 collective-permute-start.8
  34.8 0.0 collective-permute-done.7.refs_5_.refs_1_
  34.8 1.4 %collective-permute-done.8.refs_9_ = f32[1,368,128]{2,1,0:T(8,128)S(1)} collective-permute-done((f32[1,368,128]{2,1,0:T(8,128)S(1)}, f32[1,368,128]{2,1,0:T(8,128)S(1)}, u32[]{:S(2)}, u32[]{:S(2)}) %collective-permute-start.8) | collective-permute-done | bytes 188448 | tf_op jit(solution)/shard_map/ppermute | solution.py:332
  36.2 0.0 collective-permute-done.9.refs_10_
  36.2 4.4 %stencil_crossing.1 = (f32[21,16,128]{2,1,0:T(8,128)S(1)}, f32[21,16,128]{2,1,0:T(8,128)S(1)}, f32[21,16,128]{2,1,0:T(8,128)S(1)}, f32[21,16,128]{2,1,0:T(8,128)S(1)}) custom-call(s32[1]{0:T(128)} %bitcast.j_ref, s32[294]{0:T(512)S(1)} %reshape.117.source_ref, s32[672]{0:T(1024)S(1)} %reshape.118.take_ref, f32[672]{0:T(1024)S(1)} %reshape.119.factor_ref, ...), custom_call_target="tpu_custom_call" | custom-call | tf_op jit(solution)/shard_map/stencil_crossing/pallas_call | solution.py:287
  40.6 0.6 collective-permute-start.10
  41.2 1.8 %collective-permute-start.11 = (f32[21,16,128]{2,1,0:T(8,128)S(1)}, f32[21,16,128]{2,1,0:T(8,128)S(1)}, u32[]{:S(2)}, u32[]{:S(2)}) collective-permute-start(f32[21,16,128]{2,1,0:T(8,128)S(1)} %get-tuple-element.43), channel_id=1, source_target_pairs={{0,7},{1,6},{2,5},{3,4},{4,3},{5,2},{6,1},{7,0},{8,15},{9,14},{10,... | collective-permute-start | bytes 516104 | tf_op jit(solution)/shard_map/ppermute | solution.py:332
  43.1 0.0 collective-permute-done.12.refs_8_
  43.1 0.5 collective-permute-done.13.refs_9_
  43.5 4.4 %stencil_own.1 = (f32[21,16,128]{2,1,0:T(8,128)S(1)}, f32[21,16,128]{2,1,0:T(8,128)S(1)}, f32[21,16,128]{2,1,0:T(8,128)S(1)}, f32[21,16,128]{2,1,0:T(8,128)S(1)}) custom-call(s32[1]{0:T(128)} %bitcast.j_ref, s32[294]{0:T(512)S(1)} %reshape.117.source_ref, s32[672]{0:T(1024)S(1)} %reshape.118.take_ref, f32[672]{0:T(1024)S(1)} %reshape.119.factor_ref, ...), custom_call_target="tpu_custom_call" | custom-call | tf_op jit(solution)/shard_map/stencil_own/pallas_call | solution.py:287
  48.0 1.5 %collective-permute-start.14 = (f32[21,16,128]{2,1,0:T(8,128)S(1)}, f32[21,16,128]{2,1,0:T(8,128)S(1)}, u32[]{:S(2)}, u32[]{:S(2)}) collective-permute-start(f32[21,16,128]{2,1,0:T(8,128)S(1)} %get-tuple-element.47), channel_id=1, source_target_pairs={{0,2},{1,3},{2,0},{3,1},{4,6},{5,7},{6,4},{7,5},{8,10},{9,11},{10,... | collective-permute-start | bytes 516104 | tf_op jit(solution)/shard_map/ppermute | solution.py:332
  49.4 2.0 %collective-permute-start.17 = (f32[21,16,128]{2,1,0:T(8,128)S(1)}, f32[21,16,128]{2,1,0:T(8,128)S(1)}, u32[]{:S(2)}, u32[]{:S(2)}) collective-permute-start(f32[21,16,128]{2,1,0:T(8,128)S(1)} %get-tuple-element.52), channel_id=1, source_target_pairs={{0,5},{1,4},{2,7},{3,6},{4,1},{5,0},{6,3},{7,2},{8,13},{9,12},{10,... | collective-permute-start | bytes 516104 | tf_op jit(solution)/shard_map/ppermute | solution.py:332
  51.4 1.9 %collective-permute-start.15 = (f32[21,16,128]{2,1,0:T(8,128)S(1)}, f32[21,16,128]{2,1,0:T(8,128)S(1)}, u32[]{:S(2)}, u32[]{:S(2)}) collective-permute-start(f32[21,16,128]{2,1,0:T(8,128)S(1)} %get-tuple-element.51), channel_id=1, source_target_pairs={{0,4},{1,5},{2,6},{3,7},{4,0},{5,1},{6,2},{7,3},{8,12},{9,13},{10,... | collective-permute-start | bytes 516104 | tf_op jit(solution)/shard_map/ppermute | solution.py:332
  53.3 0.0 collective-permute-done.10.refs_0_
  53.3 0.2 collective-permute-start.16
  53.5 0.0 collective-permute-done.11.refs_1_
  53.5 0.4 collective-permute-start.18
  53.9 0.9 %collective-permute-done.17.refs_5_ = f32[21,16,128]{2,1,0:T(8,128)S(1)} collective-permute-done((f32[21,16,128]{2,1,0:T(8,128)S(1)}, f32[21,16,128]{2,1,0:T(8,128)S(1)}, u32[]{:S(2)}, u32[]{:S(2)}) %collective-permute-start.17) | collective-permute-done | bytes 172064 | tf_op jit(solution)/shard_map/ppermute | solution.py:332
  54.9 5.5 %collective-permute-done.15.refs_3_ = f32[21,16,128]{2,1,0:T(8,128)S(1)} collective-permute-done((f32[21,16,128]{2,1,0:T(8,128)S(1)}, f32[21,16,128]{2,1,0:T(8,128)S(1)}, u32[]{:S(2)}, u32[]{:S(2)}) %collective-permute-start.15) | collective-permute-done | bytes 172064 | tf_op jit(solution)/shard_map/ppermute | solution.py:332
  60.4 0.0 collective-permute-done.14.refs_2_
  60.4 0.0 collective-permute-done.16.refs_4_
  60.4 0.0 collective-permute-done.18.refs_7_
  60.4 1.1 %unpack.1 = f32[21,128,128]{2,1,0:T(8,128)} custom-call(s32[1]{0:T(128)} %bitcast.j_ref, f32[21,16,128]{2,1,0:T(8,128)S(1)} %collective-permute-done.10.refs_0_, f32[21,16,128]{2,1,0:T(8,128)S(1)} %collective-permute-done.11.refs_1_, f32[21,16,128]{2,1,0:T(8,128)S(1)} %collective-permute-done.14.refs_2_, f32[21,16,128]{2,1,0:T(8,128)S(1)} %collective-permute-done.15.refs_3_, ...), custom_call_target="tpu_custom_call" | custom-call | tf_op jit(solution)/shard_map/unpack/pallas_call | solution.py:145
  (21 shorter events, 0.2 us)
Async XLA Ops:
  0.0 8.2 %copy-start.1 = (s32[84]{0:T(128)S(1)}, s32[84]{0:T(128)}, u32[]{:S(2)}) copy-start(s32[84]{0:T(128)} %param.11) | copy-start | bytes 1012
  2.0 9.5 %collective-permute-start.1 = (f32[416,128]{1,0:T(8,128)S(1)}, f32[416,128]{1,0:T(8,128)S(1)}, u32[]{:S(2)}, u32[]{:S(2)}) collective-permute-start(f32[416,128]{1,0:T(8,128)S(1)} %bitcast.45), channel_id=1, source_target_pairs={{0,4},{1,5},{2,6},{3,7},{4,0},{5,1},{6,2},{7,3},{8,12},{9,13},{10,... | collective-permute-start | bytes 638984 | tf_op jit(solution)/shard_map/ppermute | solution.py:332
  5.0 9.1 %collective-permute-start.2 = (f32[416,128]{1,0:T(8,128)S(1)}, f32[416,128]{1,0:T(8,128)S(1)}, u32[]{:S(2)}, u32[]{:S(2)}) collective-permute-start(f32[416,128]{1,0:T(8,128)S(1)} %bitcast.44), channel_id=1, source_target_pairs={{0,5},{1,4},{2,7},{3,6},{4,1},{5,0},{6,3},{7,2},{8,13},{9,12},{10,... | collective-permute-start | bytes 638984 | tf_op jit(solution)/shard_map/ppermute | solution.py:332
  5.0 9.1 %collective-permute-start.3 = (f32[416,128]{1,0:T(8,128)S(1)}, f32[416,128]{1,0:T(8,128)S(1)}, u32[]{:S(2)}, u32[]{:S(2)}) collective-permute-start(f32[416,128]{1,0:T(8,128)S(1)} %bitcast.43), channel_id=1, source_target_pairs={{0,2},{1,3},{2,0},{3,1},{4,6},{5,7},{6,4},{7,5},{8,10},{9,11},{10,... | collective-permute-start | bytes 638984 | tf_op jit(solution)/shard_map/ppermute | solution.py:332
  6.5 10.1 %collective-permute-start.4 = (f32[416,128]{1,0:T(8,128)S(1)}, f32[416,128]{1,0:T(8,128)S(1)}, u32[]{:S(2)}, u32[]{:S(2)}) collective-permute-start(f32[416,128]{1,0:T(8,128)S(1)} %bitcast.42), channel_id=1, source_target_pairs={{0,3},{1,2},{2,1},{3,0},{4,7},{5,6},{6,5},{7,4},{8,11},{9,10},{10,... | collective-permute-start | bytes 638984 | tf_op jit(solution)/shard_map/ppermute | solution.py:332
  6.8 16.0 %collective-permute-start = (f32[2,368,128]{2,1,0:T(8,128)S(1)}, f32[2,368,128]{2,1,0:T(8,128)}, u32[]{:S(2)}, u32[]{:S(2)}) collective-permute-start(f32[2,368,128]{2,1,0:T(8,128)S(1)} %bitcast.38), channel_id=1, source_target_pairs={{4,12},{5,13},{6,14},{7,15},{8,0},{9,1},{10,2},{11,3},{12,20},{13,... | collective-permute-start | bytes 1130504 | tf_op jit(solution)/shard_map/ppermute | solution.py:341
  11.5 23.3 %collective-permute-start.7 = (f32[416,128]{1,0:T(8,128)S(1)}, f32[416,128]{1,0:T(8,128)S(1)}, u32[]{:S(2)}, u32[]{:S(2)}) collective-permute-start(f32[416,128]{1,0:T(8,128)S(1)} %bitcast.39), channel_id=1, source_target_pairs={{0,1},{1,0},{2,3},{3,2},{4,5},{5,4},{6,7},{7,6},{8,9},{9,8},{10,11... | collective-permute-start | bytes 638984 | tf_op jit(solution)/shard_map/ppermute | solution.py:332
  16.7 13.3 %collective-permute-start.6 = (f32[416,128]{1,0:T(8,128)S(1)}, f32[416,128]{1,0:T(8,128)S(1)}, u32[]{:S(2)}, u32[]{:S(2)}) collective-permute-start(f32[416,128]{1,0:T(8,128)S(1)} %bitcast.40), channel_id=1, source_target_pairs={{0,7},{1,6},{2,5},{3,4},{4,3},{5,2},{6,1},{7,0},{8,15},{9,14},{10,... | collective-permute-start | bytes 638984 | tf_op jit(solution)/shard_map/ppermute | solution.py:332
  19.5 10.4 %collective-permute-start.5 = (f32[416,128]{1,0:T(8,128)S(1)}, f32[416,128]{1,0:T(8,128)S(1)}, u32[]{:S(2)}, u32[]{:S(2)}) collective-permute-start(f32[416,128]{1,0:T(8,128)S(1)} %bitcast.41), channel_id=1, source_target_pairs={{0,6},{1,7},{2,4},{3,5},{4,2},{5,3},{6,0},{7,1},{8,14},{9,15},{10,... | collective-permute-start | bytes 638984 | tf_op jit(solution)/shard_map/ppermute | solution.py:332
  19.9 7.5 %copy-start = (s32[7,84,84]{1,2,0:T(8,128)S(1)}, s32[7,84,84]{1,2,0:T(8,128)}, u32[]{:S(2)}) copy-start(s32[7,84,84]{1,2,0:T(8,128)} %copy.9) | copy-start | bytes 592708
  20.7 15.5 %collective-permute-start.9 = (f32[2,368,128]{2,1,0:T(8,128)}, f32[2,368,128]{2,1,0:T(8,128)S(1)}, u32[]{:S(2)}, u32[]{:S(2)}) collective-permute-start(f32[2,368,128]{2,1,0:T(8,128)} %pad_maximum_fusion), channel_id=1, source_target_pairs={{4,12},{5,13},{6,14},{7,15},{8,0},{9,1},{10,2},{11,3},{12,20},{13,... | collective-permute-start | bytes 1130504 | tf_op jit(solution)/shard_map/ppermute | solution.py:341
  22.8 20.3 %collective-permute-start.12 = (f32[2,368,128]{2,1,0:T(8,128)}, f32[2,368,128]{2,1,0:T(8,128)S(1)}, u32[]{:S(2)}, u32[]{:S(2)}) collective-permute-start(f32[2,368,128]{2,1,0:T(8,128)} %pad_maximum_fusion.1), channel_id=1, source_target_pairs={{0,8},{1,9},{2,10},{3,11},{8,16},{9,17},{10,18},{11,19},{12,4},{13... | collective-permute-start | bytes 1130504 | tf_op jit(solution)/shard_map/ppermute | solution.py:341
  30.0 13.6 %collective-permute-start.13 = (f32[2,368,128]{2,1,0:T(8,128)S(1)}, f32[2,368,128]{2,1,0:T(8,128)S(1)}, u32[]{:S(2)}, u32[]{:S(2)}) collective-permute-start(f32[2,368,128]{2,1,0:T(8,128)S(1)} %pad_maximum_fusion.2), channel_id=1, source_target_pairs={{0,8},{1,9},{2,10},{3,11},{8,16},{9,17},{10,18},{11,19},{12,4},{13... | collective-permute-start | bytes 1130504 | tf_op jit(solution)/shard_map/ppermute | solution.py:341
  34.7 1.5 %collective-permute-start.8 = (f32[1,368,128]{2,1,0:T(8,128)S(1)}, f32[1,368,128]{2,1,0:T(8,128)S(1)}, u32[]{:S(2)}, u32[]{:S(2)}) collective-permute-start(f32[1,368,128]{2,1,0:T(8,128)S(1)} %get-tuple-element.60), channel_id=1, source_target_pairs={{0,1},{1,0},{2,3},{3,2},{4,5},{5,4},{6,7},{7,6},{8,9},{9,8},{10,11... | collective-permute-start | bytes 565256 | tf_op jit(solution)/shard_map/ppermute | solution.py:332
  40.6 12.7 %collective-permute-start.10 = (f32[21,16,128]{2,1,0:T(8,128)S(1)}, f32[21,16,128]{2,1,0:T(8,128)S(1)}, u32[]{:S(2)}, u32[]{:S(2)}) collective-permute-start(f32[21,16,128]{2,1,0:T(8,128)S(1)} %get-tuple-element.42), channel_id=1, source_target_pairs={{0,6},{1,7},{2,4},{3,5},{4,2},{5,3},{6,0},{7,1},{8,14},{9,15},{10,... | collective-permute-start | bytes 516104 | tf_op jit(solution)/shard_map/ppermute | solution.py:332
  41.2 12.3 %collective-permute-start.11 = (f32[21,16,128]{2,1,0:T(8,128)S(1)}, f32[21,16,128]{2,1,0:T(8,128)S(1)}, u32[]{:S(2)}, u32[]{:S(2)}) collective-permute-start(f32[21,16,128]{2,1,0:T(8,128)S(1)} %get-tuple-element.43), channel_id=1, source_target_pairs={{0,7},{1,6},{2,5},{3,4},{4,3},{5,2},{6,1},{7,0},{8,15},{9,14},{10,... | collective-permute-start | bytes 516104 | tf_op jit(solution)/shard_map/ppermute | solution.py:332
  48.0 12.4 %collective-permute-start.14 = (f32[21,16,128]{2,1,0:T(8,128)S(1)}, f32[21,16,128]{2,1,0:T(8,128)S(1)}, u32[]{:S(2)}, u32[]{:S(2)}) collective-permute-start(f32[21,16,128]{2,1,0:T(8,128)S(1)} %get-tuple-element.47), channel_id=1, source_target_pairs={{0,2},{1,3},{2,0},{3,1},{4,6},{5,7},{6,4},{7,5},{8,10},{9,11},{10,... | collective-permute-start | bytes 516104 | tf_op jit(solution)/shard_map/ppermute | solution.py:332
  49.4 5.5 %collective-permute-start.17 = (f32[21,16,128]{2,1,0:T(8,128)S(1)}, f32[21,16,128]{2,1,0:T(8,128)S(1)}, u32[]{:S(2)}, u32[]{:S(2)}) collective-permute-start(f32[21,16,128]{2,1,0:T(8,128)S(1)} %get-tuple-element.52), channel_id=1, source_target_pairs={{0,5},{1,4},{2,7},{3,6},{4,1},{5,0},{6,3},{7,2},{8,13},{9,12},{10,... | collective-permute-start | bytes 516104 | tf_op jit(solution)/shard_map/ppermute | solution.py:332
  51.4 8.9 %collective-permute-start.15 = (f32[21,16,128]{2,1,0:T(8,128)S(1)}, f32[21,16,128]{2,1,0:T(8,128)S(1)}, u32[]{:S(2)}, u32[]{:S(2)}) collective-permute-start(f32[21,16,128]{2,1,0:T(8,128)S(1)} %get-tuple-element.51), channel_id=1, source_target_pairs={{0,4},{1,5},{2,6},{3,7},{4,0},{5,1},{6,2},{7,3},{8,12},{9,13},{10,... | collective-permute-start | bytes 516104 | tf_op jit(solution)/shard_map/ppermute | solution.py:332
  53.3 7.0 %collective-permute-start.16 = (f32[21,16,128]{2,1,0:T(8,128)S(1)}, f32[21,16,128]{2,1,0:T(8,128)S(1)}, u32[]{:S(2)}, u32[]{:S(2)}) collective-permute-start(f32[21,16,128]{2,1,0:T(8,128)S(1)} %get-tuple-element.50), channel_id=1, source_target_pairs={{0,3},{1,2},{2,1},{3,0},{4,7},{5,6},{6,5},{7,4},{8,11},{9,10},{10,... | collective-permute-start | bytes 516104 | tf_op jit(solution)/shard_map/ppermute | solution.py:332
  53.5 6.8 %collective-permute-start.18 = (f32[21,16,128]{2,1,0:T(8,128)S(1)}, f32[21,16,128]{2,1,0:T(8,128)S(1)}, u32[]{:S(2)}, u32[]{:S(2)}) collective-permute-start(f32[21,16,128]{2,1,0:T(8,128)S(1)} %get-tuple-element.49), channel_id=1, source_target_pairs={{0,1},{1,0},{2,3},{3,2},{4,5},{5,4},{6,7},{7,6},{8,9},{9,8},{10,11... | collective-permute-start | bytes 516104 | tf_op jit(solution)/shard_map/ppermute | solution.py:332

commit v11 on v10

--- a/solution.py
+++ b/solution.py
@@ -10,7 +10,6 @@
 CORES = 2
 ACTIVE = 49
 MOST = 8
-GROUP = 7
 
 
 class Layout:
@@ -38,8 +37,9 @@
         return self.slots + block * self.share + (i - self.quota)
 
     def term_place(self, term, mode):
-        block = jnp.bitwise_xor(term // self.share, mode)
-        return self.slots + block * self.share + term % self.share
+        owner = lax.div(term, self.share)
+        block = jnp.bitwise_xor(owner, mode)
+        return self.slots + block * self.share + (term - owner * self.share)
 
 
 def vmem(count):
@@ -189,126 +189,101 @@
     chosen = valid[None] & (rank[None] == place)
     take = jnp.sum(jnp.where(chosen, products[None], 0), 1)
     factor = jnp.sum(jnp.where(chosen, factors[None], 0.0), 1)
-    return sources.reshape(-1), take.T.reshape(-1), factor.T.reshape(-1)
-
-
-def gather_products(s, take_ref, factor_ref, product_ref, total):
-    for n in range(MOST):
-        e = s * MOST + n
-        total = total + factor_ref[e] * product_ref[take_ref[e]]
-    return total
+    return jnp.concatenate([sources.reshape(-1), take.T.reshape(-1)]), factor.T.reshape(-1)
+
+
+def tree_sum(values):
+    while len(values) > 1:
+        values = [sum(values[n : n + 2][1:], values[n]) for n in range(0, len(values), 2)]
+    return values[0]
 
 
 def stencil(pieces, others, halos, lists, j, name, lay):
     rows, width = lay.rows, lay.width
     full = (rows, width)
-
-    def kernel(j_ref, source_ref, take_ref, factor_ref, *refs):
+    arrays = list({id(array): array for array, _ in halos}.values())
+    products = (lay.terms - 1) * ACTIVE
+
+    def kernel(j_ref, index_ref, factor_ref, *refs):
         piece_refs, refs = refs[: lay.modes], refs[lay.modes :]
         other_refs, refs = refs[: lay.modes], refs[lay.modes :]
-        halo_refs, refs = refs[: len(halos)], refs[len(halos) :]
+        halo_refs, refs = refs[: len(arrays)], refs[len(arrays) :]
         out_refs, (near_ref, product_ref) = refs[: lay.modes], refs[lay.modes :]
         lane = lax.broadcasted_iota(jnp.int32, full, 1)
         line = lax.broadcasted_iota(jnp.int32, full, 0)
         mode = lax.rem(j_ref[0], lay.modes)
-        halo_parts = [(ref, n) for ref in halo_refs for n in range(ref.shape[0])]
+        ref_of = {id(array): ref for array, ref in zip(arrays, halo_refs)}
+        halo_parts = [(ref_of[id(array)], n) for array, n in halos]
+
+        def to_right(value):
+            return pltpu.roll(value, width - 1, 1)
+
+        def to_left(value):
+            return pltpu.roll(value, 1, 1)
 
         for block in range(lay.modes):
-
-            def spread(i, block=block):
-                piece_ref = piece_refs[block]
-                halo_ref, n = halo_parts[block]
-                here = piece_ref[pl.ds(i * rows, rows), :]
-                low = piece_ref[pl.ds(lay.main + 2 * i, 1), :]
-                high = piece_ref[pl.ds(lay.main + 2 * i + 1, 1), :]
-                return (
-                    here,
-                    pltpu.roll(here, width - 1, 1),
-                    pltpu.roll(here, 1, 1),
-                    jnp.where(line == rows - 1, high, pltpu.roll(here, rows - 1, 0)),
-                    jnp.where(line == 0, low, pltpu.roll(here, 1, 0)),
-                    other_refs[block][pl.ds(i * rows, rows), :],
-                    halo_ref[n, pl.ds(i * rows, rows), :],
-                )
-
-            def keep(at, values):
-                for n, value in enumerate(values):
-                    near_ref[at, n] = value
-
-            def keep_slot(i, values, block=block):
-                keep(block * lay.quota + i, values)
-
-            grouped(0, lay.quota, spread, keep_slot)
-            for i in range(lay.quota, lay.fields):
-                keep(lay.place(block, i), spread(i))
+            piece_ref, other_ref = piece_refs[block], other_refs[block]
+            halo_ref, n = halo_parts[block]
+            for i in range(lay.fields):
+                own = i < lay.quota
+                at, rows_i = lay.place(block, i), slice(i * rows, (i + 1) * rows)
+                edge = lay.main + 2 * i
+                here = piece_ref[rows_i, :]
+                right = to_right(here)
+                near_ref[at, 0] = here
+                near_ref[at, 1] = jnp.where(lane == width - 1, 0.0, here - right) if own else right
+                high, low = piece_ref[edge + 1 : edge + 2, :], piece_ref[edge : edge + 1, :]
+                near_ref[at, 2] = jnp.where(line == rows - 1, high, pltpu.roll(here, rows - 1, 0))
+                near_ref[at, 3] = jnp.where(line == 0, low, pltpu.roll(here, 1, 0))
+                near_ref[at, 4] = other_ref[rows_i, :]
+                near_ref[at, 5] = halo_ref[n, rows_i, :]
 
         def operator_of(term):
             at = lay.term_place(term, mode)
-            here, right, left, *rest = [near_ref[at, n] for n in range(7)]
-            right = jnp.where(lane == width - 1, 0.0, right)
-            left = jnp.where(lane == 0, 0.0, left)
-            faces = [0.5 * (here + n) for n in (right, left, *rest)]
-            diagonal = faces[0] + faces[1] + faces[2] + faces[3] + faces[4] + faces[5]
-            faces[0] = jnp.where(lane == width - 1, 0.0, faces[0])
-            faces[1] = jnp.where(lane == 0, 0.0, faces[1])
+            here, right, *rest = [near_ref[at, n] for n in range(6)]
+            across = jnp.where(lane == width - 1, 0.0, 0.5 * (here + right))
+            ends = jnp.where((lane == 0) | (lane == width - 1), 0.5 * here, 0.0)
+            faces = [0.5 * (here + n) for n in rest]
+            diagonal = tree_sum([ends, *faces])
 
             def operator(t):
-                total = diagonal * near_ref[t, 0]
-                for n, face in enumerate(faces):
-                    total = total - face * near_ref[t, n + 1]
-                return total
+                flux = across * near_ref[t, 1]
+                rest = [face * near_ref[t, n + 2] for n, face in enumerate(faces)]
+                return (flux - to_left(flux)) + (diagonal * near_ref[t, 0] - tree_sum(rest))
 
             return operator
 
-        def keep_product(e, value):
-            product_ref[e] = value
-
-        for term in range(1, lay.terms):
+        def apply(term, carry):
             operator = operator_of(term)
-            grouped(
-                (term - 1) * ACTIVE,
-                ACTIVE,
-                lambda e, operator=operator: operator(source_ref[e]),
-                keep_product,
-            )
+            first = (term - 1) * ACTIVE
+            for n in range(ACTIVE):
+                product_ref[first + n] = operator(index_ref[first + n])
+            return carry
+
+        lax.fori_loop(1, lay.terms, apply, 0)
 
         operator = operator_of(0)
         for block in range(lay.modes):
-
-            def collect(i, block=block):
+            for i in range(lay.quota):
                 s = block * lay.quota + i
-                return gather_products(s, take_ref, factor_ref, product_ref, operator(s))
-
-            def keep_out(i, value, out_ref=out_refs[block]):
-                out_ref[i] = value
-
-            grouped(0, lay.quota, collect, keep_out)
+                values = [operator(s)]
+                for n in range(MOST):
+                    e = s * MOST + n
+                    values.append(factor_ref[e] * product_ref[index_ref[products + e]])
+                out_refs[block][i] = tree_sum(values)
 
     return pl.pallas_call(
         kernel,
         out_shape=[jax.ShapeDtypeStruct((lay.quota, rows, width), jnp.float32)] * lay.modes,
-        in_specs=smem(4) + vmem(2 * lay.modes + len(halos)),
+        in_specs=smem(3) + vmem(2 * lay.modes + len(arrays)),
         out_specs=vmem(lay.modes),
         scratch_shapes=[
-            pltpu.VMEM((lay.places, 7, rows, width), jnp.float32),
-            pltpu.VMEM(((lay.terms - 1) * ACTIVE, rows, width), jnp.float32),
+            pltpu.VMEM((lay.places, 6, rows, width), jnp.float32),
+            pltpu.VMEM((products, rows, width), jnp.float32),
         ],
         compiler_params=pltpu.CompilerParams(vmem_limit_bytes=VMEM_LIMIT),
         name=name,
-    )(j, *lists, *pieces, *others, *halos)
-
-
-def grouped(first, count, compute, store):
-    size = max(n for n in range(1, GROUP + 1) if count % n == 0)
-
-    def step(g, carry):
-        numbers = [first + g * size + n for n in range(size)]
-        values = [compute(n) for n in numbers]
-        for n, value in zip(numbers, values):
-            store(n, value)
-        return carry
-
-    lax.fori_loop(0, count // size, step, 0)
+    )(j, *lists, *pieces, *others, *arrays)
 
 
 def after(value, *done):
@@ -347,19 +322,27 @@
     sent, chip_rows = pack(field, mean_field, kl, j, lay)
     half = modes // 2
     pieces = sent[:1] + [None] * (lay.group - 1)
-    for r in [half, *range(half + 1, modes), *range(modes, modes + half), *range(1, half)]:
+    for r in [*range(half, modes), *range(modes, modes + half)]:
         pieces[r] = swap(sent[r], r)
     chip_halo = shift(chip_rows, False)
+    for r in range(1, half):
+        pieces[r] = swap(after(sent[r], chip_halo), r)
     first, last = modes + half, lay.group - 1
     pieces[first] = swap(after(sent[first], *pieces[half:first]), first)
     pieces[last] = swap(after(sent[last], *pieces[half:first]), last)
+    core_halo = swap(chip_halo, 1)
     number = jnp.arange(modes, dtype=jnp.int32)
     mine = jnp.bitwise_xor(number, mode)[:, None, None] == number[None, :, None]
     slot_mode = jnp.sum(jnp.where(mine, slot_mode.reshape(1, modes, quota), 0), 1).reshape(-1)
-    lists = coupling_lists(pattern, coupling, after(slot_mode, chip_halo))
-    pieces[first] = after(pieces[first], *lists)
-    own_halos = [chip_halo[:1], swap(chip_halo[1:], 1), shift(mains(pieces[half:modes]), False)]
-    crossing_halos = [shift(mains(pieces[r : r + half]), True) for r in (modes, first)]
+    lists = coupling_lists(pattern, coupling, slot_mode)
+    pieces[half] = after(pieces[half], *lists)
+    pieces[first] = after(pieces[first], core_halo, *pieces[1:half])
+    own_halo = shift(mains(pieces[half:modes]), False)
+    own_halos = [(chip_halo, 0), (core_halo, 1), (own_halo, 0), (own_halo, 1)]
+    crossing_halos = []
+    for r in (modes, first):
+        halo = shift(mains(pieces[r : r + half]), True)
+        crossing_halos += [(halo, 0), (halo, 1)]
 
     own, crossing = pieces[:modes], pieces[modes:]
     crossing_out = stencil(crossing, own, own_halos, lists, j, "stencil_crossing", lay)

time: 61.8 us -> 63.3 us (1.024)
  Pallas kernels: 11.9 us -> 9.72 us
  matrix products: 0.68 us -> 2.42 us
  waiting for transfers between devices: 13.5 us -> 15.2 us
  starting transfers between devices: 27.7 us -> 28.8 us
    ppermute x4, waiting for transfers between devices: 0.48 us -> 3.09 us  [shift(): return lax.ppermute(fields, axes, pairs)]
    pallas_call x2, Pallas kernels: 8.82 us -> 6.61 us  [stencil(): pl.pallas_call(kernel, out_shape=[jax.ShapeDtypeStruct((lay.quota, rows,...]
    dot_general x2, matrix products: 0.68 us -> 2.42 us  [coupling_lists(): jnp.einsum('sa,kab,tb->kst', one_hot, masked, one_hot, precision=lax.Prec...]
    another operation x3, other arithmetic: 1.56 us -> 0.1 us  [mains(): return jnp.stack([piece[:lay.main] for piece in pieces])]
    ppermute x15, starting transfers between devices: 17 us -> 18.3 us  [swap(): return lax.ppermute(piece, axes, [(d, d ^ r) for d in range(devices)])]
    slice x1 -> x0, local copies, waits for them, and re-layouts: 1.04 us -> none  [on_device(): chip_halo[1:]]
    reduce_sum x1, other arithmetic: 0.09 us -> 1.06 us  [coupling_lists(): jnp.sum(jnp.where(column == chosen_t[:, :, None], coupled, 0.0), 2)]
    ppermute x15, waiting for transfers between devices: 13 us -> 12.1 us  [swap(): return lax.ppermute(piece, axes, [(d, d ^ r) for d in range(devices)])]
  transfers between devices with their start and end apart: 19 -> 19, of which waited for: 7 -> 6; matrix products, arithmetic and copies ran while one was open for 13% -> 14% of each run, Pallas kernels for 14% -> 10%
where the time goes in v11:
time: 63.3 us; the launch traced here: 63 us
  starting transfers between devices  28.8 us (45%)
  waiting for transfers between devices  15.2 us (24%)
  Pallas kernels  9.72 us (15%)
  local copies, waits for them, and re-layouts  4.44 us (7%)
  matrix products  2.42 us (4%)
  other arithmetic  2.22 us (4%)
    ppermute x15, starting transfers between devices, swap(): return lax.ppermute(piece, axes, [(d, d ^ r) for d in range(devices)])  18.3 us
    ppermute x15, waiting for transfers between devices, swap(): return lax.ppermute(piece, axes, [(d, d ^ r) for d in range(devices)])  12.1 us
    ppermute x4, starting transfers between devices, shift(): return lax.ppermute(fields, axes, pairs)  10.5 us
    pallas_call x2, Pallas kernels, stencil(): pl.pallas_call(kernel, out_shape=[jax.ShapeDtypeStruct((lay.quota, rows,...  6.61 us
    unnamed x4, local copies, waits for them, and re-layouts  3.74 us
    ppermute x4, waiting for transfers between devices, shift(): return lax.ppermute(fields, axes, pairs)  3.09 us
    dot_general x2, matrix products, coupling_lists(): jnp.einsum('sa,kab,tb->kst', one_hot, masked, one_hot, precision=lax.Prec...  2.42 us
    pallas_call x1, Pallas kernels, pack(): pl.pallas_call(kernel, out_shape=[pltpu.VMEM(shape, jnp.float32)] * lay.g...  1.97 us
  transfers between devices with their start and end apart: 19, of which 6 were waited for; matrix products, arithmetic and copies ran while one was open for 14% of the time, Pallas kernels for 10%

profile of v11, /device:TPU:0, one launch (start us, length us, event | category | flops | bytes accessed | tf_op | source)
XLA Modules:
  0.0 63.0 jit_solution(1227140743039454728)
XLA Ops:
  0.0 0.0 copy-start
  0.0 2.0 %pack.1 = (f32[26,16,128]{2,1,0:T(8,128)S(1)}, f32[26,16,128]{2,1,0:T(8,128)S(1)}, f32[26,16,128]{2,1,0:T(8,128)S(1)}, f32[26,16,128]{2,1,0:T(8,128)S(1)}, f32[2...) custom-call(s32[1]{0:T(128)} %bitcast.j_ref, ...), custom_call_target="tpu_custom_call" | custom-call | tf_op jit(solution)/shard_map/pack/pallas_call | solution.py:112
  2.0 3.0 %collective-permute-start = (f32[416,128]{1,0:T(8,128)S(1)}, f32[416,128]{1,0:T(8,128)S(1)}, u32[]{:S(2)}, u32[]{:S(2)}) collective-permute-start(f32[416,128]{1,0:T(8,128)S(1)} %bitcast.45), channel_id=1, source_target_pairs={{0,4},{1,5},{2,6},{3,7},{4,0},{5,1},{6,2},{7,3},{8,12},{9,13},{10,... | collective-permute-start | bytes 638984 | tf_op jit(solution)/shard_map/ppermute | solution.py:307
  5.0 0.0 collective-permute-start.1
  5.0 1.5 %collective-permute-start.2 = (f32[416,128]{1,0:T(8,128)S(1)}, f32[416,128]{1,0:T(8,128)S(1)}, u32[]{:S(2)}, u32[]{:S(2)}) collective-permute-start(f32[416,128]{1,0:T(8,128)S(1)} %bitcast.43), channel_id=1, source_target_pairs={{0,2},{1,3},{2,0},{3,1},{4,6},{5,7},{6,4},{7,5},{8,10},{9,11},{10,... | collective-permute-start | bytes 638984 | tf_op jit(solution)/shard_map/ppermute | solution.py:307
  6.5 0.3 collective-permute-start.3
  6.8 1.3 %collective-permute-start.5 = (f32[2,368,128]{2,1,0:T(8,128)S(1)}, f32[2,368,128]{2,1,0:T(8,128)S(1)}, u32[]{:S(2)}, u32[]{:S(2)}) collective-permute-start(f32[2,368,128]{2,1,0:T(8,128)S(1)} %bitcast.38), channel_id=1, source_target_pairs={{4,12},{5,13},{6,14},{7,15},{8,0},{9,1},{10,2},{11,3},{12,20},{13,... | collective-permute-start | bytes 1130504 | tf_op jit(solution)/shard_map/ppermute | solution.py:316
  8.1 1.9 %copy.10 = f32[7,84,84]{1,2,0:T(8,128)} copy(f32[7,84,84]{2,1,0:T(8,128)} %param.10) | data formatting | bytes 395136 | tf_op args[4]
  10.0 1.9 %copy.9 = s32[7,84,84]{1,2,0:T(8,128)} copy(s32[7,84,84]{2,1,0:T(8,128)} %param.9) | data formatting | bytes 395136 | tf_op args[3]
  11.9 0.0 copy-done
  11.9 0.1 broadcast_in_dim.135
  12.0 0.1 iota_compare_fusion.9
  12.0 0.1 select_reduce_fusion.9
  12.1 0.1 eq.38
  12.2 1.4 %fusion = f32[6,84,84]{2,1,0:T(8,128)S(1)} fusion(f32[7,84,84]{1,2,0:T(8,128)} %copy.10, s32[7,84,84]{1,2,0:T(8,128)} %copy.9, s32[84]{0:T(128)S(1)} %eq.38), kind=kOutput, calls=%fused_computation.3 | convolution fusion | flops 42780528 | bytes 564816 | tf_op jit(solution)/shard_map/sa,kab,tb->kst/dot_general | solution.py:161
  13.6 1.0 %fusion.10 = (u8[84,84]{0,1:T(8,128)(4,1)S(1)}, f32[6,84,84]{1,2,0:T(8,128)}) fusion(f32[6,84,84]{2,1,0:T(8,128)S(1)} %fusion, s32[84]{0:T(128)S(1)} %eq.38), kind=kOutput, calls=%fused_computation.33 | convolution fusion | flops 42886368 | bytes 346080 | tf_op jit(solution)/shard_map/sa,kab,tb->kst/dot_general | solution.py:161
  14.6 0.1 fusion.5
  14.8 0.2 select_reduce_fusion.4
  15.0 0.1 broadcast_add_fusion.1
  15.1 0.1 select_reduce_fusion.6
  15.3 0.1 copy.11
  15.4 0.1 reshape.113
  15.5 0.2 select_reduce_fusion.5
  15.6 0.1 reshape.112
  15.7 1.1 %select_reduce_fusion.1 = (f32[6,84]{1,0:T(8,128)S(1)}, f32[6,84]{1,0:T(8,128)S(1)}) fusion(f32[6,84,84]{1,2,0:T(8,128)} %get-tuple-element.67, s32[6,84]{1,0:T(8,128)S(1)} %get-tuple-element.57, s32[6,84]{1,0:T(8,128)S(1)} %get-tuple-element.58), kind=kLoop, calls=%fused_computation.14 | loop fusion | flops 253008 | bytes 177408 | tf_op jit(solution)/shard_map/reduce_sum | solution.py:180
  16.8 0.1 copy.12
  16.9 0.1 reshape.114.factor_ref
  17.0 0.1 pad_add_fusion.2.index_ref
  17.1 0.0 collective-permute-done.refs_0_.refs_4_
  17.1 0.0 collective-permute-done.1.refs_1_.refs_5_
  17.1 0.0 collective-permute-done.2.refs_6_.refs_2_
  17.1 0.0 collective-permute-done.3.refs_7_.refs_3_
  17.1 4.9 %collective-permute-start.4 = (f32[416,128]{1,0:T(8,128)S(1)}, f32[416,128]{1,0:T(8,128)S(1)}, u32[]{:S(2)}, u32[]{:S(2)}) collective-permute-start(f32[416,128]{1,0:T(8,128)S(1)} %bitcast.40), channel_id=1, source_target_pairs={{0,6},{1,7},{2,4},{3,5},{4,2},{5,3},{6,0},{7,1},{8,14},{9,15},{10,... | collective-permute-start | bytes 638984 | tf_op jit(solution)/shard_map/ppermute | solution.py:307
  22.0 0.0 collective-permute-start.8
  22.1 1.3 %collective-permute-start.9 = (f32[2,368,128]{2,1,0:T(8,128)S(1)}, f32[2,368,128]{2,1,0:T(8,128)S(1)}, u32[]{:S(2)}, u32[]{:S(2)}) collective-permute-start(f32[2,368,128]{2,1,0:T(8,128)S(1)} %pad_maximum_fusion), channel_id=1, source_target_pairs={{4,12},{5,13},{6,14},{7,15},{8,0},{9,1},{10,2},{11,3},{12,20},{13,... | collective-permute-start | bytes 1130504 | tf_op jit(solution)/shard_map/ppermute | solution.py:316
  23.4 0.0 collective-permute-done.5.refs_8_
  23.4 0.3 collective-permute-start.6
  23.7 4.4 %collective-permute-start.12 = (f32[2,368,128]{2,1,0:T(8,128)S(1)}, f32[2,368,128]{2,1,0:T(8,128)S(1)}, u32[]{:S(2)}, u32[]{:S(2)}) collective-permute-start(f32[2,368,128]{2,1,0:T(8,128)S(1)} %pad_maximum_fusion.1), channel_id=1, source_target_pairs={{0,8},{1,9},{2,10},{3,11},{8,16},{9,17},{10,18},{11,19},{12,4},{13... | collective-permute-start | bytes 1130504 | tf_op jit(solution)/shard_map/ppermute | solution.py:316
  28.1 2.7 %collective-permute-done.8.refs_3_.refs_7_ = f32[416,128]{1,0:T(8,128)S(1)} collective-permute-done((f32[416,128]{1,0:T(8,128)S(1)}, f32[416,128]{1,0:T(8,128)S(1)}, u32[]{:S(2)}, u32[]{:S(2)}) %collective-permute-start.8) | collective-permute-done | bytes 213024 | tf_op jit(solution)/shard_map/ppermute | solution.py:307
  30.8 0.6 collective-permute-start.7
  31.4 0.0 collective-permute-done.4.refs_2_.refs_6_
  31.4 1.1 %collective-permute-done.7.refs_5_.refs_1_ = f32[416,128]{1,0:T(8,128)S(1)} collective-permute-done((f32[416,128]{1,0:T(8,128)S(1)}, f32[416,128]{1,0:T(8,128)S(1)}, u32[]{:S(2)}, u32[]{:S(2)}) %collective-permute-start.7) | collective-permute-done | bytes 213024 | tf_op jit(solution)/shard_map/ppermute | solution.py:307
  32.5 0.0 collective-permute-done.6.refs_9_
  32.5 3.5 %collective-permute-start.13 = (f32[2,368,128]{2,1,0:T(8,128)S(1)}, f32[2,368,128]{2,1,0:T(8,128)S(1)}, u32[]{:S(2)}, u32[]{:S(2)}) collective-permute-start(f32[2,368,128]{2,1,0:T(8,128)S(1)} %pad_maximum_fusion.2), channel_id=1, source_target_pairs={{0,8},{1,9},{2,10},{3,11},{8,16},{9,17},{10,18},{11,19},{12,4},{13... | collective-permute-start | bytes 1130504 | tf_op jit(solution)/shard_map/ppermute | solution.py:316
  36.0 0.0 collective-permute-done.9.refs_10_
  36.0 3.3 %stencil_crossing.1 = (f32[21,16,128]{2,1,0:T(8,128)S(1)}, f32[21,16,128]{2,1,0:T(8,128)S(1)}, f32[21,16,128]{2,1,0:T(8,128)S(1)}, f32[21,16,128]{2,1,0:T(8,128)S(1)}) custom-call(s32[1]{0:T(128)} %bitcast.j_ref, s32[966]{0:T(1024)S(1)} %pad_add_fusion.2.index_ref, f32[672]{0:T(1024)S(1)} %reshape.114.factor_ref, ...), custom_call_target="tpu_custom_call" | custom-call | tf_op jit(solution)/shard_map/stencil_crossing/pallas_call | solution.py:275
  39.4 0.5 collective-permute-start.10
  39.9 1.9 %collective-permute-start.11 = (f32[21,16,128]{2,1,0:T(8,128)S(1)}, f32[21,16,128]{2,1,0:T(8,128)S(1)}, u32[]{:S(2)}, u32[]{:S(2)}) collective-permute-start(f32[21,16,128]{2,1,0:T(8,128)S(1)} %get-tuple-element.45), channel_id=1, source_target_pairs={{0,7},{1,6},{2,5},{3,4},{4,3},{5,2},{6,1},{7,0},{8,15},{9,14},{10,... | collective-permute-start | bytes 516104 | tf_op jit(solution)/shard_map/ppermute | solution.py:307
  41.8 0.0 collective-permute-done.12.refs_8_
  41.8 3.1 %collective-permute-done.13.refs_9_ = f32[2,368,128]{2,1,0:T(8,128)S(1)} collective-permute-done((f32[2,368,128]{2,1,0:T(8,128)S(1)}, f32[2,368,128]{2,1,0:T(8,128)S(1)}, u32[]{:S(2)}, u32[]{:S(2)}) %collective-permute-start.13) | collective-permute-done | bytes 376864 | tf_op jit(solution)/shard_map/ppermute | solution.py:316
  44.9 3.3 %stencil_own.1 = (f32[21,16,128]{2,1,0:T(8,128)S(1)}, f32[21,16,128]{2,1,0:T(8,128)S(1)}, f32[21,16,128]{2,1,0:T(8,128)S(1)}, f32[21,16,128]{2,1,0:T(8,128)S(1)}) custom-call(s32[1]{0:T(128)} %bitcast.j_ref, s32[966]{0:T(1024)S(1)} %pad_add_fusion.2.index_ref, f32[672]{0:T(1024)S(1)} %reshape.114.factor_ref, f32[416,128]{1,0:T(8,128)S(1)} %bitcast.37, ...), custom_call_target="tpu_custom_call" | custom-call | tf_op jit(solution)/shard_map/stencil_own/pallas_call | solution.py:275
  48.2 0.7 %collective-permute-start.14 = (f32[21,16,128]{2,1,0:T(8,128)S(1)}, f32[21,16,128]{2,1,0:T(8,128)S(1)}, u32[]{:S(2)}, u32[]{:S(2)}) collective-permute-start(f32[21,16,128]{2,1,0:T(8,128)S(1)} %get-tuple-element.49), channel_id=1, source_target_pairs={{0,2},{1,3},{2,0},{3,1},{4,6},{5,7},{6,4},{7,5},{8,10},{9,11},{10,... | collective-permute-start | bytes 516104 | tf_op jit(solution)/shard_map/ppermute | solution.py:307
  48.8 0.6 collective-permute-start.16
  49.4 3.7 %collective-permute-start.15 = (f32[21,16,128]{2,1,0:T(8,128)S(1)}, f32[21,16,128]{2,1,0:T(8,128)S(1)}, u32[]{:S(2)}, u32[]{:S(2)}) collective-permute-start(f32[21,16,128]{2,1,0:T(8,128)S(1)} %get-tuple-element.53), channel_id=1, source_target_pairs={{0,4},{1,5},{2,6},{3,7},{4,0},{5,1},{6,2},{7,3},{8,12},{9,13},{10,... | collective-permute-start | bytes 516104 | tf_op jit(solution)/shard_map/ppermute | solution.py:307
  53.1 0.0 collective-permute-done.10.refs_0_
  53.1 0.2 collective-permute-start.17
  53.3 0.0 collective-permute-done.11.refs_1_
  53.3 0.2 collective-permute-start.18
  53.5 2.0 %collective-permute-done.14.refs_2_ = f32[21,16,128]{2,1,0:T(8,128)S(1)} collective-permute-done((f32[21,16,128]{2,1,0:T(8,128)S(1)}, f32[21,16,128]{2,1,0:T(8,128)S(1)}, u32[]{:S(2)}, u32[]{:S(2)}) %collective-permute-start.14) | collective-permute-done | bytes 172064 | tf_op jit(solution)/shard_map/ppermute | solution.py:307
  55.5 2.8 %collective-permute-done.15.refs_3_ = f32[21,16,128]{2,1,0:T(8,128)S(1)} collective-permute-done((f32[21,16,128]{2,1,0:T(8,128)S(1)}, f32[21,16,128]{2,1,0:T(8,128)S(1)}, u32[]{:S(2)}, u32[]{:S(2)}) %collective-permute-start.15) | collective-permute-done | bytes 172064 | tf_op jit(solution)/shard_map/ppermute | solution.py:307
  58.3 0.0 collective-permute-done.16.refs_4_
  58.3 3.5 %collective-permute-done.17.refs_5_ = f32[21,16,128]{2,1,0:T(8,128)S(1)} collective-permute-done((f32[21,16,128]{2,1,0:T(8,128)S(1)}, f32[21,16,128]{2,1,0:T(8,128)S(1)}, u32[]{:S(2)}, u32[]{:S(2)}) %collective-permute-start.17) | collective-permute-done | bytes 172064 | tf_op jit(solution)/shard_map/ppermute | solution.py:307
  61.8 0.0 collective-permute-done.18.refs_7_
  61.8 1.1 %unpack.1 = f32[21,128,128]{2,1,0:T(8,128)} custom-call(s32[1]{0:T(128)} %bitcast.j_ref, f32[21,16,128]{2,1,0:T(8,128)S(1)} %collective-permute-done.10.refs_0_, f32[21,16,128]{2,1,0:T(8,128)S(1)} %collective-permute-done.11.refs_1_, f32[21,16,128]{2,1,0:T(8,128)S(1)} %collective-permute-done.14.refs_2_, f32[21,16,128]{2,1,0:T(8,128)S(1)} %collective-permute-done.15.refs_3_, ...), custom_call_target="tpu_custom_call" | custom-call | tf_op jit(solution)/shard_map/unpack/pallas_call | solution.py:145
  (19 shorter events, 0.3 us)
Async XLA Ops:
  0.0 11.9 %copy-start = (s32[84]{0:T(128)S(1)}, s32[84]{0:T(128)}, u32[]{:S(2)}) copy-start(s32[84]{0:T(128)} %param.11) | copy-start | bytes 1012
  2.0 15.1 %collective-permute-start = (f32[416,128]{1,0:T(8,128)S(1)}, f32[416,128]{1,0:T(8,128)S(1)}, u32[]{:S(2)}, u32[]{:S(2)}) collective-permute-start(f32[416,128]{1,0:T(8,128)S(1)} %bitcast.45), channel_id=1, source_target_pairs={{0,4},{1,5},{2,6},{3,7},{4,0},{5,1},{6,2},{7,3},{8,12},{9,13},{10,... | collective-permute-start | bytes 638984 | tf_op jit(solution)/shard_map/ppermute | solution.py:307
  5.0 12.1 %collective-permute-start.1 = (f32[416,128]{1,0:T(8,128)S(1)}, f32[416,128]{1,0:T(8,128)S(1)}, u32[]{:S(2)}, u32[]{:S(2)}) collective-permute-start(f32[416,128]{1,0:T(8,128)S(1)} %bitcast.44), channel_id=1, source_target_pairs={{0,5},{1,4},{2,7},{3,6},{4,1},{5,0},{6,3},{7,2},{8,13},{9,12},{10,... | collective-permute-start | bytes 638984 | tf_op jit(solution)/shard_map/ppermute | solution.py:307
  5.0 12.1 %collective-permute-start.2 = (f32[416,128]{1,0:T(8,128)S(1)}, f32[416,128]{1,0:T(8,128)S(1)}, u32[]{:S(2)}, u32[]{:S(2)}) collective-permute-start(f32[416,128]{1,0:T(8,128)S(1)} %bitcast.43), channel_id=1, source_target_pairs={{0,2},{1,3},{2,0},{3,1},{4,6},{5,7},{6,4},{7,5},{8,10},{9,11},{10,... | collective-permute-start | bytes 638984 | tf_op jit(solution)/shard_map/ppermute | solution.py:307
  6.5 10.6 %collective-permute-start.3 = (f32[416,128]{1,0:T(8,128)S(1)}, f32[416,128]{1,0:T(8,128)S(1)}, u32[]{:S(2)}, u32[]{:S(2)}) collective-permute-start(f32[416,128]{1,0:T(8,128)S(1)} %bitcast.42), channel_id=1, source_target_pairs={{0,3},{1,2},{2,1},{3,0},{4,7},{5,6},{6,5},{7,4},{8,11},{9,10},{10,... | collective-permute-start | bytes 638984 | tf_op jit(solution)/shard_map/ppermute | solution.py:307
  6.8 16.6 %collective-permute-start.5 = (f32[2,368,128]{2,1,0:T(8,128)S(1)}, f32[2,368,128]{2,1,0:T(8,128)S(1)}, u32[]{:S(2)}, u32[]{:S(2)}) collective-permute-start(f32[2,368,128]{2,1,0:T(8,128)S(1)} %bitcast.38), channel_id=1, source_target_pairs={{4,12},{5,13},{6,14},{7,15},{8,0},{9,1},{10,2},{11,3},{12,20},{13,... | collective-permute-start | bytes 1130504 | tf_op jit(solution)/shard_map/ppermute | solution.py:316
  17.1 14.3 %collective-permute-start.4 = (f32[416,128]{1,0:T(8,128)S(1)}, f32[416,128]{1,0:T(8,128)S(1)}, u32[]{:S(2)}, u32[]{:S(2)}) collective-permute-start(f32[416,128]{1,0:T(8,128)S(1)} %bitcast.40), channel_id=1, source_target_pairs={{0,6},{1,7},{2,4},{3,5},{4,2},{5,3},{6,0},{7,1},{8,14},{9,15},{10,... | collective-permute-start | bytes 638984 | tf_op jit(solution)/shard_map/ppermute | solution.py:307
  22.0 8.8 %collective-permute-start.8 = (f32[416,128]{1,0:T(8,128)S(1)}, f32[416,128]{1,0:T(8,128)S(1)}, u32[]{:S(2)}, u32[]{:S(2)}) collective-permute-start(f32[416,128]{1,0:T(8,128)S(1)} %bitcast.41), channel_id=1, source_target_pairs={{0,7},{1,6},{2,5},{3,4},{4,3},{5,2},{6,1},{7,0},{8,15},{9,14},{10,... | collective-permute-start | bytes 638984 | tf_op jit(solution)/shard_map/ppermute | solution.py:307
  22.1 13.9 %collective-permute-start.9 = (f32[2,368,128]{2,1,0:T(8,128)S(1)}, f32[2,368,128]{2,1,0:T(8,128)S(1)}, u32[]{:S(2)}, u32[]{:S(2)}) collective-permute-start(f32[2,368,128]{2,1,0:T(8,128)S(1)} %pad_maximum_fusion), channel_id=1, source_target_pairs={{4,12},{5,13},{6,14},{7,15},{8,0},{9,1},{10,2},{11,3},{12,20},{13,... | collective-permute-start | bytes 1130504 | tf_op jit(solution)/shard_map/ppermute | solution.py:316
  23.4 9.0 %collective-permute-start.6 = (f32[2,368,128]{2,1,0:T(8,128)S(1)}, f32[2,368,128]{2,1,0:T(8,128)S(1)}, u32[]{:S(2)}, u32[]{:S(2)}) collective-permute-start(f32[2,368,128]{2,1,0:T(8,128)S(1)} %collective-permute-done.5.refs_8_), channel_id=1, source_target_pairs={{0,1},{1,0},{2,3},{3,2},{4,5},{5,4},{6,7},{7,6},{8,9},{9,8},{10,11... | collective-permute-start | bytes 1130504 | tf_op jit(solution)/shard_map/ppermute | solution.py:307
  23.7 18.0 %collective-permute-start.12 = (f32[2,368,128]{2,1,0:T(8,128)S(1)}, f32[2,368,128]{2,1,0:T(8,128)S(1)}, u32[]{:S(2)}, u32[]{:S(2)}) collective-permute-start(f32[2,368,128]{2,1,0:T(8,128)S(1)} %pad_maximum_fusion.1), channel_id=1, source_target_pairs={{0,8},{1,9},{2,10},{3,11},{8,16},{9,17},{10,18},{11,19},{12,4},{13... | collective-permute-start | bytes 1130504 | tf_op jit(solution)/shard_map/ppermute | solution.py:316
  30.8 1.7 %collective-permute-start.7 = (f32[416,128]{1,0:T(8,128)S(1)}, f32[416,128]{1,0:T(8,128)S(1)}, u32[]{:S(2)}, u32[]{:S(2)}) collective-permute-start(f32[416,128]{1,0:T(8,128)S(1)} %bitcast.39), channel_id=1, source_target_pairs={{0,1},{1,0},{2,3},{3,2},{4,5},{5,4},{6,7},{7,6},{8,9},{9,8},{10,11... | collective-permute-start | bytes 638984 | tf_op jit(solution)/shard_map/ppermute | solution.py:307
  32.5 12.3 %collective-permute-start.13 = (f32[2,368,128]{2,1,0:T(8,128)S(1)}, f32[2,368,128]{2,1,0:T(8,128)S(1)}, u32[]{:S(2)}, u32[]{:S(2)}) collective-permute-start(f32[2,368,128]{2,1,0:T(8,128)S(1)} %pad_maximum_fusion.2), channel_id=1, source_target_pairs={{0,8},{1,9},{2,10},{3,11},{8,16},{9,17},{10,18},{11,19},{12,4},{13... | collective-permute-start | bytes 1130504 | tf_op jit(solution)/shard_map/ppermute | solution.py:316
  39.4 13.7 %collective-permute-start.10 = (f32[21,16,128]{2,1,0:T(8,128)S(1)}, f32[21,16,128]{2,1,0:T(8,128)S(1)}, u32[]{:S(2)}, u32[]{:S(2)}) collective-permute-start(f32[21,16,128]{2,1,0:T(8,128)S(1)} %get-tuple-element.44), channel_id=1, source_target_pairs={{0,6},{1,7},{2,4},{3,5},{4,2},{5,3},{6,0},{7,1},{8,14},{9,15},{10,... | collective-permute-start | bytes 516104 | tf_op jit(solution)/shard_map/ppermute | solution.py:307
  39.9 13.5 %collective-permute-start.11 = (f32[21,16,128]{2,1,0:T(8,128)S(1)}, f32[21,16,128]{2,1,0:T(8,128)S(1)}, u32[]{:S(2)}, u32[]{:S(2)}) collective-permute-start(f32[21,16,128]{2,1,0:T(8,128)S(1)} %get-tuple-element.45), channel_id=1, source_target_pairs={{0,7},{1,6},{2,5},{3,4},{4,3},{5,2},{6,1},{7,0},{8,15},{9,14},{10,... | collective-permute-start | bytes 516104 | tf_op jit(solution)/shard_map/ppermute | solution.py:307
  48.2 7.3 %collective-permute-start.14 = (f32[21,16,128]{2,1,0:T(8,128)S(1)}, f32[21,16,128]{2,1,0:T(8,128)S(1)}, u32[]{:S(2)}, u32[]{:S(2)}) collective-permute-start(f32[21,16,128]{2,1,0:T(8,128)S(1)} %get-tuple-element.49), channel_id=1, source_target_pairs={{0,2},{1,3},{2,0},{3,1},{4,6},{5,7},{6,4},{7,5},{8,10},{9,11},{10,... | collective-permute-start | bytes 516104 | tf_op jit(solution)/shard_map/ppermute | solution.py:307
  48.8 9.5 %collective-permute-start.16 = (f32[21,16,128]{2,1,0:T(8,128)S(1)}, f32[21,16,128]{2,1,0:T(8,128)S(1)}, u32[]{:S(2)}, u32[]{:S(2)}) collective-permute-start(f32[21,16,128]{2,1,0:T(8,128)S(1)} %get-tuple-element.52), channel_id=1, source_target_pairs={{0,3},{1,2},{2,1},{3,0},{4,7},{5,6},{6,5},{7,4},{8,11},{9,10},{10,... | collective-permute-start | bytes 516104 | tf_op jit(solution)/shard_map/ppermute | solution.py:307
  49.4 8.9 %collective-permute-start.15 = (f32[21,16,128]{2,1,0:T(8,128)S(1)}, f32[21,16,128]{2,1,0:T(8,128)S(1)}, u32[]{:S(2)}, u32[]{:S(2)}) collective-permute-start(f32[21,16,128]{2,1,0:T(8,128)S(1)} %get-tuple-element.53), channel_id=1, source_target_pairs={{0,4},{1,5},{2,6},{3,7},{4,0},{5,1},{6,2},{7,3},{8,12},{9,13},{10,... | collective-permute-start | bytes 516104 | tf_op jit(solution)/shard_map/ppermute | solution.py:307
  53.1 8.8 %collective-permute-start.17 = (f32[21,16,128]{2,1,0:T(8,128)S(1)}, f32[21,16,128]{2,1,0:T(8,128)S(1)}, u32[]{:S(2)}, u32[]{:S(2)}) collective-permute-start(f32[21,16,128]{2,1,0:T(8,128)S(1)} %get-tuple-element.54), channel_id=1, source_target_pairs={{0,5},{1,4},{2,7},{3,6},{4,1},{5,0},{6,3},{7,2},{8,13},{9,12},{10,... | collective-permute-start | bytes 516104 | tf_op jit(solution)/shard_map/ppermute | solution.py:307
  53.3 8.5 %collective-permute-start.18 = (f32[21,16,128]{2,1,0:T(8,128)S(1)}, f32[21,16,128]{2,1,0:T(8,128)S(1)}, u32[]{:S(2)}, u32[]{:S(2)}) collective-permute-start(f32[21,16,128]{2,1,0:T(8,128)S(1)} %get-tuple-element.51), channel_id=1, source_target_pairs={{0,1},{1,0},{2,3},{3,2},{4,5},{5,4},{6,7},{7,6},{8,9},{9,8},{10,11... | collective-permute-start | bytes 516104 | tf_op jit(solution)/shard_map/ppermute | solution.py:307

commit v12 on v11

--- a/solution.py
+++ b/solution.py
@@ -7,7 +7,6 @@
 
 VMEM_LIMIT = 40 * 1024 * 1024
 PLANES = 2
-CORES = 2
 ACTIVE = 49
 MOST = 8
 
@@ -50,26 +49,35 @@
     return [pl.BlockSpec(memory_space=pltpu.SMEM)] * count
 
 
-def pack(field, mean, kl, j, lay):
+def pack(field, mean, kl, j, crossing, lay):
     kl_terms = kl.shape[0]
-    rows, width, quota = lay.rows, lay.width, lay.quota
+    rows, width, modes, quota = lay.rows, lay.width, lay.modes, lay.quota
+    half = modes * rows
+    tile = 8
 
     def kernel(j_ref, field_ref, mean_ref, kl_ref, *refs):
-        out_refs, (halo_ref, stage_ref, sems) = refs[: lay.group], refs[lay.group :]
-        mode = lax.rem(j_ref[0], lay.modes)
+        out_refs, (stage_ref, past_ref, in_sems) = refs[:modes], refs[modes:]
+        plane = j_ref[0] // modes
+        mode = j_ref[0] - plane * modes
+        side = 1 - plane if crossing else plane
+        start = side * half
+        beside = pl.multiple_of(half - side * tile, tile)
 
         def load(n, begin=True):
-            at, target = pl.ds(n * rows, rows), stage_ref.at[n]
+            if n < modes:
+                at, target = pl.ds(pl.multiple_of(start + n * rows, tile), rows), stage_ref.at[n]
+            else:
+                at, target = pl.ds(beside, tile), past_ref
             copies = [
                 pltpu.make_async_copy(
-                    field_ref.at[:, at, :], target.at[pl.ds(0, quota)], sems.at[n, 0]
+                    field_ref.at[:, at, :], target.at[pl.ds(0, quota)], in_sems.at[n, 0]
                 )
             ]
             if begin:
                 copies[0].start()
             for i in range(lay.share):
                 term = mode * lay.share + i
-                into, sem = target.at[quota + i], sems.at[n, 1 + i]
+                into, sem = target.at[quota + i], in_sems.at[n, 1 + i]
                 if not begin:
                     copies.append(pltpu.make_async_copy(mean_ref.at[0, at, :], into, sem))
                     continue
@@ -85,45 +93,49 @@
 
             return copies
 
-        for n in range(lay.group):
+        for n in range(modes + 1):
             load(n)
-        for n in range(lay.group):
+        for n in range(modes + 1):
             for made in load(n, begin=False):
                 made.wait()
-        none = jnp.zeros((1, width), jnp.float32)
-        for n in range(lay.group):
+        low_there = jnp.where(side == 0, 0.0, 1.0)
+        high_there = jnp.where(side == PLANES - 1, 0.0, 1.0)
+        for n in range(modes):
             for i in range(lay.fields):
+                if n > 0:
+                    low = stage_ref[n - 1, i, rows - 1 :]
+                else:
+                    low = past_ref[i, tile - 1 :] * low_there
+                if n < modes - 1:
+                    high = stage_ref[n + 1, i, :1]
+                else:
+                    high = past_ref[i, :1] * high_there
                 part, line = lay.edge(i)
-                low = stage_ref[n - 1, i, rows - 1 :] if n > 0 else none
-                high = stage_ref[n + 1, i, :1] if n < lay.group - 1 else none
                 stage_ref[n, part, line : line + 1] = low
                 stage_ref[n, part, line + 1 : line + 2] = high
             part, line = lay.edge(lay.fields)
             if part < lay.parts:
                 stage_ref[n, part, line:] = jnp.zeros((rows - line, width), jnp.float32)
-        for r, out_ref in enumerate(out_refs):
-            to = jnp.bitwise_xor(j_ref[0], r)
+        for n, out_ref in enumerate(out_refs):
+            to = jnp.bitwise_xor(mode, n)
             for part in range(lay.parts):
                 out_ref[part] = stage_ref[to, part]
-                if r < CORES and part < lay.fields:
-                    halo_ref[r, part] = stage_ref[to, part]
 
     shape = (lay.parts, rows, width)
-    *sent, halo = pl.pallas_call(
+    sent = pl.pallas_call(
         kernel,
-        out_shape=[pltpu.VMEM(shape, jnp.float32)] * lay.group
-        + [pltpu.VMEM((CORES, lay.fields, rows, width), jnp.float32)],
+        out_shape=[pltpu.VMEM(shape, jnp.float32)] * modes,
         in_specs=smem(1) + [pl.BlockSpec(memory_space=pltpu.HBM)] * 3,
-        out_specs=vmem(lay.group + 1),
+        out_specs=vmem(modes),
         scratch_shapes=[
-            pltpu.VMEM((lay.group, *shape), jnp.float32),
-            pltpu.SemaphoreType.DMA((lay.group, 1 + lay.share)),
+            pltpu.VMEM((modes, *shape), jnp.float32),
+            pltpu.VMEM((lay.fields, tile, width), jnp.float32),
+            pltpu.SemaphoreType.DMA((modes + 1, 1 + lay.share)),
         ],
         compiler_params=pltpu.CompilerParams(vmem_limit_bytes=VMEM_LIMIT),
-        name="pack",
+        name="pack_crossing" if crossing else "pack_own",
     )(j, *[pltpu.with_memory_space_constraint(x, pltpu.HBM) for x in (field, mean, kl)])
-    sent = [piece.reshape(lay.piece, width) for piece in sent]
-    return sent, halo.reshape(CORES, lay.main, width)
+    return [piece.reshape(lay.piece, width) for piece in sent]
 
 
 def unpack(pieces, j, shape, lay):
@@ -306,43 +318,37 @@
             return piece
         return lax.ppermute(piece, axes, [(d, d ^ r) for d in range(devices)])
 
-    def shift(fields, crossing):
+    def shift(pieces, crossing):
         pairs = []
         for d in range(devices):
             upper = (d // modes) % PLANES == (0 if crossing else 1)
             other = d + lay.group if upper else d - lay.group
             if 0 <= other < devices:
                 pairs.append((d, other))
-        return lax.ppermute(fields, axes, pairs)
-
-    def mains(pieces):
-        return jnp.stack([piece[: lay.main] for piece in pieces])
+        main = jnp.stack([piece[: lay.main] for piece in pieces])
+        return lax.ppermute(main, axes, pairs)
 
     field, kl = chaos_field[:, 0], kl_fields[:, 0]
-    sent, chip_rows = pack(field, mean_field, kl, j, lay)
+    sent = [None] * lay.group
+    sent[:modes] = pack(field, mean_field, kl, j, False, lay)
+    sent[modes:] = pack(field, mean_field, kl, after(j, *sent[:modes]), True, lay)
     half = modes // 2
     pieces = sent[:1] + [None] * (lay.group - 1)
-    for r in [*range(half, modes), *range(modes, modes + half)]:
+    for r in [*range(half, modes), *range(1, half), *range(modes, modes + half)]:
         pieces[r] = swap(sent[r], r)
-    chip_halo = shift(chip_rows, False)
-    for r in range(1, half):
-        pieces[r] = swap(after(sent[r], chip_halo), r)
-    first, last = modes + half, lay.group - 1
-    pieces[first] = swap(after(sent[first], *pieces[half:first]), first)
-    pieces[last] = swap(after(sent[last], *pieces[half:first]), last)
-    core_halo = swap(chip_halo, 1)
+    for r in range(modes + half, lay.group):
+        pieces[r] = swap(after(sent[r], *pieces[half:modes]), r)
     number = jnp.arange(modes, dtype=jnp.int32)
     mine = jnp.bitwise_xor(number, mode)[:, None, None] == number[None, :, None]
     slot_mode = jnp.sum(jnp.where(mine, slot_mode.reshape(1, modes, quota), 0), 1).reshape(-1)
     lists = coupling_lists(pattern, coupling, slot_mode)
     pieces[half] = after(pieces[half], *lists)
-    pieces[first] = after(pieces[first], core_halo, *pieces[1:half])
-    own_halo = shift(mains(pieces[half:modes]), False)
-    own_halos = [(chip_halo, 0), (core_halo, 1), (own_halo, 0), (own_halo, 1)]
+    own_halo = shift(pieces[:modes], False)
+    own_halos = [(own_halo, n) for n in range(modes)]
     crossing_halos = []
-    for r in (modes, first):
-        halo = shift(mains(pieces[r : r + half]), True)
-        crossing_halos += [(halo, 0), (halo, 1)]
+    for r in (modes, modes + half):
+        halo = shift(pieces[r : r + half], True)
+        crossing_halos += [(halo, n) for n in range(half)]
 
     own, crossing = pieces[:modes], pieces[modes:]
     crossing_out = stencil(crossing, own, own_halos, lists, j, "stencil_crossing", lay)

time: 63.3 us -> 58.3 us (0.921)
  starting transfers between devices: 28.8 us -> 26.3 us
  matrix products: 2.42 us -> 0.69 us
  local copies, waits for them, and re-layouts: 4.44 us -> 2.78 us
  Pallas kernels: 9.72 us -> 10.8 us
  other arithmetic: 2.22 us -> 1.26 us
  waiting for transfers between devices: 15.2 us -> 15.9 us
    unnamed x4 -> x8, local copies, waits for them, and re-layouts: 3.74 us -> 1.37 us
    ppermute x4 -> x3, starting transfers between devices: 10.5 us -> 8.21 us  [shift(): return lax.ppermute(main, axes, pairs)]
    dot_general x2, matrix products: 2.42 us -> 0.69 us  [coupling_lists(): jnp.einsum('sa,kab,tb->kst', one_hot, masked, one_hot, precision=lax.Prec...]
    ppermute x15 -> x14, waiting for transfers between devices: 12.1 us -> 13.3 us  [swap(): return lax.ppermute(piece, axes, [(d, d ^ r) for d in range(devices)])]
    pallas_call x1 -> x2, Pallas kernels: 1.97 us -> 3.1 us  [pack(): pl.pallas_call(kernel, out_shape=[pltpu.VMEM(shape, jnp.float32)] * modes...]
    reduce_sum x1, other arithmetic: 1.06 us -> 0.09 us  [coupling_lists(): jnp.sum(jnp.where(column == chosen_t[:, :, None], coupled, 0.0), 2)]
    slice x0 -> x1, local copies, waits for them, and re-layouts: none -> 0.69 us  [shift(): main = jnp.stack([piece[:lay.main] for piece in pieces])]
    ppermute x4 -> x3, waiting for transfers between devices: 3.09 us -> 2.6 us  [shift(): return lax.ppermute(main, axes, pairs)]
  transfers between devices with their start and end apart: 19 -> 17, of which waited for: 6 -> 9; matrix products, arithmetic and copies ran while one was open for 14% -> 8% of each run, Pallas kernels for 10% -> 14%
where the time goes in v12:
time: 58.3 us; the launch traced here: 58 us
  starting transfers between devices  26.3 us (45%)
  waiting for transfers between devices  15.9 us (27%)
  Pallas kernels  10.8 us (19%)
  local copies, waits for them, and re-layouts  2.78 us (5%)
  other arithmetic  1.26 us (2%)
  matrix products  0.69 us (1%)
    ppermute x14, starting transfers between devices, swap(): return lax.ppermute(piece, axes, [(d, d ^ r) for d in range(devices)])  18.1 us
    ppermute x14, waiting for transfers between devices, swap(): return lax.ppermute(piece, axes, [(d, d ^ r) for d in range(devices)])  13.3 us
    ppermute x3, starting transfers between devices, shift(): return lax.ppermute(main, axes, pairs)  8.21 us
    pallas_call x2, Pallas kernels, stencil(): pl.pallas_call(kernel, out_shape=[jax.ShapeDtypeStruct((lay.quota, rows,...  6.6 us
    pallas_call x2, Pallas kernels, pack(): pl.pallas_call(kernel, out_shape=[pltpu.VMEM(shape, jnp.float32)] * modes...  3.1 us
    ppermute x3, waiting for transfers between devices, shift(): return lax.ppermute(main, axes, pairs)  2.6 us
    unnamed x8, local copies, waits for them, and re-layouts  1.37 us
  transfers between devices with their start and end apart: 17, of which 9 were waited for; matrix products, arithmetic and copies ran while one was open for 8% of the time, Pallas kernels for 14%

profile of v12, /device:TPU:0, one launch (start us, length us, event | category | flops | bytes accessed | tf_op | source)
XLA Modules:
  0.0 58.0 jit_solution(17696271639704699799)
XLA Ops:
  0.0 1.5 %pack_own.1 = (f32[26,16,128]{2,1,0:T(8,128)S(1)}, f32[26,16,128]{2,1,0:T(8,128)S(1)}, f32[26,16,128]{2,1,0:T(8,128)S(1)}, f32[26,16,128]{2,1,0:T(8,128)S(1)}) custom-call(s32[1]{0:T(128)} %bitcast.j_ref, f32[21,128,128]{2,1,0:T(8,128)} %bitcast.47, f32[1,128,128]{2,1,0:T(8,128)} %mean_ref.3, f32[6,128,128]{2,1,0:T(8,128)} %bitcast.49), custom_call_target="tpu_custom_call" | custom-call | tf_op jit(solution)/shard_map/pack_own/pallas_call | solution.py:125
  1.6 0.0 copy-start.2
  1.6 0.0 copy-start.1
  1.6 3.0 %collective-permute-start.2 = (f32[416,128]{1,0:T(8,128)S(1)}, f32[416,128]{1,0:T(8,128)S(1)}, u32[]{:S(2)}, u32[]{:S(2)}) collective-permute-start(f32[416,128]{1,0:T(8,128)S(1)} %bitcast.46), channel_id=1, source_target_pairs={{0,2},{1,3},{2,0},{3,1},{4,6},{5,7},{6,4},{7,5},{8,10},{9,11},{10,... | collective-permute-start | bytes 638984 | tf_op jit(solution)/shard_map/ppermute | solution.py:319
  4.6 0.0 collective-permute-start.6
  4.6 0.2 collective-permute-start.3
  4.8 1.5 %pack_crossing.1 = (f32[26,16,128]{2,1,0:T(8,128)S(1)}, f32[26,16,128]{2,1,0:T(8,128)S(1)}, f32[26,16,128]{2,1,0:T(8,128)S(1)}, f32[26,16,128]{2,1,0:T(8,128)S(1)}) custom-call(s32[1]{0:T(128)} %bitcast.j_ref, f32[21,128,128]{2,1,0:T(8,128)} %bitcast.48, f32[1,128,128]{2,1,0:T(8,128)} %mean_ref.3, f32[6,128,128]{2,1,0:T(8,128)} %bitcast.50), custom_call_target="tpu_custom_call" | custom-call | tf_op jit(solution)/shard_map/pack_crossing/pallas_call | solution.py:125
  6.4 1.6 %collective-permute-start.1 = (f32[416,128]{1,0:T(8,128)S(1)}, f32[416,128]{1,0:T(8,128)S(1)}, u32[]{:S(2)}, u32[]{:S(2)}) collective-permute-start(f32[416,128]{1,0:T(8,128)S(1)} %bitcast.43), channel_id=1, source_target_pairs={{0,5},{1,4},{2,7},{3,6},{4,1},{5,0},{6,3},{7,2},{8,13},{9,12},{10,... | collective-permute-start | bytes 638984 | tf_op jit(solution)/shard_map/ppermute | solution.py:319
  8.0 0.5 collective-permute-start
  8.5 0.7 %slice.29 = f32[23,16,128]{2,1,0:T(8,128)} slice(f32[26,16,128]{2,1,0:T(8,128)S(1)} %get-tuple-element.28), slice={[0:23], [0:16], [0:128]} | slice | bytes 376832 | tf_op jit(solution)/shard_map/slice | solution.py:328
  9.1 0.1 iota_compare_fusion.9
  9.2 0.1 broadcast_in_dim.135
  9.3 0.1 select_reduce_fusion.9
  9.4 0.1 eq.38
  9.5 0.2 copy.9
  9.7 1.2 %copy.10 = f32[7,84,84]{1,2,0:T(8,128)S(1)} copy(f32[7,84,84]{2,1,0:T(8,128)} %param.10) | data formatting | bytes 395136 | tf_op args[4]
  10.8 0.3 fusion
  11.2 0.0 copy-start
  11.2 0.3 fusion.10
  11.6 0.1 fusion.5
  11.7 0.1 select_reduce_fusion.1
  11.8 0.2 select_reduce_fusion.4
  12.0 0.2 select_reduce_fusion.5
  12.2 0.1 reshape.111
  12.3 0.1 select_reduce_fusion.6
  12.4 0.1 broadcast_add_fusion.1
  12.5 0.1 copy.11
  12.6 0.1 reshape.112
  12.8 0.1 copy.12
  12.9 0.1 reshape.113.factor_ref
  13.0 0.1 pad_add_fusion.2.index_ref
  13.0 0.0 collective-permute-done.2.refs_6_.refs_2_
  13.1 0.0 collective-permute-done.6.refs_5_.refs_1_
  13.1 0.6 %collective-permute-done.3.refs_7_.refs_3_ = f32[416,128]{1,0:T(8,128)S(1)} collective-permute-done((f32[416,128]{1,0:T(8,128)S(1)}, f32[416,128]{1,0:T(8,128)S(1)}, u32[]{:S(2)}, u32[]{:S(2)}) %collective-permute-start.3) | collective-permute-done | bytes 213024 | tf_op jit(solution)/shard_map/ppermute | solution.py:319
  13.7 0.1 pad_maximum_fusion
  13.8 1.3 %collective-permute-start.7 = (f32[4,368,128]{2,1,0:T(8,128)S(1)}, f32[4,368,128]{2,1,0:T(8,128)S(1)}, u32[]{:S(2)}, u32[]{:S(2)}) collective-permute-start(f32[4,368,128]{2,1,0:T(8,128)S(1)} %pad_maximum_fusion), channel_id=1, source_target_pairs={{4,12},{5,13},{6,14},{7,15},{8,0},{9,1},{10,2},{11,3},{12,20},{13,... | collective-permute-start | bytes 2261000 | tf_op jit(solution)/shard_map/ppermute | solution.py:329
  15.1 5.1 %collective-permute-start.5 = (f32[416,128]{1,0:T(8,128)S(1)}, f32[416,128]{1,0:T(8,128)S(1)}, u32[]{:S(2)}, u32[]{:S(2)}) collective-permute-start(f32[416,128]{1,0:T(8,128)S(1)} %bitcast.41), channel_id=1, source_target_pairs={{0,7},{1,6},{2,5},{3,4},{4,3},{5,2},{6,1},{7,0},{8,15},{9,14},{10,... | collective-permute-start | bytes 638984 | tf_op jit(solution)/shard_map/ppermute | solution.py:319
  20.2 0.0 collective-permute-start.4
  20.2 0.0 collective-permute-done.1.refs_1_.refs_5_
  20.2 0.0 collective-permute-done.refs_0_.refs_4_
  20.3 3.5 %collective-permute-start.10 = (f32[2,368,128]{2,1,0:T(8,128)S(1)}, f32[2,368,128]{2,1,0:T(8,128)S(1)}, u32[]{:S(2)}, u32[]{:S(2)}) collective-permute-start(f32[2,368,128]{2,1,0:T(8,128)S(1)} %pad_maximum_fusion.1), channel_id=1, source_target_pairs={{0,8},{1,9},{2,10},{3,11},{8,16},{9,17},{10,18},{11,19},{12,4},{13... | collective-permute-start | bytes 1130504 | tf_op jit(solution)/shard_map/ppermute | solution.py:329
  23.8 2.3 %collective-permute-done.5.refs_3_.refs_7_ = f32[416,128]{1,0:T(8,128)S(1)} collective-permute-done((f32[416,128]{1,0:T(8,128)S(1)}, f32[416,128]{1,0:T(8,128)S(1)}, u32[]{:S(2)}, u32[]{:S(2)}) %collective-permute-start.5) | collective-permute-done | bytes 213024 | tf_op jit(solution)/shard_map/ppermute | solution.py:319
  26.1 3.9 %collective-permute-done.4.refs_2_.refs_6_ = f32[416,128]{1,0:T(8,128)S(1)} collective-permute-done((f32[416,128]{1,0:T(8,128)S(1)}, f32[416,128]{1,0:T(8,128)S(1)}, u32[]{:S(2)}, u32[]{:S(2)}) %collective-permute-start.4) | collective-permute-done | bytes 213024 | tf_op jit(solution)/shard_map/ppermute | solution.py:319
  30.0 3.5 %collective-permute-start.11 = (f32[2,368,128]{2,1,0:T(8,128)S(1)}, f32[2,368,128]{2,1,0:T(8,128)S(1)}, u32[]{:S(2)}, u32[]{:S(2)}) collective-permute-start(f32[2,368,128]{2,1,0:T(8,128)S(1)} %pad_maximum_fusion.2), channel_id=1, source_target_pairs={{0,8},{1,9},{2,10},{3,11},{8,16},{9,17},{10,18},{11,19},{12,4},{13... | collective-permute-start | bytes 1130504 | tf_op jit(solution)/shard_map/ppermute | solution.py:329
  33.5 1.8 %collective-permute-done.7.refs_8_ = f32[4,368,128]{2,1,0:T(8,128)S(1)} collective-permute-done((f32[4,368,128]{2,1,0:T(8,128)S(1)}, f32[4,368,128]{2,1,0:T(8,128)S(1)}, u32[]{:S(2)}, u32[]{:S(2)}) %collective-permute-start.7) | collective-permute-done | bytes 753696 | tf_op jit(solution)/shard_map/ppermute | solution.py:329
  35.3 3.3 %stencil_crossing.1 = (f32[21,16,128]{2,1,0:T(8,128)S(1)}, f32[21,16,128]{2,1,0:T(8,128)S(1)}, f32[21,16,128]{2,1,0:T(8,128)S(1)}, f32[21,16,128]{2,1,0:T(8,128)S(1)}) custom-call(s32[1]{0:T(128)} %bitcast.j_ref, s32[966]{0:T(1024)S(1)} %pad_add_fusion.2.index_ref, f32[672]{0:T(1024)S(1)} %reshape.113.factor_ref, ...), custom_call_target="tpu_custom_call" | custom-call | tf_op jit(solution)/shard_map/stencil_crossing/pallas_call | solution.py:287
  38.6 1.1 %collective-permute-start.8 = (f32[21,16,128]{2,1,0:T(8,128)S(1)}, f32[21,16,128]{2,1,0:T(8,128)S(1)}, u32[]{:S(2)}, u32[]{:S(2)}) collective-permute-start(f32[21,16,128]{2,1,0:T(8,128)S(1)} %get-tuple-element.40), channel_id=1, source_target_pairs={{0,6},{1,7},{2,4},{3,5},{4,2},{5,3},{6,0},{7,1},{8,14},{9,15},{10,... | collective-permute-start | bytes 516104 | tf_op jit(solution)/shard_map/ppermute | solution.py:319
  39.8 1.2 %collective-permute-start.9 = (f32[21,16,128]{2,1,0:T(8,128)S(1)}, f32[21,16,128]{2,1,0:T(8,128)S(1)}, u32[]{:S(2)}, u32[]{:S(2)}) collective-permute-start(f32[21,16,128]{2,1,0:T(8,128)S(1)} %get-tuple-element.41), channel_id=1, source_target_pairs={{0,7},{1,6},{2,5},{3,4},{4,3},{5,2},{6,1},{7,0},{8,15},{9,14},{10,... | collective-permute-start | bytes 516104 | tf_op jit(solution)/shard_map/ppermute | solution.py:319
  41.0 0.0 collective-permute-done.10.refs_8_
  41.0 0.8 %collective-permute-done.11.refs_9_ = f32[2,368,128]{2,1,0:T(8,128)S(1)} collective-permute-done((f32[2,368,128]{2,1,0:T(8,128)S(1)}, f32[2,368,128]{2,1,0:T(8,128)S(1)}, u32[]{:S(2)}, u32[]{:S(2)}) %collective-permute-start.11) | collective-permute-done | bytes 376864 | tf_op jit(solution)/shard_map/ppermute | solution.py:329
  41.8 3.3 %stencil_own.1 = (f32[21,16,128]{2,1,0:T(8,128)S(1)}, f32[21,16,128]{2,1,0:T(8,128)S(1)}, f32[21,16,128]{2,1,0:T(8,128)S(1)}, f32[21,16,128]{2,1,0:T(8,128)S(1)}) custom-call(s32[1]{0:T(128)} %bitcast.j_ref, s32[966]{0:T(1024)S(1)} %pad_add_fusion.2.index_ref, f32[672]{0:T(1024)S(1)} %reshape.113.factor_ref, f32[416,128]{1,0:T(8,128)S(1)} %bitcast.39, ...), custom_call_target="tpu_custom_call" | custom-call | tf_op jit(solution)/shard_map/stencil_own/pallas_call | solution.py:287
  45.1 0.6 collective-permute-start.12
  45.7 2.5 %collective-permute-start.13 = (f32[21,16,128]{2,1,0:T(8,128)S(1)}, f32[21,16,128]{2,1,0:T(8,128)S(1)}, u32[]{:S(2)}, u32[]{:S(2)}) collective-permute-start(f32[21,16,128]{2,1,0:T(8,128)S(1)} %get-tuple-element.49), channel_id=1, source_target_pairs={{0,4},{1,5},{2,6},{3,7},{4,0},{5,1},{6,2},{7,3},{8,12},{9,13},{10,... | collective-permute-start | bytes 516104 | tf_op jit(solution)/shard_map/ppermute | solution.py:319
  48.1 0.0 collective-permute-start.15
  48.1 0.0 collective-permute-done.8.refs_0_
  48.1 0.1 collective-permute-start.16
  48.3 0.6 collective-permute-done.9.refs_1_
  48.8 2.1 %collective-permute-start.14 = (f32[21,16,128]{2,1,0:T(8,128)S(1)}, f32[21,16,128]{2,1,0:T(8,128)S(1)}, u32[]{:S(2)}, u32[]{:S(2)}) collective-permute-start(f32[21,16,128]{2,1,0:T(8,128)S(1)} %get-tuple-element.48), channel_id=1, source_target_pairs={{0,3},{1,2},{2,1},{3,0},{4,7},{5,6},{6,5},{7,4},{8,11},{9,10},{10,... | collective-permute-start | bytes 516104 | tf_op jit(solution)/shard_map/ppermute | solution.py:319
  50.9 2.8 %collective-permute-done.13.refs_3_ = f32[21,16,128]{2,1,0:T(8,128)S(1)} collective-permute-done((f32[21,16,128]{2,1,0:T(8,128)S(1)}, f32[21,16,128]{2,1,0:T(8,128)S(1)}, u32[]{:S(2)}, u32[]{:S(2)}) %collective-permute-start.13) | collective-permute-done | bytes 172064 | tf_op jit(solution)/shard_map/ppermute | solution.py:319
  53.7 2.2 %collective-permute-done.15.refs_5_ = f32[21,16,128]{2,1,0:T(8,128)S(1)} collective-permute-done((f32[21,16,128]{2,1,0:T(8,128)S(1)}, f32[21,16,128]{2,1,0:T(8,128)S(1)}, u32[]{:S(2)}, u32[]{:S(2)}) %collective-permute-start.15) | collective-permute-done | bytes 172064 | tf_op jit(solution)/shard_map/ppermute | solution.py:319
  55.9 0.0 collective-permute-done.12.refs_2_
  55.9 0.0 collective-permute-done.16.refs_7_
  55.9 1.0 %collective-permute-done.14.refs_4_ = f32[21,16,128]{2,1,0:T(8,128)S(1)} collective-permute-done((f32[21,16,128]{2,1,0:T(8,128)S(1)}, f32[21,16,128]{2,1,0:T(8,128)S(1)}, u32[]{:S(2)}, u32[]{:S(2)}) %collective-permute-start.14) | collective-permute-done | bytes 172064 | tf_op jit(solution)/shard_map/ppermute | solution.py:319
  56.9 1.1 %unpack.1 = f32[21,128,128]{2,1,0:T(8,128)} custom-call(s32[1]{0:T(128)} %bitcast.j_ref, f32[21,16,128]{2,1,0:T(8,128)S(1)} %collective-permute-done.8.refs_0_, f32[21,16,128]{2,1,0:T(8,128)S(1)} %collective-permute-done.9.refs_1_, f32[21,16,128]{2,1,0:T(8,128)S(1)} %collective-permute-done.12.refs_2_, f32[21,16,128]{2,1,0:T(8,128)S(1)} %collective-permute-done.13.refs_3_, ...), custom_call_target="tpu_custom_call" | custom-call | tf_op jit(solution)/shard_map/unpack/pallas_call | solution.py:157
  (22 shorter events, 0.3 us)
Async XLA Ops:
  1.6 7.7 %copy-start.2 = (s32[84]{0:T(128)S(1)}, s32[84]{0:T(128)}, u32[]{:S(2)}) copy-start(s32[84]{0:T(128)} %param.11) | copy-start | bytes 1012
  1.6 7.9 %copy-start.1 = (s32[7,84,84]{2,1,0:T(8,128)S(1)}, s32[7,84,84]{2,1,0:T(8,128)}, u32[]{:S(2)}) copy-start(s32[7,84,84]{2,1,0:T(8,128)} %param.9) | copy-start | bytes 592708
  1.6 11.5 %collective-permute-start.2 = (f32[416,128]{1,0:T(8,128)S(1)}, f32[416,128]{1,0:T(8,128)S(1)}, u32[]{:S(2)}, u32[]{:S(2)}) collective-permute-start(f32[416,128]{1,0:T(8,128)S(1)} %bitcast.46), channel_id=1, source_target_pairs={{0,2},{1,3},{2,0},{3,1},{4,6},{5,7},{6,4},{7,5},{8,10},{9,11},{10,... | collective-permute-start | bytes 638984 | tf_op jit(solution)/shard_map/ppermute | solution.py:319
  4.6 8.5 %collective-permute-start.6 = (f32[416,128]{1,0:T(8,128)S(1)}, f32[416,128]{1,0:T(8,128)S(1)}, u32[]{:S(2)}, u32[]{:S(2)}) collective-permute-start(f32[416,128]{1,0:T(8,128)S(1)} %bitcast.45), channel_id=1, source_target_pairs={{0,1},{1,0},{2,3},{3,2},{4,5},{5,4},{6,7},{7,6},{8,9},{9,8},{10,11... | collective-permute-start | bytes 638984 | tf_op jit(solution)/shard_map/ppermute | solution.py:319
  4.6 9.1 %collective-permute-start.3 = (f32[416,128]{1,0:T(8,128)S(1)}, f32[416,128]{1,0:T(8,128)S(1)}, u32[]{:S(2)}, u32[]{:S(2)}) collective-permute-start(f32[416,128]{1,0:T(8,128)S(1)} %bitcast.44), channel_id=1, source_target_pairs={{0,3},{1,2},{2,1},{3,0},{4,7},{5,6},{6,5},{7,4},{8,11},{9,10},{10,... | collective-permute-start | bytes 638984 | tf_op jit(solution)/shard_map/ppermute | solution.py:319
  6.4 13.9 %collective-permute-start.1 = (f32[416,128]{1,0:T(8,128)S(1)}, f32[416,128]{1,0:T(8,128)S(1)}, u32[]{:S(2)}, u32[]{:S(2)}) collective-permute-start(f32[416,128]{1,0:T(8,128)S(1)} %bitcast.43), channel_id=1, source_target_pairs={{0,5},{1,4},{2,7},{3,6},{4,1},{5,0},{6,3},{7,2},{8,13},{9,12},{10,... | collective-permute-start | bytes 638984 | tf_op jit(solution)/shard_map/ppermute | solution.py:319
  8.0 12.3 %collective-permute-start = (f32[416,128]{1,0:T(8,128)S(1)}, f32[416,128]{1,0:T(8,128)S(1)}, u32[]{:S(2)}, u32[]{:S(2)}) collective-permute-start(f32[416,128]{1,0:T(8,128)S(1)} %bitcast.42), channel_id=1, source_target_pairs={{0,4},{1,5},{2,6},{3,7},{4,0},{5,1},{6,2},{7,3},{8,12},{9,13},{10,... | collective-permute-start | bytes 638984 | tf_op jit(solution)/shard_map/ppermute | solution.py:319
  11.2 2.5 %copy-start = (f32[23,16,128]{2,1,0:T(8,128)S(1)}, f32[23,16,128]{2,1,0:T(8,128)}, u32[]{:S(2)}) copy-start(f32[23,16,128]{2,1,0:T(8,128)} %slice.29) | copy-start | bytes 565252
  13.8 21.6 %collective-permute-start.7 = (f32[4,368,128]{2,1,0:T(8,128)S(1)}, f32[4,368,128]{2,1,0:T(8,128)S(1)}, u32[]{:S(2)}, u32[]{:S(2)}) collective-permute-start(f32[4,368,128]{2,1,0:T(8,128)S(1)} %pad_maximum_fusion), channel_id=1, source_target_pairs={{4,12},{5,13},{6,14},{7,15},{8,0},{9,1},{10,2},{11,3},{12,20},{13,... | collective-permute-start | bytes 2261000 | tf_op jit(solution)/shard_map/ppermute | solution.py:329
  15.1 11.0 %collective-permute-start.5 = (f32[416,128]{1,0:T(8,128)S(1)}, f32[416,128]{1,0:T(8,128)S(1)}, u32[]{:S(2)}, u32[]{:S(2)}) collective-permute-start(f32[416,128]{1,0:T(8,128)S(1)} %bitcast.41), channel_id=1, source_target_pairs={{0,7},{1,6},{2,5},{3,4},{4,3},{5,2},{6,1},{7,0},{8,15},{9,14},{10,... | collective-permute-start | bytes 638984 | tf_op jit(solution)/shard_map/ppermute | solution.py:319
  20.2 9.8 %collective-permute-start.4 = (f32[416,128]{1,0:T(8,128)S(1)}, f32[416,128]{1,0:T(8,128)S(1)}, u32[]{:S(2)}, u32[]{:S(2)}) collective-permute-start(f32[416,128]{1,0:T(8,128)S(1)} %bitcast.40), channel_id=1, source_target_pairs={{0,6},{1,7},{2,4},{3,5},{4,2},{5,3},{6,0},{7,1},{8,14},{9,15},{10,... | collective-permute-start | bytes 638984 | tf_op jit(solution)/shard_map/ppermute | solution.py:319
  20.3 20.7 %collective-permute-start.10 = (f32[2,368,128]{2,1,0:T(8,128)S(1)}, f32[2,368,128]{2,1,0:T(8,128)S(1)}, u32[]{:S(2)}, u32[]{:S(2)}) collective-permute-start(f32[2,368,128]{2,1,0:T(8,128)S(1)} %pad_maximum_fusion.1), channel_id=1, source_target_pairs={{0,8},{1,9},{2,10},{3,11},{8,16},{9,17},{10,18},{11,19},{12,4},{13... | collective-permute-start | bytes 1130504 | tf_op jit(solution)/shard_map/ppermute | solution.py:329
  30.0 11.7 %collective-permute-start.11 = (f32[2,368,128]{2,1,0:T(8,128)S(1)}, f32[2,368,128]{2,1,0:T(8,128)S(1)}, u32[]{:S(2)}, u32[]{:S(2)}) collective-permute-start(f32[2,368,128]{2,1,0:T(8,128)S(1)} %pad_maximum_fusion.2), channel_id=1, source_target_pairs={{0,8},{1,9},{2,10},{3,11},{8,16},{9,17},{10,18},{11,19},{12,4},{13... | collective-permute-start | bytes 1130504 | tf_op jit(solution)/shard_map/ppermute | solution.py:329
  38.6 9.5 %collective-permute-start.8 = (f32[21,16,128]{2,1,0:T(8,128)S(1)}, f32[21,16,128]{2,1,0:T(8,128)S(1)}, u32[]{:S(2)}, u32[]{:S(2)}) collective-permute-start(f32[21,16,128]{2,1,0:T(8,128)S(1)} %get-tuple-element.40), channel_id=1, source_target_pairs={{0,6},{1,7},{2,4},{3,5},{4,2},{5,3},{6,0},{7,1},{8,14},{9,15},{10,... | collective-permute-start | bytes 516104 | tf_op jit(solution)/shard_map/ppermute | solution.py:319
  39.8 9.0 %collective-permute-start.9 = (f32[21,16,128]{2,1,0:T(8,128)S(1)}, f32[21,16,128]{2,1,0:T(8,128)S(1)}, u32[]{:S(2)}, u32[]{:S(2)}) collective-permute-start(f32[21,16,128]{2,1,0:T(8,128)S(1)} %get-tuple-element.41), channel_id=1, source_target_pairs={{0,7},{1,6},{2,5},{3,4},{4,3},{5,2},{6,1},{7,0},{8,15},{9,14},{10,... | collective-permute-start | bytes 516104 | tf_op jit(solution)/shard_map/ppermute | solution.py:319
  45.1 10.8 %collective-permute-start.12 = (f32[21,16,128]{2,1,0:T(8,128)S(1)}, f32[21,16,128]{2,1,0:T(8,128)S(1)}, u32[]{:S(2)}, u32[]{:S(2)}) collective-permute-start(f32[21,16,128]{2,1,0:T(8,128)S(1)} %get-tuple-element.45), channel_id=1, source_target_pairs={{0,2},{1,3},{2,0},{3,1},{4,6},{5,7},{6,4},{7,5},{8,10},{9,11},{10,... | collective-permute-start | bytes 516104 | tf_op jit(solution)/shard_map/ppermute | solution.py:319
  45.7 8.1 %collective-permute-start.13 = (f32[21,16,128]{2,1,0:T(8,128)S(1)}, f32[21,16,128]{2,1,0:T(8,128)S(1)}, u32[]{:S(2)}, u32[]{:S(2)}) collective-permute-start(f32[21,16,128]{2,1,0:T(8,128)S(1)} %get-tuple-element.49), channel_id=1, source_target_pairs={{0,4},{1,5},{2,6},{3,7},{4,0},{5,1},{6,2},{7,3},{8,12},{9,13},{10,... | collective-permute-start | bytes 516104 | tf_op jit(solution)/shard_map/ppermute | solution.py:319
  48.1 7.8 %collective-permute-start.15 = (f32[21,16,128]{2,1,0:T(8,128)S(1)}, f32[21,16,128]{2,1,0:T(8,128)S(1)}, u32[]{:S(2)}, u32[]{:S(2)}) collective-permute-start(f32[21,16,128]{2,1,0:T(8,128)S(1)} %get-tuple-element.50), channel_id=1, source_target_pairs={{0,5},{1,4},{2,7},{3,6},{4,1},{5,0},{6,3},{7,2},{8,13},{9,12},{10,... | collective-permute-start | bytes 516104 | tf_op jit(solution)/shard_map/ppermute | solution.py:319
  48.1 7.8 %collective-permute-start.16 = (f32[21,16,128]{2,1,0:T(8,128)S(1)}, f32[21,16,128]{2,1,0:T(8,128)S(1)}, u32[]{:S(2)}, u32[]{:S(2)}) collective-permute-start(f32[21,16,128]{2,1,0:T(8,128)S(1)} %get-tuple-element.47), channel_id=1, source_target_pairs={{0,1},{1,0},{2,3},{3,2},{4,5},{5,4},{6,7},{7,6},{8,9},{9,8},{10,11... | collective-permute-start | bytes 516104 | tf_op jit(solution)/shard_map/ppermute | solution.py:319
  48.8 8.1 %collective-permute-start.14 = (f32[21,16,128]{2,1,0:T(8,128)S(1)}, f32[21,16,128]{2,1,0:T(8,128)S(1)}, u32[]{:S(2)}, u32[]{:S(2)}) collective-permute-start(f32[21,16,128]{2,1,0:T(8,128)S(1)} %get-tuple-element.48), channel_id=1, source_target_pairs={{0,3},{1,2},{2,1},{3,0},{4,7},{5,6},{6,5},{7,4},{8,11},{9,10},{10,... | collective-permute-start | bytes 516104 | tf_op jit(solution)/shard_map/ppermute | solution.py:319

commit v13 on v12

--- a/solution.py
+++ b/solution.py
@@ -138,16 +138,17 @@
     return [piece.reshape(lay.piece, width) for piece in sent]
 
 
-def unpack(pieces, j, shape, lay):
+def unpack(pieces, j, shape, lay, whole=None):
     rows = lay.rows
+    there = [] if whole is None else [whole]
 
     def kernel(j_ref, *refs):
-        piece_refs, out_ref, sems = refs[:-2], refs[-2], refs[-1]
+        piece_refs, out_ref, sems = refs[: len(pieces)], refs[-2], refs[-1]
         copies = []
-        for r, piece_ref in zip(pieces, piece_refs):
+        for n, (r, piece_ref) in enumerate(zip(pieces, piece_refs)):
             start = pl.multiple_of(jnp.bitwise_xor(j_ref[0], r) * rows, 8)
             made = pltpu.make_async_copy(
-                piece_ref, out_ref.at[:, pl.ds(start, rows), :], sems.at[r]
+                piece_ref, out_ref.at[:, pl.ds(start, rows), :], sems.at[n]
             )
             made.start()
             copies.append(made)
@@ -156,13 +157,14 @@
 
     return pl.pallas_call(
         kernel,
-        out_shape=jax.ShapeDtypeStruct(shape, jnp.float32),
-        in_specs=smem(1) + vmem(lay.group),
+        out_shape=pltpu.HBM(shape, jnp.float32),
+        in_specs=smem(1) + vmem(len(pieces)) + [pl.BlockSpec(memory_space=pltpu.HBM)] * len(there),
         out_specs=pl.BlockSpec(memory_space=pltpu.HBM),
-        scratch_shapes=[pltpu.SemaphoreType.DMA((lay.group,))],
+        scratch_shapes=[pltpu.SemaphoreType.DMA((len(pieces),))],
+        input_output_aliases={1 + len(pieces): 0} if there else {},
         compiler_params=pltpu.CompilerParams(vmem_limit_bytes=VMEM_LIMIT),
-        name="unpack",
-    )(j, *pieces.values())
+        name="unpack_last" if there else "unpack_first",
+    )(j, *pieces.values(), *there)
 
 
 def coupling_lists(pattern, coupling, slot_mode):
@@ -355,12 +357,21 @@
     own_j = after(j, *crossing_out)
     own_out = stencil(own, crossing, crossing_halos, lists, own_j, "stencil_own", lay)
     out = [*own_out, *crossing_out]
-    for r in range(modes, modes + half):
-        out[r] = after(out[r], *own_out)
-    first = [*range(modes + half, lay.group)]
-    rest = [r + n for n in range(half) for r in (half, modes)] + [*range(half)]
-    back = {r: swap(out[r], r) for r in first + rest}
-    return unpack(back, j, (quota, height, width), lay).reshape(chaos_field.shape)
+    first = range(modes + half, lay.group)
+    back = {r: swap(out[r], r) for r in first}
+    for r in range(half, modes):
+        back[r] = swap(out[r], r)
+    for n in range(half):
+        ahead = [back[r] for r in first[:n]]
+        ahead = [*own_out, *ahead] if n else []
+        back[modes + n] = swap(after(out[modes + n], *ahead), modes + n)
+    for r in range(half):
+        back[r] = swap(after(out[r], *[back[r] for r in first]) if r else out[r], r)
+    last = range(half, modes + half)
+    shape = (quota, height, width)
+    whole = unpack({r: back[r] for r in back if r not in last}, j, shape, lay)
+    whole = unpack({r: back[r] for r in last}, j, shape, lay, whole)
+    return whole.reshape(chaos_field.shape)
 
 
 def solution(mesh):

time: 58.3 us -> 58.1 us (level)
  starting transfers between devices: 26.3 us -> 25 us
  Pallas kernels: 10.8 us -> 11.4 us
    ppermute x14, starting transfers between devices: 18.1 us -> 16.8 us  [swap(): return lax.ppermute(piece, axes, [(d, d ^ r) for d in range(devices)])]
    ppermute x14, waiting for transfers between devices: 13.3 us -> 14.5 us  [swap(): return lax.ppermute(piece, axes, [(d, d ^ r) for d in range(devices)])]
    ppermute x3, waiting for transfers between devices: 2.6 us -> 1.83 us  [shift(): return lax.ppermute(main, axes, pairs)]
    pallas_call x1 -> x2, Pallas kernels: 1.13 us -> 1.74 us  [unpack(): pl.pallas_call(kernel, out_shape=pltpu.HBM(shape, jnp.float32), in_specs=...]
  transfers between devices with their start and end apart: 17 -> 17, of which waited for: 9 -> 10; matrix products, arithmetic and copies ran while one was open for 8% -> 8% of each run, Pallas kernels for 14% -> 16%
where the time goes in v13:
time: 58.1 us; the launch traced here: 57.8 us
  starting transfers between devices  25 us (43%)
  waiting for transfers between devices  16.3 us (28%)
  Pallas kernels  11.4 us (20%)
  local copies, waits for them, and re-layouts  2.78 us (5%)
  other arithmetic  1.26 us (2%)
  matrix products  0.69 us (1%)
    ppermute x14, starting transfers between devices, swap(): return lax.ppermute(piece, axes, [(d, d ^ r) for d in range(devices)])  16.8 us
    ppermute x14, waiting for transfers between devices, swap(): return lax.ppermute(piece, axes, [(d, d ^ r) for d in range(devices)])  14.5 us
    ppermute x3, starting transfers between devices, shift(): return lax.ppermute(main, axes, pairs)  8.21 us
    pallas_call x2, Pallas kernels, stencil(): pl.pallas_call(kernel, out_shape=[jax.ShapeDtypeStruct((lay.quota, rows,...  6.6 us
    pallas_call x2, Pallas kernels, pack(): pl.pallas_call(kernel, out_shape=[pltpu.VMEM(shape, jnp.float32)] * modes...  3.1 us
    ppermute x3, waiting for transfers between devices, shift(): return lax.ppermute(main, axes, pairs)  1.83 us
    pallas_call x2, Pallas kernels, unpack(): pl.pallas_call(kernel, out_shape=pltpu.HBM(shape, jnp.float32), in_specs=...  1.74 us
    unnamed x8, local copies, waits for them, and re-layouts  1.37 us
  transfers between devices with their start and end apart: 17, of which 10 were waited for; matrix products, arithmetic and copies ran while one was open for 8% of the time, Pallas kernels for 16%

profile of v13, /device:TPU:0, one launch (start us, length us, event | category | flops | bytes accessed | tf_op | source)
XLA Modules:
  0.0 57.8 jit_solution(15596088707599247884)
XLA Ops:
  0.0 1.5 %pack_own.1 = (f32[26,16,128]{2,1,0:T(8,128)S(1)}, f32[26,16,128]{2,1,0:T(8,128)S(1)}, f32[26,16,128]{2,1,0:T(8,128)S(1)}, f32[26,16,128]{2,1,0:T(8,128)S(1)}) custom-call(s32[1]{0:T(128)} %bitcast.j_ref, f32[21,128,128]{2,1,0:T(8,128)} %bitcast.47, f32[1,128,128]{2,1,0:T(8,128)} %mean_ref.3, f32[6,128,128]{2,1,0:T(8,128)} %bitcast.49), custom_call_target="tpu_custom_call" | custom-call | tf_op jit(solution)/shard_map/pack_own/pallas_call | solution.py:125
  1.6 0.0 copy-start.2
  1.6 0.0 copy-start.1
  1.6 3.0 %collective-permute-start.2 = (f32[416,128]{1,0:T(8,128)S(1)}, f32[416,128]{1,0:T(8,128)S(1)}, u32[]{:S(2)}, u32[]{:S(2)}) collective-permute-start(f32[416,128]{1,0:T(8,128)S(1)} %bitcast.46), channel_id=1, source_target_pairs={{0,2},{1,3},{2,0},{3,1},{4,6},{5,7},{6,4},{7,5},{8,10},{9,11},{10,... | collective-permute-start | bytes 638984 | tf_op jit(solution)/shard_map/ppermute | solution.py:321
  4.6 0.0 collective-permute-start.6
  4.6 0.2 collective-permute-start.3
  4.8 1.5 %pack_crossing.1 = (f32[26,16,128]{2,1,0:T(8,128)S(1)}, f32[26,16,128]{2,1,0:T(8,128)S(1)}, f32[26,16,128]{2,1,0:T(8,128)S(1)}, f32[26,16,128]{2,1,0:T(8,128)S(1)}) custom-call(s32[1]{0:T(128)} %bitcast.j_ref, f32[21,128,128]{2,1,0:T(8,128)} %bitcast.48, f32[1,128,128]{2,1,0:T(8,128)} %mean_ref.3, f32[6,128,128]{2,1,0:T(8,128)} %bitcast.50), custom_call_target="tpu_custom_call" | custom-call | tf_op jit(solution)/shard_map/pack_crossing/pallas_call | solution.py:125
  6.4 1.6 %collective-permute-start.1 = (f32[416,128]{1,0:T(8,128)S(1)}, f32[416,128]{1,0:T(8,128)S(1)}, u32[]{:S(2)}, u32[]{:S(2)}) collective-permute-start(f32[416,128]{1,0:T(8,128)S(1)} %bitcast.43), channel_id=1, source_target_pairs={{0,5},{1,4},{2,7},{3,6},{4,1},{5,0},{6,3},{7,2},{8,13},{9,12},{10,... | collective-permute-start | bytes 638984 | tf_op jit(solution)/shard_map/ppermute | solution.py:321
  8.0 0.5 collective-permute-start
  8.5 0.7 %slice.29 = f32[23,16,128]{2,1,0:T(8,128)} slice(f32[26,16,128]{2,1,0:T(8,128)S(1)} %get-tuple-element.28), slice={[0:23], [0:16], [0:128]} | slice | bytes 376832 | tf_op jit(solution)/shard_map/slice | solution.py:330
  9.1 0.1 iota_compare_fusion.9
  9.2 0.1 broadcast_in_dim.135
  9.3 0.1 select_reduce_fusion.9
  9.4 0.1 eq.38
  9.5 0.2 copy.10
  9.7 1.2 %copy.11 = f32[7,84,84]{1,2,0:T(8,128)S(1)} copy(f32[7,84,84]{2,1,0:T(8,128)} %param.10) | data formatting | bytes 395136 | tf_op args[4]
  10.8 0.3 fusion
  11.2 0.0 copy-start
  11.2 0.3 fusion.10
  11.6 0.1 fusion.5
  11.7 0.1 select_reduce_fusion.1
  11.8 0.2 select_reduce_fusion.4
  12.0 0.2 select_reduce_fusion.5
  12.2 0.1 reshape.111
  12.3 0.1 select_reduce_fusion.6
  12.4 0.1 broadcast_add_fusion.1
  12.5 0.1 copy.12
  12.6 0.1 reshape.112
  12.8 0.1 copy.13
  12.9 0.1 reshape.113.factor_ref
  13.0 0.1 pad_add_fusion.2.index_ref
  13.1 0.0 collective-permute-done.6.refs_5_.refs_1_
  13.1 0.6 %collective-permute-done.3.refs_7_.refs_3_ = f32[416,128]{1,0:T(8,128)S(1)} collective-permute-done((f32[416,128]{1,0:T(8,128)S(1)}, f32[416,128]{1,0:T(8,128)S(1)}, u32[]{:S(2)}, u32[]{:S(2)}) %collective-permute-start.3) | collective-permute-done | bytes 213024 | tf_op jit(solution)/shard_map/ppermute | solution.py:321
  13.7 0.1 pad_maximum_fusion
  13.8 1.3 %collective-permute-start.7 = (f32[4,368,128]{2,1,0:T(8,128)S(1)}, f32[4,368,128]{2,1,0:T(8,128)S(1)}, u32[]{:S(2)}, u32[]{:S(2)}) collective-permute-start(f32[4,368,128]{2,1,0:T(8,128)S(1)} %pad_maximum_fusion), channel_id=1, source_target_pairs={{4,12},{5,13},{6,14},{7,15},{8,0},{9,1},{10,2},{11,3},{12,20},{13,... | collective-permute-start | bytes 2261000 | tf_op jit(solution)/shard_map/ppermute | solution.py:331
  15.1 5.1 %collective-permute-start.5 = (f32[416,128]{1,0:T(8,128)S(1)}, f32[416,128]{1,0:T(8,128)S(1)}, u32[]{:S(2)}, u32[]{:S(2)}) collective-permute-start(f32[416,128]{1,0:T(8,128)S(1)} %bitcast.41), channel_id=1, source_target_pairs={{0,7},{1,6},{2,5},{3,4},{4,3},{5,2},{6,1},{7,0},{8,15},{9,14},{10,... | collective-permute-start | bytes 638984 | tf_op jit(solution)/shard_map/ppermute | solution.py:321
  20.2 0.0 collective-permute-start.4
  20.2 0.0 collective-permute-done.1.refs_1_.refs_5_
  20.2 0.0 collective-permute-done.refs_0_.refs_4_
  20.3 3.5 %collective-permute-start.8 = (f32[2,368,128]{2,1,0:T(8,128)S(1)}, f32[2,368,128]{2,1,0:T(8,128)S(1)}, u32[]{:S(2)}, u32[]{:S(2)}) collective-permute-start(f32[2,368,128]{2,1,0:T(8,128)S(1)} %pad_maximum_fusion.1), channel_id=1, source_target_pairs={{0,8},{1,9},{2,10},{3,11},{8,16},{9,17},{10,18},{11,19},{12,4},{13... | collective-permute-start | bytes 1130504 | tf_op jit(solution)/shard_map/ppermute | solution.py:331
  23.8 2.3 %collective-permute-done.5.refs_3_.refs_7_ = f32[416,128]{1,0:T(8,128)S(1)} collective-permute-done((f32[416,128]{1,0:T(8,128)S(1)}, f32[416,128]{1,0:T(8,128)S(1)}, u32[]{:S(2)}, u32[]{:S(2)}) %collective-permute-start.5) | collective-permute-done | bytes 213024 | tf_op jit(solution)/shard_map/ppermute | solution.py:321
  26.1 3.9 %collective-permute-done.4.refs_2_.refs_6_ = f32[416,128]{1,0:T(8,128)S(1)} collective-permute-done((f32[416,128]{1,0:T(8,128)S(1)}, f32[416,128]{1,0:T(8,128)S(1)}, u32[]{:S(2)}, u32[]{:S(2)}) %collective-permute-start.4) | collective-permute-done | bytes 213024 | tf_op jit(solution)/shard_map/ppermute | solution.py:321
  30.0 3.5 %collective-permute-start.9 = (f32[2,368,128]{2,1,0:T(8,128)S(1)}, f32[2,368,128]{2,1,0:T(8,128)S(1)}, u32[]{:S(2)}, u32[]{:S(2)}) collective-permute-start(f32[2,368,128]{2,1,0:T(8,128)S(1)} %pad_maximum_fusion.2), channel_id=1, source_target_pairs={{0,8},{1,9},{2,10},{3,11},{8,16},{9,17},{10,18},{11,19},{12,4},{13... | collective-permute-start | bytes 1130504 | tf_op jit(solution)/shard_map/ppermute | solution.py:331
  33.5 1.8 %collective-permute-done.7.refs_8_ = f32[4,368,128]{2,1,0:T(8,128)S(1)} collective-permute-done((f32[4,368,128]{2,1,0:T(8,128)S(1)}, f32[4,368,128]{2,1,0:T(8,128)S(1)}, u32[]{:S(2)}, u32[]{:S(2)}) %collective-permute-start.7) | collective-permute-done | bytes 753696 | tf_op jit(solution)/shard_map/ppermute | solution.py:331
  35.3 3.3 %stencil_crossing.1 = (f32[21,16,128]{2,1,0:T(8,128)S(1)}, f32[21,16,128]{2,1,0:T(8,128)S(1)}, f32[21,16,128]{2,1,0:T(8,128)S(1)}, f32[21,16,128]{2,1,0:T(8,128)S(1)}) custom-call(s32[1]{0:T(128)} %bitcast.j_ref, s32[966]{0:T(1024)S(1)} %pad_add_fusion.2.index_ref, f32[672]{0:T(1024)S(1)} %reshape.113.factor_ref, ...), custom_call_target="tpu_custom_call" | custom-call | tf_op jit(solution)/shard_map/stencil_crossing/pallas_call | solution.py:289
  38.6 1.1 %collective-permute-start.13 = (f32[21,16,128]{2,1,0:T(8,128)S(1)}, f32[21,16,128]{2,1,0:T(8,128)S(1)}, u32[]{:S(2)}, u32[]{:S(2)}) collective-permute-start(f32[21,16,128]{2,1,0:T(8,128)S(1)} %get-tuple-element.42), channel_id=1, source_target_pairs={{0,6},{1,7},{2,4},{3,5},{4,2},{5,3},{6,0},{7,1},{8,14},{9,15},{10,... | collective-permute-start | bytes 516104 | tf_op jit(solution)/shard_map/ppermute | solution.py:321
  39.8 1.2 %collective-permute-start.15 = (f32[21,16,128]{2,1,0:T(8,128)S(1)}, f32[21,16,128]{2,1,0:T(8,128)S(1)}, u32[]{:S(2)}, u32[]{:S(2)}) collective-permute-start(f32[21,16,128]{2,1,0:T(8,128)S(1)} %get-tuple-element.43), channel_id=1, source_target_pairs={{0,7},{1,6},{2,5},{3,4},{4,3},{5,2},{6,1},{7,0},{8,15},{9,14},{10,... | collective-permute-start | bytes 516104 | tf_op jit(solution)/shard_map/ppermute | solution.py:321
  41.0 0.8 %collective-permute-start.12 = (f32[21,16,128]{2,1,0:T(8,128)S(1)}, f32[21,16,128]{2,1,0:T(8,128)S(1)}, u32[]{:S(2)}, u32[]{:S(2)}) collective-permute-start(f32[21,16,128]{2,1,0:T(8,128)S(1)} %get-tuple-element.40), channel_id=1, source_target_pairs={{0,4},{1,5},{2,6},{3,7},{4,0},{5,1},{6,2},{7,3},{8,12},{9,13},{10,... | collective-permute-start | bytes 516104 | tf_op jit(solution)/shard_map/ppermute | solution.py:321
  41.8 0.0 collective-permute-done.8.refs_8_
  41.8 0.0 collective-permute-done.9.refs_9_
  41.8 3.3 %stencil_own.1 = (f32[21,16,128]{2,1,0:T(8,128)S(1)}, f32[21,16,128]{2,1,0:T(8,128)S(1)}, f32[21,16,128]{2,1,0:T(8,128)S(1)}, f32[21,16,128]{2,1,0:T(8,128)S(1)}) custom-call(s32[1]{0:T(128)} %bitcast.j_ref, s32[966]{0:T(1024)S(1)} %pad_add_fusion.2.index_ref, f32[672]{0:T(1024)S(1)} %reshape.113.factor_ref, f32[416,128]{1,0:T(8,128)S(1)} %bitcast.39, ...), custom_call_target="tpu_custom_call" | custom-call | tf_op jit(solution)/shard_map/stencil_own/pallas_call | solution.py:289
  45.1 1.3 %collective-permute-start.10 = (f32[21,16,128]{2,1,0:T(8,128)S(1)}, f32[21,16,128]{2,1,0:T(8,128)S(1)}, u32[]{:S(2)}, u32[]{:S(2)}) collective-permute-start(f32[21,16,128]{2,1,0:T(8,128)S(1)} %get-tuple-element.45), channel_id=1, source_target_pairs={{0,2},{1,3},{2,0},{3,1},{4,6},{5,7},{6,4},{7,5},{8,10},{9,11},{10,... | collective-permute-start | bytes 516104 | tf_op jit(solution)/shard_map/ppermute | solution.py:321
  46.4 0.3 collective-permute-start.11
  46.7 0.1 collective-permute-done.13.refs_0_
  46.8 2.0 %collective-permute-done.15.refs_1_ = f32[21,16,128]{2,1,0:T(8,128)S(1)} collective-permute-done((f32[21,16,128]{2,1,0:T(8,128)S(1)}, f32[21,16,128]{2,1,0:T(8,128)S(1)}, u32[]{:S(2)}, u32[]{:S(2)}) %collective-permute-start.15) | collective-permute-done | bytes 172064 | tf_op jit(solution)/shard_map/ppermute | solution.py:321
  48.8 1.5 %collective-permute-start.16 = (f32[21,16,128]{2,1,0:T(8,128)S(1)}, f32[21,16,128]{2,1,0:T(8,128)S(1)}, u32[]{:S(2)}, u32[]{:S(2)}) collective-permute-start(f32[21,16,128]{2,1,0:T(8,128)S(1)} %get-tuple-element.50), channel_id=1, source_target_pairs={{0,1},{1,0},{2,3},{3,2},{4,5},{5,4},{6,7},{7,6},{8,9},{9,8},{10,11... | collective-permute-start | bytes 516104 | tf_op jit(solution)/shard_map/ppermute | solution.py:321
  50.3 0.1 collective-permute-start.14
  50.4 0.9 %collective-permute-done.16.refs_3_ = f32[21,16,128]{2,1,0:T(8,128)S(1)} collective-permute-done((f32[21,16,128]{2,1,0:T(8,128)S(1)}, f32[21,16,128]{2,1,0:T(8,128)S(1)}, u32[]{:S(2)}, u32[]{:S(2)}) %collective-permute-start.16) | collective-permute-done | bytes 172064 | tf_op jit(solution)/shard_map/ppermute | solution.py:321
  51.4 0.9 %unpack_first.1.refs_4_ = f32[21,128,128]{2,1,0:T(8,128)} custom-call(s32[1]{0:T(128)} %bitcast.j_ref, f32[21,16,128]{2,1,0:T(8,128)S(1)} %collective-permute-done.13.refs_0_, f32[21,16,128]{2,1,0:T(8,128)S(1)} %collective-permute-done.15.refs_1_, f32[21,16,128]{2,1,0:T(8,128)S(1)} %get-tuple-element.47.refs_2_, ...), custom_call_target="tpu_custom_call" | custom-call | tf_op jit(solution)/shard_map/unpack_first/pallas_call | solution.py:158
  52.3 0.7 %collective-permute-done.12.refs_2_ = f32[21,16,128]{2,1,0:T(8,128)S(1)} collective-permute-done((f32[21,16,128]{2,1,0:T(8,128)S(1)}, f32[21,16,128]{2,1,0:T(8,128)S(1)}, u32[]{:S(2)}, u32[]{:S(2)}) %collective-permute-start.12) | collective-permute-done | bytes 172064 | tf_op jit(solution)/shard_map/ppermute | solution.py:321
  53.0 0.4 collective-permute-done.10.refs_0_
  53.4 3.5 %collective-permute-done.11.refs_1_ = f32[21,16,128]{2,1,0:T(8,128)S(1)} collective-permute-done((f32[21,16,128]{2,1,0:T(8,128)S(1)}, f32[21,16,128]{2,1,0:T(8,128)S(1)}, u32[]{:S(2)}, u32[]{:S(2)}) %collective-permute-start.11) | collective-permute-done | bytes 172064 | tf_op jit(solution)/shard_map/ppermute | solution.py:321
  56.9 0.0 collective-permute-done.14.refs_3_
  56.9 0.9 %unpack_last.1 = f32[21,128,128]{2,1,0:T(8,128)} custom-call(s32[1]{0:T(128)} %bitcast.j_ref, f32[21,16,128]{2,1,0:T(8,128)S(1)} %collective-permute-done.10.refs_0_, f32[21,16,128]{2,1,0:T(8,128)S(1)} %collective-permute-done.11.refs_1_, f32[21,16,128]{2,1,0:T(8,128)S(1)} %collective-permute-done.12.refs_2_, ...), custom_call_target="tpu_custom_call", output_to_operand_aliasing={{}: (5, {})} | custom-call | tf_op jit(solution)/shard_map/unpack_last/pallas_call | solution.py:158
  (23 shorter events, 0.3 us)
Async XLA Ops:
  1.6 7.7 %copy-start.2 = (s32[84]{0:T(128)S(1)}, s32[84]{0:T(128)}, u32[]{:S(2)}) copy-start(s32[84]{0:T(128)} %param.11) | copy-start | bytes 1012
  1.6 7.9 %copy-start.1 = (s32[7,84,84]{2,1,0:T(8,128)S(1)}, s32[7,84,84]{2,1,0:T(8,128)}, u32[]{:S(2)}) copy-start(s32[7,84,84]{2,1,0:T(8,128)} %param.9) | copy-start | bytes 592708
  1.6 11.5 %collective-permute-start.2 = (f32[416,128]{1,0:T(8,128)S(1)}, f32[416,128]{1,0:T(8,128)S(1)}, u32[]{:S(2)}, u32[]{:S(2)}) collective-permute-start(f32[416,128]{1,0:T(8,128)S(1)} %bitcast.46), channel_id=1, source_target_pairs={{0,2},{1,3},{2,0},{3,1},{4,6},{5,7},{6,4},{7,5},{8,10},{9,11},{10,... | collective-permute-start | bytes 638984 | tf_op jit(solution)/shard_map/ppermute | solution.py:321
  4.6 8.5 %collective-permute-start.6 = (f32[416,128]{1,0:T(8,128)S(1)}, f32[416,128]{1,0:T(8,128)S(1)}, u32[]{:S(2)}, u32[]{:S(2)}) collective-permute-start(f32[416,128]{1,0:T(8,128)S(1)} %bitcast.45), channel_id=1, source_target_pairs={{0,1},{1,0},{2,3},{3,2},{4,5},{5,4},{6,7},{7,6},{8,9},{9,8},{10,11... | collective-permute-start | bytes 638984 | tf_op jit(solution)/shard_map/ppermute | solution.py:321
  4.6 9.1 %collective-permute-start.3 = (f32[416,128]{1,0:T(8,128)S(1)}, f32[416,128]{1,0:T(8,128)S(1)}, u32[]{:S(2)}, u32[]{:S(2)}) collective-permute-start(f32[416,128]{1,0:T(8,128)S(1)} %bitcast.44), channel_id=1, source_target_pairs={{0,3},{1,2},{2,1},{3,0},{4,7},{5,6},{6,5},{7,4},{8,11},{9,10},{10,... | collective-permute-start | bytes 638984 | tf_op jit(solution)/shard_map/ppermute | solution.py:321
  6.4 13.9 %collective-permute-start.1 = (f32[416,128]{1,0:T(8,128)S(1)}, f32[416,128]{1,0:T(8,128)S(1)}, u32[]{:S(2)}, u32[]{:S(2)}) collective-permute-start(f32[416,128]{1,0:T(8,128)S(1)} %bitcast.43), channel_id=1, source_target_pairs={{0,5},{1,4},{2,7},{3,6},{4,1},{5,0},{6,3},{7,2},{8,13},{9,12},{10,... | collective-permute-start | bytes 638984 | tf_op jit(solution)/shard_map/ppermute | solution.py:321
  8.0 12.3 %collective-permute-start = (f32[416,128]{1,0:T(8,128)S(1)}, f32[416,128]{1,0:T(8,128)S(1)}, u32[]{:S(2)}, u32[]{:S(2)}) collective-permute-start(f32[416,128]{1,0:T(8,128)S(1)} %bitcast.42), channel_id=1, source_target_pairs={{0,4},{1,5},{2,6},{3,7},{4,0},{5,1},{6,2},{7,3},{8,12},{9,13},{10,... | collective-permute-start | bytes 638984 | tf_op jit(solution)/shard_map/ppermute | solution.py:321
  11.2 2.5 %copy-start = (f32[23,16,128]{2,1,0:T(8,128)S(1)}, f32[23,16,128]{2,1,0:T(8,128)}, u32[]{:S(2)}) copy-start(f32[23,16,128]{2,1,0:T(8,128)} %slice.29) | copy-start | bytes 565252
  13.8 21.6 %collective-permute-start.7 = (f32[4,368,128]{2,1,0:T(8,128)S(1)}, f32[4,368,128]{2,1,0:T(8,128)S(1)}, u32[]{:S(2)}, u32[]{:S(2)}) collective-permute-start(f32[4,368,128]{2,1,0:T(8,128)S(1)} %pad_maximum_fusion), channel_id=1, source_target_pairs={{4,12},{5,13},{6,14},{7,15},{8,0},{9,1},{10,2},{11,3},{12,20},{13,... | collective-permute-start | bytes 2261000 | tf_op jit(solution)/shard_map/ppermute | solution.py:331
  15.1 11.0 %collective-permute-start.5 = (f32[416,128]{1,0:T(8,128)S(1)}, f32[416,128]{1,0:T(8,128)S(1)}, u32[]{:S(2)}, u32[]{:S(2)}) collective-permute-start(f32[416,128]{1,0:T(8,128)S(1)} %bitcast.41), channel_id=1, source_target_pairs={{0,7},{1,6},{2,5},{3,4},{4,3},{5,2},{6,1},{7,0},{8,15},{9,14},{10,... | collective-permute-start | bytes 638984 | tf_op jit(solution)/shard_map/ppermute | solution.py:321
  20.2 9.8 %collective-permute-start.4 = (f32[416,128]{1,0:T(8,128)S(1)}, f32[416,128]{1,0:T(8,128)S(1)}, u32[]{:S(2)}, u32[]{:S(2)}) collective-permute-start(f32[416,128]{1,0:T(8,128)S(1)} %bitcast.40), channel_id=1, source_target_pairs={{0,6},{1,7},{2,4},{3,5},{4,2},{5,3},{6,0},{7,1},{8,14},{9,15},{10,... | collective-permute-start | bytes 638984 | tf_op jit(solution)/shard_map/ppermute | solution.py:321
  20.3 21.5 %collective-permute-start.8 = (f32[2,368,128]{2,1,0:T(8,128)S(1)}, f32[2,368,128]{2,1,0:T(8,128)S(1)}, u32[]{:S(2)}, u32[]{:S(2)}) collective-permute-start(f32[2,368,128]{2,1,0:T(8,128)S(1)} %pad_maximum_fusion.1), channel_id=1, source_target_pairs={{0,8},{1,9},{2,10},{3,11},{8,16},{9,17},{10,18},{11,19},{12,4},{13... | collective-permute-start | bytes 1130504 | tf_op jit(solution)/shard_map/ppermute | solution.py:331
  30.0 11.7 %collective-permute-start.9 = (f32[2,368,128]{2,1,0:T(8,128)S(1)}, f32[2,368,128]{2,1,0:T(8,128)S(1)}, u32[]{:S(2)}, u32[]{:S(2)}) collective-permute-start(f32[2,368,128]{2,1,0:T(8,128)S(1)} %pad_maximum_fusion.2), channel_id=1, source_target_pairs={{0,8},{1,9},{2,10},{3,11},{8,16},{9,17},{10,18},{11,19},{12,4},{13... | collective-permute-start | bytes 1130504 | tf_op jit(solution)/shard_map/ppermute | solution.py:331
  38.6 8.2 %collective-permute-start.13 = (f32[21,16,128]{2,1,0:T(8,128)S(1)}, f32[21,16,128]{2,1,0:T(8,128)S(1)}, u32[]{:S(2)}, u32[]{:S(2)}) collective-permute-start(f32[21,16,128]{2,1,0:T(8,128)S(1)} %get-tuple-element.42), channel_id=1, source_target_pairs={{0,6},{1,7},{2,4},{3,5},{4,2},{5,3},{6,0},{7,1},{8,14},{9,15},{10,... | collective-permute-start | bytes 516104 | tf_op jit(solution)/shard_map/ppermute | solution.py:321
  39.8 9.0 %collective-permute-start.15 = (f32[21,16,128]{2,1,0:T(8,128)S(1)}, f32[21,16,128]{2,1,0:T(8,128)S(1)}, u32[]{:S(2)}, u32[]{:S(2)}) collective-permute-start(f32[21,16,128]{2,1,0:T(8,128)S(1)} %get-tuple-element.43), channel_id=1, source_target_pairs={{0,7},{1,6},{2,5},{3,4},{4,3},{5,2},{6,1},{7,0},{8,15},{9,14},{10,... | collective-permute-start | bytes 516104 | tf_op jit(solution)/shard_map/ppermute | solution.py:321
  41.0 12.0 %collective-permute-start.12 = (f32[21,16,128]{2,1,0:T(8,128)S(1)}, f32[21,16,128]{2,1,0:T(8,128)S(1)}, u32[]{:S(2)}, u32[]{:S(2)}) collective-permute-start(f32[21,16,128]{2,1,0:T(8,128)S(1)} %get-tuple-element.40), channel_id=1, source_target_pairs={{0,4},{1,5},{2,6},{3,7},{4,0},{5,1},{6,2},{7,3},{8,12},{9,13},{10,... | collective-permute-start | bytes 516104 | tf_op jit(solution)/shard_map/ppermute | solution.py:321
  45.1 8.3 %collective-permute-start.10 = (f32[21,16,128]{2,1,0:T(8,128)S(1)}, f32[21,16,128]{2,1,0:T(8,128)S(1)}, u32[]{:S(2)}, u32[]{:S(2)}) collective-permute-start(f32[21,16,128]{2,1,0:T(8,128)S(1)} %get-tuple-element.45), channel_id=1, source_target_pairs={{0,2},{1,3},{2,0},{3,1},{4,6},{5,7},{6,4},{7,5},{8,10},{9,11},{10,... | collective-permute-start | bytes 516104 | tf_op jit(solution)/shard_map/ppermute | solution.py:321
  46.4 10.5 %collective-permute-start.11 = (f32[21,16,128]{2,1,0:T(8,128)S(1)}, f32[21,16,128]{2,1,0:T(8,128)S(1)}, u32[]{:S(2)}, u32[]{:S(2)}) collective-permute-start(f32[21,16,128]{2,1,0:T(8,128)S(1)} %get-tuple-element.46), channel_id=1, source_target_pairs={{0,3},{1,2},{2,1},{3,0},{4,7},{5,6},{6,5},{7,4},{8,11},{9,10},{10,... | collective-permute-start | bytes 516104 | tf_op jit(solution)/shard_map/ppermute | solution.py:321
  48.8 2.6 %collective-permute-start.16 = (f32[21,16,128]{2,1,0:T(8,128)S(1)}, f32[21,16,128]{2,1,0:T(8,128)S(1)}, u32[]{:S(2)}, u32[]{:S(2)}) collective-permute-start(f32[21,16,128]{2,1,0:T(8,128)S(1)} %get-tuple-element.50), channel_id=1, source_target_pairs={{0,1},{1,0},{2,3},{3,2},{4,5},{5,4},{6,7},{7,6},{8,9},{9,8},{10,11... | collective-permute-start | bytes 516104 | tf_op jit(solution)/shard_map/ppermute | solution.py:321
  50.3 6.6 %collective-permute-start.14 = (f32[21,16,128]{2,1,0:T(8,128)S(1)}, f32[21,16,128]{2,1,0:T(8,128)S(1)}, u32[]{:S(2)}, u32[]{:S(2)}) collective-permute-start(f32[21,16,128]{2,1,0:T(8,128)S(1)} %get-tuple-element.49), channel_id=1, source_target_pairs={{0,5},{1,4},{2,7},{3,6},{4,1},{5,0},{6,3},{7,2},{8,13},{9,12},{10,... | collective-permute-start | bytes 516104 | tf_op jit(solution)/shard_map/ppermute | solution.py:321

commit v14 on v13

--- a/solution.py
+++ b/solution.py
@@ -9,6 +9,8 @@
 PLANES = 2
 ACTIVE = 49
 MOST = 8
+FEW = 3
+MANY = 28
 
 
 class Layout:
@@ -203,7 +205,23 @@
     chosen = valid[None] & (rank[None] == place)
     take = jnp.sum(jnp.where(chosen, products[None], 0), 1)
     factor = jnp.sum(jnp.where(chosen, factors[None], 0.0), 1)
-    return jnp.concatenate([sources.reshape(-1), take.T.reshape(-1)]), factor.T.reshape(-1)
+    return sources, take, factor, jnp.sum(jnp.where(valid, 1, 0), 0)
+
+
+def kernel_lists(sources, take, factor, count):
+    number = jnp.arange(count.shape[0], dtype=jnp.int32)
+    many = count > FEW
+    rank = jnp.sum(jnp.where(many[None, :] & (number[None, :] < number[:, None]), 1, 0), 1)
+    place = jnp.arange(MANY, dtype=jnp.int32)[None, :, None]
+    chosen = many[None, None, :] & (rank[None, None, :] == place)
+    take_more = jnp.sum(jnp.where(chosen, take[FEW:, None, :], 0), 2)
+    factor_more = jnp.sum(jnp.where(chosen, factor[FEW:, None, :], 0.0), 2)
+    more = jnp.where(many, rank, MANY)
+    indices = [sources, take[:FEW].T, take_more.T, more]
+    factors = [factor[:FEW].T, factor_more.T]
+    return tuple(
+        jnp.concatenate([part.reshape(-1) for part in parts]) for parts in (indices, factors)
+    )
 
 
 def tree_sum(values):
@@ -222,7 +240,7 @@
         piece_refs, refs = refs[: lay.modes], refs[lay.modes :]
         other_refs, refs = refs[: lay.modes], refs[lay.modes :]
         halo_refs, refs = refs[: len(arrays)], refs[len(arrays) :]
-        out_refs, (near_ref, product_ref) = refs[: lay.modes], refs[lay.modes :]
+        out_refs, (near_ref, product_ref, more_ref) = refs[: lay.modes], refs[lay.modes :]
         lane = lax.broadcasted_iota(jnp.int32, full, 1)
         line = lax.broadcasted_iota(jnp.int32, full, 0)
         mode = lax.rem(j_ref[0], lay.modes)
@@ -276,15 +294,23 @@
 
         lax.fori_loop(1, lay.terms, apply, 0)
 
+        def taken(first, count):
+            return [
+                factor_ref[e] * product_ref[index_ref[products + e]]
+                for e in range(first, first + count)
+            ]
+
+        few, rest = FEW * lay.slots, MOST - FEW
+        for n in range(MANY):
+            more_ref[n] = tree_sum(taken(few + n * rest, rest))
+        more_ref[MANY] = jnp.zeros(full, jnp.float32)
+        more_at = products + few + MANY * rest
         operator = operator_of(0)
         for block in range(lay.modes):
             for i in range(lay.quota):
                 s = block * lay.quota + i
-                values = [operator(s)]
-                for n in range(MOST):
-                    e = s * MOST + n
-                    values.append(factor_ref[e] * product_ref[index_ref[products + e]])
-                out_refs[block][i] = tree_sum(values)
+                more = more_ref[index_ref[more_at + s]]
+                out_refs[block][i] = tree_sum([operator(s), *taken(FEW * s, FEW), more])
 
     return pl.pallas_call(
         kernel,
@@ -294,6 +320,7 @@
         scratch_shapes=[
             pltpu.VMEM((lay.places, 6, rows, width), jnp.float32),
             pltpu.VMEM((products, rows, width), jnp.float32),
+            pltpu.VMEM((MANY + 1, rows, width), jnp.float32),
         ],
         compiler_params=pltpu.CompilerParams(vmem_limit_bytes=VMEM_LIMIT),
         name=name,
@@ -343,14 +370,15 @@
     number = jnp.arange(modes, dtype=jnp.int32)
     mine = jnp.bitwise_xor(number, mode)[:, None, None] == number[None, :, None]
     slot_mode = jnp.sum(jnp.where(mine, slot_mode.reshape(1, modes, quota), 0), 1).reshape(-1)
-    lists = coupling_lists(pattern, coupling, slot_mode)
-    pieces[half] = after(pieces[half], *lists)
+    *lists, count = coupling_lists(pattern, coupling, slot_mode)
+    pieces[half] = after(pieces[half], *lists, count)
+    lists = kernel_lists(*lists, after(count, pieces[modes]))
     own_halo = shift(pieces[:modes], False)
     own_halos = [(own_halo, n) for n in range(modes)]
-    crossing_halos = []
-    for r in (modes, modes + half):
-        halo = shift(pieces[r : r + half], True)
-        crossing_halos += [(halo, n) for n in range(half)]
+    early_halo = shift(pieces[modes : modes + half], True)
+    crossing_halos = [(early_halo, n) for n in range(half)]
+    for r in range(modes + half, lay.group):
+        crossing_halos.append((shift(pieces[r : r + 1], True), 0))
 
     own, crossing = pieces[:modes], pieces[modes:]
     crossing_out = stencil(crossing, own, own_halos, lists, j, "stencil_crossing", lay)
@@ -363,10 +391,9 @@
         back[r] = swap(out[r], r)
     for n in range(half):
         ahead = [back[r] for r in first[:n]]
-        ahead = [*own_out, *ahead] if n else []
-        back[modes + n] = swap(after(out[modes + n], *ahead), modes + n)
+        back[modes + n] = swap(after(out[modes + n], *own_out, *ahead), modes + n)
     for r in range(half):
-        back[r] = swap(after(out[r], *[back[r] for r in first]) if r else out[r], r)
+        back[r] = swap(after(out[r], back[first[-1]]) if r else out[r], r)
     last = range(half, modes + half)
     shape = (quota, height, width)
     whole = unpack({r: back[r] for r in back if r not in last}, j, shape, lay)

time: 58.1 us -> 59.2 us (1.019)
  starting transfers between devices: 25 us -> 28.6 us
  waiting for transfers between devices: 16.3 us -> 13.1 us
  other arithmetic: 1.26 us -> 2.62 us
    ppermute x3 -> x4, starting transfers between devices: 8.21 us -> 11.6 us  [shift(): return lax.ppermute(main, axes, pairs)]
    ppermute x14, waiting for transfers between devices: 14.5 us -> 11.1 us  [swap(): return lax.ppermute(piece, axes, [(d, d ^ r) for d in range(devices)])]
    another operation x3 -> x2, other arithmetic: 0.11 us -> 0.97 us  [shift(): main = jnp.stack([piece[:lay.main] for piece in pieces])]
    slice x1, local copies, waits for them, and re-layouts: 0.69 us -> 0.01 us  [shift(): main = jnp.stack([piece[:lay.main] for piece in pieces])]
    ppermute x3 -> x4, waiting for transfers between devices: 1.83 us -> 2.01 us  [shift(): return lax.ppermute(main, axes, pairs)]
    unnamed x8 -> x6, local copies, waits for them, and re-layouts: 1.37 us -> 1.37 us
  transfers between devices with their start and end apart: 17 -> 18, of which waited for: 10 -> 8; matrix products, arithmetic and copies ran while one was open for 8% -> 10% of each run, Pallas kernels for 16% -> 14%
where the time goes in v14:
time: 59.2 us; the launch traced here: 58.9 us
  starting transfers between devices  28.6 us (48%)
  waiting for transfers between devices  13.1 us (22%)
  Pallas kernels  10.9 us (18%)
  local copies, waits for them, and re-layouts  2.69 us (5%)
  other arithmetic  2.62 us (4%)
  matrix products  0.69 us (1%)
    ppermute x14, starting transfers between devices, swap(): return lax.ppermute(piece, axes, [(d, d ^ r) for d in range(devices)])  17 us
    ppermute x4, starting transfers between devices, shift(): return lax.ppermute(main, axes, pairs)  11.6 us
    ppermute x14, waiting for transfers between devices, swap(): return lax.ppermute(piece, axes, [(d, d ^ r) for d in range(devices)])  11.1 us
    pallas_call x2, Pallas kernels, stencil(): pl.pallas_call(kernel, out_shape=[jax.ShapeDtypeStruct((lay.quota, rows,...  6.05 us
    pallas_call x2, Pallas kernels, pack(): pl.pallas_call(kernel, out_shape=[pltpu.VMEM(shape, jnp.float32)] * modes...  3.1 us
    ppermute x4, waiting for transfers between devices, shift(): return lax.ppermute(main, axes, pairs)  2.01 us
    pallas_call x2, Pallas kernels, unpack(): pl.pallas_call(kernel, out_shape=pltpu.HBM(shape, jnp.float32), in_specs=...  1.75 us
    unnamed x6, local copies, waits for them, and re-layouts  1.37 us
  transfers between devices with their start and end apart: 18, of which 8 were waited for; matrix products, arithmetic and copies ran while one was open for 10% of the time, Pallas kernels for 14%

profile of v14, /device:TPU:0, one launch (start us, length us, event | category | flops | bytes accessed | tf_op | source)
XLA Modules:
  0.0 58.9 jit_solution(9980466273684408683)
XLA Ops:
  0.0 1.5 %pack_own.1 = (f32[26,16,128]{2,1,0:T(8,128)S(1)}, f32[26,16,128]{2,1,0:T(8,128)S(1)}, f32[26,16,128]{2,1,0:T(8,128)S(1)}, f32[26,16,128]{2,1,0:T(8,128)S(1)}) custom-call(s32[1]{0:T(128)} %bitcast.j_ref, f32[21,128,128]{2,1,0:T(8,128)} %bitcast.51, f32[1,128,128]{2,1,0:T(8,128)} %mean_ref.3, f32[6,128,128]{2,1,0:T(8,128)} %bitcast.53), custom_call_target="tpu_custom_call" | custom-call | tf_op jit(solution)/shard_map/pack_own/pallas_call | solution.py:127
  1.6 0.0 copy-start.1
  1.6 0.0 copy-start
  1.6 3.0 %collective-permute-start.2 = (f32[416,128]{1,0:T(8,128)S(1)}, f32[416,128]{1,0:T(8,128)S(1)}, u32[]{:S(2)}, u32[]{:S(2)}) collective-permute-start(f32[416,128]{1,0:T(8,128)S(1)} %bitcast.50), channel_id=1, source_target_pairs={{0,2},{1,3},{2,0},{3,1},{4,6},{5,7},{6,4},{7,5},{8,10},{9,11},{10,... | collective-permute-start | bytes 638984 | tf_op jit(solution)/shard_map/ppermute | solution.py:348
  4.6 0.0 collective-permute-start.6
  4.6 0.2 collective-permute-start.3
  4.8 1.5 %pack_crossing.1 = (f32[26,16,128]{2,1,0:T(8,128)S(1)}, f32[26,16,128]{2,1,0:T(8,128)S(1)}, f32[26,16,128]{2,1,0:T(8,128)S(1)}, f32[26,16,128]{2,1,0:T(8,128)S(1)}) custom-call(s32[1]{0:T(128)} %bitcast.j_ref, f32[21,128,128]{2,1,0:T(8,128)} %bitcast.52, f32[1,128,128]{2,1,0:T(8,128)} %mean_ref.3, f32[6,128,128]{2,1,0:T(8,128)} %bitcast.54), custom_call_target="tpu_custom_call" | custom-call | tf_op jit(solution)/shard_map/pack_crossing/pallas_call | solution.py:127
  6.4 1.6 %collective-permute-start.1 = (f32[416,128]{1,0:T(8,128)S(1)}, f32[416,128]{1,0:T(8,128)S(1)}, u32[]{:S(2)}, u32[]{:S(2)}) collective-permute-start(f32[416,128]{1,0:T(8,128)S(1)} %bitcast.46), channel_id=1, source_target_pairs={{0,5},{1,4},{2,7},{3,6},{4,1},{5,0},{6,3},{7,2},{8,13},{9,12},{10,... | collective-permute-start | bytes 638984 | tf_op jit(solution)/shard_map/ppermute | solution.py:348
  8.0 0.5 collective-permute-start
  8.5 0.1 iota_compare_fusion.10
  8.5 0.1 broadcast_in_dim.201
  8.6 0.1 select_reduce_fusion.13
  8.7 0.1 eq.98
  8.8 0.2 copy.12
  9.0 1.2 %copy.13 = f32[7,84,84]{1,2,0:T(8,128)S(1)} copy(f32[7,84,84]{2,1,0:T(8,128)} %param.10) | data formatting | bytes 395136 | tf_op args[4]
  10.2 0.4 fusion
  10.5 0.3 fusion.10
  10.9 0.1 fusion.5
  11.0 0.2 select_reduce_fusion.4
  11.3 0.1 select_reduce_fusion.6
  11.4 0.1 broadcast_add_fusion.1
  11.5 0.1 select_reduce_fusion.1
  11.6 0.2 select_reduce_fusion.5
  11.8 0.1 reshape.164
  11.9 0.1 copy.14
  12.1 0.2 reshape.165
  12.2 0.1 copy.16
  12.3 0.2 reshape.172
  12.5 0.0 collective-permute-done.2.refs_6_.refs_2_
  12.6 1.1 %collective-permute-done.3.refs_7_.refs_3_ = f32[416,128]{1,0:T(8,128)S(1)} collective-permute-done((f32[416,128]{1,0:T(8,128)S(1)}, f32[416,128]{1,0:T(8,128)S(1)}, u32[]{:S(2)}, u32[]{:S(2)}) %collective-permute-start.3) | collective-permute-done | bytes 213024 | tf_op jit(solution)/shard_map/ppermute | solution.py:348
  13.7 0.9 %pad_maximum_fusion = f32[4,368,128]{2,1,0:T(8,128)} fusion(f32[1,368,128]{2,1,0:T(8,128)S(1)} %slice_bitcast_fusion.4, f32[1,368,128]{2,1,0:T(8,128)S(1)} %slice_bitcast_fusion.6, f32[1,368,128]{2,1,0:T(8,128)S(1)} %slice_bitcast_fusion.5, f32[1,368,128]{2,1,0:T(8,128)S(1)} %bitcast.55), kind=kLoop, calls=%fused_computation | loop fusion | flops 565248 | bytes 1507328 | tf_op jit(solution)/shard_map/stack | solution.py:357
  14.6 1.3 %collective-permute-start.7 = (f32[4,368,128]{2,1,0:T(8,128)}, f32[4,368,128]{2,1,0:T(8,128)S(1)}, u32[]{:S(2)}, u32[]{:S(2)}) collective-permute-start(f32[4,368,128]{2,1,0:T(8,128)} %pad_maximum_fusion), channel_id=1, source_target_pairs={{4,12},{5,13},{6,14},{7,15},{8,0},{9,1},{10,2},{11,3},{12,20},{13,... | collective-permute-start | bytes 2261000 | tf_op jit(solution)/shard_map/ppermute | solution.py:358
  15.9 5.1 %collective-permute-start.5 = (f32[416,128]{1,0:T(8,128)S(1)}, f32[416,128]{1,0:T(8,128)S(1)}, u32[]{:S(2)}, u32[]{:S(2)}) collective-permute-start(f32[416,128]{1,0:T(8,128)S(1)} %bitcast.45), channel_id=1, source_target_pairs={{0,7},{1,6},{2,5},{3,4},{4,3},{5,2},{6,1},{7,0},{8,15},{9,14},{10,... | collective-permute-start | bytes 638984 | tf_op jit(solution)/shard_map/ppermute | solution.py:348
  21.1 0.0 collective-permute-start.4
  21.1 0.0 collective-permute-done.refs_0_.refs_4_
  21.1 0.1 select_reduce_fusion.11
  21.2 0.1 select_reduce_fusion.7
  21.3 0.2 select_reduce_fusion.8
  21.5 0.1 copy.17
  21.6 0.1 reshape.173
  21.7 0.1 copy.15
  21.8 0.1 reshape.171
  22.0 3.5 %collective-permute-start.8 = (f32[2,368,128]{2,1,0:T(8,128)S(1)}, f32[2,368,128]{2,1,0:T(8,128)S(1)}, u32[]{:S(2)}, u32[]{:S(2)}) collective-permute-start(f32[2,368,128]{2,1,0:T(8,128)S(1)} %pad_maximum_fusion.1), channel_id=1, source_target_pairs={{0,8},{1,9},{2,10},{3,11},{8,16},{9,17},{10,18},{11,19},{12,4},{13... | collective-permute-start | bytes 1130504 | tf_op jit(solution)/shard_map/ppermute | solution.py:358
  25.5 0.1 pad_add_fusion.2.index_ref
  25.6 1.3 %collective-permute-done.5.refs_3_.refs_7_ = f32[416,128]{1,0:T(8,128)S(1)} collective-permute-done((f32[416,128]{1,0:T(8,128)S(1)}, f32[416,128]{1,0:T(8,128)S(1)}, u32[]{:S(2)}, u32[]{:S(2)}) %collective-permute-start.5) | collective-permute-done | bytes 213024 | tf_op jit(solution)/shard_map/ppermute | solution.py:348
  26.9 3.4 %collective-permute-start.10 = (f32[1,368,128]{2,1,0:T(8,128)S(1)}, f32[1,368,128]{2,1,0:T(8,128)S(1)}, u32[]{:S(2)}, u32[]{:S(2)}) collective-permute-start(f32[1,368,128]{2,1,0:T(8,128)S(1)} %slice_bitcast_fusion), channel_id=1, source_target_pairs={{0,8},{1,9},{2,10},{3,11},{8,16},{9,17},{10,18},{11,19},{12,4},{13... | collective-permute-start | bytes 565256 | tf_op jit(solution)/shard_map/ppermute | solution.py:358
  30.4 0.5 collective-permute-done.4.refs_2_.refs_6_
  30.9 3.4 %collective-permute-start.9 = (f32[1,368,128]{2,1,0:T(8,128)S(1)}, f32[1,368,128]{2,1,0:T(8,128)S(1)}, u32[]{:S(2)}, u32[]{:S(2)}) collective-permute-start(f32[1,368,128]{2,1,0:T(8,128)S(1)} %slice_bitcast_fusion.1), channel_id=1, source_target_pairs={{0,8},{1,9},{2,10},{3,11},{8,16},{9,17},{10,18},{11,19},{12,4},{13... | collective-permute-start | bytes 565256 | tf_op jit(solution)/shard_map/ppermute | solution.py:358
  34.3 0.1 pad_maximum_fusion.3.factor_ref
  34.4 2.0 %collective-permute-done.7.refs_8_ = f32[4,368,128]{2,1,0:T(8,128)S(1)} collective-permute-done((f32[4,368,128]{2,1,0:T(8,128)}, f32[4,368,128]{2,1,0:T(8,128)S(1)}, u32[]{:S(2)}, u32[]{:S(2)}) %collective-permute-start.7) | collective-permute-done | bytes 753696 | tf_op jit(solution)/shard_map/ppermute | solution.py:358
  36.4 3.0 %stencil_crossing.1 = (f32[21,16,128]{2,1,0:T(8,128)S(1)}, f32[21,16,128]{2,1,0:T(8,128)S(1)}, f32[21,16,128]{2,1,0:T(8,128)S(1)}, f32[21,16,128]{2,1,0:T(8,128)S(1)}) custom-call(s32[1]{0:T(128)} %bitcast.j_ref, s32[770]{0:T(1024)S(1)} %pad_add_fusion.2.index_ref, f32[392]{0:T(512)S(1)} %pad_maximum_fusion.3.factor_ref, ...), custom_call_target="tpu_custom_call" | custom-call | tf_op jit(solution)/shard_map/stencil_crossing/pallas_call | solution.py:315
  39.4 1.3 %collective-permute-start.16 = (f32[21,16,128]{2,1,0:T(8,128)S(1)}, f32[21,16,128]{2,1,0:T(8,128)S(1)}, u32[]{:S(2)}, u32[]{:S(2)}) collective-permute-start(f32[21,16,128]{2,1,0:T(8,128)S(1)} %get-tuple-element.46), channel_id=1, source_target_pairs={{0,7},{1,6},{2,5},{3,4},{4,3},{5,2},{6,1},{7,0},{8,15},{9,14},{10,... | collective-permute-start | bytes 516104 | tf_op jit(solution)/shard_map/ppermute | solution.py:348
  40.7 1.4 %collective-permute-start.14 = (f32[21,16,128]{2,1,0:T(8,128)S(1)}, f32[21,16,128]{2,1,0:T(8,128)S(1)}, u32[]{:S(2)}, u32[]{:S(2)}) collective-permute-start(f32[21,16,128]{2,1,0:T(8,128)S(1)} %get-tuple-element.45), channel_id=1, source_target_pairs={{0,6},{1,7},{2,4},{3,5},{4,2},{5,3},{6,0},{7,1},{8,14},{9,15},{10,... | collective-permute-start | bytes 516104 | tf_op jit(solution)/shard_map/ppermute | solution.py:348
  42.1 3.0 %stencil_own.1 = (f32[21,16,128]{2,1,0:T(8,128)S(1)}, f32[21,16,128]{2,1,0:T(8,128)S(1)}, f32[21,16,128]{2,1,0:T(8,128)S(1)}, f32[21,16,128]{2,1,0:T(8,128)S(1)}) custom-call(s32[1]{0:T(128)} %bitcast.j_ref, s32[770]{0:T(1024)S(1)} %pad_add_fusion.2.index_ref, f32[392]{0:T(512)S(1)} %pad_maximum_fusion.3.factor_ref, f32[416,128]{1,0:T(8,128)S(1)} %bitcast.43, ...), custom_call_target="tpu_custom_call" | custom-call | tf_op jit(solution)/shard_map/stencil_own/pallas_call | solution.py:315
  45.1 1.2 %collective-permute-start.11 = (f32[21,16,128]{2,1,0:T(8,128)S(1)}, f32[21,16,128]{2,1,0:T(8,128)S(1)}, u32[]{:S(2)}, u32[]{:S(2)}) collective-permute-start(f32[21,16,128]{2,1,0:T(8,128)S(1)} %get-tuple-element.48), channel_id=1, source_target_pairs={{0,2},{1,3},{2,0},{3,1},{4,6},{5,7},{6,4},{7,5},{8,10},{9,11},{10,... | collective-permute-start | bytes 516104 | tf_op jit(solution)/shard_map/ppermute | solution.py:348
  46.4 0.4 collective-permute-start.12
  46.7 1.7 %collective-permute-start.13 = (f32[21,16,128]{2,1,0:T(8,128)S(1)}, f32[21,16,128]{2,1,0:T(8,128)S(1)}, u32[]{:S(2)}, u32[]{:S(2)}) collective-permute-start(f32[21,16,128]{2,1,0:T(8,128)S(1)} %get-tuple-element.52), channel_id=1, source_target_pairs={{0,4},{1,5},{2,6},{3,7},{4,0},{5,1},{6,2},{7,3},{8,12},{9,13},{10,... | collective-permute-start | bytes 516104 | tf_op jit(solution)/shard_map/ppermute | solution.py:348
  48.5 0.5 collective-permute-start.17
  49.0 1.9 %collective-permute-done.14.refs_0_ = f32[21,16,128]{2,1,0:T(8,128)S(1)} collective-permute-done((f32[21,16,128]{2,1,0:T(8,128)S(1)}, f32[21,16,128]{2,1,0:T(8,128)S(1)}, u32[]{:S(2)}, u32[]{:S(2)}) %collective-permute-start.14) | collective-permute-done | bytes 172064 | tf_op jit(solution)/shard_map/ppermute | solution.py:348
  50.9 0.9 %unpack_first.1.refs_4_ = f32[21,128,128]{2,1,0:T(8,128)} custom-call(s32[1]{0:T(128)} %bitcast.j_ref, f32[21,16,128]{2,1,0:T(8,128)S(1)} %collective-permute-done.14.refs_0_, f32[21,16,128]{2,1,0:T(8,128)S(1)} %collective-permute-done.16.refs_1_, f32[21,16,128]{2,1,0:T(8,128)S(1)} %get-tuple-element.50.refs_2_, ...), custom_call_target="tpu_custom_call" | custom-call | tf_op jit(solution)/shard_map/unpack_first/pallas_call | solution.py:160
  51.8 2.6 %collective-permute-done.13.refs_2_ = f32[21,16,128]{2,1,0:T(8,128)S(1)} collective-permute-done((f32[21,16,128]{2,1,0:T(8,128)S(1)}, f32[21,16,128]{2,1,0:T(8,128)S(1)}, u32[]{:S(2)}, u32[]{:S(2)}) %collective-permute-start.13) | collective-permute-done | bytes 172064 | tf_op jit(solution)/shard_map/ppermute | solution.py:348
  54.3 0.2 collective-permute-done.11.refs_0_
  54.5 3.5 %collective-permute-done.12.refs_1_ = f32[21,16,128]{2,1,0:T(8,128)S(1)} collective-permute-done((f32[21,16,128]{2,1,0:T(8,128)S(1)}, f32[21,16,128]{2,1,0:T(8,128)S(1)}, u32[]{:S(2)}, u32[]{:S(2)}) %collective-permute-start.12) | collective-permute-done | bytes 172064 | tf_op jit(solution)/shard_map/ppermute | solution.py:348
  58.1 0.9 %unpack_last.1 = f32[21,128,128]{2,1,0:T(8,128)} custom-call(s32[1]{0:T(128)} %bitcast.j_ref, f32[21,16,128]{2,1,0:T(8,128)S(1)} %collective-permute-done.11.refs_0_, f32[21,16,128]{2,1,0:T(8,128)S(1)} %collective-permute-done.12.refs_1_, f32[21,16,128]{2,1,0:T(8,128)S(1)} %collective-permute-done.13.refs_2_, ...), custom_call_target="tpu_custom_call", output_to_operand_aliasing={{}: (5, {})} | custom-call | tf_op jit(solution)/shard_map/unpack_last/pallas_call | solution.py:160
  (38 shorter events, 0.3 us)
Async XLA Ops:
  1.6 7.0 %copy-start.1 = (s32[84]{0:T(128)S(1)}, s32[84]{0:T(128)}, u32[]{:S(2)}) copy-start(s32[84]{0:T(128)} %param.11) | copy-start | bytes 1012
  1.6 7.2 %copy-start = (s32[7,84,84]{2,1,0:T(8,128)S(1)}, s32[7,84,84]{2,1,0:T(8,128)}, u32[]{:S(2)}) copy-start(s32[7,84,84]{2,1,0:T(8,128)} %param.9) | copy-start | bytes 592708
  1.6 11.0 %collective-permute-start.2 = (f32[416,128]{1,0:T(8,128)S(1)}, f32[416,128]{1,0:T(8,128)S(1)}, u32[]{:S(2)}, u32[]{:S(2)}) collective-permute-start(f32[416,128]{1,0:T(8,128)S(1)} %bitcast.50), channel_id=1, source_target_pairs={{0,2},{1,3},{2,0},{3,1},{4,6},{5,7},{6,4},{7,5},{8,10},{9,11},{10,... | collective-permute-start | bytes 638984 | tf_op jit(solution)/shard_map/ppermute | solution.py:348
  4.6 8.0 %collective-permute-start.6 = (f32[416,128]{1,0:T(8,128)S(1)}, f32[416,128]{1,0:T(8,128)S(1)}, u32[]{:S(2)}, u32[]{:S(2)}) collective-permute-start(f32[416,128]{1,0:T(8,128)S(1)} %bitcast.49), channel_id=1, source_target_pairs={{0,1},{1,0},{2,3},{3,2},{4,5},{5,4},{6,7},{7,6},{8,9},{9,8},{10,11... | collective-permute-start | bytes 638984 | tf_op jit(solution)/shard_map/ppermute | solution.py:348
  4.6 9.1 %collective-permute-start.3 = (f32[416,128]{1,0:T(8,128)S(1)}, f32[416,128]{1,0:T(8,128)S(1)}, u32[]{:S(2)}, u32[]{:S(2)}) collective-permute-start(f32[416,128]{1,0:T(8,128)S(1)} %bitcast.48), channel_id=1, source_target_pairs={{0,3},{1,2},{2,1},{3,0},{4,7},{5,6},{6,5},{7,4},{8,11},{9,10},{10,... | collective-permute-start | bytes 638984 | tf_op jit(solution)/shard_map/ppermute | solution.py:348
  6.4 15.6 %collective-permute-start.1 = (f32[416,128]{1,0:T(8,128)S(1)}, f32[416,128]{1,0:T(8,128)S(1)}, u32[]{:S(2)}, u32[]{:S(2)}) collective-permute-start(f32[416,128]{1,0:T(8,128)S(1)} %bitcast.46), channel_id=1, source_target_pairs={{0,5},{1,4},{2,7},{3,6},{4,1},{5,0},{6,3},{7,2},{8,13},{9,12},{10,... | collective-permute-start | bytes 638984 | tf_op jit(solution)/shard_map/ppermute | solution.py:348
  8.0 13.1 %collective-permute-start = (f32[416,128]{1,0:T(8,128)S(1)}, f32[416,128]{1,0:T(8,128)S(1)}, u32[]{:S(2)}, u32[]{:S(2)}) collective-permute-start(f32[416,128]{1,0:T(8,128)S(1)} %bitcast.47), channel_id=1, source_target_pairs={{0,4},{1,5},{2,6},{3,7},{4,0},{5,1},{6,2},{7,3},{8,12},{9,13},{10,... | collective-permute-start | bytes 638984 | tf_op jit(solution)/shard_map/ppermute | solution.py:348
  14.6 21.8 %collective-permute-start.7 = (f32[4,368,128]{2,1,0:T(8,128)}, f32[4,368,128]{2,1,0:T(8,128)S(1)}, u32[]{:S(2)}, u32[]{:S(2)}) collective-permute-start(f32[4,368,128]{2,1,0:T(8,128)} %pad_maximum_fusion), channel_id=1, source_target_pairs={{4,12},{5,13},{6,14},{7,15},{8,0},{9,1},{10,2},{11,3},{12,20},{13,... | collective-permute-start | bytes 2261000 | tf_op jit(solution)/shard_map/ppermute | solution.py:358
  15.9 11.0 %collective-permute-start.5 = (f32[416,128]{1,0:T(8,128)S(1)}, f32[416,128]{1,0:T(8,128)S(1)}, u32[]{:S(2)}, u32[]{:S(2)}) collective-permute-start(f32[416,128]{1,0:T(8,128)S(1)} %bitcast.45), channel_id=1, source_target_pairs={{0,7},{1,6},{2,5},{3,4},{4,3},{5,2},{6,1},{7,0},{8,15},{9,14},{10,... | collective-permute-start | bytes 638984 | tf_op jit(solution)/shard_map/ppermute | solution.py:348
  21.1 9.8 %collective-permute-start.4 = (f32[416,128]{1,0:T(8,128)S(1)}, f32[416,128]{1,0:T(8,128)S(1)}, u32[]{:S(2)}, u32[]{:S(2)}) collective-permute-start(f32[416,128]{1,0:T(8,128)S(1)} %bitcast.44), channel_id=1, source_target_pairs={{0,6},{1,7},{2,4},{3,5},{4,2},{5,3},{6,0},{7,1},{8,14},{9,15},{10,... | collective-permute-start | bytes 638984 | tf_op jit(solution)/shard_map/ppermute | solution.py:348
  22.0 20.1 %collective-permute-start.8 = (f32[2,368,128]{2,1,0:T(8,128)S(1)}, f32[2,368,128]{2,1,0:T(8,128)S(1)}, u32[]{:S(2)}, u32[]{:S(2)}) collective-permute-start(f32[2,368,128]{2,1,0:T(8,128)S(1)} %pad_maximum_fusion.1), channel_id=1, source_target_pairs={{0,8},{1,9},{2,10},{3,11},{8,16},{9,17},{10,18},{11,19},{12,4},{13... | collective-permute-start | bytes 1130504 | tf_op jit(solution)/shard_map/ppermute | solution.py:358
  26.9 15.2 %collective-permute-start.10 = (f32[1,368,128]{2,1,0:T(8,128)S(1)}, f32[1,368,128]{2,1,0:T(8,128)S(1)}, u32[]{:S(2)}, u32[]{:S(2)}) collective-permute-start(f32[1,368,128]{2,1,0:T(8,128)S(1)} %slice_bitcast_fusion), channel_id=1, source_target_pairs={{0,8},{1,9},{2,10},{3,11},{8,16},{9,17},{10,18},{11,19},{12,4},{13... | collective-permute-start | bytes 565256 | tf_op jit(solution)/shard_map/ppermute | solution.py:358
  30.9 11.2 %collective-permute-start.9 = (f32[1,368,128]{2,1,0:T(8,128)S(1)}, f32[1,368,128]{2,1,0:T(8,128)S(1)}, u32[]{:S(2)}, u32[]{:S(2)}) collective-permute-start(f32[1,368,128]{2,1,0:T(8,128)S(1)} %slice_bitcast_fusion.1), channel_id=1, source_target_pairs={{0,8},{1,9},{2,10},{3,11},{8,16},{9,17},{10,18},{11,19},{12,4},{13... | collective-permute-start | bytes 565256 | tf_op jit(solution)/shard_map/ppermute | solution.py:358
  39.4 9.0 %collective-permute-start.16 = (f32[21,16,128]{2,1,0:T(8,128)S(1)}, f32[21,16,128]{2,1,0:T(8,128)S(1)}, u32[]{:S(2)}, u32[]{:S(2)}) collective-permute-start(f32[21,16,128]{2,1,0:T(8,128)S(1)} %get-tuple-element.46), channel_id=1, source_target_pairs={{0,7},{1,6},{2,5},{3,4},{4,3},{5,2},{6,1},{7,0},{8,15},{9,14},{10,... | collective-permute-start | bytes 516104 | tf_op jit(solution)/shard_map/ppermute | solution.py:348
  40.7 10.1 %collective-permute-start.14 = (f32[21,16,128]{2,1,0:T(8,128)S(1)}, f32[21,16,128]{2,1,0:T(8,128)S(1)}, u32[]{:S(2)}, u32[]{:S(2)}) collective-permute-start(f32[21,16,128]{2,1,0:T(8,128)S(1)} %get-tuple-element.45), channel_id=1, source_target_pairs={{0,6},{1,7},{2,4},{3,5},{4,2},{5,3},{6,0},{7,1},{8,14},{9,15},{10,... | collective-permute-start | bytes 516104 | tf_op jit(solution)/shard_map/ppermute | solution.py:348
  45.1 9.4 %collective-permute-start.11 = (f32[21,16,128]{2,1,0:T(8,128)S(1)}, f32[21,16,128]{2,1,0:T(8,128)S(1)}, u32[]{:S(2)}, u32[]{:S(2)}) collective-permute-start(f32[21,16,128]{2,1,0:T(8,128)S(1)} %get-tuple-element.48), channel_id=1, source_target_pairs={{0,2},{1,3},{2,0},{3,1},{4,6},{5,7},{6,4},{7,5},{8,10},{9,11},{10,... | collective-permute-start | bytes 516104 | tf_op jit(solution)/shard_map/ppermute | solution.py:348
  46.4 11.7 %collective-permute-start.12 = (f32[21,16,128]{2,1,0:T(8,128)S(1)}, f32[21,16,128]{2,1,0:T(8,128)S(1)}, u32[]{:S(2)}, u32[]{:S(2)}) collective-permute-start(f32[21,16,128]{2,1,0:T(8,128)S(1)} %get-tuple-element.49), channel_id=1, source_target_pairs={{0,3},{1,2},{2,1},{3,0},{4,7},{5,6},{6,5},{7,4},{8,11},{9,10},{10,... | collective-permute-start | bytes 516104 | tf_op jit(solution)/shard_map/ppermute | solution.py:348
  46.7 7.6 %collective-permute-start.13 = (f32[21,16,128]{2,1,0:T(8,128)S(1)}, f32[21,16,128]{2,1,0:T(8,128)S(1)}, u32[]{:S(2)}, u32[]{:S(2)}) collective-permute-start(f32[21,16,128]{2,1,0:T(8,128)S(1)} %get-tuple-element.52), channel_id=1, source_target_pairs={{0,4},{1,5},{2,6},{3,7},{4,0},{5,1},{6,2},{7,3},{8,12},{9,13},{10,... | collective-permute-start | bytes 516104 | tf_op jit(solution)/shard_map/ppermute | solution.py:348
  48.5 2.4 %collective-permute-start.17 = (f32[21,16,128]{2,1,0:T(8,128)S(1)}, f32[21,16,128]{2,1,0:T(8,128)S(1)}, u32[]{:S(2)}, u32[]{:S(2)}) collective-permute-start(f32[21,16,128]{2,1,0:T(8,128)S(1)} %get-tuple-element.54), channel_id=1, source_target_pairs={{0,1},{1,0},{2,3},{3,2},{4,5},{5,4},{6,7},{7,6},{8,9},{9,8},{10,11... | collective-permute-start | bytes 516104 | tf_op jit(solution)/shard_map/ppermute | solution.py:348
  50.9 7.2 %collective-permute-start.15 = (f32[21,16,128]{2,1,0:T(8,128)S(1)}, f32[21,16,128]{2,1,0:T(8,128)S(1)}, u32[]{:S(2)}, u32[]{:S(2)}) collective-permute-start(f32[21,16,128]{2,1,0:T(8,128)S(1)} %get-tuple-element.53), channel_id=1, source_target_pairs={{0,5},{1,4},{2,7},{3,6},{4,1},{5,0},{6,3},{7,2},{8,13},{9,12},{10,... | collective-permute-start | bytes 516104 | tf_op jit(solution)/shard_map/ppermute | solution.py:348

commit v15 on v14

--- a/solution.py
+++ b/solution.py
@@ -5,7 +5,7 @@
 from jax.experimental.pallas import tpu as pltpu
 from jax.sharding import PartitionSpec as P
 
-VMEM_LIMIT = 40 * 1024 * 1024
+VMEM_LIMIT = 20 * 1024 * 1024
 PLANES = 2
 ACTIVE = 49
 MOST = 8

time: 59.2 us -> 59.2 us (level)
  no operation moved by 1% of the time
where the time goes in v15:
time: 59.2 us; the launch traced here: 58.9 us
  starting transfers between devices  28.6 us (48%)
  waiting for transfers between devices  13.1 us (22%)
  Pallas kernels  10.9 us (18%)
  local copies, waits for them, and re-layouts  2.69 us (5%)
  other arithmetic  2.62 us (4%)
  matrix products  0.69 us (1%)
    ppermute x14, starting transfers between devices, swap(): return lax.ppermute(piece, axes, [(d, d ^ r) for d in range(devices)])  17 us
    ppermute x4, starting transfers between devices, shift(): return lax.ppermute(main, axes, pairs)  11.6 us
    ppermute x14, waiting for transfers between devices, swap(): return lax.ppermute(piece, axes, [(d, d ^ r) for d in range(devices)])  11.1 us
    pallas_call x2, Pallas kernels, stencil(): pl.pallas_call(kernel, out_shape=[jax.ShapeDtypeStruct((lay.quota, rows,...  6.05 us
    pallas_call x2, Pallas kernels, pack(): pl.pallas_call(kernel, out_shape=[pltpu.VMEM(shape, jnp.float32)] * modes...  3.1 us
    ppermute x4, waiting for transfers between devices, shift(): return lax.ppermute(main, axes, pairs)  2.01 us
    pallas_call x2, Pallas kernels, unpack(): pl.pallas_call(kernel, out_shape=pltpu.HBM(shape, jnp.float32), in_specs=...  1.75 us
    unnamed x6, local copies, waits for them, and re-layouts  1.37 us
  transfers between devices with their start and end apart: 18, of which 8 were waited for; matrix products, arithmetic and copies ran while one was open for 10% of the time, Pallas kernels for 14%

profile of v15, /device:TPU:0, one launch (start us, length us, event | category | flops | bytes accessed | tf_op | source)
XLA Modules:
  0.0 58.9 jit_solution(18239249019691880192)
XLA Ops:
  0.0 1.5 %pack_own.1 = (f32[26,16,128]{2,1,0:T(8,128)S(1)}, f32[26,16,128]{2,1,0:T(8,128)S(1)}, f32[26,16,128]{2,1,0:T(8,128)S(1)}, f32[26,16,128]{2,1,0:T(8,128)S(1)}) custom-call(s32[1]{0:T(128)} %bitcast.j_ref, f32[21,128,128]{2,1,0:T(8,128)} %bitcast.51, f32[1,128,128]{2,1,0:T(8,128)} %mean_ref.3, f32[6,128,128]{2,1,0:T(8,128)} %bitcast.53), custom_call_target="tpu_custom_call" | custom-call | tf_op jit(solution)/shard_map/pack_own/pallas_call | solution.py:127
  1.6 0.0 copy-start.1
  1.6 0.0 copy-start
  1.6 3.0 %collective-permute-start.2 = (f32[416,128]{1,0:T(8,128)S(1)}, f32[416,128]{1,0:T(8,128)S(1)}, u32[]{:S(2)}, u32[]{:S(2)}) collective-permute-start(f32[416,128]{1,0:T(8,128)S(1)} %bitcast.50), channel_id=1, source_target_pairs={{0,2},{1,3},{2,0},{3,1},{4,6},{5,7},{6,4},{7,5},{8,10},{9,11},{10,... | collective-permute-start | bytes 638984 | tf_op jit(solution)/shard_map/ppermute | solution.py:348
  4.6 0.2 collective-permute-start.3
  4.8 1.5 %pack_crossing.1 = (f32[26,16,128]{2,1,0:T(8,128)S(1)}, f32[26,16,128]{2,1,0:T(8,128)S(1)}, f32[26,16,128]{2,1,0:T(8,128)S(1)}, f32[26,16,128]{2,1,0:T(8,128)S(1)}) custom-call(s32[1]{0:T(128)} %bitcast.j_ref, f32[21,128,128]{2,1,0:T(8,128)} %bitcast.52, f32[1,128,128]{2,1,0:T(8,128)} %mean_ref.3, f32[6,128,128]{2,1,0:T(8,128)} %bitcast.54), custom_call_target="tpu_custom_call" | custom-call | tf_op jit(solution)/shard_map/pack_crossing/pallas_call | solution.py:127
  6.4 1.6 %collective-permute-start.1 = (f32[416,128]{1,0:T(8,128)S(1)}, f32[416,128]{1,0:T(8,128)S(1)}, u32[]{:S(2)}, u32[]{:S(2)}) collective-permute-start(f32[416,128]{1,0:T(8,128)S(1)} %bitcast.46), channel_id=1, source_target_pairs={{0,5},{1,4},{2,7},{3,6},{4,1},{5,0},{6,3},{7,2},{8,13},{9,12},{10,... | collective-permute-start | bytes 638984 | tf_op jit(solution)/shard_map/ppermute | solution.py:348
  8.0 0.5 collective-permute-start
  8.5 0.1 iota_compare_fusion.10
  8.5 0.1 broadcast_in_dim.201
  8.6 0.1 select_reduce_fusion.13
  8.7 0.1 eq.98
  8.8 0.2 copy.12
  9.0 1.2 %copy.13 = f32[7,84,84]{1,2,0:T(8,128)S(1)} copy(f32[7,84,84]{2,1,0:T(8,128)} %param.10) | data formatting | bytes 395136 | tf_op args[4]
  10.2 0.4 fusion
  10.5 0.3 fusion.10
  10.9 0.1 fusion.5
  11.0 0.2 select_reduce_fusion.4
  11.3 0.1 select_reduce_fusion.6
  11.4 0.1 broadcast_add_fusion.1
  11.5 0.1 select_reduce_fusion.1
  11.6 0.2 select_reduce_fusion.5
  11.8 0.1 reshape.164
  11.9 0.1 copy.14
  12.1 0.2 reshape.165
  12.2 0.1 copy.16
  12.3 0.2 reshape.172
  12.5 0.0 collective-permute-done.2.refs_6_.refs_2_
  12.6 0.0 collective-permute-done.6.refs_5_.refs_1_
  12.6 1.1 %collective-permute-done.3.refs_7_.refs_3_ = f32[416,128]{1,0:T(8,128)S(1)} collective-permute-done((f32[416,128]{1,0:T(8,128)S(1)}, f32[416,128]{1,0:T(8,128)S(1)}, u32[]{:S(2)}, u32[]{:S(2)}) %collective-permute-start.3) | collective-permute-done | bytes 213024 | tf_op jit(solution)/shard_map/ppermute | solution.py:348
  13.7 0.9 %pad_maximum_fusion = f32[4,368,128]{2,1,0:T(8,128)} fusion(f32[1,368,128]{2,1,0:T(8,128)S(1)} %slice_bitcast_fusion.4, f32[1,368,128]{2,1,0:T(8,128)S(1)} %slice_bitcast_fusion.6, f32[1,368,128]{2,1,0:T(8,128)S(1)} %slice_bitcast_fusion.5, f32[1,368,128]{2,1,0:T(8,128)S(1)} %bitcast.55), kind=kLoop, calls=%fused_computation | loop fusion | flops 565248 | bytes 1507328 | tf_op jit(solution)/shard_map/stack | solution.py:357
  14.6 1.3 %collective-permute-start.7 = (f32[4,368,128]{2,1,0:T(8,128)}, f32[4,368,128]{2,1,0:T(8,128)S(1)}, u32[]{:S(2)}, u32[]{:S(2)}) collective-permute-start(f32[4,368,128]{2,1,0:T(8,128)} %pad_maximum_fusion), channel_id=1, source_target_pairs={{4,12},{5,13},{6,14},{7,15},{8,0},{9,1},{10,2},{11,3},{12,20},{13,... | collective-permute-start | bytes 2261000 | tf_op jit(solution)/shard_map/ppermute | solution.py:358
  15.9 5.1 %collective-permute-start.5 = (f32[416,128]{1,0:T(8,128)S(1)}, f32[416,128]{1,0:T(8,128)S(1)}, u32[]{:S(2)}, u32[]{:S(2)}) collective-permute-start(f32[416,128]{1,0:T(8,128)S(1)} %bitcast.45), channel_id=1, source_target_pairs={{0,7},{1,6},{2,5},{3,4},{4,3},{5,2},{6,1},{7,0},{8,15},{9,14},{10,... | collective-permute-start | bytes 638984 | tf_op jit(solution)/shard_map/ppermute | solution.py:348
  21.1 0.1 select_reduce_fusion.11
  21.2 0.1 select_reduce_fusion.7
  21.3 0.2 select_reduce_fusion.8
  21.5 0.1 copy.17
  21.6 0.1 reshape.173
  21.7 0.1 copy.15
  21.8 0.1 reshape.171
  21.9 0.0 collective-permute-done.1.refs_1_.refs_5_
  22.0 3.5 %collective-permute-start.8 = (f32[2,368,128]{2,1,0:T(8,128)S(1)}, f32[2,368,128]{2,1,0:T(8,128)S(1)}, u32[]{:S(2)}, u32[]{:S(2)}) collective-permute-start(f32[2,368,128]{2,1,0:T(8,128)S(1)} %pad_maximum_fusion.1), channel_id=1, source_target_pairs={{0,8},{1,9},{2,10},{3,11},{8,16},{9,17},{10,18},{11,19},{12,4},{13... | collective-permute-start | bytes 1130504 | tf_op jit(solution)/shard_map/ppermute | solution.py:358
  25.5 0.1 pad_add_fusion.2.index_ref
  25.6 1.3 %collective-permute-done.5.refs_3_.refs_7_ = f32[416,128]{1,0:T(8,128)S(1)} collective-permute-done((f32[416,128]{1,0:T(8,128)S(1)}, f32[416,128]{1,0:T(8,128)S(1)}, u32[]{:S(2)}, u32[]{:S(2)}) %collective-permute-start.5) | collective-permute-done | bytes 213024 | tf_op jit(solution)/shard_map/ppermute | solution.py:348
  26.9 3.4 %collective-permute-start.10 = (f32[1,368,128]{2,1,0:T(8,128)S(1)}, f32[1,368,128]{2,1,0:T(8,128)S(1)}, u32[]{:S(2)}, u32[]{:S(2)}) collective-permute-start(f32[1,368,128]{2,1,0:T(8,128)S(1)} %slice_bitcast_fusion), channel_id=1, source_target_pairs={{0,8},{1,9},{2,10},{3,11},{8,16},{9,17},{10,18},{11,19},{12,4},{13... | collective-permute-start | bytes 565256 | tf_op jit(solution)/shard_map/ppermute | solution.py:358
  30.4 0.5 collective-permute-done.4.refs_2_.refs_6_
  30.9 3.4 %collective-permute-start.9 = (f32[1,368,128]{2,1,0:T(8,128)S(1)}, f32[1,368,128]{2,1,0:T(8,128)S(1)}, u32[]{:S(2)}, u32[]{:S(2)}) collective-permute-start(f32[1,368,128]{2,1,0:T(8,128)S(1)} %slice_bitcast_fusion.1), channel_id=1, source_target_pairs={{0,8},{1,9},{2,10},{3,11},{8,16},{9,17},{10,18},{11,19},{12,4},{13... | collective-permute-start | bytes 565256 | tf_op jit(solution)/shard_map/ppermute | solution.py:358
  34.3 0.1 pad_maximum_fusion.3.factor_ref
  34.4 2.0 %collective-permute-done.7.refs_8_ = f32[4,368,128]{2,1,0:T(8,128)S(1)} collective-permute-done((f32[4,368,128]{2,1,0:T(8,128)}, f32[4,368,128]{2,1,0:T(8,128)S(1)}, u32[]{:S(2)}, u32[]{:S(2)}) %collective-permute-start.7) | collective-permute-done | bytes 753696 | tf_op jit(solution)/shard_map/ppermute | solution.py:358
  36.4 3.0 %stencil_crossing.1 = (f32[21,16,128]{2,1,0:T(8,128)S(1)}, f32[21,16,128]{2,1,0:T(8,128)S(1)}, f32[21,16,128]{2,1,0:T(8,128)S(1)}, f32[21,16,128]{2,1,0:T(8,128)S(1)}) custom-call(s32[1]{0:T(128)} %bitcast.j_ref, s32[770]{0:T(1024)S(1)} %pad_add_fusion.2.index_ref, f32[392]{0:T(512)S(1)} %pad_maximum_fusion.3.factor_ref, ...), custom_call_target="tpu_custom_call" | custom-call | tf_op jit(solution)/shard_map/stencil_crossing/pallas_call | solution.py:315
  39.4 1.3 %collective-permute-start.16 = (f32[21,16,128]{2,1,0:T(8,128)S(1)}, f32[21,16,128]{2,1,0:T(8,128)S(1)}, u32[]{:S(2)}, u32[]{:S(2)}) collective-permute-start(f32[21,16,128]{2,1,0:T(8,128)S(1)} %get-tuple-element.46), channel_id=1, source_target_pairs={{0,7},{1,6},{2,5},{3,4},{4,3},{5,2},{6,1},{7,0},{8,15},{9,14},{10,... | collective-permute-start | bytes 516104 | tf_op jit(solution)/shard_map/ppermute | solution.py:348
  40.7 1.4 %collective-permute-start.14 = (f32[21,16,128]{2,1,0:T(8,128)S(1)}, f32[21,16,128]{2,1,0:T(8,128)S(1)}, u32[]{:S(2)}, u32[]{:S(2)}) collective-permute-start(f32[21,16,128]{2,1,0:T(8,128)S(1)} %get-tuple-element.45), channel_id=1, source_target_pairs={{0,6},{1,7},{2,4},{3,5},{4,2},{5,3},{6,0},{7,1},{8,14},{9,15},{10,... | collective-permute-start | bytes 516104 | tf_op jit(solution)/shard_map/ppermute | solution.py:348
  42.1 0.0 collective-permute-done.8.refs_8_
  42.1 3.0 %stencil_own.1 = (f32[21,16,128]{2,1,0:T(8,128)S(1)}, f32[21,16,128]{2,1,0:T(8,128)S(1)}, f32[21,16,128]{2,1,0:T(8,128)S(1)}, f32[21,16,128]{2,1,0:T(8,128)S(1)}) custom-call(s32[1]{0:T(128)} %bitcast.j_ref, s32[770]{0:T(1024)S(1)} %pad_add_fusion.2.index_ref, f32[392]{0:T(512)S(1)} %pad_maximum_fusion.3.factor_ref, f32[416,128]{1,0:T(8,128)S(1)} %bitcast.43, ...), custom_call_target="tpu_custom_call" | custom-call | tf_op jit(solution)/shard_map/stencil_own/pallas_call | solution.py:315
  45.1 1.2 %collective-permute-start.11 = (f32[21,16,128]{2,1,0:T(8,128)S(1)}, f32[21,16,128]{2,1,0:T(8,128)S(1)}, u32[]{:S(2)}, u32[]{:S(2)}) collective-permute-start(f32[21,16,128]{2,1,0:T(8,128)S(1)} %get-tuple-element.48), channel_id=1, source_target_pairs={{0,2},{1,3},{2,0},{3,1},{4,6},{5,7},{6,4},{7,5},{8,10},{9,11},{10,... | collective-permute-start | bytes 516104 | tf_op jit(solution)/shard_map/ppermute | solution.py:348
  46.4 0.4 collective-permute-start.12
  46.7 1.7 %collective-permute-start.13 = (f32[21,16,128]{2,1,0:T(8,128)S(1)}, f32[21,16,128]{2,1,0:T(8,128)S(1)}, u32[]{:S(2)}, u32[]{:S(2)}) collective-permute-start(f32[21,16,128]{2,1,0:T(8,128)S(1)} %get-tuple-element.52), channel_id=1, source_target_pairs={{0,4},{1,5},{2,6},{3,7},{4,0},{5,1},{6,2},{7,3},{8,12},{9,13},{10,... | collective-permute-start | bytes 516104 | tf_op jit(solution)/shard_map/ppermute | solution.py:348
  48.5 0.5 collective-permute-start.17
  49.0 1.9 %collective-permute-done.14.refs_0_ = f32[21,16,128]{2,1,0:T(8,128)S(1)} collective-permute-done((f32[21,16,128]{2,1,0:T(8,128)S(1)}, f32[21,16,128]{2,1,0:T(8,128)S(1)}, u32[]{:S(2)}, u32[]{:S(2)}) %collective-permute-start.14) | collective-permute-done | bytes 172064 | tf_op jit(solution)/shard_map/ppermute | solution.py:348
  50.9 0.9 %unpack_first.1.refs_4_ = f32[21,128,128]{2,1,0:T(8,128)} custom-call(s32[1]{0:T(128)} %bitcast.j_ref, f32[21,16,128]{2,1,0:T(8,128)S(1)} %collective-permute-done.14.refs_0_, f32[21,16,128]{2,1,0:T(8,128)S(1)} %collective-permute-done.16.refs_1_, f32[21,16,128]{2,1,0:T(8,128)S(1)} %get-tuple-element.50.refs_2_, ...), custom_call_target="tpu_custom_call" | custom-call | tf_op jit(solution)/shard_map/unpack_first/pallas_call | solution.py:160
  51.7 2.5 %collective-permute-done.13.refs_2_ = f32[21,16,128]{2,1,0:T(8,128)S(1)} collective-permute-done((f32[21,16,128]{2,1,0:T(8,128)S(1)}, f32[21,16,128]{2,1,0:T(8,128)S(1)}, u32[]{:S(2)}, u32[]{:S(2)}) %collective-permute-start.13) | collective-permute-done | bytes 172064 | tf_op jit(solution)/shard_map/ppermute | solution.py:348
  54.3 0.2 collective-permute-done.11.refs_0_
  54.5 3.5 %collective-permute-done.12.refs_1_ = f32[21,16,128]{2,1,0:T(8,128)S(1)} collective-permute-done((f32[21,16,128]{2,1,0:T(8,128)S(1)}, f32[21,16,128]{2,1,0:T(8,128)S(1)}, u32[]{:S(2)}, u32[]{:S(2)}) %collective-permute-start.12) | collective-permute-done | bytes 172064 | tf_op jit(solution)/shard_map/ppermute | solution.py:348
  58.1 0.9 %unpack_last.1 = f32[21,128,128]{2,1,0:T(8,128)} custom-call(s32[1]{0:T(128)} %bitcast.j_ref, f32[21,16,128]{2,1,0:T(8,128)S(1)} %collective-permute-done.11.refs_0_, f32[21,16,128]{2,1,0:T(8,128)S(1)} %collective-permute-done.12.refs_1_, f32[21,16,128]{2,1,0:T(8,128)S(1)} %collective-permute-done.13.refs_2_, ...), custom_call_target="tpu_custom_call", output_to_operand_aliasing={{}: (5, {})} | custom-call | tf_op jit(solution)/shard_map/unpack_last/pallas_call | solution.py:160
  (38 shorter events, 0.3 us)
Async XLA Ops:
  1.6 7.0 %copy-start.1 = (s32[84]{0:T(128)S(1)}, s32[84]{0:T(128)}, u32[]{:S(2)}) copy-start(s32[84]{0:T(128)} %param.11) | copy-start | bytes 1012
  1.6 7.2 %copy-start = (s32[7,84,84]{2,1,0:T(8,128)S(1)}, s32[7,84,84]{2,1,0:T(8,128)}, u32[]{:S(2)}) copy-start(s32[7,84,84]{2,1,0:T(8,128)} %param.9) | copy-start | bytes 592708
  1.6 11.0 %collective-permute-start.2 = (f32[416,128]{1,0:T(8,128)S(1)}, f32[416,128]{1,0:T(8,128)S(1)}, u32[]{:S(2)}, u32[]{:S(2)}) collective-permute-start(f32[416,128]{1,0:T(8,128)S(1)} %bitcast.50), channel_id=1, source_target_pairs={{0,2},{1,3},{2,0},{3,1},{4,6},{5,7},{6,4},{7,5},{8,10},{9,11},{10,... | collective-permute-start | bytes 638984 | tf_op jit(solution)/shard_map/ppermute | solution.py:348
  4.6 8.0 %collective-permute-start.6 = (f32[416,128]{1,0:T(8,128)S(1)}, f32[416,128]{1,0:T(8,128)S(1)}, u32[]{:S(2)}, u32[]{:S(2)}) collective-permute-start(f32[416,128]{1,0:T(8,128)S(1)} %bitcast.49), channel_id=1, source_target_pairs={{0,1},{1,0},{2,3},{3,2},{4,5},{5,4},{6,7},{7,6},{8,9},{9,8},{10,11... | collective-permute-start | bytes 638984 | tf_op jit(solution)/shard_map/ppermute | solution.py:348
  4.6 9.1 %collective-permute-start.3 = (f32[416,128]{1,0:T(8,128)S(1)}, f32[416,128]{1,0:T(8,128)S(1)}, u32[]{:S(2)}, u32[]{:S(2)}) collective-permute-start(f32[416,128]{1,0:T(8,128)S(1)} %bitcast.48), channel_id=1, source_target_pairs={{0,3},{1,2},{2,1},{3,0},{4,7},{5,6},{6,5},{7,4},{8,11},{9,10},{10,... | collective-permute-start | bytes 638984 | tf_op jit(solution)/shard_map/ppermute | solution.py:348
  6.4 15.6 %collective-permute-start.1 = (f32[416,128]{1,0:T(8,128)S(1)}, f32[416,128]{1,0:T(8,128)S(1)}, u32[]{:S(2)}, u32[]{:S(2)}) collective-permute-start(f32[416,128]{1,0:T(8,128)S(1)} %bitcast.46), channel_id=1, source_target_pairs={{0,5},{1,4},{2,7},{3,6},{4,1},{5,0},{6,3},{7,2},{8,13},{9,12},{10,... | collective-permute-start | bytes 638984 | tf_op jit(solution)/shard_map/ppermute | solution.py:348
  8.0 13.1 %collective-permute-start = (f32[416,128]{1,0:T(8,128)S(1)}, f32[416,128]{1,0:T(8,128)S(1)}, u32[]{:S(2)}, u32[]{:S(2)}) collective-permute-start(f32[416,128]{1,0:T(8,128)S(1)} %bitcast.47), channel_id=1, source_target_pairs={{0,4},{1,5},{2,6},{3,7},{4,0},{5,1},{6,2},{7,3},{8,12},{9,13},{10,... | collective-permute-start | bytes 638984 | tf_op jit(solution)/shard_map/ppermute | solution.py:348
  14.6 21.8 %collective-permute-start.7 = (f32[4,368,128]{2,1,0:T(8,128)}, f32[4,368,128]{2,1,0:T(8,128)S(1)}, u32[]{:S(2)}, u32[]{:S(2)}) collective-permute-start(f32[4,368,128]{2,1,0:T(8,128)} %pad_maximum_fusion), channel_id=1, source_target_pairs={{4,12},{5,13},{6,14},{7,15},{8,0},{9,1},{10,2},{11,3},{12,20},{13,... | collective-permute-start | bytes 2261000 | tf_op jit(solution)/shard_map/ppermute | solution.py:358
  15.9 11.0 %collective-permute-start.5 = (f32[416,128]{1,0:T(8,128)S(1)}, f32[416,128]{1,0:T(8,128)S(1)}, u32[]{:S(2)}, u32[]{:S(2)}) collective-permute-start(f32[416,128]{1,0:T(8,128)S(1)} %bitcast.45), channel_id=1, source_target_pairs={{0,7},{1,6},{2,5},{3,4},{4,3},{5,2},{6,1},{7,0},{8,15},{9,14},{10,... | collective-permute-start | bytes 638984 | tf_op jit(solution)/shard_map/ppermute | solution.py:348
  21.1 9.8 %collective-permute-start.4 = (f32[416,128]{1,0:T(8,128)S(1)}, f32[416,128]{1,0:T(8,128)S(1)}, u32[]{:S(2)}, u32[]{:S(2)}) collective-permute-start(f32[416,128]{1,0:T(8,128)S(1)} %bitcast.44), channel_id=1, source_target_pairs={{0,6},{1,7},{2,4},{3,5},{4,2},{5,3},{6,0},{7,1},{8,14},{9,15},{10,... | collective-permute-start | bytes 638984 | tf_op jit(solution)/shard_map/ppermute | solution.py:348
  22.0 20.1 %collective-permute-start.8 = (f32[2,368,128]{2,1,0:T(8,128)S(1)}, f32[2,368,128]{2,1,0:T(8,128)S(1)}, u32[]{:S(2)}, u32[]{:S(2)}) collective-permute-start(f32[2,368,128]{2,1,0:T(8,128)S(1)} %pad_maximum_fusion.1), channel_id=1, source_target_pairs={{0,8},{1,9},{2,10},{3,11},{8,16},{9,17},{10,18},{11,19},{12,4},{13... | collective-permute-start | bytes 1130504 | tf_op jit(solution)/shard_map/ppermute | solution.py:358
  26.9 15.2 %collective-permute-start.10 = (f32[1,368,128]{2,1,0:T(8,128)S(1)}, f32[1,368,128]{2,1,0:T(8,128)S(1)}, u32[]{:S(2)}, u32[]{:S(2)}) collective-permute-start(f32[1,368,128]{2,1,0:T(8,128)S(1)} %slice_bitcast_fusion), channel_id=1, source_target_pairs={{0,8},{1,9},{2,10},{3,11},{8,16},{9,17},{10,18},{11,19},{12,4},{13... | collective-permute-start | bytes 565256 | tf_op jit(solution)/shard_map/ppermute | solution.py:358
  30.9 11.2 %collective-permute-start.9 = (f32[1,368,128]{2,1,0:T(8,128)S(1)}, f32[1,368,128]{2,1,0:T(8,128)S(1)}, u32[]{:S(2)}, u32[]{:S(2)}) collective-permute-start(f32[1,368,128]{2,1,0:T(8,128)S(1)} %slice_bitcast_fusion.1), channel_id=1, source_target_pairs={{0,8},{1,9},{2,10},{3,11},{8,16},{9,17},{10,18},{11,19},{12,4},{13... | collective-permute-start | bytes 565256 | tf_op jit(solution)/shard_map/ppermute | solution.py:358
  39.4 9.0 %collective-permute-start.16 = (f32[21,16,128]{2,1,0:T(8,128)S(1)}, f32[21,16,128]{2,1,0:T(8,128)S(1)}, u32[]{:S(2)}, u32[]{:S(2)}) collective-permute-start(f32[21,16,128]{2,1,0:T(8,128)S(1)} %get-tuple-element.46), channel_id=1, source_target_pairs={{0,7},{1,6},{2,5},{3,4},{4,3},{5,2},{6,1},{7,0},{8,15},{9,14},{10,... | collective-permute-start | bytes 516104 | tf_op jit(solution)/shard_map/ppermute | solution.py:348
  40.7 10.1 %collective-permute-start.14 = (f32[21,16,128]{2,1,0:T(8,128)S(1)}, f32[21,16,128]{2,1,0:T(8,128)S(1)}, u32[]{:S(2)}, u32[]{:S(2)}) collective-permute-start(f32[21,16,128]{2,1,0:T(8,128)S(1)} %get-tuple-element.45), channel_id=1, source_target_pairs={{0,6},{1,7},{2,4},{3,5},{4,2},{5,3},{6,0},{7,1},{8,14},{9,15},{10,... | collective-permute-start | bytes 516104 | tf_op jit(solution)/shard_map/ppermute | solution.py:348
  45.1 9.4 %collective-permute-start.11 = (f32[21,16,128]{2,1,0:T(8,128)S(1)}, f32[21,16,128]{2,1,0:T(8,128)S(1)}, u32[]{:S(2)}, u32[]{:S(2)}) collective-permute-start(f32[21,16,128]{2,1,0:T(8,128)S(1)} %get-tuple-element.48), channel_id=1, source_target_pairs={{0,2},{1,3},{2,0},{3,1},{4,6},{5,7},{6,4},{7,5},{8,10},{9,11},{10,... | collective-permute-start | bytes 516104 | tf_op jit(solution)/shard_map/ppermute | solution.py:348
  46.4 11.7 %collective-permute-start.12 = (f32[21,16,128]{2,1,0:T(8,128)S(1)}, f32[21,16,128]{2,1,0:T(8,128)S(1)}, u32[]{:S(2)}, u32[]{:S(2)}) collective-permute-start(f32[21,16,128]{2,1,0:T(8,128)S(1)} %get-tuple-element.49), channel_id=1, source_target_pairs={{0,3},{1,2},{2,1},{3,0},{4,7},{5,6},{6,5},{7,4},{8,11},{9,10},{10,... | collective-permute-start | bytes 516104 | tf_op jit(solution)/shard_map/ppermute | solution.py:348
  46.7 7.6 %collective-permute-start.13 = (f32[21,16,128]{2,1,0:T(8,128)S(1)}, f32[21,16,128]{2,1,0:T(8,128)S(1)}, u32[]{:S(2)}, u32[]{:S(2)}) collective-permute-start(f32[21,16,128]{2,1,0:T(8,128)S(1)} %get-tuple-element.52), channel_id=1, source_target_pairs={{0,4},{1,5},{2,6},{3,7},{4,0},{5,1},{6,2},{7,3},{8,12},{9,13},{10,... | collective-permute-start | bytes 516104 | tf_op jit(solution)/shard_map/ppermute | solution.py:348
  48.5 2.4 %collective-permute-start.17 = (f32[21,16,128]{2,1,0:T(8,128)S(1)}, f32[21,16,128]{2,1,0:T(8,128)S(1)}, u32[]{:S(2)}, u32[]{:S(2)}) collective-permute-start(f32[21,16,128]{2,1,0:T(8,128)S(1)} %get-tuple-element.54), channel_id=1, source_target_pairs={{0,1},{1,0},{2,3},{3,2},{4,5},{5,4},{6,7},{7,6},{8,9},{9,8},{10,11... | collective-permute-start | bytes 516104 | tf_op jit(solution)/shard_map/ppermute | solution.py:348
  50.9 7.2 %collective-permute-start.15 = (f32[21,16,128]{2,1,0:T(8,128)S(1)}, f32[21,16,128]{2,1,0:T(8,128)S(1)}, u32[]{:S(2)}, u32[]{:S(2)}) collective-permute-start(f32[21,16,128]{2,1,0:T(8,128)S(1)} %get-tuple-element.53), channel_id=1, source_target_pairs={{0,5},{1,4},{2,7},{3,6},{4,1},{5,0},{6,3},{7,2},{8,13},{9,12},{10,... | collective-permute-start | bytes 516104 | tf_op jit(solution)/shard_map/ppermute | solution.py:348

commit v16 on v15

--- a/solution.py
+++ b/solution.py
@@ -169,6 +169,21 @@
     )(j, *pieces.values(), *there)
 
 
+def mains(pieces, lay):
+    def kernel(*refs):
+        for n in range(len(pieces)):
+            refs[-1][n] = refs[n][: lay.main, :]
+
+    return pl.pallas_call(
+        kernel,
+        out_shape=pltpu.VMEM((len(pieces), lay.main, lay.width), jnp.float32),
+        in_specs=vmem(len(pieces)),
+        out_specs=vmem(1)[0],
+        compiler_params=pltpu.CompilerParams(vmem_limit_bytes=VMEM_LIMIT),
+        name="mains",
+    )(*pieces)
+
+
 def coupling_lists(pattern, coupling, slot_mode):
     masked = (coupling * pattern.astype(jnp.float32))[1:]
     terms, modes = masked.shape[0], masked.shape[1]
@@ -354,8 +369,7 @@
             other = d + lay.group if upper else d - lay.group
             if 0 <= other < devices:
                 pairs.append((d, other))
-        main = jnp.stack([piece[: lay.main] for piece in pieces])
-        return lax.ppermute(main, axes, pairs)
+        return lax.ppermute(mains(pieces, lay), axes, pairs)
 
     field, kl = chaos_field[:, 0], kl_fields[:, 0]
     sent = [None] * lay.group

time: 59.2 us -> 58.8 us (level)
  local copies, waits for them, and re-layouts: 2.69 us -> 1.62 us
  other arithmetic: 2.62 us -> 1.65 us
  Pallas kernels: 10.9 us -> 11.8 us
  starting transfers between devices: 28.6 us -> 29.2 us
    another operation x2 -> x0, other arithmetic: 0.97 us -> none  [shift(): main = jnp.stack([piece[:lay.main] for piece in pieces])]
    unnamed x6 -> x8, local copies, waits for them, and re-layouts: 1.37 us -> 0.41 us
    pallas_call x2, Pallas kernels: 3.1 us -> 3.88 us  [pack(): pl.pallas_call(kernel, out_shape=[pltpu.VMEM(shape, jnp.float32)] * modes...]
    ppermute x14, starting transfers between devices: 17 us -> 17.6 us  [swap(): return lax.ppermute(piece, axes, [(d, d ^ r) for d in range(devices)])]
  transfers between devices with their start and end apart: 18 -> 18, of which waited for: 8 -> 8; matrix products, arithmetic and copies ran while one was open for 10% -> 7% of each run, Pallas kernels for 14% -> 16%
where the time goes in v16:
time: 58.8 us; the launch traced here: 58.6 us
  starting transfers between devices  29.2 us (50%)
  waiting for transfers between devices  13.3 us (23%)
  Pallas kernels  11.8 us (20%)
  other arithmetic  1.65 us (3%)
  local copies, waits for them, and re-layouts  1.62 us (3%)
  matrix products  0.69 us (1%)
    ppermute x14, starting transfers between devices, swap(): return lax.ppermute(piece, axes, [(d, d ^ r) for d in range(devices)])  17.6 us
    ppermute x4, starting transfers between devices, shift(): return lax.ppermute(mains(pieces, lay), axes, pairs)  11.6 us
    ppermute x14, waiting for transfers between devices, swap(): return lax.ppermute(piece, axes, [(d, d ^ r) for d in range(devices)])  11.3 us
    pallas_call x2, Pallas kernels, stencil(): pl.pallas_call(kernel, out_shape=[jax.ShapeDtypeStruct((lay.quota, rows,...  6.04 us
    pallas_call x2, Pallas kernels, pack(): pl.pallas_call(kernel, out_shape=[pltpu.VMEM(shape, jnp.float32)] * modes...  3.88 us
    ppermute x4, waiting for transfers between devices, shift(): return lax.ppermute(mains(pieces, lay), axes, pairs)  1.99 us
    pallas_call x2, Pallas kernels, unpack(): pl.pallas_call(kernel, out_shape=pltpu.HBM(shape, jnp.float32), in_specs=...  1.74 us
  transfers between devices with their start and end apart: 18, of which 8 were waited for; matrix products, arithmetic and copies ran while one was open for 7% of the time, Pallas kernels for 16%

profile of v16, /device:TPU:0, one launch (start us, length us, event | category | flops | bytes accessed | tf_op | source)
XLA Modules:
  0.0 58.6 jit_solution(14639424913828478701)
XLA Ops:
  0.0 1.5 %pack_own.1 = (f32[26,16,128]{2,1,0:T(8,128)S(1)}, f32[26,16,128]{2,1,0:T(8,128)S(1)}, f32[26,16,128]{2,1,0:T(8,128)S(1)}, f32[26,16,128]{2,1,0:T(8,128)S(1)}) custom-call(s32[1]{0:T(128)} %bitcast.j_ref, f32[21,128,128]{2,1,0:T(8,128)} %bitcast.34, f32[1,128,128]{2,1,0:T(8,128)} %mean_ref.3, f32[6,128,128]{2,1,0:T(8,128)} %bitcast.36), custom_call_target="tpu_custom_call" | custom-call | tf_op jit(solution)/shard_map/pack_own/pallas_call | solution.py:127
  1.6 0.0 copy-start.2
  1.6 0.0 copy-start
  1.6 0.0 copy-start.1
  1.6 0.5 collective-permute-start.6
  2.1 2.6 %collective-permute-start.2 = (f32[416,128]{1,0:T(8,128)S(1)}, f32[416,128]{1,0:T(8,128)S(1)}, u32[]{:S(2)}, u32[]{:S(2)}) collective-permute-start(f32[416,128]{1,0:T(8,128)S(1)} %bitcast.33), channel_id=1, source_target_pairs={{0,2},{1,3},{2,0},{3,1},{4,6},{5,7},{6,4},{7,5},{8,10},{9,11},{10,... | collective-permute-start | bytes 638984 | tf_op jit(solution)/shard_map/ppermute | solution.py:363
  4.7 0.1 collective-permute-start.3
  4.8 2.3 %pack_crossing.1 = (f32[26,16,128]{2,1,0:T(8,128)}, f32[26,16,128]{2,1,0:T(8,128)}, f32[26,16,128]{2,1,0:T(8,128)S(1)}, f32[26,16,128]{2,1,0:T(8,128)}) custom-call(s32[1]{0:T(128)} %bitcast.j_ref, f32[21,128,128]{2,1,0:T(8,128)} %bitcast.35, f32[1,128,128]{2,1,0:T(8,128)} %mean_ref.3, f32[6,128,128]{2,1,0:T(8,128)} %bitcast.37), custom_call_target="tpu_custom_call" | custom-call | tf_op jit(solution)/shard_map/pack_crossing/pallas_call | solution.py:127
  7.1 1.7 %collective-permute-start.1 = (f32[416,128]{1,0:T(8,128)}, f32[416,128]{1,0:T(8,128)S(1)}, u32[]{:S(2)}, u32[]{:S(2)}) collective-permute-start(f32[416,128]{1,0:T(8,128)} %bitcast.13), channel_id=1, source_target_pairs={{0,5},{1,4},{2,7},{3,6},{4,1},{5,0},{6,3},{7,2},{8,13},{9,12},{10,... | collective-permute-start | bytes 638984 | tf_op jit(solution)/shard_map/ppermute | solution.py:363
  8.8 0.1 collective-permute-start
  9.0 0.1 iota_compare_fusion.10
  9.1 0.1 broadcast_in_dim.201
  9.2 0.1 select_reduce_fusion.13
  9.3 0.1 eq.98
  9.3 0.2 copy.12
  9.5 0.2 copy.13
  9.7 0.4 fusion
  10.1 0.3 fusion.10
  10.4 0.1 fusion.5
  10.6 0.2 select_reduce_fusion.4
  10.8 0.1 select_reduce_fusion.6
  11.0 0.1 broadcast_add_fusion.1
  11.1 0.1 select_reduce_fusion.1
  11.2 0.2 select_reduce_fusion.5
  11.4 0.1 reshape.162
  11.5 0.1 copy.14
  11.6 0.2 reshape.163
  11.8 0.1 copy.16
  11.9 0.2 reshape.170
  12.1 0.0 collective-permute-done.2.refs_2_.refs_6_
  12.1 2.7 %collective-permute-done.3.refs_3_.refs_7_ = f32[416,128]{1,0:T(8,128)S(1)} collective-permute-done((f32[416,128]{1,0:T(8,128)S(1)}, f32[416,128]{1,0:T(8,128)S(1)}, u32[]{:S(2)}, u32[]{:S(2)}) %collective-permute-start.3) | collective-permute-done | bytes 213024 | tf_op jit(solution)/shard_map/ppermute | solution.py:363
  14.9 1.3 %collective-permute-start.7 = (f32[4,368,128]{2,1,0:T(8,128)S(1)}, f32[4,368,128]{2,1,0:T(8,128)S(1)}, u32[]{:S(2)}, u32[]{:S(2)}) collective-permute-start(f32[4,368,128]{2,1,0:T(8,128)S(1)} %mains.4), channel_id=1, source_target_pairs={{4,12},{5,13},{6,14},{7,15},{8,0},{9,1},{10,2},{11,3},{12,20},{13,... | collective-permute-start | bytes 2261000 | tf_op jit(solution)/shard_map/ppermute | solution.py:372
  16.2 4.4 %collective-permute-start.5 = (f32[416,128]{1,0:T(8,128)}, f32[416,128]{1,0:T(8,128)S(1)}, u32[]{:S(2)}, u32[]{:S(2)}) collective-permute-start(f32[416,128]{1,0:T(8,128)} %bitcast.15), channel_id=1, source_target_pairs={{0,7},{1,6},{2,5},{3,4},{4,3},{5,2},{6,1},{7,0},{8,15},{9,14},{10,... | collective-permute-start | bytes 638984 | tf_op jit(solution)/shard_map/ppermute | solution.py:363
  20.6 0.5 collective-permute-start.4
  21.1 0.1 select_reduce_fusion.11
  21.2 0.1 select_reduce_fusion.7
  21.3 0.1 copy.17
  21.4 0.1 reshape.171
  21.5 0.2 select_reduce_fusion.8
  21.7 0.1 copy.15
  21.8 0.1 reshape.169
  22.0 3.5 %collective-permute-start.8 = (f32[2,368,128]{2,1,0:T(8,128)S(1)}, f32[2,368,128]{2,1,0:T(8,128)S(1)}, u32[]{:S(2)}, u32[]{:S(2)}) collective-permute-start(f32[2,368,128]{2,1,0:T(8,128)S(1)} %mains.5), channel_id=1, source_target_pairs={{0,8},{1,9},{2,10},{3,11},{8,16},{9,17},{10,18},{11,19},{12,4},{13... | collective-permute-start | bytes 1130504 | tf_op jit(solution)/shard_map/ppermute | solution.py:372
  25.4 0.1 pad_add_fusion.2.index_ref
  25.5 1.1 %collective-permute-done.5.refs_3_.refs_0_.refs_7_ = f32[416,128]{1,0:T(8,128)S(1)} collective-permute-done((f32[416,128]{1,0:T(8,128)}, f32[416,128]{1,0:T(8,128)S(1)}, u32[]{:S(2)}, u32[]{:S(2)}) %collective-permute-start.5) | collective-permute-done | bytes 213024 | tf_op jit(solution)/shard_map/ppermute | solution.py:363
  26.6 3.4 %collective-permute-start.10 = (f32[1,368,128]{2,1,0:T(8,128)S(1)}, f32[1,368,128]{2,1,0:T(8,128)S(1)}, u32[]{:S(2)}, u32[]{:S(2)}) collective-permute-start(f32[1,368,128]{2,1,0:T(8,128)S(1)} %mains.7), channel_id=1, source_target_pairs={{0,8},{1,9},{2,10},{3,11},{8,16},{9,17},{10,18},{11,19},{12,4},{13... | collective-permute-start | bytes 565256 | tf_op jit(solution)/shard_map/ppermute | solution.py:372
  30.0 1.2 %collective-permute-done.4.refs_2_.refs_0_.refs_6_ = f32[416,128]{1,0:T(8,128)S(1)} collective-permute-done((f32[416,128]{1,0:T(8,128)S(1)}, f32[416,128]{1,0:T(8,128)S(1)}, u32[]{:S(2)}, u32[]{:S(2)}) %collective-permute-start.4) | collective-permute-done | bytes 213024 | tf_op jit(solution)/shard_map/ppermute | solution.py:363
  31.2 3.4 %collective-permute-start.9 = (f32[1,368,128]{2,1,0:T(8,128)S(1)}, f32[1,368,128]{2,1,0:T(8,128)S(1)}, u32[]{:S(2)}, u32[]{:S(2)}) collective-permute-start(f32[1,368,128]{2,1,0:T(8,128)S(1)} %mains.6), channel_id=1, source_target_pairs={{0,8},{1,9},{2,10},{3,11},{8,16},{9,17},{10,18},{11,19},{12,4},{13... | collective-permute-start | bytes 565256 | tf_op jit(solution)/shard_map/ppermute | solution.py:372
  34.7 0.1 pad_maximum_fusion.1.factor_ref
  34.7 1.0 %collective-permute-done.7.refs_8_ = f32[4,368,128]{2,1,0:T(8,128)S(1)} collective-permute-done((f32[4,368,128]{2,1,0:T(8,128)S(1)}, f32[4,368,128]{2,1,0:T(8,128)S(1)}, u32[]{:S(2)}, u32[]{:S(2)}) %collective-permute-start.7) | collective-permute-done | bytes 753696 | tf_op jit(solution)/shard_map/ppermute | solution.py:372
  35.7 3.0 %stencil_crossing.1 = (f32[21,16,128]{2,1,0:T(8,128)S(1)}, f32[21,16,128]{2,1,0:T(8,128)S(1)}, f32[21,16,128]{2,1,0:T(8,128)S(1)}, f32[21,16,128]{2,1,0:T(8,128)S(1)}) custom-call(s32[1]{0:T(128)} %bitcast.j_ref, s32[770]{0:T(1024)S(1)} %pad_add_fusion.2.index_ref, f32[392]{0:T(512)S(1)} %pad_maximum_fusion.1.factor_ref, ...), custom_call_target="tpu_custom_call" | custom-call | tf_op jit(solution)/shard_map/stencil_crossing/pallas_call | solution.py:330
  38.7 0.8 %collective-permute-start.16 = (f32[21,16,128]{2,1,0:T(8,128)S(1)}, f32[21,16,128]{2,1,0:T(8,128)S(1)}, u32[]{:S(2)}, u32[]{:S(2)}) collective-permute-start(f32[21,16,128]{2,1,0:T(8,128)S(1)} %get-tuple-element.46), channel_id=1, source_target_pairs={{0,7},{1,6},{2,5},{3,4},{4,3},{5,2},{6,1},{7,0},{8,15},{9,14},{10,... | collective-permute-start | bytes 516104 | tf_op jit(solution)/shard_map/ppermute | solution.py:363
  39.6 1.1 %collective-permute-start.14 = (f32[21,16,128]{2,1,0:T(8,128)S(1)}, f32[21,16,128]{2,1,0:T(8,128)S(1)}, u32[]{:S(2)}, u32[]{:S(2)}) collective-permute-start(f32[21,16,128]{2,1,0:T(8,128)S(1)} %get-tuple-element.45), channel_id=1, source_target_pairs={{0,6},{1,7},{2,4},{3,5},{4,2},{5,3},{6,0},{7,1},{8,14},{9,15},{10,... | collective-permute-start | bytes 516104 | tf_op jit(solution)/shard_map/ppermute | solution.py:363
  40.7 1.0 %collective-permute-done.9.refs_9_ = f32[1,368,128]{2,1,0:T(8,128)S(1)} collective-permute-done((f32[1,368,128]{2,1,0:T(8,128)S(1)}, f32[1,368,128]{2,1,0:T(8,128)S(1)}, u32[]{:S(2)}, u32[]{:S(2)}) %collective-permute-start.9) | collective-permute-done | bytes 188448 | tf_op jit(solution)/shard_map/ppermute | solution.py:372
  41.7 3.0 %stencil_own.1 = (f32[21,16,128]{2,1,0:T(8,128)S(1)}, f32[21,16,128]{2,1,0:T(8,128)S(1)}, f32[21,16,128]{2,1,0:T(8,128)S(1)}, f32[21,16,128]{2,1,0:T(8,128)S(1)}) custom-call(s32[1]{0:T(128)} %bitcast.j_ref, s32[770]{0:T(1024)S(1)} %pad_add_fusion.2.index_ref, f32[392]{0:T(512)S(1)} %pad_maximum_fusion.1.factor_ref, f32[416,128]{1,0:T(8,128)S(1)} %bitcast.29, ...), custom_call_target="tpu_custom_call" | custom-call | tf_op jit(solution)/shard_map/stencil_own/pallas_call | solution.py:330
  44.7 0.9 %collective-permute-start.11 = (f32[21,16,128]{2,1,0:T(8,128)S(1)}, f32[21,16,128]{2,1,0:T(8,128)S(1)}, u32[]{:S(2)}, u32[]{:S(2)}) collective-permute-start(f32[21,16,128]{2,1,0:T(8,128)S(1)} %get-tuple-element.48), channel_id=1, source_target_pairs={{0,2},{1,3},{2,0},{3,1},{4,6},{5,7},{6,4},{7,5},{8,10},{9,11},{10,... | collective-permute-start | bytes 516104 | tf_op jit(solution)/shard_map/ppermute | solution.py:363
  45.6 0.5 collective-permute-start.12
  46.0 2.9 %collective-permute-start.13 = (f32[21,16,128]{2,1,0:T(8,128)S(1)}, f32[21,16,128]{2,1,0:T(8,128)S(1)}, u32[]{:S(2)}, u32[]{:S(2)}) collective-permute-start(f32[21,16,128]{2,1,0:T(8,128)S(1)} %get-tuple-element.52), channel_id=1, source_target_pairs={{0,4},{1,5},{2,6},{3,7},{4,0},{5,1},{6,2},{7,3},{8,12},{9,13},{10,... | collective-permute-start | bytes 516104 | tf_op jit(solution)/shard_map/ppermute | solution.py:363
  48.9 0.3 collective-permute-start.17
  49.3 1.2 %collective-permute-start.15 = (f32[21,16,128]{2,1,0:T(8,128)S(1)}, f32[21,16,128]{2,1,0:T(8,128)S(1)}, u32[]{:S(2)}, u32[]{:S(2)}) collective-permute-start(f32[21,16,128]{2,1,0:T(8,128)S(1)} %get-tuple-element.53), channel_id=1, source_target_pairs={{0,5},{1,4},{2,7},{3,6},{4,1},{5,0},{6,3},{7,2},{8,13},{9,12},{10,... | collective-permute-start | bytes 516104 | tf_op jit(solution)/shard_map/ppermute | solution.py:363
  50.5 0.9 %unpack_first.1.refs_4_ = f32[21,128,128]{2,1,0:T(8,128)} custom-call(s32[1]{0:T(128)} %bitcast.j_ref, f32[21,16,128]{2,1,0:T(8,128)S(1)} %collective-permute-done.14.refs_0_, f32[21,16,128]{2,1,0:T(8,128)S(1)} %collective-permute-done.16.refs_1_, f32[21,16,128]{2,1,0:T(8,128)S(1)} %get-tuple-element.50.refs_2_, ...), custom_call_target="tpu_custom_call" | custom-call | tf_op jit(solution)/shard_map/unpack_first/pallas_call | solution.py:160
  51.4 2.8 %collective-permute-done.13.refs_2_ = f32[21,16,128]{2,1,0:T(8,128)S(1)} collective-permute-done((f32[21,16,128]{2,1,0:T(8,128)S(1)}, f32[21,16,128]{2,1,0:T(8,128)S(1)}, u32[]{:S(2)}, u32[]{:S(2)}) %collective-permute-start.13) | collective-permute-done | bytes 172064 | tf_op jit(solution)/shard_map/ppermute | solution.py:363
  54.2 2.7 %collective-permute-done.12.refs_1_ = f32[21,16,128]{2,1,0:T(8,128)S(1)} collective-permute-done((f32[21,16,128]{2,1,0:T(8,128)S(1)}, f32[21,16,128]{2,1,0:T(8,128)S(1)}, u32[]{:S(2)}, u32[]{:S(2)}) %collective-permute-start.12) | collective-permute-done | bytes 172064 | tf_op jit(solution)/shard_map/ppermute | solution.py:363
  56.8 0.9 %collective-permute-done.15.refs_3_ = f32[21,16,128]{2,1,0:T(8,128)S(1)} collective-permute-done((f32[21,16,128]{2,1,0:T(8,128)S(1)}, f32[21,16,128]{2,1,0:T(8,128)S(1)}, u32[]{:S(2)}, u32[]{:S(2)}) %collective-permute-start.15) | collective-permute-done | bytes 172064 | tf_op jit(solution)/shard_map/ppermute | solution.py:363
  57.7 0.9 %unpack_last.1 = f32[21,128,128]{2,1,0:T(8,128)} custom-call(s32[1]{0:T(128)} %bitcast.j_ref, f32[21,16,128]{2,1,0:T(8,128)S(1)} %collective-permute-done.11.refs_0_, f32[21,16,128]{2,1,0:T(8,128)S(1)} %collective-permute-done.12.refs_1_, f32[21,16,128]{2,1,0:T(8,128)S(1)} %collective-permute-done.13.refs_2_, ...), custom_call_target="tpu_custom_call", output_to_operand_aliasing={{}: (5, {})} | custom-call | tf_op jit(solution)/shard_map/unpack_last/pallas_call | solution.py:160
  (34 shorter events, 0.3 us)
Async XLA Ops:
  1.6 7.5 %copy-start.2 = (s32[84]{0:T(128)S(1)}, s32[84]{0:T(128)}, u32[]{:S(2)}) copy-start(s32[84]{0:T(128)} %param.11) | copy-start | bytes 1012
  1.6 7.8 %copy-start = (s32[7,84,84]{2,1,0:T(8,128)S(1)}, s32[7,84,84]{2,1,0:T(8,128)}, u32[]{:S(2)}) copy-start(s32[7,84,84]{2,1,0:T(8,128)} %param.9) | copy-start | bytes 592708
  1.6 8.0 %copy-start.1 = (f32[7,84,84]{2,1,0:T(8,128)S(1)}, f32[7,84,84]{2,1,0:T(8,128)}, u32[]{:S(2)}) copy-start(f32[7,84,84]{2,1,0:T(8,128)} %param.10) | copy-start | bytes 592708
  1.6 10.5 %collective-permute-start.6 = (f32[416,128]{1,0:T(8,128)S(1)}, f32[416,128]{1,0:T(8,128)S(1)}, u32[]{:S(2)}, u32[]{:S(2)}) collective-permute-start(f32[416,128]{1,0:T(8,128)S(1)} %bitcast.32), channel_id=1, source_target_pairs={{0,1},{1,0},{2,3},{3,2},{4,5},{5,4},{6,7},{7,6},{8,9},{9,8},{10,11... | collective-permute-start | bytes 638984 | tf_op jit(solution)/shard_map/ppermute | solution.py:363
  2.1 10.0 %collective-permute-start.2 = (f32[416,128]{1,0:T(8,128)S(1)}, f32[416,128]{1,0:T(8,128)S(1)}, u32[]{:S(2)}, u32[]{:S(2)}) collective-permute-start(f32[416,128]{1,0:T(8,128)S(1)} %bitcast.33), channel_id=1, source_target_pairs={{0,2},{1,3},{2,0},{3,1},{4,6},{5,7},{6,4},{7,5},{8,10},{9,11},{10,... | collective-permute-start | bytes 638984 | tf_op jit(solution)/shard_map/ppermute | solution.py:363
  4.7 10.1 %collective-permute-start.3 = (f32[416,128]{1,0:T(8,128)S(1)}, f32[416,128]{1,0:T(8,128)S(1)}, u32[]{:S(2)}, u32[]{:S(2)}) collective-permute-start(f32[416,128]{1,0:T(8,128)S(1)} %bitcast.31), channel_id=1, source_target_pairs={{0,3},{1,2},{2,1},{3,0},{4,7},{5,6},{6,5},{7,4},{8,11},{9,10},{10,... | collective-permute-start | bytes 638984 | tf_op jit(solution)/shard_map/ppermute | solution.py:363
  7.1 14.8 %collective-permute-start.1 = (f32[416,128]{1,0:T(8,128)}, f32[416,128]{1,0:T(8,128)S(1)}, u32[]{:S(2)}, u32[]{:S(2)}) collective-permute-start(f32[416,128]{1,0:T(8,128)} %bitcast.13), channel_id=1, source_target_pairs={{0,5},{1,4},{2,7},{3,6},{4,1},{5,0},{6,3},{7,2},{8,13},{9,12},{10,... | collective-permute-start | bytes 638984 | tf_op jit(solution)/shard_map/ppermute | solution.py:363
  8.8 12.2 %collective-permute-start = (f32[416,128]{1,0:T(8,128)}, f32[416,128]{1,0:T(8,128)S(1)}, u32[]{:S(2)}, u32[]{:S(2)}) collective-permute-start(f32[416,128]{1,0:T(8,128)} %bitcast.9), channel_id=1, source_target_pairs={{0,4},{1,5},{2,6},{3,7},{4,0},{5,1},{6,2},{7,3},{8,12},{9,13},{10,... | collective-permute-start | bytes 638984 | tf_op jit(solution)/shard_map/ppermute | solution.py:363
  14.9 20.8 %collective-permute-start.7 = (f32[4,368,128]{2,1,0:T(8,128)S(1)}, f32[4,368,128]{2,1,0:T(8,128)S(1)}, u32[]{:S(2)}, u32[]{:S(2)}) collective-permute-start(f32[4,368,128]{2,1,0:T(8,128)S(1)} %mains.4), channel_id=1, source_target_pairs={{4,12},{5,13},{6,14},{7,15},{8,0},{9,1},{10,2},{11,3},{12,20},{13,... | collective-permute-start | bytes 2261000 | tf_op jit(solution)/shard_map/ppermute | solution.py:372
  16.2 10.4 %collective-permute-start.5 = (f32[416,128]{1,0:T(8,128)}, f32[416,128]{1,0:T(8,128)S(1)}, u32[]{:S(2)}, u32[]{:S(2)}) collective-permute-start(f32[416,128]{1,0:T(8,128)} %bitcast.15), channel_id=1, source_target_pairs={{0,7},{1,6},{2,5},{3,4},{4,3},{5,2},{6,1},{7,0},{8,15},{9,14},{10,... | collective-permute-start | bytes 638984 | tf_op jit(solution)/shard_map/ppermute | solution.py:363
  20.6 10.6 %collective-permute-start.4 = (f32[416,128]{1,0:T(8,128)S(1)}, f32[416,128]{1,0:T(8,128)S(1)}, u32[]{:S(2)}, u32[]{:S(2)}) collective-permute-start(f32[416,128]{1,0:T(8,128)S(1)} %bitcast.30), channel_id=1, source_target_pairs={{0,6},{1,7},{2,4},{3,5},{4,2},{5,3},{6,0},{7,1},{8,14},{9,15},{10,... | collective-permute-start | bytes 638984 | tf_op jit(solution)/shard_map/ppermute | solution.py:363
  22.0 18.7 %collective-permute-start.8 = (f32[2,368,128]{2,1,0:T(8,128)S(1)}, f32[2,368,128]{2,1,0:T(8,128)S(1)}, u32[]{:S(2)}, u32[]{:S(2)}) collective-permute-start(f32[2,368,128]{2,1,0:T(8,128)S(1)} %mains.5), channel_id=1, source_target_pairs={{0,8},{1,9},{2,10},{3,11},{8,16},{9,17},{10,18},{11,19},{12,4},{13... | collective-permute-start | bytes 1130504 | tf_op jit(solution)/shard_map/ppermute | solution.py:372
  26.6 14.1 %collective-permute-start.10 = (f32[1,368,128]{2,1,0:T(8,128)S(1)}, f32[1,368,128]{2,1,0:T(8,128)S(1)}, u32[]{:S(2)}, u32[]{:S(2)}) collective-permute-start(f32[1,368,128]{2,1,0:T(8,128)S(1)} %mains.7), channel_id=1, source_target_pairs={{0,8},{1,9},{2,10},{3,11},{8,16},{9,17},{10,18},{11,19},{12,4},{13... | collective-permute-start | bytes 565256 | tf_op jit(solution)/shard_map/ppermute | solution.py:372
  31.2 10.5 %collective-permute-start.9 = (f32[1,368,128]{2,1,0:T(8,128)S(1)}, f32[1,368,128]{2,1,0:T(8,128)S(1)}, u32[]{:S(2)}, u32[]{:S(2)}) collective-permute-start(f32[1,368,128]{2,1,0:T(8,128)S(1)} %mains.6), channel_id=1, source_target_pairs={{0,8},{1,9},{2,10},{3,11},{8,16},{9,17},{10,18},{11,19},{12,4},{13... | collective-permute-start | bytes 565256 | tf_op jit(solution)/shard_map/ppermute | solution.py:372
  38.7 10.2 %collective-permute-start.16 = (f32[21,16,128]{2,1,0:T(8,128)S(1)}, f32[21,16,128]{2,1,0:T(8,128)S(1)}, u32[]{:S(2)}, u32[]{:S(2)}) collective-permute-start(f32[21,16,128]{2,1,0:T(8,128)S(1)} %get-tuple-element.46), channel_id=1, source_target_pairs={{0,7},{1,6},{2,5},{3,4},{4,3},{5,2},{6,1},{7,0},{8,15},{9,14},{10,... | collective-permute-start | bytes 516104 | tf_op jit(solution)/shard_map/ppermute | solution.py:363
  39.6 9.7 %collective-permute-start.14 = (f32[21,16,128]{2,1,0:T(8,128)S(1)}, f32[21,16,128]{2,1,0:T(8,128)S(1)}, u32[]{:S(2)}, u32[]{:S(2)}) collective-permute-start(f32[21,16,128]{2,1,0:T(8,128)S(1)} %get-tuple-element.45), channel_id=1, source_target_pairs={{0,6},{1,7},{2,4},{3,5},{4,2},{5,3},{6,0},{7,1},{8,14},{9,15},{10,... | collective-permute-start | bytes 516104 | tf_op jit(solution)/shard_map/ppermute | solution.py:363
  44.7 9.4 %collective-permute-start.11 = (f32[21,16,128]{2,1,0:T(8,128)S(1)}, f32[21,16,128]{2,1,0:T(8,128)S(1)}, u32[]{:S(2)}, u32[]{:S(2)}) collective-permute-start(f32[21,16,128]{2,1,0:T(8,128)S(1)} %get-tuple-element.48), channel_id=1, source_target_pairs={{0,2},{1,3},{2,0},{3,1},{4,6},{5,7},{6,4},{7,5},{8,10},{9,11},{10,... | collective-permute-start | bytes 516104 | tf_op jit(solution)/shard_map/ppermute | solution.py:363
  45.6 11.3 %collective-permute-start.12 = (f32[21,16,128]{2,1,0:T(8,128)S(1)}, f32[21,16,128]{2,1,0:T(8,128)S(1)}, u32[]{:S(2)}, u32[]{:S(2)}) collective-permute-start(f32[21,16,128]{2,1,0:T(8,128)S(1)} %get-tuple-element.49), channel_id=1, source_target_pairs={{0,3},{1,2},{2,1},{3,0},{4,7},{5,6},{6,5},{7,4},{8,11},{9,10},{10,... | collective-permute-start | bytes 516104 | tf_op jit(solution)/shard_map/ppermute | solution.py:363
  46.0 8.1 %collective-permute-start.13 = (f32[21,16,128]{2,1,0:T(8,128)S(1)}, f32[21,16,128]{2,1,0:T(8,128)S(1)}, u32[]{:S(2)}, u32[]{:S(2)}) collective-permute-start(f32[21,16,128]{2,1,0:T(8,128)S(1)} %get-tuple-element.52), channel_id=1, source_target_pairs={{0,4},{1,5},{2,6},{3,7},{4,0},{5,1},{6,2},{7,3},{8,12},{9,13},{10,... | collective-permute-start | bytes 516104 | tf_op jit(solution)/shard_map/ppermute | solution.py:363
  48.9 1.5 %collective-permute-start.17 = (f32[21,16,128]{2,1,0:T(8,128)S(1)}, f32[21,16,128]{2,1,0:T(8,128)S(1)}, u32[]{:S(2)}, u32[]{:S(2)}) collective-permute-start(f32[21,16,128]{2,1,0:T(8,128)S(1)} %get-tuple-element.54), channel_id=1, source_target_pairs={{0,1},{1,0},{2,3},{3,2},{4,5},{5,4},{6,7},{7,6},{8,9},{9,8},{10,11... | collective-permute-start | bytes 516104 | tf_op jit(solution)/shard_map/ppermute | solution.py:363
  49.3 8.4 %collective-permute-start.15 = (f32[21,16,128]{2,1,0:T(8,128)S(1)}, f32[21,16,128]{2,1,0:T(8,128)S(1)}, u32[]{:S(2)}, u32[]{:S(2)}) collective-permute-start(f32[21,16,128]{2,1,0:T(8,128)S(1)} %get-tuple-element.53), channel_id=1, source_target_pairs={{0,5},{1,4},{2,7},{3,6},{4,1},{5,0},{6,3},{7,2},{8,13},{9,12},{10,... | collective-permute-start | bytes 516104 | tf_op jit(solution)/shard_map/ppermute | solution.py:363

commit v17 on v16

--- a/solution.py
+++ b/solution.py
@@ -389,10 +389,10 @@
     lists = kernel_lists(*lists, after(count, pieces[modes]))
     own_halo = shift(pieces[:modes], False)
     own_halos = [(own_halo, n) for n in range(modes)]
-    early_halo = shift(pieces[modes : modes + half], True)
-    crossing_halos = [(early_halo, n) for n in range(half)]
-    for r in range(modes + half, lay.group):
-        crossing_halos.append((shift(pieces[r : r + 1], True), 0))
+    crossing_halos = []
+    for r in (modes, modes + half):
+        halo = shift(pieces[r : r + half], True)
+        crossing_halos += [(halo, n) for n in range(half)]
 
     own, crossing = pieces[:modes], pieces[modes:]
     crossing_out = stencil(crossing, own, own_halos, lists, j, "stencil_crossing", lay)
@@ -405,9 +405,10 @@
         back[r] = swap(out[r], r)
     for n in range(half):
         ahead = [back[r] for r in first[:n]]
-        back[modes + n] = swap(after(out[modes + n], *own_out, *ahead), modes + n)
+        ahead = [*own_out, *ahead] if n else []
+        back[modes + n] = swap(after(out[modes + n], *ahead), modes + n)
     for r in range(half):
-        back[r] = swap(after(out[r], back[first[-1]]) if r else out[r], r)
+        back[r] = swap(after(out[r], *[back[r] for r in first]) if r else out[r], r)
     last = range(half, modes + half)
     shape = (quota, height, width)
     whole = unpack({r: back[r] for r in back if r not in last}, j, shape, lay)

time: 58.8 us -> 57.5 us (0.978)
  starting transfers between devices: 29.2 us -> 24.4 us
  waiting for transfers between devices: 13.3 us -> 16.9 us
    ppermute x14, waiting for transfers between devices: 11.3 us -> 15.5 us  [swap(): return lax.ppermute(piece, axes, [(d, d ^ r) for d in range(devices)])]
    ppermute x4 -> x3, starting transfers between devices: 11.6 us -> 8.21 us  [shift(): return lax.ppermute(mains(pieces, lay), axes, pairs)]
    ppermute x14, starting transfers between devices: 17.6 us -> 16.2 us  [swap(): return lax.ppermute(piece, axes, [(d, d ^ r) for d in range(devices)])]
    ppermute x4 -> x3, waiting for transfers between devices: 1.99 us -> 1.35 us  [shift(): return lax.ppermute(mains(pieces, lay), axes, pairs)]
  transfers between devices with their start and end apart: 18 -> 17, of which waited for: 8 -> 9; matrix products, arithmetic and copies ran while one was open for 7% -> 7% of each run, Pallas kernels for 16% -> 16%
where the time goes in v17:
time: 57.5 us; the launch traced here: 57.3 us
  starting transfers between devices  24.4 us (42%)
  waiting for transfers between devices  16.9 us (29%)
  Pallas kernels  11.8 us (21%)
  other arithmetic  1.65 us (3%)
  local copies, waits for them, and re-layouts  1.62 us (3%)
  matrix products  0.69 us (1%)
    ppermute x14, starting transfers between devices, swap(): return lax.ppermute(piece, axes, [(d, d ^ r) for d in range(devices)])  16.2 us
    ppermute x14, waiting for transfers between devices, swap(): return lax.ppermute(piece, axes, [(d, d ^ r) for d in range(devices)])  15.5 us
    ppermute x3, starting transfers between devices, shift(): return lax.ppermute(mains(pieces, lay), axes, pairs)  8.21 us
    pallas_call x2, Pallas kernels, stencil(): pl.pallas_call(kernel, out_shape=[jax.ShapeDtypeStruct((lay.quota, rows,...  6.03 us
    pallas_call x2, Pallas kernels, pack(): pl.pallas_call(kernel, out_shape=[pltpu.VMEM(shape, jnp.float32)] * modes...  3.88 us
    pallas_call x2, Pallas kernels, unpack(): pl.pallas_call(kernel, out_shape=pltpu.HBM(shape, jnp.float32), in_specs=...  1.74 us
    ppermute x3, waiting for transfers between devices, shift(): return lax.ppermute(mains(pieces, lay), axes, pairs)  1.35 us
  transfers between devices with their start and end apart: 17, of which 9 were waited for; matrix products, arithmetic and copies ran while one was open for 7% of the time, Pallas kernels for 16%

profile of v17, /device:TPU:0, one launch (start us, length us, event | category | flops | bytes accessed | tf_op | source)
XLA Modules:
  0.0 57.3 jit_solution(17286265490080575917)
XLA Ops:
  0.0 1.5 %pack_own.1 = (f32[26,16,128]{2,1,0:T(8,128)S(1)}, f32[26,16,128]{2,1,0:T(8,128)S(1)}, f32[26,16,128]{2,1,0:T(8,128)S(1)}, f32[26,16,128]{2,1,0:T(8,128)S(1)}) custom-call(s32[1]{0:T(128)} %bitcast.j_ref, f32[21,128,128]{2,1,0:T(8,128)} %bitcast.34, f32[1,128,128]{2,1,0:T(8,128)} %mean_ref.3, f32[6,128,128]{2,1,0:T(8,128)} %bitcast.36), custom_call_target="tpu_custom_call" | custom-call | tf_op jit(solution)/shard_map/pack_own/pallas_call | solution.py:127
  1.6 0.0 copy-start.2
  1.6 0.0 copy-start
  1.6 0.0 copy-start.1
  1.6 0.5 collective-permute-start.6
  2.1 2.6 %collective-permute-start.2 = (f32[416,128]{1,0:T(8,128)S(1)}, f32[416,128]{1,0:T(8,128)S(1)}, u32[]{:S(2)}, u32[]{:S(2)}) collective-permute-start(f32[416,128]{1,0:T(8,128)S(1)} %bitcast.33), channel_id=1, source_target_pairs={{0,2},{1,3},{2,0},{3,1},{4,6},{5,7},{6,4},{7,5},{8,10},{9,11},{10,... | collective-permute-start | bytes 638984 | tf_op jit(solution)/shard_map/ppermute | solution.py:363
  4.7 0.1 collective-permute-start.3
  4.8 2.3 %pack_crossing.1 = (f32[26,16,128]{2,1,0:T(8,128)}, f32[26,16,128]{2,1,0:T(8,128)}, f32[26,16,128]{2,1,0:T(8,128)S(1)}, f32[26,16,128]{2,1,0:T(8,128)}) custom-call(s32[1]{0:T(128)} %bitcast.j_ref, f32[21,128,128]{2,1,0:T(8,128)} %bitcast.35, f32[1,128,128]{2,1,0:T(8,128)} %mean_ref.3, f32[6,128,128]{2,1,0:T(8,128)} %bitcast.37), custom_call_target="tpu_custom_call" | custom-call | tf_op jit(solution)/shard_map/pack_crossing/pallas_call | solution.py:127
  7.1 1.7 %collective-permute-start.1 = (f32[416,128]{1,0:T(8,128)}, f32[416,128]{1,0:T(8,128)S(1)}, u32[]{:S(2)}, u32[]{:S(2)}) collective-permute-start(f32[416,128]{1,0:T(8,128)} %bitcast.13), channel_id=1, source_target_pairs={{0,5},{1,4},{2,7},{3,6},{4,1},{5,0},{6,3},{7,2},{8,13},{9,12},{10,... | collective-permute-start | bytes 638984 | tf_op jit(solution)/shard_map/ppermute | solution.py:363
  8.8 0.1 collective-permute-start
  9.0 0.1 iota_compare_fusion.10
  9.1 0.1 broadcast_in_dim.201
  9.2 0.1 select_reduce_fusion.13
  9.3 0.1 eq.98
  9.3 0.2 copy.12
  9.5 0.2 copy.13
  9.7 0.4 fusion
  10.1 0.3 fusion.10
  10.4 0.1 fusion.5
  10.6 0.2 select_reduce_fusion.4
  10.8 0.1 select_reduce_fusion.6
  11.0 0.1 broadcast_add_fusion.1
  11.1 0.1 select_reduce_fusion.1
  11.2 0.2 select_reduce_fusion.5
  11.4 0.1 reshape.162
  11.5 0.1 copy.14
  11.6 0.2 reshape.163
  11.8 0.1 copy.16
  11.9 0.2 reshape.170
  12.1 0.0 collective-permute-done.2.refs_2_.refs_6_
  12.1 2.7 %collective-permute-done.3.refs_3_.refs_7_ = f32[416,128]{1,0:T(8,128)S(1)} collective-permute-done((f32[416,128]{1,0:T(8,128)S(1)}, f32[416,128]{1,0:T(8,128)S(1)}, u32[]{:S(2)}, u32[]{:S(2)}) %collective-permute-start.3) | collective-permute-done | bytes 213024 | tf_op jit(solution)/shard_map/ppermute | solution.py:363
  14.9 1.3 %collective-permute-start.7 = (f32[4,368,128]{2,1,0:T(8,128)S(1)}, f32[4,368,128]{2,1,0:T(8,128)S(1)}, u32[]{:S(2)}, u32[]{:S(2)}) collective-permute-start(f32[4,368,128]{2,1,0:T(8,128)S(1)} %mains.3), channel_id=1, source_target_pairs={{4,12},{5,13},{6,14},{7,15},{8,0},{9,1},{10,2},{11,3},{12,20},{13,... | collective-permute-start | bytes 2261000 | tf_op jit(solution)/shard_map/ppermute | solution.py:372
  16.2 4.4 %collective-permute-start.5 = (f32[416,128]{1,0:T(8,128)}, f32[416,128]{1,0:T(8,128)S(1)}, u32[]{:S(2)}, u32[]{:S(2)}) collective-permute-start(f32[416,128]{1,0:T(8,128)} %bitcast.15), channel_id=1, source_target_pairs={{0,7},{1,6},{2,5},{3,4},{4,3},{5,2},{6,1},{7,0},{8,15},{9,14},{10,... | collective-permute-start | bytes 638984 | tf_op jit(solution)/shard_map/ppermute | solution.py:363
  20.6 0.5 collective-permute-start.4
  21.1 0.1 select_reduce_fusion.11
  21.2 0.1 select_reduce_fusion.7
  21.3 0.1 copy.17
  21.4 0.1 reshape.171
  21.5 0.2 select_reduce_fusion.8
  21.7 0.1 copy.15
  21.8 0.1 reshape.169
  21.9 0.0 collective-permute-done.1.refs_1_.refs_5_
  21.9 3.5 %collective-permute-start.8 = (f32[2,368,128]{2,1,0:T(8,128)S(1)}, f32[2,368,128]{2,1,0:T(8,128)S(1)}, u32[]{:S(2)}, u32[]{:S(2)}) collective-permute-start(f32[2,368,128]{2,1,0:T(8,128)S(1)} %mains.4), channel_id=1, source_target_pairs={{0,8},{1,9},{2,10},{3,11},{8,16},{9,17},{10,18},{11,19},{12,4},{13... | collective-permute-start | bytes 1130504 | tf_op jit(solution)/shard_map/ppermute | solution.py:372
  25.4 1.1 %collective-permute-done.5.refs_3_.refs_1_.refs_7_ = f32[416,128]{1,0:T(8,128)S(1)} collective-permute-done((f32[416,128]{1,0:T(8,128)}, f32[416,128]{1,0:T(8,128)S(1)}, u32[]{:S(2)}, u32[]{:S(2)}) %collective-permute-start.5) | collective-permute-done | bytes 213024 | tf_op jit(solution)/shard_map/ppermute | solution.py:363
  26.6 4.6 %collective-permute-done.4.refs_2_.refs_0_.refs_6_ = f32[416,128]{1,0:T(8,128)S(1)} collective-permute-done((f32[416,128]{1,0:T(8,128)S(1)}, f32[416,128]{1,0:T(8,128)S(1)}, u32[]{:S(2)}, u32[]{:S(2)}) %collective-permute-start.4) | collective-permute-done | bytes 213024 | tf_op jit(solution)/shard_map/ppermute | solution.py:363
  31.2 3.5 %collective-permute-start.9 = (f32[2,368,128]{2,1,0:T(8,128)S(1)}, f32[2,368,128]{2,1,0:T(8,128)S(1)}, u32[]{:S(2)}, u32[]{:S(2)}) collective-permute-start(f32[2,368,128]{2,1,0:T(8,128)S(1)} %mains.5), channel_id=1, source_target_pairs={{0,8},{1,9},{2,10},{3,11},{8,16},{9,17},{10,18},{11,19},{12,4},{13... | collective-permute-start | bytes 1130504 | tf_op jit(solution)/shard_map/ppermute | solution.py:372
  34.7 0.1 pad_maximum_fusion.1.factor_ref
  34.8 0.1 pad_add_fusion.2.index_ref
  34.8 0.9 %collective-permute-done.7.refs_8_ = f32[4,368,128]{2,1,0:T(8,128)S(1)} collective-permute-done((f32[4,368,128]{2,1,0:T(8,128)S(1)}, f32[4,368,128]{2,1,0:T(8,128)S(1)}, u32[]{:S(2)}, u32[]{:S(2)}) %collective-permute-start.7) | collective-permute-done | bytes 753696 | tf_op jit(solution)/shard_map/ppermute | solution.py:372
  35.7 3.0 %stencil_crossing.1 = (f32[21,16,128]{2,1,0:T(8,128)S(1)}, f32[21,16,128]{2,1,0:T(8,128)S(1)}, f32[21,16,128]{2,1,0:T(8,128)S(1)}, f32[21,16,128]{2,1,0:T(8,128)S(1)}) custom-call(s32[1]{0:T(128)} %bitcast.j_ref, s32[770]{0:T(1024)S(1)} %pad_add_fusion.2.index_ref, f32[392]{0:T(512)S(1)} %pad_maximum_fusion.1.factor_ref, ...), custom_call_target="tpu_custom_call" | custom-call | tf_op jit(solution)/shard_map/stencil_crossing/pallas_call | solution.py:330
  38.7 1.8 %collective-permute-start.13 = (f32[21,16,128]{2,1,0:T(8,128)S(1)}, f32[21,16,128]{2,1,0:T(8,128)S(1)}, u32[]{:S(2)}, u32[]{:S(2)}) collective-permute-start(f32[21,16,128]{2,1,0:T(8,128)S(1)} %get-tuple-element.44), channel_id=1, source_target_pairs={{0,6},{1,7},{2,4},{3,5},{4,2},{5,3},{6,0},{7,1},{8,14},{9,15},{10,... | collective-permute-start | bytes 516104 | tf_op jit(solution)/shard_map/ppermute | solution.py:363
  40.5 1.4 %collective-permute-start.12 = (f32[21,16,128]{2,1,0:T(8,128)S(1)}, f32[21,16,128]{2,1,0:T(8,128)S(1)}, u32[]{:S(2)}, u32[]{:S(2)}) collective-permute-start(f32[21,16,128]{2,1,0:T(8,128)S(1)} %get-tuple-element.42), channel_id=1, source_target_pairs={{0,4},{1,5},{2,6},{3,7},{4,0},{5,1},{6,2},{7,3},{8,12},{9,13},{10,... | collective-permute-start | bytes 516104 | tf_op jit(solution)/shard_map/ppermute | solution.py:363
  41.9 0.5 collective-permute-done.9.refs_9_
  42.4 3.0 %stencil_own.1 = (f32[21,16,128]{2,1,0:T(8,128)S(1)}, f32[21,16,128]{2,1,0:T(8,128)S(1)}, f32[21,16,128]{2,1,0:T(8,128)S(1)}, f32[21,16,128]{2,1,0:T(8,128)S(1)}) custom-call(s32[1]{0:T(128)} %bitcast.j_ref, s32[770]{0:T(1024)S(1)} %pad_add_fusion.2.index_ref, f32[392]{0:T(512)S(1)} %pad_maximum_fusion.1.factor_ref, f32[416,128]{1,0:T(8,128)S(1)} %bitcast.29, ...), custom_call_target="tpu_custom_call" | custom-call | tf_op jit(solution)/shard_map/stencil_own/pallas_call | solution.py:330
  45.5 1.4 %collective-permute-start.10 = (f32[21,16,128]{2,1,0:T(8,128)S(1)}, f32[21,16,128]{2,1,0:T(8,128)S(1)}, u32[]{:S(2)}, u32[]{:S(2)}) collective-permute-start(f32[21,16,128]{2,1,0:T(8,128)S(1)} %get-tuple-element.47), channel_id=1, source_target_pairs={{0,2},{1,3},{2,0},{3,1},{4,6},{5,7},{6,4},{7,5},{8,10},{9,11},{10,... | collective-permute-start | bytes 516104 | tf_op jit(solution)/shard_map/ppermute | solution.py:363
  46.8 2.2 %collective-permute-done.15.refs_1_ = f32[21,16,128]{2,1,0:T(8,128)S(1)} collective-permute-done((f32[21,16,128]{2,1,0:T(8,128)S(1)}, f32[21,16,128]{2,1,0:T(8,128)S(1)}, u32[]{:S(2)}, u32[]{:S(2)}) %collective-permute-start.15) | collective-permute-done | bytes 172064 | tf_op jit(solution)/shard_map/ppermute | solution.py:363
  49.0 0.7 %collective-permute-start.16 = (f32[21,16,128]{2,1,0:T(8,128)S(1)}, f32[21,16,128]{2,1,0:T(8,128)S(1)}, u32[]{:S(2)}, u32[]{:S(2)}) collective-permute-start(f32[21,16,128]{2,1,0:T(8,128)S(1)} %get-tuple-element.52), channel_id=1, source_target_pairs={{0,1},{1,0},{2,3},{3,2},{4,5},{5,4},{6,7},{7,6},{8,9},{9,8},{10,11... | collective-permute-start | bytes 516104 | tf_op jit(solution)/shard_map/ppermute | solution.py:363
  49.7 1.0 %collective-permute-start.14 = (f32[21,16,128]{2,1,0:T(8,128)S(1)}, f32[21,16,128]{2,1,0:T(8,128)S(1)}, u32[]{:S(2)}, u32[]{:S(2)}) collective-permute-start(f32[21,16,128]{2,1,0:T(8,128)S(1)} %get-tuple-element.51), channel_id=1, source_target_pairs={{0,5},{1,4},{2,7},{3,6},{4,1},{5,0},{6,3},{7,2},{8,13},{9,12},{10,... | collective-permute-start | bytes 516104 | tf_op jit(solution)/shard_map/ppermute | solution.py:363
  50.7 0.0 collective-permute-done.16.refs_3_
  50.8 0.9 %unpack_first.1.refs_4_ = f32[21,128,128]{2,1,0:T(8,128)} custom-call(s32[1]{0:T(128)} %bitcast.j_ref, f32[21,16,128]{2,1,0:T(8,128)S(1)} %collective-permute-done.13.refs_0_, f32[21,16,128]{2,1,0:T(8,128)S(1)} %collective-permute-done.15.refs_1_, f32[21,16,128]{2,1,0:T(8,128)S(1)} %get-tuple-element.49.refs_2_, ...), custom_call_target="tpu_custom_call" | custom-call | tf_op jit(solution)/shard_map/unpack_first/pallas_call | solution.py:160
  51.6 1.6 %collective-permute-done.12.refs_2_ = f32[21,16,128]{2,1,0:T(8,128)S(1)} collective-permute-done((f32[21,16,128]{2,1,0:T(8,128)S(1)}, f32[21,16,128]{2,1,0:T(8,128)S(1)}, u32[]{:S(2)}, u32[]{:S(2)}) %collective-permute-start.12) | collective-permute-done | bytes 172064 | tf_op jit(solution)/shard_map/ppermute | solution.py:363
  53.3 2.6 %collective-permute-done.11.refs_1_ = f32[21,16,128]{2,1,0:T(8,128)S(1)} collective-permute-done((f32[21,16,128]{2,1,0:T(8,128)S(1)}, f32[21,16,128]{2,1,0:T(8,128)S(1)}, u32[]{:S(2)}, u32[]{:S(2)}) %collective-permute-start.11) | collective-permute-done | bytes 172064 | tf_op jit(solution)/shard_map/ppermute | solution.py:363
  55.9 0.6 %collective-permute-done.14.refs_3_ = f32[21,16,128]{2,1,0:T(8,128)S(1)} collective-permute-done((f32[21,16,128]{2,1,0:T(8,128)S(1)}, f32[21,16,128]{2,1,0:T(8,128)S(1)}, u32[]{:S(2)}, u32[]{:S(2)}) %collective-permute-start.14) | collective-permute-done | bytes 172064 | tf_op jit(solution)/shard_map/ppermute | solution.py:363
  56.5 0.9 %unpack_last.1 = f32[21,128,128]{2,1,0:T(8,128)} custom-call(s32[1]{0:T(128)} %bitcast.j_ref, f32[21,16,128]{2,1,0:T(8,128)S(1)} %collective-permute-done.10.refs_0_, f32[21,16,128]{2,1,0:T(8,128)S(1)} %collective-permute-done.11.refs_1_, f32[21,16,128]{2,1,0:T(8,128)S(1)} %collective-permute-done.12.refs_2_, ...), custom_call_target="tpu_custom_call", output_to_operand_aliasing={{}: (5, {})} | custom-call | tf_op jit(solution)/shard_map/unpack_last/pallas_call | solution.py:160
  (31 shorter events, 0.3 us)
Async XLA Ops:
  1.6 7.5 %copy-start.2 = (s32[84]{0:T(128)S(1)}, s32[84]{0:T(128)}, u32[]{:S(2)}) copy-start(s32[84]{0:T(128)} %param.11) | copy-start | bytes 1012
  1.6 7.8 %copy-start = (s32[7,84,84]{2,1,0:T(8,128)S(1)}, s32[7,84,84]{2,1,0:T(8,128)}, u32[]{:S(2)}) copy-start(s32[7,84,84]{2,1,0:T(8,128)} %param.9) | copy-start | bytes 592708
  1.6 8.0 %copy-start.1 = (f32[7,84,84]{2,1,0:T(8,128)S(1)}, f32[7,84,84]{2,1,0:T(8,128)}, u32[]{:S(2)}) copy-start(f32[7,84,84]{2,1,0:T(8,128)} %param.10) | copy-start | bytes 592708
  1.6 10.5 %collective-permute-start.6 = (f32[416,128]{1,0:T(8,128)S(1)}, f32[416,128]{1,0:T(8,128)S(1)}, u32[]{:S(2)}, u32[]{:S(2)}) collective-permute-start(f32[416,128]{1,0:T(8,128)S(1)} %bitcast.32), channel_id=1, source_target_pairs={{0,1},{1,0},{2,3},{3,2},{4,5},{5,4},{6,7},{7,6},{8,9},{9,8},{10,11... | collective-permute-start | bytes 638984 | tf_op jit(solution)/shard_map/ppermute | solution.py:363
  2.1 10.0 %collective-permute-start.2 = (f32[416,128]{1,0:T(8,128)S(1)}, f32[416,128]{1,0:T(8,128)S(1)}, u32[]{:S(2)}, u32[]{:S(2)}) collective-permute-start(f32[416,128]{1,0:T(8,128)S(1)} %bitcast.33), channel_id=1, source_target_pairs={{0,2},{1,3},{2,0},{3,1},{4,6},{5,7},{6,4},{7,5},{8,10},{9,11},{10,... | collective-permute-start | bytes 638984 | tf_op jit(solution)/shard_map/ppermute | solution.py:363
  4.7 10.1 %collective-permute-start.3 = (f32[416,128]{1,0:T(8,128)S(1)}, f32[416,128]{1,0:T(8,128)S(1)}, u32[]{:S(2)}, u32[]{:S(2)}) collective-permute-start(f32[416,128]{1,0:T(8,128)S(1)} %bitcast.31), channel_id=1, source_target_pairs={{0,3},{1,2},{2,1},{3,0},{4,7},{5,6},{6,5},{7,4},{8,11},{9,10},{10,... | collective-permute-start | bytes 638984 | tf_op jit(solution)/shard_map/ppermute | solution.py:363
  7.1 14.8 %collective-permute-start.1 = (f32[416,128]{1,0:T(8,128)}, f32[416,128]{1,0:T(8,128)S(1)}, u32[]{:S(2)}, u32[]{:S(2)}) collective-permute-start(f32[416,128]{1,0:T(8,128)} %bitcast.13), channel_id=1, source_target_pairs={{0,5},{1,4},{2,7},{3,6},{4,1},{5,0},{6,3},{7,2},{8,13},{9,12},{10,... | collective-permute-start | bytes 638984 | tf_op jit(solution)/shard_map/ppermute | solution.py:363
  8.8 12.2 %collective-permute-start = (f32[416,128]{1,0:T(8,128)}, f32[416,128]{1,0:T(8,128)S(1)}, u32[]{:S(2)}, u32[]{:S(2)}) collective-permute-start(f32[416,128]{1,0:T(8,128)} %bitcast.9), channel_id=1, source_target_pairs={{0,4},{1,5},{2,6},{3,7},{4,0},{5,1},{6,2},{7,3},{8,12},{9,13},{10,... | collective-permute-start | bytes 638984 | tf_op jit(solution)/shard_map/ppermute | solution.py:363
  14.9 20.8 %collective-permute-start.7 = (f32[4,368,128]{2,1,0:T(8,128)S(1)}, f32[4,368,128]{2,1,0:T(8,128)S(1)}, u32[]{:S(2)}, u32[]{:S(2)}) collective-permute-start(f32[4,368,128]{2,1,0:T(8,128)S(1)} %mains.3), channel_id=1, source_target_pairs={{4,12},{5,13},{6,14},{7,15},{8,0},{9,1},{10,2},{11,3},{12,20},{13,... | collective-permute-start | bytes 2261000 | tf_op jit(solution)/shard_map/ppermute | solution.py:372
  16.2 10.4 %collective-permute-start.5 = (f32[416,128]{1,0:T(8,128)}, f32[416,128]{1,0:T(8,128)S(1)}, u32[]{:S(2)}, u32[]{:S(2)}) collective-permute-start(f32[416,128]{1,0:T(8,128)} %bitcast.15), channel_id=1, source_target_pairs={{0,7},{1,6},{2,5},{3,4},{4,3},{5,2},{6,1},{7,0},{8,15},{9,14},{10,... | collective-permute-start | bytes 638984 | tf_op jit(solution)/shard_map/ppermute | solution.py:363
  20.6 10.6 %collective-permute-start.4 = (f32[416,128]{1,0:T(8,128)S(1)}, f32[416,128]{1,0:T(8,128)S(1)}, u32[]{:S(2)}, u32[]{:S(2)}) collective-permute-start(f32[416,128]{1,0:T(8,128)S(1)} %bitcast.30), channel_id=1, source_target_pairs={{0,6},{1,7},{2,4},{3,5},{4,2},{5,3},{6,0},{7,1},{8,14},{9,15},{10,... | collective-permute-start | bytes 638984 | tf_op jit(solution)/shard_map/ppermute | solution.py:363
  21.9 20.0 %collective-permute-start.8 = (f32[2,368,128]{2,1,0:T(8,128)S(1)}, f32[2,368,128]{2,1,0:T(8,128)S(1)}, u32[]{:S(2)}, u32[]{:S(2)}) collective-permute-start(f32[2,368,128]{2,1,0:T(8,128)S(1)} %mains.4), channel_id=1, source_target_pairs={{0,8},{1,9},{2,10},{3,11},{8,16},{9,17},{10,18},{11,19},{12,4},{13... | collective-permute-start | bytes 1130504 | tf_op jit(solution)/shard_map/ppermute | solution.py:372
  31.2 11.2 %collective-permute-start.9 = (f32[2,368,128]{2,1,0:T(8,128)S(1)}, f32[2,368,128]{2,1,0:T(8,128)S(1)}, u32[]{:S(2)}, u32[]{:S(2)}) collective-permute-start(f32[2,368,128]{2,1,0:T(8,128)S(1)} %mains.5), channel_id=1, source_target_pairs={{0,8},{1,9},{2,10},{3,11},{8,16},{9,17},{10,18},{11,19},{12,4},{13... | collective-permute-start | bytes 1130504 | tf_op jit(solution)/shard_map/ppermute | solution.py:372
  38.7 8.1 %collective-permute-start.13 = (f32[21,16,128]{2,1,0:T(8,128)S(1)}, f32[21,16,128]{2,1,0:T(8,128)S(1)}, u32[]{:S(2)}, u32[]{:S(2)}) collective-permute-start(f32[21,16,128]{2,1,0:T(8,128)S(1)} %get-tuple-element.44), channel_id=1, source_target_pairs={{0,6},{1,7},{2,4},{3,5},{4,2},{5,3},{6,0},{7,1},{8,14},{9,15},{10,... | collective-permute-start | bytes 516104 | tf_op jit(solution)/shard_map/ppermute | solution.py:363
  40.5 8.5 %collective-permute-start.15 = (f32[21,16,128]{2,1,0:T(8,128)S(1)}, f32[21,16,128]{2,1,0:T(8,128)S(1)}, u32[]{:S(2)}, u32[]{:S(2)}) collective-permute-start(f32[21,16,128]{2,1,0:T(8,128)S(1)} %get-tuple-element.45), channel_id=1, source_target_pairs={{0,7},{1,6},{2,5},{3,4},{4,3},{5,2},{6,1},{7,0},{8,15},{9,14},{10,... | collective-permute-start | bytes 516104 | tf_op jit(solution)/shard_map/ppermute | solution.py:363
  40.5 12.8 %collective-permute-start.12 = (f32[21,16,128]{2,1,0:T(8,128)S(1)}, f32[21,16,128]{2,1,0:T(8,128)S(1)}, u32[]{:S(2)}, u32[]{:S(2)}) collective-permute-start(f32[21,16,128]{2,1,0:T(8,128)S(1)} %get-tuple-element.42), channel_id=1, source_target_pairs={{0,4},{1,5},{2,6},{3,7},{4,0},{5,1},{6,2},{7,3},{8,12},{9,13},{10,... | collective-permute-start | bytes 516104 | tf_op jit(solution)/shard_map/ppermute | solution.py:363
  45.5 7.8 %collective-permute-start.10 = (f32[21,16,128]{2,1,0:T(8,128)S(1)}, f32[21,16,128]{2,1,0:T(8,128)S(1)}, u32[]{:S(2)}, u32[]{:S(2)}) collective-permute-start(f32[21,16,128]{2,1,0:T(8,128)S(1)} %get-tuple-element.47), channel_id=1, source_target_pairs={{0,2},{1,3},{2,0},{3,1},{4,6},{5,7},{6,4},{7,5},{8,10},{9,11},{10,... | collective-permute-start | bytes 516104 | tf_op jit(solution)/shard_map/ppermute | solution.py:363
  46.8 9.0 %collective-permute-start.11 = (f32[21,16,128]{2,1,0:T(8,128)S(1)}, f32[21,16,128]{2,1,0:T(8,128)S(1)}, u32[]{:S(2)}, u32[]{:S(2)}) collective-permute-start(f32[21,16,128]{2,1,0:T(8,128)S(1)} %get-tuple-element.48), channel_id=1, source_target_pairs={{0,3},{1,2},{2,1},{3,0},{4,7},{5,6},{6,5},{7,4},{8,11},{9,10},{10,... | collective-permute-start | bytes 516104 | tf_op jit(solution)/shard_map/ppermute | solution.py:363
  49.0 1.8 %collective-permute-start.16 = (f32[21,16,128]{2,1,0:T(8,128)S(1)}, f32[21,16,128]{2,1,0:T(8,128)S(1)}, u32[]{:S(2)}, u32[]{:S(2)}) collective-permute-start(f32[21,16,128]{2,1,0:T(8,128)S(1)} %get-tuple-element.52), channel_id=1, source_target_pairs={{0,1},{1,0},{2,3},{3,2},{4,5},{5,4},{6,7},{7,6},{8,9},{9,8},{10,11... | collective-permute-start | bytes 516104 | tf_op jit(solution)/shard_map/ppermute | solution.py:363
  49.7 6.7 %collective-permute-start.14 = (f32[21,16,128]{2,1,0:T(8,128)S(1)}, f32[21,16,128]{2,1,0:T(8,128)S(1)}, u32[]{:S(2)}, u32[]{:S(2)}) collective-permute-start(f32[21,16,128]{2,1,0:T(8,128)S(1)} %get-tuple-element.51), channel_id=1, source_target_pairs={{0,5},{1,4},{2,7},{3,6},{4,1},{5,0},{6,3},{7,2},{8,13},{9,12},{10,... | collective-permute-start | bytes 516104 | tf_op jit(solution)/shard_map/ppermute | solution.py:363

commit v18 on v17

--- a/solution.py
+++ b/solution.py
@@ -405,10 +405,9 @@
         back[r] = swap(out[r], r)
     for n in range(half):
         ahead = [back[r] for r in first[:n]]
-        ahead = [*own_out, *ahead] if n else []
-        back[modes + n] = swap(after(out[modes + n], *ahead), modes + n)
+        back[modes + n] = swap(after(out[modes + n], *own_out, *ahead), modes + n)
     for r in range(half):
-        back[r] = swap(after(out[r], *[back[r] for r in first]) if r else out[r], r)
+        back[r] = swap(after(out[r], back[first[-1]]) if r else out[r], r)
     last = range(half, modes + half)
     shape = (quota, height, width)
     whole = unpack({r: back[r] for r in back if r not in last}, j, shape, lay)

time: 57.5 us -> 60.3 us (1.049)
  waiting for transfers between devices: 16.9 us -> 18.7 us
  starting transfers between devices: 24.4 us -> 25.3 us
    ppermute x3, waiting for transfers between devices: 1.35 us -> 2.63 us  [shift(): return lax.ppermute(mains(pieces, lay), axes, pairs)]
    ppermute x14, starting transfers between devices: 16.2 us -> 17.1 us  [swap(): return lax.ppermute(piece, axes, [(d, d ^ r) for d in range(devices)])]
where the time goes in v18:
time: 60.3 us; the launch traced here: 60.1 us
  starting transfers between devices  25.3 us (42%)
  waiting for transfers between devices  18.7 us (31%)
  Pallas kernels  11.8 us (20%)
  other arithmetic  1.65 us (3%)
  local copies, waits for them, and re-layouts  1.62 us (3%)
  matrix products  0.69 us (1%)
    ppermute x14, starting transfers between devices, swap(): return lax.ppermute(piece, axes, [(d, d ^ r) for d in range(devices)])  17.1 us
    ppermute x14, waiting for transfers between devices, swap(): return lax.ppermute(piece, axes, [(d, d ^ r) for d in range(devices)])  16.1 us
    ppermute x3, starting transfers between devices, shift(): return lax.ppermute(mains(pieces, lay), axes, pairs)  8.21 us
    pallas_call x2, Pallas kernels, stencil(): pl.pallas_call(kernel, out_shape=[jax.ShapeDtypeStruct((lay.quota, rows,...  6.05 us
    pallas_call x2, Pallas kernels, pack(): pl.pallas_call(kernel, out_shape=[pltpu.VMEM(shape, jnp.float32)] * modes...  3.88 us
    ppermute x3, waiting for transfers between devices, shift(): return lax.ppermute(mains(pieces, lay), axes, pairs)  2.63 us
    pallas_call x2, Pallas kernels, unpack(): pl.pallas_call(kernel, out_shape=pltpu.HBM(shape, jnp.float32), in_specs=...  1.74 us
  transfers between devices with their start and end apart: 17, of which 9 were waited for; matrix products, arithmetic and copies ran while one was open for 7% of the time, Pallas kernels for 16%

profile of v18, /device:TPU:0, one launch (start us, length us, event | category | flops | bytes accessed | tf_op | source)
XLA Modules:
  0.0 60.1 jit_solution(7987700228821828355)
XLA Ops:
  0.0 1.5 %pack_own.1 = (f32[26,16,128]{2,1,0:T(8,128)S(1)}, f32[26,16,128]{2,1,0:T(8,128)S(1)}, f32[26,16,128]{2,1,0:T(8,128)S(1)}, f32[26,16,128]{2,1,0:T(8,128)S(1)}) custom-call(s32[1]{0:T(128)} %bitcast.j_ref, f32[21,128,128]{2,1,0:T(8,128)} %bitcast.34, f32[1,128,128]{2,1,0:T(8,128)} %mean_ref.3, f32[6,128,128]{2,1,0:T(8,128)} %bitcast.36), custom_call_target="tpu_custom_call" | custom-call | tf_op jit(solution)/shard_map/pack_own/pallas_call | solution.py:127
  1.6 0.0 copy-start.2
  1.6 0.0 copy-start
  1.6 0.0 copy-start.1
  1.6 0.5 collective-permute-start.6
  2.1 2.6 %collective-permute-start.2 = (f32[416,128]{1,0:T(8,128)S(1)}, f32[416,128]{1,0:T(8,128)S(1)}, u32[]{:S(2)}, u32[]{:S(2)}) collective-permute-start(f32[416,128]{1,0:T(8,128)S(1)} %bitcast.33), channel_id=1, source_target_pairs={{0,2},{1,3},{2,0},{3,1},{4,6},{5,7},{6,4},{7,5},{8,10},{9,11},{10,... | collective-permute-start | bytes 638984 | tf_op jit(solution)/shard_map/ppermute | solution.py:363
  4.7 0.1 collective-permute-start.3
  4.8 2.3 %pack_crossing.1 = (f32[26,16,128]{2,1,0:T(8,128)}, f32[26,16,128]{2,1,0:T(8,128)}, f32[26,16,128]{2,1,0:T(8,128)S(1)}, f32[26,16,128]{2,1,0:T(8,128)}) custom-call(s32[1]{0:T(128)} %bitcast.j_ref, f32[21,128,128]{2,1,0:T(8,128)} %bitcast.35, f32[1,128,128]{2,1,0:T(8,128)} %mean_ref.3, f32[6,128,128]{2,1,0:T(8,128)} %bitcast.37), custom_call_target="tpu_custom_call" | custom-call | tf_op jit(solution)/shard_map/pack_crossing/pallas_call | solution.py:127
  7.1 1.7 %collective-permute-start.1 = (f32[416,128]{1,0:T(8,128)}, f32[416,128]{1,0:T(8,128)S(1)}, u32[]{:S(2)}, u32[]{:S(2)}) collective-permute-start(f32[416,128]{1,0:T(8,128)} %bitcast.13), channel_id=1, source_target_pairs={{0,5},{1,4},{2,7},{3,6},{4,1},{5,0},{6,3},{7,2},{8,13},{9,12},{10,... | collective-permute-start | bytes 638984 | tf_op jit(solution)/shard_map/ppermute | solution.py:363
  8.8 0.1 collective-permute-start
  9.0 0.1 iota_compare_fusion.10
  9.1 0.1 broadcast_in_dim.201
  9.2 0.1 select_reduce_fusion.13
  9.3 0.1 eq.98
  9.3 0.2 copy.12
  9.5 0.2 copy.13
  9.7 0.4 fusion
  10.1 0.3 fusion.10
  10.4 0.1 fusion.5
  10.6 0.2 select_reduce_fusion.4
  10.8 0.1 select_reduce_fusion.6
  11.0 0.1 broadcast_add_fusion.1
  11.1 0.1 select_reduce_fusion.1
  11.2 0.2 select_reduce_fusion.5
  11.4 0.1 reshape.162
  11.5 0.1 copy.14
  11.6 0.2 reshape.163
  11.8 0.1 copy.16
  11.9 0.2 reshape.170
  12.1 0.0 collective-permute-done.2.refs_2_.refs_6_
  12.1 0.0 collective-permute-done.6.refs_1_.refs_5_
  12.1 2.7 %collective-permute-done.3.refs_3_.refs_7_ = f32[416,128]{1,0:T(8,128)S(1)} collective-permute-done((f32[416,128]{1,0:T(8,128)S(1)}, f32[416,128]{1,0:T(8,128)S(1)}, u32[]{:S(2)}, u32[]{:S(2)}) %collective-permute-start.3) | collective-permute-done | bytes 213024 | tf_op jit(solution)/shard_map/ppermute | solution.py:363
  14.9 1.3 %collective-permute-start.7 = (f32[4,368,128]{2,1,0:T(8,128)S(1)}, f32[4,368,128]{2,1,0:T(8,128)S(1)}, u32[]{:S(2)}, u32[]{:S(2)}) collective-permute-start(f32[4,368,128]{2,1,0:T(8,128)S(1)} %mains.3), channel_id=1, source_target_pairs={{4,12},{5,13},{6,14},{7,15},{8,0},{9,1},{10,2},{11,3},{12,20},{13,... | collective-permute-start | bytes 2261000 | tf_op jit(solution)/shard_map/ppermute | solution.py:372
  16.2 4.4 %collective-permute-start.5 = (f32[416,128]{1,0:T(8,128)}, f32[416,128]{1,0:T(8,128)S(1)}, u32[]{:S(2)}, u32[]{:S(2)}) collective-permute-start(f32[416,128]{1,0:T(8,128)} %bitcast.15), channel_id=1, source_target_pairs={{0,7},{1,6},{2,5},{3,4},{4,3},{5,2},{6,1},{7,0},{8,15},{9,14},{10,... | collective-permute-start | bytes 638984 | tf_op jit(solution)/shard_map/ppermute | solution.py:363
  20.6 0.5 collective-permute-start.4
  21.1 0.0 collective-permute-done.refs_0_.refs_4_
  21.1 0.1 select_reduce_fusion.11
  21.2 0.1 select_reduce_fusion.7
  21.3 0.1 copy.17
  21.4 0.1 reshape.171
  21.5 0.2 select_reduce_fusion.8
  21.7 0.1 copy.15
  21.8 0.1 reshape.169
  21.9 3.5 %collective-permute-start.8 = (f32[2,368,128]{2,1,0:T(8,128)S(1)}, f32[2,368,128]{2,1,0:T(8,128)S(1)}, u32[]{:S(2)}, u32[]{:S(2)}) collective-permute-start(f32[2,368,128]{2,1,0:T(8,128)S(1)} %mains.4), channel_id=1, source_target_pairs={{0,8},{1,9},{2,10},{3,11},{8,16},{9,17},{10,18},{11,19},{12,4},{13... | collective-permute-start | bytes 1130504 | tf_op jit(solution)/shard_map/ppermute | solution.py:372
  25.4 1.1 %collective-permute-done.5.refs_3_.refs_1_.refs_7_ = f32[416,128]{1,0:T(8,128)S(1)} collective-permute-done((f32[416,128]{1,0:T(8,128)}, f32[416,128]{1,0:T(8,128)S(1)}, u32[]{:S(2)}, u32[]{:S(2)}) %collective-permute-start.5) | collective-permute-done | bytes 213024 | tf_op jit(solution)/shard_map/ppermute | solution.py:363
  26.6 4.6 %collective-permute-done.4.refs_2_.refs_0_.refs_6_ = f32[416,128]{1,0:T(8,128)S(1)} collective-permute-done((f32[416,128]{1,0:T(8,128)S(1)}, f32[416,128]{1,0:T(8,128)S(1)}, u32[]{:S(2)}, u32[]{:S(2)}) %collective-permute-start.4) | collective-permute-done | bytes 213024 | tf_op jit(solution)/shard_map/ppermute | solution.py:363
  31.2 3.5 %collective-permute-start.9 = (f32[2,368,128]{2,1,0:T(8,128)S(1)}, f32[2,368,128]{2,1,0:T(8,128)S(1)}, u32[]{:S(2)}, u32[]{:S(2)}) collective-permute-start(f32[2,368,128]{2,1,0:T(8,128)S(1)} %mains.5), channel_id=1, source_target_pairs={{0,8},{1,9},{2,10},{3,11},{8,16},{9,17},{10,18},{11,19},{12,4},{13... | collective-permute-start | bytes 1130504 | tf_op jit(solution)/shard_map/ppermute | solution.py:372
  34.7 0.1 pad_maximum_fusion.1.factor_ref
  34.8 0.1 pad_add_fusion.2.index_ref
  34.8 0.9 %collective-permute-done.7.refs_8_ = f32[4,368,128]{2,1,0:T(8,128)S(1)} collective-permute-done((f32[4,368,128]{2,1,0:T(8,128)S(1)}, f32[4,368,128]{2,1,0:T(8,128)S(1)}, u32[]{:S(2)}, u32[]{:S(2)}) %collective-permute-start.7) | collective-permute-done | bytes 753696 | tf_op jit(solution)/shard_map/ppermute | solution.py:372
  35.7 3.0 %stencil_crossing.1 = (f32[21,16,128]{2,1,0:T(8,128)S(1)}, f32[21,16,128]{2,1,0:T(8,128)S(1)}, f32[21,16,128]{2,1,0:T(8,128)S(1)}, f32[21,16,128]{2,1,0:T(8,128)S(1)}) custom-call(s32[1]{0:T(128)} %bitcast.j_ref, s32[770]{0:T(1024)S(1)} %pad_add_fusion.2.index_ref, f32[392]{0:T(512)S(1)} %pad_maximum_fusion.1.factor_ref, ...), custom_call_target="tpu_custom_call" | custom-call | tf_op jit(solution)/shard_map/stencil_crossing/pallas_call | solution.py:330
  38.7 0.8 %collective-permute-start.15 = (f32[21,16,128]{2,1,0:T(8,128)S(1)}, f32[21,16,128]{2,1,0:T(8,128)S(1)}, u32[]{:S(2)}, u32[]{:S(2)}) collective-permute-start(f32[21,16,128]{2,1,0:T(8,128)S(1)} %get-tuple-element.46), channel_id=1, source_target_pairs={{0,7},{1,6},{2,5},{3,4},{4,3},{5,2},{6,1},{7,0},{8,15},{9,14},{10,... | collective-permute-start | bytes 516104 | tf_op jit(solution)/shard_map/ppermute | solution.py:363
  39.6 1.1 %collective-permute-start.13 = (f32[21,16,128]{2,1,0:T(8,128)S(1)}, f32[21,16,128]{2,1,0:T(8,128)S(1)}, u32[]{:S(2)}, u32[]{:S(2)}) collective-permute-start(f32[21,16,128]{2,1,0:T(8,128)S(1)} %get-tuple-element.45), channel_id=1, source_target_pairs={{0,6},{1,7},{2,4},{3,5},{4,2},{5,3},{6,0},{7,1},{8,14},{9,15},{10,... | collective-permute-start | bytes 516104 | tf_op jit(solution)/shard_map/ppermute | solution.py:363
  40.7 1.8 %collective-permute-done.9.refs_9_ = f32[2,368,128]{2,1,0:T(8,128)S(1)} collective-permute-done((f32[2,368,128]{2,1,0:T(8,128)S(1)}, f32[2,368,128]{2,1,0:T(8,128)S(1)}, u32[]{:S(2)}, u32[]{:S(2)}) %collective-permute-start.9) | collective-permute-done | bytes 376864 | tf_op jit(solution)/shard_map/ppermute | solution.py:372
  42.4 3.0 %stencil_own.1 = (f32[21,16,128]{2,1,0:T(8,128)S(1)}, f32[21,16,128]{2,1,0:T(8,128)S(1)}, f32[21,16,128]{2,1,0:T(8,128)S(1)}, f32[21,16,128]{2,1,0:T(8,128)S(1)}) custom-call(s32[1]{0:T(128)} %bitcast.j_ref, s32[770]{0:T(1024)S(1)} %pad_add_fusion.2.index_ref, f32[392]{0:T(512)S(1)} %pad_maximum_fusion.1.factor_ref, f32[416,128]{1,0:T(8,128)S(1)} %bitcast.29, ...), custom_call_target="tpu_custom_call" | custom-call | tf_op jit(solution)/shard_map/stencil_own/pallas_call | solution.py:330
  45.5 1.3 %collective-permute-start.10 = (f32[21,16,128]{2,1,0:T(8,128)S(1)}, f32[21,16,128]{2,1,0:T(8,128)S(1)}, u32[]{:S(2)}, u32[]{:S(2)}) collective-permute-start(f32[21,16,128]{2,1,0:T(8,128)S(1)} %get-tuple-element.48), channel_id=1, source_target_pairs={{0,2},{1,3},{2,0},{3,1},{4,6},{5,7},{6,4},{7,5},{8,10},{9,11},{10,... | collective-permute-start | bytes 516104 | tf_op jit(solution)/shard_map/ppermute | solution.py:363
  46.8 3.6 %collective-permute-start.12 = (f32[21,16,128]{2,1,0:T(8,128)S(1)}, f32[21,16,128]{2,1,0:T(8,128)S(1)}, u32[]{:S(2)}, u32[]{:S(2)}) collective-permute-start(f32[21,16,128]{2,1,0:T(8,128)S(1)} %get-tuple-element.52), channel_id=1, source_target_pairs={{0,4},{1,5},{2,6},{3,7},{4,0},{5,1},{6,2},{7,3},{8,12},{9,13},{10,... | collective-permute-start | bytes 516104 | tf_op jit(solution)/shard_map/ppermute | solution.py:363
  50.4 0.3 collective-permute-start.16
  50.8 1.1 %collective-permute-done.16.refs_3_ = f32[21,16,128]{2,1,0:T(8,128)S(1)} collective-permute-done((f32[21,16,128]{2,1,0:T(8,128)S(1)}, f32[21,16,128]{2,1,0:T(8,128)S(1)}, u32[]{:S(2)}, u32[]{:S(2)}) %collective-permute-start.16) | collective-permute-done | bytes 172064 | tf_op jit(solution)/shard_map/ppermute | solution.py:363
  51.8 0.9 %unpack_first.1.refs_4_ = f32[21,128,128]{2,1,0:T(8,128)} custom-call(s32[1]{0:T(128)} %bitcast.j_ref, f32[21,16,128]{2,1,0:T(8,128)S(1)} %collective-permute-done.13.refs_0_, f32[21,16,128]{2,1,0:T(8,128)S(1)} %collective-permute-done.15.refs_1_, f32[21,16,128]{2,1,0:T(8,128)S(1)} %get-tuple-element.50.refs_2_, ...), custom_call_target="tpu_custom_call" | custom-call | tf_op jit(solution)/shard_map/unpack_first/pallas_call | solution.py:160
  52.7 2.9 %collective-permute-done.12.refs_2_ = f32[21,16,128]{2,1,0:T(8,128)S(1)} collective-permute-done((f32[21,16,128]{2,1,0:T(8,128)S(1)}, f32[21,16,128]{2,1,0:T(8,128)S(1)}, u32[]{:S(2)}, u32[]{:S(2)}) %collective-permute-start.12) | collective-permute-done | bytes 172064 | tf_op jit(solution)/shard_map/ppermute | solution.py:363
  55.6 1.2 %collective-permute-done.11.refs_1_ = f32[21,16,128]{2,1,0:T(8,128)S(1)} collective-permute-done((f32[21,16,128]{2,1,0:T(8,128)S(1)}, f32[21,16,128]{2,1,0:T(8,128)S(1)}, u32[]{:S(2)}, u32[]{:S(2)}) %collective-permute-start.11) | collective-permute-done | bytes 172064 | tf_op jit(solution)/shard_map/ppermute | solution.py:363
  56.8 2.3 %collective-permute-done.14.refs_3_ = f32[21,16,128]{2,1,0:T(8,128)S(1)} collective-permute-done((f32[21,16,128]{2,1,0:T(8,128)S(1)}, f32[21,16,128]{2,1,0:T(8,128)S(1)}, u32[]{:S(2)}, u32[]{:S(2)}) %collective-permute-start.14) | collective-permute-done | bytes 172064 | tf_op jit(solution)/shard_map/ppermute | solution.py:363
  59.2 0.9 %unpack_last.1 = f32[21,128,128]{2,1,0:T(8,128)} custom-call(s32[1]{0:T(128)} %bitcast.j_ref, f32[21,16,128]{2,1,0:T(8,128)S(1)} %collective-permute-done.10.refs_0_, f32[21,16,128]{2,1,0:T(8,128)S(1)} %collective-permute-done.11.refs_1_, f32[21,16,128]{2,1,0:T(8,128)S(1)} %collective-permute-done.12.refs_2_, ...), custom_call_target="tpu_custom_call", output_to_operand_aliasing={{}: (5, {})} | custom-call | tf_op jit(solution)/shard_map/unpack_last/pallas_call | solution.py:160
  (31 shorter events, 0.3 us)
Async XLA Ops:
  1.6 7.5 %copy-start.2 = (s32[84]{0:T(128)S(1)}, s32[84]{0:T(128)}, u32[]{:S(2)}) copy-start(s32[84]{0:T(128)} %param.11) | copy-start | bytes 1012
  1.6 7.8 %copy-start = (s32[7,84,84]{2,1,0:T(8,128)S(1)}, s32[7,84,84]{2,1,0:T(8,128)}, u32[]{:S(2)}) copy-start(s32[7,84,84]{2,1,0:T(8,128)} %param.9) | copy-start | bytes 592708
  1.6 8.0 %copy-start.1 = (f32[7,84,84]{2,1,0:T(8,128)S(1)}, f32[7,84,84]{2,1,0:T(8,128)}, u32[]{:S(2)}) copy-start(f32[7,84,84]{2,1,0:T(8,128)} %param.10) | copy-start | bytes 592708
  1.6 10.5 %collective-permute-start.6 = (f32[416,128]{1,0:T(8,128)S(1)}, f32[416,128]{1,0:T(8,128)S(1)}, u32[]{:S(2)}, u32[]{:S(2)}) collective-permute-start(f32[416,128]{1,0:T(8,128)S(1)} %bitcast.32), channel_id=1, source_target_pairs={{0,1},{1,0},{2,3},{3,2},{4,5},{5,4},{6,7},{7,6},{8,9},{9,8},{10,11... | collective-permute-start | bytes 638984 | tf_op jit(solution)/shard_map/ppermute | solution.py:363
  2.1 10.0 %collective-permute-start.2 = (f32[416,128]{1,0:T(8,128)S(1)}, f32[416,128]{1,0:T(8,128)S(1)}, u32[]{:S(2)}, u32[]{:S(2)}) collective-permute-start(f32[416,128]{1,0:T(8,128)S(1)} %bitcast.33), channel_id=1, source_target_pairs={{0,2},{1,3},{2,0},{3,1},{4,6},{5,7},{6,4},{7,5},{8,10},{9,11},{10,... | collective-permute-start | bytes 638984 | tf_op jit(solution)/shard_map/ppermute | solution.py:363
  4.7 10.1 %collective-permute-start.3 = (f32[416,128]{1,0:T(8,128)S(1)}, f32[416,128]{1,0:T(8,128)S(1)}, u32[]{:S(2)}, u32[]{:S(2)}) collective-permute-start(f32[416,128]{1,0:T(8,128)S(1)} %bitcast.31), channel_id=1, source_target_pairs={{0,3},{1,2},{2,1},{3,0},{4,7},{5,6},{6,5},{7,4},{8,11},{9,10},{10,... | collective-permute-start | bytes 638984 | tf_op jit(solution)/shard_map/ppermute | solution.py:363
  7.1 14.8 %collective-permute-start.1 = (f32[416,128]{1,0:T(8,128)}, f32[416,128]{1,0:T(8,128)S(1)}, u32[]{:S(2)}, u32[]{:S(2)}) collective-permute-start(f32[416,128]{1,0:T(8,128)} %bitcast.13), channel_id=1, source_target_pairs={{0,5},{1,4},{2,7},{3,6},{4,1},{5,0},{6,3},{7,2},{8,13},{9,12},{10,... | collective-permute-start | bytes 638984 | tf_op jit(solution)/shard_map/ppermute | solution.py:363
  8.8 12.2 %collective-permute-start = (f32[416,128]{1,0:T(8,128)}, f32[416,128]{1,0:T(8,128)S(1)}, u32[]{:S(2)}, u32[]{:S(2)}) collective-permute-start(f32[416,128]{1,0:T(8,128)} %bitcast.9), channel_id=1, source_target_pairs={{0,4},{1,5},{2,6},{3,7},{4,0},{5,1},{6,2},{7,3},{8,12},{9,13},{10,... | collective-permute-start | bytes 638984 | tf_op jit(solution)/shard_map/ppermute | solution.py:363
  14.9 20.8 %collective-permute-start.7 = (f32[4,368,128]{2,1,0:T(8,128)S(1)}, f32[4,368,128]{2,1,0:T(8,128)S(1)}, u32[]{:S(2)}, u32[]{:S(2)}) collective-permute-start(f32[4,368,128]{2,1,0:T(8,128)S(1)} %mains.3), channel_id=1, source_target_pairs={{4,12},{5,13},{6,14},{7,15},{8,0},{9,1},{10,2},{11,3},{12,20},{13,... | collective-permute-start | bytes 2261000 | tf_op jit(solution)/shard_map/ppermute | solution.py:372
  16.2 10.4 %collective-permute-start.5 = (f32[416,128]{1,0:T(8,128)}, f32[416,128]{1,0:T(8,128)S(1)}, u32[]{:S(2)}, u32[]{:S(2)}) collective-permute-start(f32[416,128]{1,0:T(8,128)} %bitcast.15), channel_id=1, source_target_pairs={{0,7},{1,6},{2,5},{3,4},{4,3},{5,2},{6,1},{7,0},{8,15},{9,14},{10,... | collective-permute-start | bytes 638984 | tf_op jit(solution)/shard_map/ppermute | solution.py:363
  20.6 10.6 %collective-permute-start.4 = (f32[416,128]{1,0:T(8,128)S(1)}, f32[416,128]{1,0:T(8,128)S(1)}, u32[]{:S(2)}, u32[]{:S(2)}) collective-permute-start(f32[416,128]{1,0:T(8,128)S(1)} %bitcast.30), channel_id=1, source_target_pairs={{0,6},{1,7},{2,4},{3,5},{4,2},{5,3},{6,0},{7,1},{8,14},{9,15},{10,... | collective-permute-start | bytes 638984 | tf_op jit(solution)/shard_map/ppermute | solution.py:363
  21.9 18.7 %collective-permute-start.8 = (f32[2,368,128]{2,1,0:T(8,128)S(1)}, f32[2,368,128]{2,1,0:T(8,128)S(1)}, u32[]{:S(2)}, u32[]{:S(2)}) collective-permute-start(f32[2,368,128]{2,1,0:T(8,128)S(1)} %mains.4), channel_id=1, source_target_pairs={{0,8},{1,9},{2,10},{3,11},{8,16},{9,17},{10,18},{11,19},{12,4},{13... | collective-permute-start | bytes 1130504 | tf_op jit(solution)/shard_map/ppermute | solution.py:372
  31.2 11.2 %collective-permute-start.9 = (f32[2,368,128]{2,1,0:T(8,128)S(1)}, f32[2,368,128]{2,1,0:T(8,128)S(1)}, u32[]{:S(2)}, u32[]{:S(2)}) collective-permute-start(f32[2,368,128]{2,1,0:T(8,128)S(1)} %mains.5), channel_id=1, source_target_pairs={{0,8},{1,9},{2,10},{3,11},{8,16},{9,17},{10,18},{11,19},{12,4},{13... | collective-permute-start | bytes 1130504 | tf_op jit(solution)/shard_map/ppermute | solution.py:372
  38.7 11.7 %collective-permute-start.15 = (f32[21,16,128]{2,1,0:T(8,128)S(1)}, f32[21,16,128]{2,1,0:T(8,128)S(1)}, u32[]{:S(2)}, u32[]{:S(2)}) collective-permute-start(f32[21,16,128]{2,1,0:T(8,128)S(1)} %get-tuple-element.46), channel_id=1, source_target_pairs={{0,7},{1,6},{2,5},{3,4},{4,3},{5,2},{6,1},{7,0},{8,15},{9,14},{10,... | collective-permute-start | bytes 516104 | tf_op jit(solution)/shard_map/ppermute | solution.py:363
  39.6 11.2 %collective-permute-start.13 = (f32[21,16,128]{2,1,0:T(8,128)S(1)}, f32[21,16,128]{2,1,0:T(8,128)S(1)}, u32[]{:S(2)}, u32[]{:S(2)}) collective-permute-start(f32[21,16,128]{2,1,0:T(8,128)S(1)} %get-tuple-element.45), channel_id=1, source_target_pairs={{0,6},{1,7},{2,4},{3,5},{4,2},{5,3},{6,0},{7,1},{8,14},{9,15},{10,... | collective-permute-start | bytes 516104 | tf_op jit(solution)/shard_map/ppermute | solution.py:363
  45.5 10.2 %collective-permute-start.10 = (f32[21,16,128]{2,1,0:T(8,128)S(1)}, f32[21,16,128]{2,1,0:T(8,128)S(1)}, u32[]{:S(2)}, u32[]{:S(2)}) collective-permute-start(f32[21,16,128]{2,1,0:T(8,128)S(1)} %get-tuple-element.48), channel_id=1, source_target_pairs={{0,2},{1,3},{2,0},{3,1},{4,6},{5,7},{6,4},{7,5},{8,10},{9,11},{10,... | collective-permute-start | bytes 516104 | tf_op jit(solution)/shard_map/ppermute | solution.py:363
  46.8 10.0 %collective-permute-start.11 = (f32[21,16,128]{2,1,0:T(8,128)S(1)}, f32[21,16,128]{2,1,0:T(8,128)S(1)}, u32[]{:S(2)}, u32[]{:S(2)}) collective-permute-start(f32[21,16,128]{2,1,0:T(8,128)S(1)} %get-tuple-element.49), channel_id=1, source_target_pairs={{0,3},{1,2},{2,1},{3,0},{4,7},{5,6},{6,5},{7,4},{8,11},{9,10},{10,... | collective-permute-start | bytes 516104 | tf_op jit(solution)/shard_map/ppermute | solution.py:363
  46.8 8.8 %collective-permute-start.12 = (f32[21,16,128]{2,1,0:T(8,128)S(1)}, f32[21,16,128]{2,1,0:T(8,128)S(1)}, u32[]{:S(2)}, u32[]{:S(2)}) collective-permute-start(f32[21,16,128]{2,1,0:T(8,128)S(1)} %get-tuple-element.52), channel_id=1, source_target_pairs={{0,4},{1,5},{2,6},{3,7},{4,0},{5,1},{6,2},{7,3},{8,12},{9,13},{10,... | collective-permute-start | bytes 516104 | tf_op jit(solution)/shard_map/ppermute | solution.py:363
  50.4 1.4 %collective-permute-start.16 = (f32[21,16,128]{2,1,0:T(8,128)S(1)}, f32[21,16,128]{2,1,0:T(8,128)S(1)}, u32[]{:S(2)}, u32[]{:S(2)}) collective-permute-start(f32[21,16,128]{2,1,0:T(8,128)S(1)} %get-tuple-element.54), channel_id=1, source_target_pairs={{0,1},{1,0},{2,3},{3,2},{4,5},{5,4},{6,7},{7,6},{8,9},{9,8},{10,11... | collective-permute-start | bytes 516104 | tf_op jit(solution)/shard_map/ppermute | solution.py:363
  50.8 8.4 %collective-permute-start.14 = (f32[21,16,128]{2,1,0:T(8,128)S(1)}, f32[21,16,128]{2,1,0:T(8,128)S(1)}, u32[]{:S(2)}, u32[]{:S(2)}) collective-permute-start(f32[21,16,128]{2,1,0:T(8,128)S(1)} %get-tuple-element.53), channel_id=1, source_target_pairs={{0,5},{1,4},{2,7},{3,6},{4,1},{5,0},{6,3},{7,2},{8,13},{9,12},{10,... | collective-permute-start | bytes 516104 | tf_op jit(solution)/shard_map/ppermute | solution.py:363
